TPU v7x, 32 devices: a whole 2x2x4 slice. The times are simulated.
32 devices in a mesh: seq: 4 (over x, core), fsdp: 8 (over z, y).
Axes of the slice: x: 2, y: 2, z: 4, core: 2. Of those that a mesh axis runs over, the one named last changes fastest.
Arguments:
- tokens: bfloat16 [8, 2048, 1152], P('fsdp', 'seq'), may hold values from -6 to 6
- patch_mask: int32 [8, 2048], P('fsdp', 'seq'), may hold values from 0 to 1, as said below
- gain_one: bfloat16 [1152], P('seq'), may hold values from 0.25 to 1.75
- shift_one: bfloat16 [1152], P('seq'), may hold values from -3 to 3
- w_query: bfloat16 [1152, 1152], P('fsdp', 'seq'), may hold values from -0.25 to 0.25
- b_query: bfloat16 [1152], P('seq'), may hold values from -3 to 3
- w_key: bfloat16 [1152, 1152], P('fsdp', 'seq'), may hold values from -0.25 to 0.25
- w_value: bfloat16 [1152, 1152], P('fsdp', 'seq'), may hold values from -0.1875 to 0.1875
- b_value: bfloat16 [1152], P('seq'), may hold values from -3 to 3
- w_output: bfloat16 [1152, 1152], P('fsdp', 'seq'), may hold values from -1.5 to 1.5
- b_output: bfloat16 [1152], P('seq'), may hold values from -3 to 3
- gain_two: bfloat16 [1152], P('seq'), may hold values from 0.25 to 1.75
- shift_two: bfloat16 [1152], P('seq'), may hold values from -3 to 3
- w_up: bfloat16 [1152, 4304], P('fsdp', 'seq'), may hold values from -0.1875 to 0.1875
- b_up: bfloat16 [4304], P('seq'), may hold values from -3 to 3
- w_down: bfloat16 [4304, 1152], P('fsdp', 'seq'), may hold values from -0.09375 to 0.09375
- b_down: bfloat16 [1152], P('seq'), may hold values from -3 to 3
- cotangent: bfloat16 [8, 2048, 1152], P('fsdp', 'seq'), may hold values from -6 to 6
Outputs:
- layer_out: bfloat16 [8, 2048, 1152], P('fsdp', 'seq')
- grad_tokens: bfloat16 [8, 2048, 1152], P('fsdp', 'seq')
- grad_gain_one: float32 [1152], P('seq')
- grad_shift_one: float32 [1152], P('seq')
- grad_w_query: float32 [1152, 1152], P('fsdp', 'seq')
- grad_b_query: float32 [1152], P('seq')
- grad_w_key: float32 [1152, 1152], P('fsdp', 'seq')
- grad_w_value: float32 [1152, 1152], P('fsdp', 'seq')
- grad_b_value: float32 [1152], P('seq')
- grad_w_output: float32 [1152, 1152], P('fsdp', 'seq')
- grad_b_output: float32 [1152], P('seq')
- grad_gain_two: float32 [1152], P('seq')
- grad_shift_two: float32 [1152], P('seq')
- grad_w_up: float32 [1152, 4304], P('fsdp', 'seq')
- grad_b_up: float32 [4304], P('seq')
- grad_w_down: float32 [4304, 1152], P('fsdp', 'seq')
- grad_b_down: float32 [1152], P('seq')
Inputs may be any that keep to these rules, and one draw needn't show every extreme that they name: `patch_mask`: in every image the ones form a prefix of 1984 or more positions and the rest are zeros.
All inputs are finite; a program needn't handle non-finite values.
Results may differ from a plain program's by a relative error of at most 0.018.
Values may be sent and summed in bfloat16 or wider, within the bound.
No kernel may reach another device: no remote copies, remote signals or barrier semaphores. Data moves between devices by JAX's collectives and lax.ppermute only.
A program may use at most 192 MiB of HBM per device.

v0:
```python
import jax
import jax.numpy as jnp
from jax import lax
from jax.sharding import PartitionSpec as P

HEAD = 72


EPS = 1e-06
ROOT = 0.7978845608028654
CUBIC = 0.044715
NEG = -1e30


def norm_rows(value, gain, shift):
    mean = jnp.mean(value, axis=-1, keepdims=True)
    centered = value - mean
    inverse = lax.rsqrt(jnp.mean(centered * centered, axis=-1, keepdims=True) + EPS)
    normed = centered * inverse
    return (normed * gain + shift, normed, inverse)


def norm_back(grad_out, normed, inverse, gain):
    scaled = grad_out * gain
    first = jnp.mean(scaled, axis=-1, keepdims=True)
    second = jnp.mean(scaled * normed, axis=-1, keepdims=True)
    return inverse * (scaled - first - normed * second)


def gelu_tanh(value):
    inner = jnp.tanh(ROOT * (value + CUBIC * value * value * value))
    return 0.5 * value * (1.0 + inner)


def gelu_slope(value):
    inner = jnp.tanh(ROOT * (value + CUBIC * value * value * value))
    return 0.5 * (1.0 + inner) + 0.5 * value * (1.0 - inner * inner) * ROOT * (
        1.0 + 3.0 * CUBIC * value * value
    )


def split_heads(value):
    return value.reshape(value.shape[0], value.shape[1], value.shape[2] // HEAD, HEAD)


def to_blocks(value, span):
    shaped = value.reshape((value.shape[0], value.shape[1] // span, span) + value.shape[2:])
    return jnp.moveaxis(shaped, 1, 0)


def from_blocks(value):
    merged = jnp.moveaxis(value, 0, 1)
    return merged.reshape((merged.shape[0], merged.shape[1] * merged.shape[2]) + merged.shape[3:])


def attend(query, keys, values, key_ok):
    scale = HEAD ** (-0.5)
    span = min(512, query.shape[1])

    def one_block(query_block):
        scores = (
            jnp.einsum("iqhd,ikhd->ihqk", query_block, keys, preferred_element_type=jnp.float32)
            * scale
        )
        scores = jnp.where(key_ok, scores, NEG)
        top = jnp.max(scores, axis=-1, keepdims=True)
        weights = jnp.exp(scores - top)
        total = jnp.sum(weights, axis=-1, keepdims=True)
        probs = (weights / total).astype(jnp.bfloat16)
        mixed = jnp.einsum("ihqk,ikhd->iqhd", probs, values, preferred_element_type=jnp.float32)
        return (mixed.astype(jnp.bfloat16), (top + jnp.log(total))[..., 0])

    mixed, log_totals = lax.map(one_block, to_blocks(query, span))
    return (from_blocks(mixed), log_totals)


def attend_back(query, keys, values, key_ok, log_totals, grad_mixed):
    scale = HEAD ** (-0.5)
    span = min(512, query.shape[1])

    def one_block(carry, items):
        grad_keys, grad_values = carry
        query_block, total_block, grad_block = items
        scores = (
            jnp.einsum("iqhd,ikhd->ihqk", query_block, keys, preferred_element_type=jnp.float32)
            * scale
        )
        scores = jnp.where(key_ok, scores, NEG)
        probs = jnp.exp(scores - total_block[..., None])
        grad_values = grad_values + jnp.einsum(
            "ihqk,iqhd->ikhd",
            probs.astype(jnp.bfloat16),
            grad_block,
            preferred_element_type=jnp.float32,
        )
        grad_probs = jnp.einsum(
            "iqhd,ikhd->ihqk", grad_block, values, preferred_element_type=jnp.float32
        )
        delta = jnp.sum(probs * grad_probs, axis=-1, keepdims=True)
        grad_scores = (probs * (grad_probs - delta)).astype(jnp.bfloat16)
        grad_query = (
            jnp.einsum("ihqk,ikhd->iqhd", grad_scores, keys, preferred_element_type=jnp.float32)
            * scale
        )
        grad_keys = (
            grad_keys
            + jnp.einsum(
                "ihqk,iqhd->ikhd", grad_scores, query_block, preferred_element_type=jnp.float32
            )
            * scale
        )
        return ((grad_keys, grad_values), grad_query.astype(jnp.bfloat16))

    empty = jnp.zeros(keys.shape, jnp.float32)
    (grad_keys, grad_values), grad_query = lax.scan(
        one_block, (empty, empty), (to_blocks(query, span), log_totals, to_blocks(grad_mixed, span))
    )
    return (
        from_blocks(grad_query),
        grad_keys.astype(jnp.bfloat16),
        grad_values.astype(jnp.bfloat16),
    )


def local(
    tokens,
    patch_mask,
    gain_one,
    shift_one,
    w_query,
    b_query,
    w_key,
    w_value,
    b_value,
    w_output,
    b_output,
    gain_two,
    shift_two,
    w_up,
    b_up,
    w_down,
    b_down,
    cotangent,
):
    rows = (
        lax.all_gather(w_query, "fsdp", axis=0, tiled=True),
        lax.all_gather(w_key, "fsdp", axis=0, tiled=True),
        lax.all_gather(w_value, "fsdp", axis=0, tiled=True),
        lax.all_gather(w_output, "fsdp", axis=0, tiled=True),
        lax.all_gather(w_up, "fsdp", axis=0, tiled=True),
        lax.all_gather(w_down, "fsdp", axis=0, tiled=True),
    )
    whole = (
        lax.all_gather(rows[0], "seq", axis=1, tiled=True),
        lax.all_gather(rows[1], "seq", axis=1, tiled=True),
        lax.all_gather(rows[2], "seq", axis=1, tiled=True),
        lax.all_gather(rows[3], "seq", axis=1, tiled=True),
        lax.all_gather(rows[4], "seq", axis=1, tiled=True),
        lax.all_gather(rows[5], "seq", axis=1, tiled=True),
        lax.all_gather(gain_one, "seq", axis=0, tiled=True),
        lax.all_gather(shift_one, "seq", axis=0, tiled=True),
        lax.all_gather(b_query, "seq", axis=0, tiled=True),
        lax.all_gather(b_value, "seq", axis=0, tiled=True),
        lax.all_gather(b_output, "seq", axis=0, tiled=True),
        lax.all_gather(gain_two, "seq", axis=0, tiled=True),
        lax.all_gather(shift_two, "seq", axis=0, tiled=True),
        lax.all_gather(b_up, "seq", axis=0, tiled=True),
        lax.all_gather(b_down, "seq", axis=0, tiled=True),
    )
    query_full, key_full, value_full, output_full, up_full, down_full = whole[:6]
    (
        norm_gain_one,
        norm_shift_one,
        bias_query,
        bias_value,
        bias_output,
        norm_gain_two,
        norm_shift_two,
        bias_up,
        bias_down,
    ) = tuple((piece.astype(jnp.float32) for piece in whole[6:]))
    tok_float = tokens.astype(jnp.float32)
    normed_in, normed_one, inverse_one = norm_rows(tok_float, norm_gain_one, norm_shift_one)
    h_one = normed_in.astype(jnp.bfloat16)
    query_tok = (
        jnp.einsum("isd,de->ise", h_one, query_full, preferred_element_type=jnp.float32)
        + bias_query
    ).astype(jnp.bfloat16)
    key_tok = jnp.einsum("isd,de->ise", h_one, key_full, preferred_element_type=jnp.float32).astype(
        jnp.bfloat16
    )
    value_tok = (
        jnp.einsum("isd,de->ise", h_one, value_full, preferred_element_type=jnp.float32)
        + bias_value
    ).astype(jnp.bfloat16)
    seq_count = lax.axis_size("seq")
    mask_rows = jnp.broadcast_to(
        patch_mask.astype(jnp.bfloat16)[:, :, None], patch_mask.shape + (seq_count,)
    )
    query_heads, key_heads, value_heads, mask_heads = (
        lax.all_to_all(query_tok, "seq", split_axis=2, concat_axis=1, tiled=True),
        lax.all_to_all(key_tok, "seq", split_axis=2, concat_axis=1, tiled=True),
        lax.all_to_all(value_tok, "seq", split_axis=2, concat_axis=1, tiled=True),
        lax.all_to_all(mask_rows, "seq", split_axis=2, concat_axis=1, tiled=True),
    )
    key_ok = (mask_heads[:, :, 0] > 0)[:, None, None, :]
    query_split = split_heads(query_heads)
    key_split = split_heads(key_heads)
    value_split = split_heads(value_heads)
    mixed_split, log_totals = attend(query_split, key_split, value_split, key_ok)
    mixed_tok = lax.all_to_all(
        mixed_split.reshape(query_heads.shape), "seq", split_axis=1, concat_axis=2, tiled=True
    )
    attn_out = (
        jnp.einsum("ise,ed->isd", mixed_tok, output_full, preferred_element_type=jnp.float32)
        + bias_output
    )
    residual = tok_float + attn_out
    normed_mid, normed_two, inverse_two = norm_rows(residual, norm_gain_two, norm_shift_two)
    h_two = normed_mid.astype(jnp.bfloat16)
    hidden = jnp.einsum("isd,df->isf", h_two, up_full, preferred_element_type=jnp.float32) + bias_up
    activated = gelu_tanh(hidden).astype(jnp.bfloat16)
    layer_out = (
        residual
        + jnp.einsum("isf,fd->isd", activated, down_full, preferred_element_type=jnp.float32)
        + bias_down
    ).astype(jnp.bfloat16)
    rows_again = (
        lax.all_gather(w_query, "fsdp", axis=0, tiled=True),
        lax.all_gather(w_key, "fsdp", axis=0, tiled=True),
        lax.all_gather(w_value, "fsdp", axis=0, tiled=True),
        lax.all_gather(w_output, "fsdp", axis=0, tiled=True),
        lax.all_gather(w_up, "fsdp", axis=0, tiled=True),
        lax.all_gather(w_down, "fsdp", axis=0, tiled=True),
    )
    again = (
        lax.all_gather(rows_again[0], "seq", axis=1, tiled=True),
        lax.all_gather(rows_again[1], "seq", axis=1, tiled=True),
        lax.all_gather(rows_again[2], "seq", axis=1, tiled=True),
        lax.all_gather(rows_again[3], "seq", axis=1, tiled=True),
        lax.all_gather(rows_again[4], "seq", axis=1, tiled=True),
        lax.all_gather(rows_again[5], "seq", axis=1, tiled=True),
    )
    query_mat, key_mat, value_mat, output_mat, up_mat, down_mat = again
    grad_final = cotangent.astype(jnp.float32)
    down_grad = jnp.einsum("isf,isd->fd", activated, cotangent, preferred_element_type=jnp.float32)
    down_bias_grad = jnp.sum(grad_final, axis=(0, 1))
    grad_act = jnp.einsum("isd,fd->isf", cotangent, down_mat, preferred_element_type=jnp.float32)
    grad_hidden = (grad_act * gelu_slope(hidden)).astype(jnp.bfloat16)
    up_grad = jnp.einsum("isd,isf->df", h_two, grad_hidden, preferred_element_type=jnp.float32)
    up_bias_grad = jnp.sum(grad_hidden, axis=(0, 1), dtype=jnp.float32)
    grad_norm_two = jnp.einsum(
        "isf,df->isd", grad_hidden, up_mat, preferred_element_type=jnp.float32
    )
    gain_two_grad = jnp.sum(grad_norm_two * normed_two, axis=(0, 1))
    shift_two_grad = jnp.sum(grad_norm_two, axis=(0, 1))
    grad_residual = grad_final + norm_back(grad_norm_two, normed_two, inverse_two, norm_gain_two)
    grad_attn = grad_residual.astype(jnp.bfloat16)
    output_bias_grad = jnp.sum(grad_attn, axis=(0, 1), dtype=jnp.float32)
    output_grad = jnp.einsum(
        "ise,isd->ed", mixed_tok, grad_attn, preferred_element_type=jnp.float32
    )
    grad_mixed_tok = jnp.einsum(
        "isd,ed->ise", grad_attn, output_mat, preferred_element_type=jnp.float32
    ).astype(jnp.bfloat16)
    grad_mixed_heads = lax.all_to_all(
        grad_mixed_tok, "seq", split_axis=2, concat_axis=1, tiled=True
    )
    grad_query_split, grad_key_split, grad_value_split = attend_back(
        query_split, key_split, value_split, key_ok, log_totals, split_heads(grad_mixed_heads)
    )
    grad_query_tok, grad_key_tok, grad_value_tok = (
        lax.all_to_all(
            grad_query_split.reshape(query_heads.shape),
            "seq",
            split_axis=1,
            concat_axis=2,
            tiled=True,
        ),
        lax.all_to_all(
            grad_key_split.reshape(query_heads.shape),
            "seq",
            split_axis=1,
            concat_axis=2,
            tiled=True,
        ),
        lax.all_to_all(
            grad_value_split.reshape(query_heads.shape),
            "seq",
            split_axis=1,
            concat_axis=2,
            tiled=True,
        ),
    )
    query_grad = jnp.einsum(
        "isd,ise->de", h_one, grad_query_tok, preferred_element_type=jnp.float32
    )
    key_grad = jnp.einsum("isd,ise->de", h_one, grad_key_tok, preferred_element_type=jnp.float32)
    value_grad = jnp.einsum(
        "isd,ise->de", h_one, grad_value_tok, preferred_element_type=jnp.float32
    )
    query_bias_grad = jnp.sum(grad_query_tok, axis=(0, 1), dtype=jnp.float32)
    value_bias_grad = jnp.sum(grad_value_tok, axis=(0, 1), dtype=jnp.float32)
    grad_norm_one = (
        jnp.einsum("ise,de->isd", grad_query_tok, query_mat, preferred_element_type=jnp.float32)
        + jnp.einsum("ise,de->isd", grad_key_tok, key_mat, preferred_element_type=jnp.float32)
        + jnp.einsum("ise,de->isd", grad_value_tok, value_mat, preferred_element_type=jnp.float32)
    )
    gain_one_grad = jnp.sum(grad_norm_one * normed_one, axis=(0, 1))
    shift_one_grad = jnp.sum(grad_norm_one, axis=(0, 1))
    grad_tokens = (
        grad_residual + norm_back(grad_norm_one, normed_one, inverse_one, norm_gain_one)
    ).astype(jnp.bfloat16)
    parts = (
        lax.psum_scatter(
            query_grad.astype(jnp.bfloat16), "seq", scatter_dimension=1, tiled=True
        ).astype(jnp.float32),
        lax.psum_scatter(
            key_grad.astype(jnp.bfloat16), "seq", scatter_dimension=1, tiled=True
        ).astype(jnp.float32),
        lax.psum_scatter(
            value_grad.astype(jnp.bfloat16), "seq", scatter_dimension=1, tiled=True
        ).astype(jnp.float32),
        lax.psum_scatter(
            output_grad.astype(jnp.bfloat16), "seq", scatter_dimension=1, tiled=True
        ).astype(jnp.float32),
        lax.psum_scatter(
            up_grad.astype(jnp.bfloat16), "seq", scatter_dimension=1, tiled=True
        ).astype(jnp.float32),
        lax.psum_scatter(
            down_grad.astype(jnp.bfloat16), "seq", scatter_dimension=1, tiled=True
        ).astype(jnp.float32),
        lax.psum_scatter(
            gain_one_grad.astype(jnp.bfloat16), "seq", scatter_dimension=0, tiled=True
        ).astype(jnp.float32),
        lax.psum_scatter(
            shift_one_grad.astype(jnp.bfloat16), "seq", scatter_dimension=0, tiled=True
        ).astype(jnp.float32),
        lax.psum_scatter(
            query_bias_grad.astype(jnp.bfloat16), "seq", scatter_dimension=0, tiled=True
        ).astype(jnp.float32),
        lax.psum_scatter(
            value_bias_grad.astype(jnp.bfloat16), "seq", scatter_dimension=0, tiled=True
        ).astype(jnp.float32),
        lax.psum_scatter(
            output_bias_grad.astype(jnp.bfloat16), "seq", scatter_dimension=0, tiled=True
        ).astype(jnp.float32),
        lax.psum_scatter(
            gain_two_grad.astype(jnp.bfloat16), "seq", scatter_dimension=0, tiled=True
        ).astype(jnp.float32),
        lax.psum_scatter(
            shift_two_grad.astype(jnp.bfloat16), "seq", scatter_dimension=0, tiled=True
        ).astype(jnp.float32),
        lax.psum_scatter(
            up_bias_grad.astype(jnp.bfloat16), "seq", scatter_dimension=0, tiled=True
        ).astype(jnp.float32),
        lax.psum_scatter(
            down_bias_grad.astype(jnp.bfloat16), "seq", scatter_dimension=0, tiled=True
        ).astype(jnp.float32),
    )
    vectors = lax.psum(
        (
            parts[6],
            parts[7],
            parts[8],
            parts[9],
            parts[10],
            parts[11],
            parts[12],
            parts[13],
            parts[14],
        ),
        "fsdp",
    )
    final = (
        lax.psum_scatter(
            parts[0].astype(jnp.bfloat16), "fsdp", scatter_dimension=0, tiled=True
        ).astype(jnp.float32),
        lax.psum_scatter(
            parts[1].astype(jnp.bfloat16), "fsdp", scatter_dimension=0, tiled=True
        ).astype(jnp.float32),
        lax.psum_scatter(
            parts[2].astype(jnp.bfloat16), "fsdp", scatter_dimension=0, tiled=True
        ).astype(jnp.float32),
        lax.psum_scatter(
            parts[3].astype(jnp.bfloat16), "fsdp", scatter_dimension=0, tiled=True
        ).astype(jnp.float32),
        lax.psum_scatter(
            parts[4].astype(jnp.bfloat16), "fsdp", scatter_dimension=0, tiled=True
        ).astype(jnp.float32),
        lax.psum_scatter(
            parts[5].astype(jnp.bfloat16), "fsdp", scatter_dimension=0, tiled=True
        ).astype(jnp.float32),
    )
    return (
        layer_out,
        grad_tokens,
        vectors[0],
        vectors[1],
        final[0],
        vectors[2],
        final[1],
        final[2],
        vectors[3],
        final[3],
        vectors[4],
        vectors[5],
        vectors[6],
        final[4],
        vectors[7],
        final[5],
        vectors[8],
    )


def solution(mesh):
    placed = (
        P("fsdp", "seq", None),
        P("fsdp", "seq"),
        P("seq"),
        P("seq"),
        P("fsdp", "seq"),
        P("seq"),
        P("fsdp", "seq"),
        P("fsdp", "seq"),
        P("seq"),
        P("fsdp", "seq"),
        P("seq"),
        P("seq"),
        P("seq"),
        P("fsdp", "seq"),
        P("seq"),
        P("fsdp", "seq"),
        P("seq"),
        P("fsdp", "seq", None),
    )
    return jax.shard_map(
        local,
        mesh=mesh,
        in_specs=placed,
        out_specs=(
            P("fsdp", "seq", None),
            P("fsdp", "seq", None),
            P("seq"),
            P("seq"),
            P("fsdp", "seq"),
            P("seq"),
            P("fsdp", "seq"),
            P("fsdp", "seq"),
            P("seq"),
            P("fsdp", "seq"),
            P("seq"),
            P("seq"),
            P("seq"),
            P("fsdp", "seq"),
            P("seq"),
            P("fsdp", "seq"),
            P("seq"),
        ),
        check_vma=False,
    )
```

profile of v0, /device:TPU:0, one launch (start us, length us, event | category | flops | bytes accessed | tf_op | source)
XLA Modules:
  0.0 1701.4 jit_solution(11165621001030637015)
XLA Ops:
  8.0 35.9 %all_gather.82 = bf16[1152,288]{1,0:T(8,128)(2,1)S(1)} all-gather(bf16[144,288]{1,0:T(8,128)(2,1)} %param.29), channel_id=1, replica_groups=mesh['seq'=4,'fsdp'=8] {'fsdp'}, dimensions={0}, use_global_device_ids=true | all-gather | bytes 746496 | tf_op jit(solution)/shard_map/all_gather | solution.py:148
  45.1 35.4 %all_gather.77 = bf16[1152,288]{1,0:T(8,128)(2,1)S(1)} all-gather(bf16[144,288]{1,0:T(8,128)(2,1)S(1)} %copy-done.23), channel_id=1, replica_groups=mesh['seq'=4,'fsdp'=8] {'fsdp'}, dimensions={0}, use_global_device_ids=true | all-gather | bytes 746496 | tf_op jit(solution)/shard_map/all_gather | solution.py:146
  81.7 32.8 %all_gather.80 = bf16[1152,288]{1,0:T(8,128)(2,1)S(1)} all-gather(bf16[144,288]{1,0:T(8,128)(2,1)S(1)} %copy-done.24), channel_id=1, replica_groups=mesh['seq'=4,'fsdp'=8] {'fsdp'}, dimensions={0}, use_global_device_ids=true | all-gather | bytes 746496 | tf_op jit(solution)/shard_map/all_gather | solution.py:147
  116.3 31.8 %all_gather.85 = bf16[1152,288]{1,0:T(8,128)(2,1)S(1)} all-gather(bf16[144,288]{1,0:T(8,128)(2,1)S(1)} %copy-done.25), channel_id=1, replica_groups=mesh['seq'=4,'fsdp'=8] {'fsdp'}, dimensions={0}, use_global_device_ids=true | all-gather | bytes 746496 | tf_op jit(solution)/shard_map/all_gather | solution.py:149
  164.3 13.4 all-reduce.23
  294.2 51.6 %while.27 = (s32[]{:T(128)}, bf16[4,1,512,4,72]{2,4,3,1,0:T(8,128)(2,1)}, f32[4,1,4,512]{3,2,1,0:T(4,128)S(1)}, pred[1,1,1,2048]{3,2,1,0:T(4,128)(4,1)S(1)}, bf1...) while((s32[]{:T(128)}, ...), condition=%wide.region_5.6_spmd, body=%wide.region_2.5_spmd.sunk | while | flops 1258436608 | bytes 53357664 | solution.py:73
  361.6 35.5 %reduce.34 = bf16[2048,288]{1,0:T(8,128)(2,1)} reduce(bf16[2048,1,288]{2,1,0:T(2,128)(2,1)} %bitcast.303, bf16[]{:T(256)} %broadcast.259), dimensions={1}, to_apply=%bitcast.215.reduce_sub_computation | reduce | bytes 2359298
  406.3 15.8 all-to-all-done.4
  459.2 12.1 convolution_add_fusion
  471.3 18.5 %fusion.114 = (bf16[4304]{0:T(1024)(128)(2,1)}, bf16[512,4304]{0,1:T(8,128)(2,1)}) fusion(f32[512,4304]{0,1:T(8,128)} %convolution_add_fusion, bf16[4304,1152]{0,1:T(8,128)(2,1)} %all-gather.21.cloned.1.call-done, bf16[1,512,1152]{2,1,0:T(8,128)(2,1)} %param.39), kind=kOutput, calls=%fused_computation.155 | convolution fusion | flops 5121273856 | bytes 24326560 | tf_op jit(solution)/shard_map/isd,fd->isf/dot_general | solution.py:248
  555.3 235.0 %while.28 = (s32[]{:T(128)}, f32[1,2048,4,72]{1,3,2,0:T(8,128)}, f32[1,2048,4,72]{1,3,2,0:T(8,128)}, bf16[4,1,512,4,72]{2,4,3,1,0:T(8,128)(2,1)}, bf16[4,1,512,4...) while((s32[]{:T(128)}, f32[1,2048,4,72]{1,3,2,0:T(8,128)}, ...), condition=%wide.region_12.13_spmd.clone, body=%wide.region_10.12_spmd.clone.sunk | while | flops 3086055424 | bytes 224236304 | solution.py:115
  564.7 14.3 multiply_reduce_fusion.5
  622.4 14.3 multiply_reduce_fusion.5
  660.4 11.8 fusion.170
  681.4 14.3 multiply_reduce_fusion.5
  740.3 14.3 multiply_reduce_fusion.5
  804.5 34.5 %reduce.36 = bf16[2048,288]{1,0:T(8,128)(2,1)} reduce(bf16[2048,1,288]{2,1,0:T(2,128)(2,1)S(1)} %bitcast.304, bf16[]{:T(256)} %broadcast.259), dimensions={1}, to_apply=%bitcast.219.reduce_sub_computation | reduce | bytes 2359298
  842.8 19.0 %all_to_all.129 = bf16[4,2,73728]{2,1,0:T(2,128)(2,1)} all-to-all(bf16[4,2,73728]{2,1,0:T(2,128)(2,1)S(1)} %reshape.498), channel_id=1, replica_groups=mesh['seq'=4,'fsdp'=8] {'seq'}, dimensions={0} | all-to-all | bytes 2359296 | tf_op jit(solution)/shard_map/all_to_all | solution.py:273
  890.4 34.5 %reduce.37 = bf16[2048,288]{1,0:T(8,128)(2,1)} reduce(bf16[2048,1,288]{2,1,0:T(2,128)(2,1)S(1)} %bitcast.305, bf16[]{:T(256)} %broadcast.259), dimensions={1}, to_apply=%bitcast.221.reduce_sub_computation | reduce | bytes 2359298
  928.7 19.0 %all_to_all.130 = bf16[4,2,73728]{2,1,0:T(2,128)(2,1)} all-to-all(bf16[4,2,73728]{2,1,0:T(2,128)(2,1)S(1)} %reshape.500), channel_id=1, replica_groups=mesh['seq'=4,'fsdp'=8] {'seq'}, dimensions={0} | all-to-all | bytes 2359296 | tf_op jit(solution)/shard_map/all_to_all | solution.py:280
  976.4 34.5 %reduce.38 = bf16[2048,288]{1,0:T(8,128)(2,1)} reduce(bf16[2048,1,288]{2,1,0:T(2,128)(2,1)S(1)} %bitcast.302, bf16[]{:T(256)} %broadcast.259), dimensions={1}, to_apply=%bitcast.223.reduce_sub_computation | reduce | bytes 2359298
  1014.7 19.0 %all_to_all.131 = bf16[4,2,73728]{2,1,0:T(2,128)(2,1)} all-to-all(bf16[4,2,73728]{2,1,0:T(2,128)(2,1)S(1)} %reshape.502), channel_id=1, replica_groups=mesh['seq'=4,'fsdp'=8] {'seq'}, dimensions={0} | all-to-all | bytes 2359296 | tf_op jit(solution)/shard_map/all_to_all | solution.py:287
  1075.4 146.2 %fusion = bf16[1152,1088]{0,1:T(8,128)(2,1)} fusion(bf16[1152,4304]{0,1:T(8,128)(2,1)} %convolution_convert_fusion), kind=kCustom, calls=%all-reduce-scatter | all-reduce-scatter fusion | flops 5013505 | bytes 12423680
  1224.7 13.2 concatenate
  1275.6 13.6 all-reduce.22
  1303.1 39.3 %all-reduce.21 = (f32[288]{0:T(512)}, f32[288]{0:T(512)}, f32[288]{0:T(512)}, f32[288]{0:T(512)}, f32[288]{0:T(512)}, /*index=5*/f32[288]{0:T(512)}, f32[288]{0:T(512)}, f32[1076]{0:T(1024)}, f32[288]{0:T(512)}) all-reduce(f32[288]{0:T(512)} %dynamic-slice_convert_fusion.9, ...), channel_id=1, replica_groups=mesh['seq'=4,'fsdp'=8] {'fsdp'}, use_global_device_ids=true, to_apply=%region_17.18 | all-reduce | flops 3380 | bytes 27040 | tf_op jit(solution)/shard_map/psum | solution.py:361
  1348.7 12.8 fusion.69
  1363.7 21.5 %reduce-scatter.40.cloned.1.call-done = bf16[144,288]{1,0:T(8,128)(2,1)} async-done(((bf16[1152,288]{1,0:T(8,128)(2,1)}), bf16[144,288]{1,0:T(8,128)(2,1)}) %reduce-scatter.40.cloned.1.call-update) | async-done | bytes 82960
  1387.0 62.0 %reduce-scatter.34.cloned.1.call-done = bf16[144,288]{1,0:T(8,128)(2,1)} async-done(((bf16[1152,288]{1,0:T(8,128)(2,1)}), bf16[144,288]{1,0:T(8,128)(2,1)}) %reduce-scatter.34.cloned.1.call-update) | async-done | bytes 82960
  1450.8 62.2 %reduce-scatter.36.cloned.1.call-done = bf16[144,288]{1,0:T(8,128)(2,1)} async-done(((bf16[1152,288]{1,0:T(8,128)(2,1)}), bf16[144,288]{1,0:T(8,128)(2,1)}) %reduce-scatter.36.cloned.1.call-update) | async-done | bytes 82960
  1514.8 61.9 %reduce-scatter.38.cloned.1.call-done = bf16[144,288]{1,0:T(8,128)(2,1)} async-done(((bf16[1152,288]{1,0:T(8,128)(2,1)}), bf16[144,288]{1,0:T(8,128)(2,1)}) %reduce-scatter.38.cloned.1.call-update) | async-done | bytes 82960
  1578.5 113.8 %all-reduce.26.cloned.1.call-done = bf16[4304,288]{0,1:T(8,128)(2,1)} async-done(((bf16[4304,288]{0,1:T(8,128)(2,1)}), bf16[4304,288]{0,1:T(8,128)(2,1)}) %all-reduce.26.cloned.1.call-update) | async-done | bytes 2479120
  (475 shorter events, 674.0 us)
Async XLA Ops:
  7.2 142.1 %all-gather.19.cloned.1.call-start = ((), (), s32[]{:S(2)}) async-start(), calls=%async_computation.23 | async-start | bytes 2985984 | tf_op jit(solution)/shard_map/all_gather | solution.py:150
  7.9 170.5 %all-gather.15.cloned.1.call-start = ((), (), s32[]{:S(2)}) async-start(), calls=%async_computation.21 | async-start | bytes 3317760 | tf_op jit(solution)/shard_map/all_gather | solution.py:156
  45.0 161.9 %all-gather.11.cloned.1.call-start = ((), (), s32[]{:S(2)}) async-start(), calls=%async_computation.19 | async-start | bytes 3317760 | tf_op jit(solution)/shard_map/all_gather | solution.py:154
  81.6 152.3 %all-gather.13.cloned.1.call-start = ((), (), s32[]{:S(2)}) async-start(), calls=%async_computation.20 | async-start | bytes 3317760 | tf_op jit(solution)/shard_map/all_gather | solution.py:155
  115.7 146.2 %all-gather.25.cloned.1.call-start = ((), (), s32[]{:S(2)}) async-start(), calls=%async_computation.31 | async-start | bytes 3317760 | tf_op jit(solution)/shard_map/all_gather | solution.py:151
  116.2 325.5 %all-gather.17.cloned.1.call-start = ((), (), s32[]{:S(2)}) async-start(), calls=%async_computation.22 | async-start | bytes 3317760 | tf_op jit(solution)/shard_map/all_gather | solution.py:157
  149.3 298.7 %all-gather.23.cloned.1.call-start = ((), (), s32[]{:S(2)}) async-start(), calls=%async_computation.30 | async-start | bytes 12441600 | tf_op jit(solution)/shard_map/all_gather | solution.py:158
  157.0 45.4 %all-to-all-start = ((bf16[4,2,256]{2,1,0:T(2,128)(2,1)}), bf16[4,2,256]{2,1,0:T(2,128)(2,1)S(1)}, u32[]{:S(2)}, u32[]{:S(2)}) async-start(bf16[4,2,256]{2,1,0:T(2,128)(2,1)} %reshape.488), calls=%async_computation | async-start | bytes 8192 | tf_op jit(solution)/shard_map/all_to_all | solution.py:204
  177.7 56.2 %copy-start.26 = (f32[1152]{0:T(1024)}, f32[1152]{0:T(1024)S(1)}, u32[]{:S(2)}) copy-start(f32[1152]{0:T(1024)S(1)} %convert_element_type.223) | copy-start | bytes 13828
  177.9 56.0 %copy-start.31 = (f32[512]{0:T(512)}, f32[512]{0:T(512)S(1)}, u32[]{:S(2)}) copy-start(f32[512]{0:T(512)S(1)} %broadcast_multiply_fusion.5) | copy-start | bytes 6148
  202.4 28.0 %all-to-all-start.3 = ((bf16[4,2,73728]{2,1,0:T(2,128)(2,1)}), bf16[4,2,73728]{2,1,0:T(2,128)(2,1)}, u32[]{:S(2)}, u32[]{:S(2)}) async-start(bf16[4,2,73728]{2,1,0:T(2,128)(2,1)} %reshape.492), calls=%async_computation.3 | async-start | bytes 2359296 | tf_op jit(solution)/shard_map/all_to_all | solution.py:203
  230.3 27.1 %all-to-all-start.1 = ((bf16[4,2,73728]{2,1,0:T(2,128)(2,1)}), bf16[4,2,73728]{2,1,0:T(2,128)(2,1)S(1)}, u32[]{:S(2)}, u32[]{:S(2)}) async-start(bf16[4,2,73728]{2,1,0:T(2,128)(2,1)} %reshape.486), calls=%async_computation.1 | async-start | bytes 2359296 | tf_op jit(solution)/shard_map/all_to_all | solution.py:201
  257.4 24.7 %all-to-all-start.2 = ((bf16[4,2,73728]{2,1,0:T(2,128)(2,1)}), bf16[4,2,73728]{2,1,0:T(2,128)(2,1)}, u32[]{:S(2)}, u32[]{:S(2)}) async-start(bf16[4,2,73728]{2,1,0:T(2,128)(2,1)} %reshape.490), calls=%async_computation.2 | async-start | bytes 2359296 | tf_op jit(solution)/shard_map/all_to_all | solution.py:202
  261.7 209.6 %all-gather.21.cloned.1.call-start = ((), (), s32[]{:S(2)}) async-start(), calls=%async_computation.24 | async-start | bytes 12533760 | tf_op jit(solution)/shard_map/all_gather | solution.py:159
  401.7 20.4 %all-to-all-start.4 = ((bf16[4,2,73728]{2,1,0:T(2,128)(2,1)}), bf16[4,2,73728]{2,1,0:T(2,128)(2,1)}, u32[]{:S(2)}, u32[]{:S(2)}) async-start(bf16[4,2,73728]{2,1,0:T(2,128)(2,1)} %reshape.494), calls=%async_computation.4 | async-start | bytes 2359296 | tf_op jit(solution)/shard_map/all_to_all | solution.py:211
  406.3 93.7 %copy-start.28 = (f32[1152]{0:T(1024)}, f32[1152]{0:T(1024)S(1)}, u32[]{:S(2)}) copy-start(f32[1152]{0:T(1024)S(1)} %convert_element_type.235) | copy-start | bytes 13828
  406.3 52.9 %copy-start.57 = (f32[1152]{0:T(1024)}, f32[1152]{0:T(1024)S(1)}, u32[]{:S(2)}) copy-start(f32[1152]{0:T(1024)S(1)} %convert_element_type.236) | copy-start | bytes 13828
  446.2 53.7 %copy-start.34 = (f32[512]{0:T(512)}, f32[512]{0:T(512)S(1)}, u32[]{:S(2)}) copy-start(f32[512]{0:T(512)S(1)} %broadcast_multiply_fusion.4) | copy-start | bytes 6148
  526.8 20.2 %all-to-all-start.5 = ((bf16[4,2,73728]{2,1,0:T(2,128)(2,1)}), bf16[4,2,73728]{2,1,0:T(2,128)(2,1)}, u32[]{:S(2)}, u32[]{:S(2)}) async-start(bf16[4,2,73728]{2,1,0:T(2,128)(2,1)} %reshape.496), calls=%async_computation.5 | async-start | bytes 2359296 | tf_op jit(solution)/shard_map/all_to_all | solution.py:266
  531.1 715.9 %reduce-scatter.30.cloned.1.call-start = ((), (), s32[]{:S(2)}) async-start(), calls=%async_computation.28 | async-start | bytes 3317760 | tf_op jit(solution)/shard_map/reduce_scatter | solution.py:324
  536.5 713.0 %reduce-scatter.24.cloned.1.call-start = ((), (), s32[]{:S(2)}) async-start(), calls=%async_computation.25 | async-start | bytes 3317760 | tf_op jit(solution)/shard_map/reduce_scatter | solution.py:315
  879.9 383.4 %reduce-scatter.26.cloned.1.call-start = ((), (), s32[]{:S(2)}) async-start(), calls=%async_computation.26 | async-start | bytes 3317760 | tf_op jit(solution)/shard_map/reduce_scatter | solution.py:318
  965.5 324.9 %reduce-scatter.28.cloned.1.call-start = ((), (), s32[]{:S(2)}) async-start(), calls=%async_computation.27 | async-start | bytes 3317760 | tf_op jit(solution)/shard_map/reduce_scatter | solution.py:321
  1051.7 293.3 %reduce-scatter.32.cloned.1.call-start = ((), (), s32[]{:S(2)}) async-start(), calls=%async_computation.29 | async-start | bytes 12533760 | tf_op jit(solution)/shard_map/reduce_scatter | solution.py:330
  1063.7 297.8 %reduce-scatter.42.cloned.1.call-start = ((), (), s32[]{:S(2)}) async-start(), calls=%async_computation.36 | async-start | bytes 2985984
  1222.5 2.2 collective-permute-start
  1246.9 138.3 %reduce-scatter.40.cloned.1.call-start = ((), (), s32[]{:S(2)}) async-start(), calls=%async_computation.35 | async-start | bytes 995328
  1249.5 199.6 %reduce-scatter.34.cloned.1.call-start = ((), (), s32[]{:S(2)}) async-start(), calls=%async_computation.32 | async-start | bytes 995328
  1251.9 261.1 %reduce-scatter.36.cloned.1.call-start = ((), (), s32[]{:S(2)}) async-start(), calls=%async_computation.33 | async-start | bytes 995328
  1265.7 311.1 %reduce-scatter.38.cloned.1.call-start = ((), (), s32[]{:S(2)}) async-start(), calls=%async_computation.34 | async-start | bytes 995328
  1290.4 54.5 %copy-start.10 = (f32[1,512,1152]{2,1,0:T(8,128)S(1)}, f32[1,512,1152]{2,1,0:T(8,128)}, u32[]{:S(2)}) copy-start(f32[1,512,1152]{2,1,0:T(8,128)} %copy-done.9) | copy-start | bytes 7077892
  1292.9 399.4 %all-reduce.26.cloned.1.call-start = ((), (), s32[]{:S(2)}) async-start(), calls=%async_computation.37 | async-start | bytes 5013504
  (91 other events, 762.4 us)
Sparse Core Ops, SparseCore 0:
  10.2 78.7 all-gather.18
  91.1 26.8 all-gather.14
  120.1 25.7 all-gather.10
  147.9 26.0 all-gather.12
  176.0 58.4 all-gather.24
  235.9 29.4 all-gather.16
  267.0 66.9 all-gather.22
  335.6 67.6 all-gather.20
  536.6 36.3 reduce-scatter.29
  880.0 35.0 reduce-scatter.23
  965.7 35.0 reduce-scatter.25
  1051.8 38.5 reduce-scatter.27
  1093.0 119.7 reduce-scatter.31
  1247.0 74.2 reduce-scatter.41
  1325.0 60.2 reduce-scatter.39
  1388.9 60.1 reduce-scatter.33
  1452.7 60.2 reduce-scatter.35
  1516.7 60.0 reduce-scatter.37
  1580.8 111.4 all-reduce.25
where the time goes:
time: 1710 us; the launch traced here: 1700 us
  blocking collectives  405 us (24%)
  waiting for transfers between devices  350 us (20%)
  matrix products  341 us (20%)
  local copies, waits for them, and re-layouts  293 us (17%)
  other arithmetic  264 us (15%)
  starting transfers between devices  27.5 us (2%)
  between operations  19.5 us (1%)
    unnamed x26, waiting for transfers between devices  323 us
    unnamed x11, other arithmetic  175 us
    unnamed x3, blocking collectives  173 us
    unnamed x220, local copies, waits for them, and re-layouts  150 us
    dot_general x4, matrix products, one_block(): jnp.einsum('iqhd,ikhd->ihqk', grad_block, values, preferred_element_type=...  57.2 us
    dot_general x8, matrix products, one_block(): jnp.einsum('iqhd,ikhd->ihqk', query_block, keys, preferred_element_type=j...  51.5 us
    dot_general x4, matrix products, one_block(): jnp.einsum('ihqk,iqhd->ikhd', probs.astype(jnp.bfloat16), grad_block, pre...  46.5 us
    convert_element_type x4, other arithmetic, one_block(): grad_scores = (probs * (grad_probs - delta)).astype(jnp.bfloat16)  43.2 us
  transfers between devices with their start and end apart: 26, of which 8 were waited for; matrix products, arithmetic and copies ran while one was open for 56% of the time, Pallas kernels for 0%

commit v1 on v0

v1 whole, which is shorter than its diff:
```python
import functools
import math

import jax
import jax.numpy as jnp
import numpy as np
from jax import lax
from jax.experimental import pallas as pl
from jax.experimental.pallas import tpu as pltpu
from jax.sharding import PartitionSpec as P

HEAD = 72
WIDE = 128
MASK_AT = HEAD
LSE_AT = HEAD + 1
SUM_AT = HEAD
CHUNKS = 2

EPS = 1e-06
ROOT = 0.7978845608028654
CUBIC = 0.044715
NEG = -1e30
LOG2E = math.log2(math.e)
SCALE = HEAD ** (-0.5)

BF = jnp.bfloat16
F32 = jnp.float32
NT = (((1,), (1,)), ((), ()))
NN = (((1,), (0,)), ((), ()))
VMEM_BYTES = 56 << 20


def mm(left, right, dims=NN):
    return lax.dot_general(left, right, dims, preferred_element_type=F32)


def cost(macs, moved, special=0):
    return pl.CostEstimate(flops=2 * macs, bytes_accessed=moved, transcendentals=special)


def swap(value, bit):
    count = lax.axis_size("seq")
    return lax.ppermute(value, "seq", [(i, i ^ bit) for i in range(count)])


def spread(value):
    count = lax.axis_size("seq")
    blocks = [None] * count
    blocks[0] = value
    have = [0]
    bit = count // 2
    while bit:
        for j in list(have):
            blocks[j | bit] = swap(blocks[j], bit)
            have.append(j | bit)
        bit //= 2
    return blocks


def collect(blocks):
    blocks = list(blocks)
    kind = blocks[0].dtype
    count = len(blocks)
    alive = list(range(count))
    bit = 1
    while bit < count:
        for j in reversed(alive):
            if j & bit:
                incoming = swap(blocks[j].astype(kind), bit)
                blocks[j ^ bit] = blocks[j ^ bit].astype(F32) + incoming.astype(F32)
        alive = [j for j in alive if not j & bit]
        bit *= 2
    return blocks[0]


def reorder(blocks, me):
    blocks = list(blocks)
    bit = 1
    while bit < len(blocks):
        odd = (me & bit) > 0
        blocks = [jnp.where(odd, blocks[j ^ bit], blocks[j]) for j in range(len(blocks))]
        bit *= 2
    return blocks


def ring_order():
    count = lax.axis_size("fsdp")
    if count == 8:
        return [0, 2, 4, 6, 7, 5, 3, 1]
    return list(range(count))


def ring_place():
    order = ring_order()
    table = np.zeros(len(order), np.int32)
    for at, device in enumerate(order):
        table[device] = at
    return jnp.asarray(table)[lax.axis_index("fsdp")]


def ring_shift(value, step):
    order = ring_order()
    count = len(order)
    return lax.ppermute(
        value, "fsdp", [(order[i], order[(i + step) % count]) for i in range(count)]
    )


def ring_owner(offset):
    order = ring_order()
    return jnp.asarray(order, jnp.int32)[(ring_place() + offset) % len(order)]


def ring_gather(value, flip):
    count = lax.axis_size("fsdp")
    found = [(0, value)]
    far = (count // 2, count - 1 - count // 2)
    for step, reach in ((1, far[flip]), (-1, far[1 - flip])):
        moving = value
        for k in range(1, reach + 1):
            moving = ring_shift(moving, step)
            found.append((-step * k, moving))
    index = jnp.stack([ring_owner(offset) for offset, _ in found])
    return place([block for _, block in found], index)


def place(blocks, index):
    count = len(blocks)

    def kernel(index_ref, *refs):
        target, sems = refs[count], refs[count + 1]
        copies = [
            pltpu.make_async_copy(refs[i], target.at[index_ref[i]], sems.at[i])
            for i in range(count)
        ]
        for copy in copies:
            copy.start()
        for copy in copies:
            copy.wait()

    block = blocks[0]
    return pl.pallas_call(
        kernel,
        grid_spec=pltpu.PrefetchScalarGridSpec(
            num_scalar_prefetch=1,
            grid=(1,),
            in_specs=[pl.BlockSpec(memory_space=pl.ANY)] * count,
            out_specs=pl.BlockSpec(memory_space=pl.ANY),
            scratch_shapes=[pltpu.SemaphoreType.DMA((count,))],
        ),
        out_shape=jax.ShapeDtypeStruct((count,) + block.shape, block.dtype),
        cost_estimate=cost(0, 2 * count * block.size * 2),
        name="place_blocks",
    )(index, *blocks)


def ring_reduce(take, flip):
    count = lax.axis_size("fsdp")
    far = (count // 2, count - 1 - count // 2)
    total = take(ring_owner(0)).astype(F32)
    for step, reach in ((1, far[flip]), (-1, far[1 - flip])):
        incoming = None
        for k in range(reach, 0, -1):
            part = take(ring_owner(step * k))
            if incoming is not None:
                part = (part.astype(F32) + incoming.astype(F32)).astype(BF)
            incoming = ring_shift(part, step)
        total = total + incoming.astype(F32)
    return total


def ring_sum(value):
    count = lax.axis_size("fsdp")
    bit = 1
    while bit < count:
        value = value + lax.ppermute(value, "fsdp", [(i, i ^ bit) for i in range(count)])
        bit *= 2
    return value


def norm_parts(value):
    mean = jnp.mean(value, axis=-1, keepdims=True)
    centered = value - mean
    inverse = lax.rsqrt(jnp.mean(centered * centered, axis=-1, keepdims=True) + EPS)
    return centered * inverse, inverse


def norm_back(grad_out, normed, inverse, gain):
    scaled = grad_out * gain
    first = jnp.mean(scaled, axis=-1, keepdims=True)
    second = jnp.mean(scaled * normed, axis=-1, keepdims=True)
    return inverse * (scaled - first - normed * second)


def three_parts(value):
    high = value.astype(BF).astype(F32)
    rest = value - high
    middle = rest.astype(BF).astype(F32)
    return high, middle, rest - middle


def put_parts(value, column, at):
    lane = lax.broadcasted_iota(jnp.int32, value.shape, 1)
    for i, part in enumerate(three_parts(column)):
        value = jnp.where(lane == at + i, -part, value)
    return value


def widen(rows, cols, dtype=BF):
    source = lax.broadcasted_iota(jnp.int32, (rows, cols), 0)
    target = lax.broadcasted_iota(jnp.int32, (rows, cols), 1)
    return ((source // HEAD) * WIDE + source % HEAD == target).astype(dtype)


def attend(qkv, wide_heads, chunk, kept):
    images, count, length, _ = qkv.shape
    heads = wide_heads // WIDE
    rows = length // CHUNKS
    keys = count * length
    flat = qkv.reshape(images, keys, 3 * wide_heads)

    def kernel(q_ref, kv_ref, *refs):
        mixed_ref, query_ref, exact_ref = refs[-3:]
        total = jnp.zeros((rows, heads * HEAD), F32)
        for e in range(heads):
            here = slice(e * WIDE, (e + 1) * WIDE)
            query = q_ref[0, 0, :, here]
            k = kv_ref[0, :, wide_heads + e * WIDE : wide_heads + (e + 1) * WIDE]
            v = kv_ref[0, :, 2 * wide_heads + e * WIDE : 2 * wide_heads + (e + 1) * WIDE]
            scores = mm(query, k, NT)
            top = jnp.max(scores, axis=-1, keepdims=True)
            weights = jnp.exp2(scores - top).astype(BF)
            mixed = mm(weights, v)
            summed = mixed[:, SUM_AT : SUM_AT + 1]
            mixed = mixed / summed
            log_total = top + jnp.log2(summed)
            exact_ref[0, 0, :, here] = mixed
            query_ref[0, 0, :, here] = put_parts(query.astype(F32), log_total, LSE_AT).astype(BF)
            source = lax.broadcasted_iota(jnp.int32, (WIDE, heads * HEAD), 0)
            target = lax.broadcasted_iota(jnp.int32, (WIDE, heads * HEAD), 1)
            pick = ((source < HEAD) & (source + e * HEAD == target)).astype(F32).astype(BF)
            total = total + mm(mixed.astype(BF), pick)
        mixed_ref[0, 0] = total.astype(BF)

    part = pl.BlockSpec((1, 1, rows, wide_heads), lambda i, b: (i, b, chunk, 0))
    shapes = [
        jax.ShapeDtypeStruct((images, count, rows, heads * HEAD), BF),
        jax.ShapeDtypeStruct((images, count, length, wide_heads), BF),
        jax.ShapeDtypeStruct((images, count, length, wide_heads), F32),
    ]
    outs = [pl.BlockSpec((1, 1, rows, heads * HEAD), lambda i, b: (i, b, 0, 0)), part, part]
    extra = list(kept)
    scores = images * count * rows * keys * heads
    return pl.pallas_call(
        kernel,
        grid=(images, count),
        in_specs=[part, pl.BlockSpec((1, keys, 3 * wide_heads), lambda i, b: (i, 0, 0))]
        + [pl.BlockSpec(memory_space=pl.ANY)] * len(extra),
        out_specs=outs,
        out_shape=shapes,
        input_output_aliases={2 + i: 1 + i for i in range(len(extra))},
        cost_estimate=cost(2 * scores * WIDE * 2, flat.size * 2 + 3 * images * keys * wide_heads, scores),
        compiler_params=pltpu.CompilerParams(vmem_limit_bytes=VMEM_BYTES),
        name="attend",
    )(qkv, flat, *extra)


def middle(mixed, tokens, cotangent, weights, chunk, kept):
    images, count, length, width = tokens.shape
    me, w_output, w_up, w_down, b_output, gain, shift, b_up = weights
    rows = length // CHUNKS
    own = mixed[0].shape[-1]
    hidden_count = w_up.shape[1]

    def kernel(me_ref, *refs):
        mixed_refs = refs[:count]
        tok_ref, cot_ref, wo_ref, up_ref, down_ref, bo_ref, g_ref, s_ref, bu_ref = refs[
            count : count + 9
        ]
        (
            h_ref,
            z_ref,
            du_ref,
            cat_ref,
            dh_ref,
            y_ref,
            x_ref,
            gb_ref,
        ) = refs[-8:]
        block = pl.program_id(1)
        x_one = tok_ref[0, 0].astype(F32) + bo_ref[...]
        pieces = []
        for i in range(count):
            piece = mixed_refs[i][0, 0]
            pieces.append(piece)
            x_one = x_one + mm(piece, wo_ref[me_ref[0] ^ i])
        cat_ref[0, 0] = jnp.concatenate(pieces, axis=-1)

        @pl.when(block == 0)
        def _():
            x_ref[0] = x_one

        normed, _ = norm_parts(x_one)
        h_two = (normed * g_ref[...] + s_ref[...]).astype(BF)
        h_ref[0, 0] = h_two
        hidden = mm(h_two, up_ref[...]) + bu_ref[...]
        grad_act = mm(cot_ref[0, 0], down_ref[...], NT)
        square = hidden * hidden
        inner = jnp.tanh(ROOT * (hidden + CUBIC * square * hidden))
        half = 0.5 * (1.0 + inner)
        z = (hidden * half).astype(BF)
        slope = half + 0.5 * hidden * (1.0 - inner * inner) * ROOT * (1.0 + 3.0 * CUBIC * square)
        wide_grad = grad_act * slope
        grad_hidden = wide_grad.astype(BF)
        z_ref[0, 0] = z
        du_ref[0, 0] = grad_hidden
        dh_ref[0, 0] = mm(grad_hidden, up_ref[...], NT).astype(BF)
        y_ref[0, 0] = mm(z, down_ref[...]).astype(BF)
        summed = jnp.sum(grad_hidden.astype(F32), axis=0, keepdims=True)
        first = (pl.program_id(0) == 0) & (block == 0)

        @pl.when(first)
        def _():
            gb_ref[...] = summed

        @pl.when(jnp.logical_not(first))
        def _():
            gb_ref[...] += summed

    def piece_spec(i):
        return pl.BlockSpec((1, 1, rows, own), lambda im, b, me_ref: (im, b ^ i, 0, 0))

    def whole_spec(array):
        return pl.BlockSpec(array.shape, lambda im, b, me_ref: (0,) * array.ndim)

    full = pl.BlockSpec((1, 1, rows, width), lambda im, b, me_ref: (im, b, chunk, 0))
    full_hidden = pl.BlockSpec((1, 1, rows, hidden_count), lambda im, b, me_ref: (im, b, chunk, 0))
    part = pl.BlockSpec((1, 1, rows, width), lambda im, b, me_ref: (im, b, 0, 0))
    constants = [w_output, w_up, w_down, b_output, gain, shift, b_up]
    extra = list(kept)
    inputs = [*mixed, tokens, cotangent, *constants, *extra]
    all_rows = images * count * rows
    return pl.pallas_call(
        kernel,
        grid_spec=pltpu.PrefetchScalarGridSpec(
            num_scalar_prefetch=1,
            grid=(images, count),
            in_specs=[piece_spec(i) for i in range(count)]
            + [full, full]
            + [whole_spec(array) for array in constants]
            + [pl.BlockSpec(memory_space=pl.ANY)] * len(extra),
            out_specs=[
                full,
                full_hidden,
                full_hidden,
                full,
                part,
                part,
                pl.BlockSpec((1, rows, width), lambda im, b, me_ref: (im, 0, 0)),
                pl.BlockSpec((1, hidden_count), lambda im, b, me_ref: (0, 0)),
            ],
        ),
        out_shape=[
            jax.ShapeDtypeStruct(tokens.shape, BF),
            jax.ShapeDtypeStruct((images, count, length, hidden_count), BF),
            jax.ShapeDtypeStruct((images, count, length, hidden_count), BF),
            jax.ShapeDtypeStruct(tokens.shape, BF),
            jax.ShapeDtypeStruct((images, count, rows, width), BF),
            jax.ShapeDtypeStruct((images, count, rows, width), BF),
            jax.ShapeDtypeStruct((images, rows, width), F32),
            jax.ShapeDtypeStruct((1, hidden_count), F32),
        ],
        input_output_aliases={1 + count + 9 + i: i for i in range(len(extra))},
        cost_estimate=cost(
            all_rows * width * (width + 4 * hidden_count) * 2,
            all_rows * (width * 16 + hidden_count * 4) + (w_output.size + 2 * w_up.size) * 2,
        ),
        compiler_params=pltpu.CompilerParams(vmem_limit_bytes=VMEM_BYTES),
        name="middle",
    )(me.reshape(1), *inputs)


def mixed_back(grad, w_wide, exact, chunk, kept):
    images, count, rows, width = grad.shape
    _, _, length, wide_heads = exact.shape
    heads = wide_heads // WIDE

    def kernel(grad_ref, w_ref, exact_ref, *refs):
        out_ref = refs[-1]
        result = mm(grad_ref[0, 0], w_ref[...], NT).astype(BF).astype(F32)
        for e in range(heads):
            here = slice(e * WIDE, (e + 1) * WIDE)
            mine = result[:, here]
            delta = jnp.sum(mine * exact_ref[0, 0, :, here], axis=-1, keepdims=True)
            out_ref[0, 0, :, here] = put_parts(mine, delta, SUM_AT).astype(BF)

    full = pl.BlockSpec((1, 1, rows, wide_heads), lambda im, b: (im, b, chunk, 0))
    extra = list(kept)
    return pl.pallas_call(
        kernel,
        grid=(images, count),
        in_specs=[
            pl.BlockSpec((1, 1, rows, width), lambda im, b: (im, b, 0, 0)),
            pl.BlockSpec(w_wide.shape, lambda im, b: (0, 0)),
            full,
        ]
        + [pl.BlockSpec(memory_space=pl.ANY)] * len(extra),
        out_specs=full,
        out_shape=jax.ShapeDtypeStruct(exact.shape, BF),
        input_output_aliases={3 + i: i for i in range(len(extra))},
        cost_estimate=cost(
            images * count * rows * width * wide_heads,
            images * count * rows * (width * 2 + wide_heads * 6) + w_wide.size * 2,
        ),
        compiler_params=pltpu.CompilerParams(vmem_limit_bytes=VMEM_BYTES),
        name="mixed_back",
    )(grad, w_wide, exact, *extra)


def attend_back(query, grad, qkv):
    images, keys, wide_heads = query.shape
    heads = wide_heads // WIDE
    rows = min(512, keys)
    span = min(512, keys)
    steps = keys // rows

    def kernel(q_ref, do_ref, k_ref, v_ref, dq_ref, dk_ref, dv_ref, kt, dk, dv):
        step = pl.program_id(2)

        @pl.when(step == 0)
        def _():
            kt[...] = k_ref[0].T
            dk[...] = jnp.zeros_like(dk)
            dv[...] = jnp.zeros_like(dv)

        q = q_ref[0]
        do = do_ref[0]
        turned = jnp.zeros((WIDE, rows), F32)
        for at in range(0, keys, span):
            here = slice(at, at + span)
            probs = jnp.exp2(mm(k_ref[0, here], q, NT))
            grad_scores = (probs * mm(v_ref[0, here], do, NT)).astype(BF)
            dv[here] += mm(probs.astype(BF), do)
            dk[here] += mm(grad_scores, q)
            turned = turned + mm(kt[:, here], grad_scores)
        dq_ref[0] = (turned.T * SCALE).astype(BF)

        @pl.when(step == steps - 1)
        def _():
            dk_ref[0] = (dk[...] * (1.0 / LOG2E)).astype(BF)
            dv_ref[0] = dv[...].astype(BF)

    row_spec = pl.BlockSpec((1, rows, WIDE), lambda i, e, b: (i, b, e))

    def all_spec(shift):
        return pl.BlockSpec((1, keys, WIDE), lambda i, e, b: (i, 0, e + shift))

    shape = jax.ShapeDtypeStruct((images, keys, wide_heads), BF)
    scores = images * heads * keys * keys
    return pl.pallas_call(
        kernel,
        grid=(images, heads, steps),
        in_specs=[row_spec, row_spec, all_spec(heads), all_spec(2 * heads)],
        out_specs=[row_spec, all_spec(0), all_spec(0)],
        out_shape=[shape] * 3,
        scratch_shapes=[
            pltpu.VMEM((WIDE, keys), BF),
            pltpu.VMEM((keys, WIDE), F32),
            pltpu.VMEM((keys, WIDE), F32),
        ],
        cost_estimate=cost(5 * scores * WIDE * 2, 7 * images * keys * wide_heads * 2, scores),
        compiler_params=pltpu.CompilerParams(vmem_limit_bytes=VMEM_BYTES),
        name="attend_back",
    )(query, grad, qkv, qkv)


def project_back(grads, w_wide):
    images, count, length, wide_heads = grads[0].shape
    width = w_wide.shape[0]

    def kernel(q_ref, k_ref, v_ref, w_ref, out_ref):
        total = jnp.zeros((length, width), F32)
        for i, ref in enumerate((q_ref, k_ref, v_ref)):
            total = total + mm(ref[0, 0], w_ref[:, i * wide_heads : (i + 1) * wide_heads], NT)
        out_ref[0, 0] = total.astype(BF)

    block = pl.BlockSpec((1, 1, length, wide_heads), lambda im, b: (im, b, 0, 0))
    return pl.pallas_call(
        kernel,
        grid=(images, count),
        in_specs=[block] * 3 + [pl.BlockSpec(w_wide.shape, lambda im, b: (0, 0))],
        out_specs=pl.BlockSpec((1, 1, length, width), lambda im, b: (im, b, 0, 0)),
        out_shape=jax.ShapeDtypeStruct((images, count, length, width), BF),
        cost_estimate=cost(
            images * count * length * width * wide_heads * 3,
            images * count * length * (wide_heads * 6 + width * 2) + w_wide.size * 2,
        ),
        compiler_params=pltpu.CompilerParams(vmem_limit_bytes=VMEM_BYTES),
        name="project_back",
    )(*grads, w_wide)


def local(
    tokens,
    patch_mask,
    gain_one,
    shift_one,
    w_query,
    b_query,
    w_key,
    w_value,
    b_value,
    w_output,
    b_output,
    gain_two,
    shift_two,
    w_up,
    b_up,
    w_down,
    b_down,
    cotangent,
):
    me = lax.axis_index("seq")
    count = lax.axis_size("seq")
    fcount = lax.axis_size("fsdp")
    images, length, width = tokens.shape
    own = w_query.shape[1]
    heads = own // HEAD
    wide_heads = heads * WIDE
    group = fcount // count
    rows = length // CHUNKS

    qkv_shard = jnp.concatenate([w_query, w_key, w_value], axis=1)
    small = jnp.concatenate(
        [patch_mask.astype(BF).reshape(-1)]
        + [gain_one, shift_one, b_output, gain_two, shift_two, b_down]
    )
    small = spread(small)
    qkv_rows = ring_gather(qkv_shard, 0).reshape(width, 3 * own)
    down_rows = ring_gather(w_down, 1)
    upper = ring_gather(jnp.concatenate([w_up, w_output], axis=1), 0)
    upper = upper.reshape(width, -1)
    up_mat = upper[:, : w_up.shape[1]]
    output_cols = upper[:, w_up.shape[1] :]

    patches = images * length
    valid = jnp.stack([block[:patches].reshape(images, length) for block in small], axis=1)
    bias_mask = jnp.where(valid > 0, 0.0, NEG).astype(F32)
    vectors = reorder([block[patches:].reshape(6, own) for block in small], me)
    vectors = jnp.concatenate(vectors, axis=1).astype(F32)
    g_one, s_one, b_out, g_two, s_two, b_dn = [vectors[i : i + 1] for i in range(6)]

    output_mat = jnp.concatenate(reorder(spread(output_cols), me), axis=1)
    output_mat = output_mat.reshape(count, own, width)

    def down_part(j):
        start = (me ^ j) * group
        return lax.dynamic_slice_in_dim(down_rows, start, group, 0)

    down_parts = [down_part(0)] + [swap(down_part(j), j) for j in range(1, count)]
    down_mat = jnp.concatenate(reorder(down_parts, me), axis=2).reshape(-1, width)

    expand = widen(own, wide_heads)
    w_wide = mm(qkv_rows, widen(3 * own, 3 * wide_heads)).astype(BF)
    own_rows = lax.dynamic_index_in_dim(output_mat, me, 0, keepdims=False)
    output_wide = mm(expand.T, own_rows).astype(BF)
    lane = np.arange(3 * wide_heads) % WIDE
    kind = np.arange(3 * wide_heads) // wide_heads
    factor = np.where(kind == 0, SCALE * LOG2E, 1.0).astype(np.float32)
    ones = (kind == 0) & (lane == MASK_AT)
    ones |= (kind == 1) & (lane >= LSE_AT) & (lane < LSE_AT + 3)
    ones |= (kind == 2) & (lane >= SUM_AT) & (lane < SUM_AT + 3)
    at_mask = ((kind == 1) & (lane == MASK_AT)).astype(np.float32)

    def widen_vector(vector):
        shaped = vector.astype(F32).reshape(heads, HEAD)
        return jnp.pad(shaped, ((0, 0), (0, WIDE - HEAD))).reshape(-1)

    def narrow(vector):
        return vector.reshape(heads, WIDE)[:, :HEAD].reshape(-1)

    bias_wide = jnp.concatenate(
        [widen_vector(b_query), jnp.zeros((wide_heads,), F32), widen_vector(b_value)]
    )
    bias_wide = bias_wide * factor + ones.astype(np.float32)
    weights = (me, output_mat, up_mat, down_mat, b_out, g_two, s_two, b_up.astype(F32)[None])

    def run(tokens, bias_mask, cotangent):
        images = tokens.shape[0]
        tok_all = jnp.stack(spread(tokens), axis=1)
        cot_all = jnp.stack(spread(cotangent), axis=1)
        normed, _ = norm_parts(tok_all.astype(F32))
        h_one = (normed * g_one + s_one).astype(BF)
        product = jnp.einsum("ijld,de->ijle", h_one, w_wide, preferred_element_type=F32)
        qkv = (product * factor + bias_wide + bias_mask[..., None] * at_mask).astype(BF)

        kept_attend, kept_middle = (), ()
        mixed_chunks = []
        for c in range(CHUNKS):
            mixed, *kept_attend = attend(qkv, wide_heads, c, kept_attend)
            mixed_chunks.append(spread(mixed))
        query_wide, mixed_exact = kept_attend
        hidden_parts, out_parts, x_parts = [], [], []
        up_bias_grad = 0.0
        for c in range(CHUNKS):
            *kept_middle, dh, y, x_own, gb = middle(
                mixed_chunks[c], tok_all, cot_all, weights, c, kept_middle
            )
            hidden_parts.append(collect([dh[:, j] for j in range(count)]))
            out_parts.append(y)
            x_parts.append(x_own)
            up_bias_grad = up_bias_grad + gb[0]
        h_two, activated, grad_hidden, mixed_all = kept_middle

        kept_back = ()
        grad_attn_all, grad_residual = [], []
        early = 0.0
        for c in range(CHUNKS):
            grad_norm = hidden_parts[c].astype(F32)
            normed_two, inverse_two = norm_parts(x_parts[c])
            cot_own = cotangent[:, c * rows : (c + 1) * rows].astype(F32)
            residual = cot_own + norm_back(grad_norm, normed_two, inverse_two, g_two)
            grad_attn = residual.astype(BF)
            grad_residual.append(residual)
            early = early + jnp.stack(
                [
                    jnp.sum(grad_norm * normed_two, axis=(0, 1)),
                    jnp.sum(grad_norm, axis=(0, 1)),
                    jnp.sum(grad_attn.astype(F32), axis=(0, 1)),
                    jnp.sum(cot_own, axis=(0, 1)),
                ]
            )
            stacked = jnp.stack(spread(grad_attn), axis=1)
            grad_attn_all.append(stacked)
            kept_back = (mixed_back(stacked, output_wide, mixed_exact, c, kept_back),)
        grad_mixed = kept_back[0]

        down_grad = jnp.einsum(
            "ijlf,ijld->fd", activated, cot_all, preferred_element_type=F32
        )
        up_grad = jnp.einsum("ijld,ijlf->df", h_two, grad_hidden, preferred_element_type=F32)
        grad_attn_all = jnp.concatenate(grad_attn_all, axis=2)
        grad_attn_cols = lax.dynamic_slice_in_dim(grad_attn_all, me * own, own, 3)
        output_grad = jnp.einsum(
            "ijle,ijld->ed", mixed_all, grad_attn_cols, preferred_element_type=F32
        )

        wide_shape = (images, count * length, wide_heads)
        grads = attend_back(
            query_wide.reshape(wide_shape),
            grad_mixed.reshape(wide_shape),
            qkv.reshape(images, count * length, 3 * wide_heads),
        )
        grads = [g.reshape(images, count, length, wide_heads) for g in grads]
        grad_h = project_back(grads, w_wide)
        grad_norm_one = collect([grad_h[:, j] for j in range(count)]).astype(F32)
        qkv_grad = [
            jnp.einsum("ijld,ijle->de", h_one, g, preferred_element_type=F32) for g in grads
        ]

        out_sum = collect(
            [jnp.concatenate([y[:, j] for y in out_parts], axis=1) for j in range(count)]
        )
        layer_out = (jnp.concatenate(x_parts, axis=1) + out_sum.astype(F32) + b_dn).astype(BF)
        normed_one, inverse_one = norm_parts(tokens.astype(F32))
        grad_tokens = (
            jnp.concatenate(grad_residual, axis=1)
            + norm_back(grad_norm_one, normed_one, inverse_one, g_one)
        ).astype(BF)
        late = jnp.stack(
            [
                jnp.sum(grad_norm_one * normed_one, axis=(0, 1)),
                jnp.sum(grad_norm_one, axis=(0, 1)),
            ]
        )
        bias_grads = [jnp.sum(grads[i].astype(F32), axis=(0, 1, 2)) for i in (0, 2)]
        sums = (down_grad, up_grad, output_grad, qkv_grad, early, up_bias_grad, late, bias_grads)
        return sums, (layer_out, grad_tokens)

    if images == 1:
        sums, (layer_out, grad_tokens) = run(tokens, bias_mask, cotangent)
    else:
        items = (tokens[:, None], bias_mask[:, None], cotangent[:, None])
        shapes = jax.eval_shape(lambda item: run(*item)[0], jax.tree.map(lambda a: a[0], items))
        empty = jax.tree.map(lambda a: jnp.zeros(a.shape, a.dtype), shapes)

        def step(totals, item):
            sums, results = run(*item)
            return jax.tree.map(jnp.add, totals, sums), results

        sums, (layer_out, grad_tokens) = lax.scan(step, empty, items)
        layer_out, grad_tokens = layer_out[:, 0], grad_tokens[:, 0]
    down_grad, up_grad, output_grad, qkv_grad, early, up_bias_grad, late, bias_grads = sums

    def relative(f):
        return ((f // group) ^ me) * group + f % group

    down_grad = down_grad.astype(BF).reshape(group, -1, width)

    def down_cols(j):
        return lax.dynamic_slice_in_dim(down_grad, (me ^ j) * own, own, 2)

    down_pieces = jnp.concatenate(
        [down_cols(0)] + [swap(down_cols(j), j) for j in range(1, count)], axis=0
    )
    final_down = ring_reduce(
        lambda f: lax.dynamic_index_in_dim(down_pieces, relative(f), 0, keepdims=False), 1
    )
    up_grad = up_grad.astype(BF).reshape(fcount, width // fcount, -1)
    final_up = ring_reduce(lambda f: lax.dynamic_index_in_dim(up_grad, f, 0, keepdims=False), 0)
    output_grad = output_grad.astype(BF).reshape(fcount, width // fcount, -1)
    final_output = ring_reduce(
        lambda f: lax.dynamic_index_in_dim(output_grad, relative(f), 0, keepdims=False), 1
    )
    qkv_grad = [mm(full.astype(BF), expand, NT).astype(BF) for full in qkv_grad]
    qkv_grad = jnp.concatenate(qkv_grad, axis=1).reshape(fcount, width // fcount, -1)
    final_qkv = ring_reduce(lambda f: lax.dynamic_index_in_dim(qkv_grad, f, 0, keepdims=False), 0)

    def to_owner(stack):
        kinds = stack.shape[0]
        parts = jnp.split(stack.reshape(kinds, count, own), count, axis=1)
        return collect(reorder([part[:, 0] for part in parts], me))

    early = to_owner(early)
    early = ring_sum(jnp.concatenate([early.reshape(-1), up_bias_grad]))
    late = to_owner(late)
    late = ring_sum(jnp.concatenate([late.reshape(-1)] + [narrow(g) for g in bias_grads]))
    gain_two_grad, shift_two_grad, b_output_grad, b_down_grad = [
        early[i * own : (i + 1) * own] for i in range(4)
    ]
    b_up_grad = early[4 * own :]
    gain_one_grad, shift_one_grad, b_query_grad, b_value_grad = [
        late[i * own : (i + 1) * own] for i in range(4)
    ]
    final_query, final_key, final_value = [
        final_qkv[:, i * own : (i + 1) * own] for i in range(3)
    ]
    return (
        layer_out,
        grad_tokens,
        gain_one_grad,
        shift_one_grad,
        final_query,
        b_query_grad,
        final_key,
        final_value,
        b_value_grad,
        final_output,
        b_output_grad,
        gain_two_grad,
        shift_two_grad,
        final_up,
        b_up_grad,
        final_down,
        b_down_grad,
    )


def solution(mesh):
    rows = P("fsdp", "seq", None)
    matrix = P("fsdp", "seq")
    vector = P("seq")
    return jax.shard_map(
        local,
        mesh=mesh,
        in_specs=(
            rows,
            matrix,
            vector,
            vector,
            matrix,
            vector,
            matrix,
            matrix,
            vector,
            matrix,
            vector,
            vector,
            vector,
            matrix,
            vector,
            matrix,
            vector,
            rows,
        ),
        out_specs=(
            rows,
            rows,
            vector,
            vector,
            matrix,
            vector,
            matrix,
            matrix,
            vector,
            matrix,
            vector,
            vector,
            vector,
            matrix,
            vector,
            matrix,
            vector,
        ),
        check_vma=False,
    )
```

time: 1710 us -> 1040 us (0.61)
  Pallas kernels: 0 us -> 438 us
  blocking collectives: 405 us -> 0 us
  matrix products: 341 us -> 71.3 us
  waiting for transfers between devices: 350 us -> 128 us
  other arithmetic: 264 us -> 108 us
  local copies, waits for them, and re-layouts: 293 us -> 162 us
  starting transfers between devices: 27.5 us -> 77.4 us
  between operations: 19.5 us -> 41.7 us
    pallas_call x0 -> x11, Pallas kernels: none -> 438 us  [the longest x3 268 us: place(): pl.pallas_call(kernel, grid_spec=pltpu.PrefetchScalarGridSpec(num_scalar_...]
    unnamed x26 -> x0, waiting for transfers between devices: 323 us -> none
    dot_general x46 -> x9, matrix products: 341 us -> 71.3 us  [the longest x5 31.8 us: mm(): return lax.dot_general(left, right, dims, preferred_element_type=F32)]
    unnamed x11 -> x0, other arithmetic: 175 us -> none
    unnamed x3 -> x0, blocking collectives: 173 us -> none
    unnamed x220 -> x162, local copies, waits for them, and re-layouts: 150 us -> 5.1 us
    all_gather x4 -> x0, blocking collectives: 136 us -> none  [the longest x1 35.9 us: local(): lax.all_gather(w_value, 'fsdp', axis=0, tiled=True)]
    ppermute x0 -> x103, waiting for transfers between devices: none -> 128 us  [the longest x49 81.9 us: ring_shift(): lax.ppermute(value, 'fsdp', [(order[i], order[(i + step) % count]) for i...]
  transfers between devices with their start and end apart: 26 -> 103, of which waited for: 8 -> 31; matrix products, arithmetic and copies ran while one was open for 56% -> 30% of each run, Pallas kernels for 0% -> 40%
where the time goes in v1:
time: 1040 us; the launch traced here: 1030 us
  Pallas kernels  438 us (42%)
  local copies, waits for them, and re-layouts  162 us (16%)
  waiting for transfers between devices  128 us (12%)
  other arithmetic  108 us (10%)
  starting transfers between devices  77.4 us (7%)
  matrix products  71.3 us (7%)
  between operations  41.7 us (4%)
    pallas_call x3, Pallas kernels, place(): pl.pallas_call(kernel, grid_spec=pltpu.PrefetchScalarGridSpec(num_scalar_...  268 us
    ppermute x49, waiting for transfers between devices, ring_shift(): lax.ppermute(value, 'fsdp', [(order[i], order[(i + step) % count]) for i...  81.9 us
    pallas_call x2, Pallas kernels, middle(): pl.pallas_call(kernel, grid_spec=pltpu.PrefetchScalarGridSpec(num_scalar_...  56.9 us
    ppermute x49, starting transfers between devices, ring_shift(): lax.ppermute(value, 'fsdp', [(order[i], order[(i + step) % count]) for i...  53.1 us
    pallas_call x1, Pallas kernels, attend_back(): pl.pallas_call(kernel, grid=(images, heads, steps), in_specs=[row_spec, r...  49.1 us
    pallas_call x2, Pallas kernels, attend(): pl.pallas_call(kernel, grid=(images, count), in_specs=[part, pl.BlockSpec...  39.3 us
    ppermute x15, local copies, waits for them, and re-layouts, swap(): return lax.ppermute(value, 'seq', [(i, i ^ bit) for i in range(count)])  33.3 us
    dot_general x5, matrix products, mm(): return lax.dot_general(left, right, dims, preferred_element_type=F32)  31.8 us
  transfers between devices with their start and end apart: 103, of which 31 were waited for; matrix products, arithmetic and copies ran while one was open for 30% of the time, Pallas kernels for 40%

profile of v1, /device:TPU:0, one launch (start us, length us, event | category | flops | bytes accessed | tf_op | source)
XLA Modules:
  0.0 1025.8 jit_solution(10509739833053206550)
XLA Ops:
  30.3 7.4 collective-permute-done.33.refs_5_
  48.5 6.9 collective-permute-done.34.refs_6_
  91.6 5.9 stack.125.index_ref
  100.0 5.8 stack.136.index_ref
  122.9 103.1 %place_blocks.5 = bf16[8,538,288]{2,1,0:T(8,128)(2,1)} custom-call(s32[8]{0:T(128)} %stack.136.index_ref, bf16[538,288]{1,0:T(8,128)(2,1)} %copy-done.25, bf16[538,288]{1,0:T(8,128)(2,1)} %collective-permute-done.29.refs_1_, bf16[538,288]{1,0:T(8,128)(2,1)} %collective-permute-done.30.refs_2_, bf16[538,288]{1,0:T(8,128)(2,1)} %collective-permute-done.31.refs_3_, ...), custom_call_target="tpu_custom_call" | custom-call | bytes 4958208 | tf_op jit(solution)/shard_map/place_blocks/pallas_call | solution.py:142
  254.9 8.6 collective-permute-done.22.refs_4_
  266.2 64.4 %place_blocks.3 = bf16[8,144,864]{2,1,0:T(8,128)(2,1)} custom-call(s32[8]{0:T(128)} %stack.125.index_ref, bf16[144,864]{1,0:T(8,128)(2,1)} %copy-done.27, bf16[144,864]{1,0:T(8,128)(2,1)} %collective-permute-done.6.refs_1_, bf16[144,864]{1,0:T(8,128)(2,1)} %collective-permute-done.7.refs_2_, bf16[144,864]{1,0:T(8,128)(2,1)} %collective-permute-done.8.refs_3_, ...), custom_call_target="tpu_custom_call" | custom-call | bytes 3981312 | tf_op jit(solution)/shard_map/place_blocks/pallas_call | solution.py:142
  330.6 100.1 %place_blocks.4 = bf16[8,144,1364]{2,1,0:T(8,128)(2,1)} custom-call(s32[8]{0:T(128)} %stack.125.index_ref, bf16[144,1364]{1,0:T(8,128)(2,1)} %copy-done.26, bf16[144,1364]{1,0:T(8,128)(2,1)} %collective-permute-done.19.refs_1_, bf16[144,1364]{1,0:T(8,128)(2,1)} %collective-permute-done.20.refs_2_, bf16[144,1364]{1,0:T(8,128)(2,1)} %collective-permute-done.21.refs_3_, ...), custom_call_target="tpu_custom_call" | custom-call | bytes 6285312 | tf_op jit(solution)/shard_map/place_blocks/pallas_call | solution.py:142
  436.5 7.7 convolution_convert_fusion.w_ref
  457.0 6.1 concatenate.114
  480.4 11.2 %add_convert_fusion = bf16[4,512,1536]{2,1,0:T(8,128)(2,1)} fusion(bf16[4,512,1152]{2,1,0:T(8,128)(2,1)S(1)} %add_convert_fusion.1, f32[1536]{0:T(1024)S(1)} %copy-done.73, f32[4,512]{1,0:T(4,128)S(1)} %copy-done.48, f32[1536]{0:T(1024)S(1)} %copy-done.51, f32[1536]{0:T(1024)S(1)} %copy-done.50, bf16[1152,1536]{1,0:T(8,128)(2,1)S(1)} %copy-done.78), kind=kOutput, calls=%fused_computation | convolution fusion | flops 7263485952 | bytes 14575616 | tf_op jit(solution)/shard_map/ijld,de->ijle/dot_general | solution.py:594
  491.6 19.4 %attend.2 = (bf16[1,4,256,288]{3,2,1,0:T(8,128)(2,1)}, bf16[1,4,512,512]{3,2,1,0:T(8,128)(2,1)}, f32[1,4,512,512]{3,2,1,0:T(8,128)}) custom-call(bf16[1,4,512,1536]{3,2,1,0:T(8,128)(2,1)} %bitcast.358, bf16[1,2048,1536]{2,1,0:T(8,128)(2,1)} %bitcast.359), custom_call_target="tpu_custom_call" | custom-call | flops 8589934592 | bytes 9437184 | tf_op jit(solution)/shard_map/attend/pallas_call | solution.py:254
  514.5 19.9 %attend.3 = (bf16[1,4,256,288]{3,2,1,0:T(8,128)(2,1)}, bf16[1,4,512,512]{3,2,1,0:T(8,128)(2,1)}, f32[1,4,512,512]{3,2,1,0:T(8,128)}) custom-call(bf16[1,4,512,1536]{3,2,1,0:T(8,128)(2,1)} %bitcast.360, bf16[1,2048,1536]{2,1,0:T(8,128)(2,1)} %bitcast.361, ...), custom_call_target="tpu_custom_call", output_to_operand_aliasing={{1}: (2, {}), {2}: (3, {})} | custom-call | flops 8589934592 | bytes 9437184 | tf_op jit(solution)/shard_map/attend/pallas_call | solution.py:254
  548.2 6.0 concatenate.113
  568.9 28.4 %middle.2 = (bf16[1,4,512,1152]{3,2,1,0:T(8,128)(2,1)}, bf16[1,4,512,1076]{3,2,1,0:T(8,128)(2,1)}, bf16[1,4,512,1076]{3,2,1,0:T(8,128)(2,1)}, bf16[1,4,512,1152]...) custom-call(s32[1]{0:T(128)} %bitcast.me_ref, ...), custom_call_target="tpu_custom_call" | custom-call | flops 25744637952 | bytes 30894080 | tf_op jit(solution)/shard_map/middle/pallas_call | solution.py:343
  598.6 28.5 %middle.3 = (bf16[1,4,512,1152]{3,2,1,0:T(8,128)(2,1)}, bf16[1,4,512,1076]{3,2,1,0:T(8,128)(2,1)}, bf16[1,4,512,1076]{3,2,1,0:T(8,128)(2,1)}, bf16[1,4,512,1152]...) custom-call(s32[1]{0:T(128)} %bitcast.me_ref, ...), custom_call_target="tpu_custom_call", output_to_operand_aliasing={{0}: (14, {}), {1}: (15, {}), {2}: (16, {}), {3}: (17, {})} | custom-call | flops 25744637952 | bytes 30894080 | tf_op jit(solution)/shard_map/middle/pallas_call | solution.py:343
  627.0 10.9 %fusion.3 = bf16[1076,1152]{1,0:T(8,128)(2,1)} fusion(bf16[1,4,512,1076]{3,2,1,0:T(8,128)(2,1)} %get-tuple-element.66, bf16[1,1,512,1152]{3,2,1,0:T(8,128)(2,1)} %bitcast.22, bf16[1,1,512,1152]{3,2,1,0:T(8,128)(2,1)} %bitcast.21, bf16[1,1,512,1152]{3,2,1,0:T(8,128)(2,1)} %bitcast.20, bf16[1,1,512,1152]{3,2,1,0:T(8,128)(2,1)S(1)} %bitcast.325), kind=kOutput, calls=%fused_computation.10 | convolution fusion | flops 5085522432 | bytes 11604992 | tf_op jit(solution)/shard_map/ijlf,ijld->fd/dot_general | solution.py:638
  653.5 11.6 %fusion.2 = bf16[1152,1076]{0,1:T(8,128)(2,1)} fusion(bf16[1,4,512,1076]{3,2,1,0:T(8,128)(2,1)} %get-tuple-element.65, bf16[1,4,512,1152]{3,2,1,0:T(8,128)(2,1)} %get-tuple-element.64), kind=kOutput, calls=%fused_computation.9 | convolution fusion | flops 5078444544 | bytes 11604992 | tf_op jit(solution)/shard_map/ijld,ijlf->df/dot_general | solution.py:641
  714.0 11.8 %collective-permute-done.47 = bf16[1,256,1152]{2,1,0:T(8,128)(2,1)} collective-permute-done((bf16[1,256,1152]{2,1,0:T(8,128)(2,1)}, bf16[1,256,1152]{2,1,0:T(8,128)(2,1)}, u32[]{:S(2)}, u32[]{:S(2)}) %collective-permute-start.47) | collective-permute-done | bytes 589856 | tf_op jit(solution)/shard_map/ppermute | solution.py:43
  748.2 5.4 collective-permute-done.96
  764.0 5.8 collective-permute-done.84
  789.8 7.2 collective-permute-done.101
  820.7 5.9 fusion.29
  831.0 6.1 mixed_back.2.refs_0_
  837.0 6.1 mixed_back.3
  843.2 49.1 %attend_back.1 = (bf16[1,2048,512]{2,1,0:T(8,128)(2,1)}, bf16[1,2048,512]{2,1,0:T(8,128)(2,1)}, bf16[1,2048,512]{2,1,0:T(8,128)(2,1)}) custom-call(bf16[1,2048,512]{2,1,0:T(8,128)(2,1)} %bitcast.366, bf16[1,2048,512]{2,1,0:T(8,128)(2,1)} %bitcast.332, bf16[1,2048,1536]{2,1,0:T(8,128)(2,1)} %bitcast.362, bf16[1,2048,1536]{2,1,0:T(8,128)(2,1)} %bitcast.363), custom_call_target="tpu_custom_call" | custom-call | flops 42949672960 | bytes 14680064 | tf_op jit(solution)/shard_map/attend_back/pallas_call | solution.py:460
  892.4 6.9 convolution_convert_fusion.3
  899.3 6.9 convolution_convert_fusion.4
  906.2 6.9 convolution_convert_fusion.2
  923.0 12.7 %project_back.1 = bf16[1,4,512,1152]{3,2,1,0:T(8,128)(2,1)} custom-call(bf16[1,4,512,512]{3,2,1,0:T(8,128)(2,1)} %bitcast.352, bf16[1,4,512,512]{3,2,1,0:T(8,128)(2,1)} %bitcast.365, bf16[1,4,512,512]{3,2,1,0:T(8,128)(2,1)} %bitcast.350, bf16[1152,1536]{1,0:T(8,128)(2,1)} %convolution_convert_fusion.w_ref), custom_call_target="tpu_custom_call" | custom-call | flops 7247757312 | bytes 14548992 | tf_op jit(solution)/shard_map/project_back/pallas_call | solution.py:488
  963.3 6.5 collective-permute-done.68
  984.1 12.9 %collective-permute-done.59 = bf16[1,512,1152]{2,1,0:T(8,128)(2,1)S(1)} collective-permute-done((bf16[1,512,1152]{2,1,0:T(8,128)(2,1)S(1)}, bf16[1,512,1152]{2,1,0:T(8,128)(2,1)S(1)}, u32[]{:S(2)}, u32[]{:S(2)}) %collective-permute-start.59) | collective-permute-done | bytes 1179680 | tf_op jit(solution)/shard_map/ppermute | solution.py:43
  (538 shorter events, 382.0 us)
Async XLA Ops:
  41.8 77.0 %collective-permute-start.31 = (bf16[538,288]{1,0:T(8,128)(2,1)}, bf16[538,288]{1,0:T(8,128)(2,1)}, u32[]{:S(2)}, u32[]{:S(2)}) collective-permute-start(bf16[538,288]{1,0:T(8,128)(2,1)} %collective-permute-done.30.refs_2_), channel_id=1, source_target_pairs={{0,2},{2,4},{4,6},{6,7},{7,5},{5,3},{3,1},{1,0},{8,10},{10,12},{12... | collective-permute-start | bytes 929672 | tf_op jit(solution)/shard_map/ppermute | solution.py:104
  46.5 181.2 %collective-permute-start.20 = (bf16[144,1364]{1,0:T(8,128)(2,1)}, bf16[144,1364]{1,0:T(8,128)(2,1)}, u32[]{:S(2)}, u32[]{:S(2)}) collective-permute-start(bf16[144,1364]{1,0:T(8,128)(2,1)} %collective-permute-done.19.refs_1_), channel_id=1, source_target_pairs={{0,2},{2,4},{4,6},{6,7},{7,5},{5,3},{3,1},{1,0},{8,10},{10,12},{12... | collective-permute-start | bytes 1178504 | tf_op jit(solution)/shard_map/ppermute | solution.py:104
  48.1 181.2 %collective-permute-start.24 = (bf16[144,1364]{1,0:T(8,128)(2,1)}, bf16[144,1364]{1,0:T(8,128)(2,1)}, u32[]{:S(2)}, u32[]{:S(2)}) collective-permute-start(bf16[144,1364]{1,0:T(8,128)(2,1)} %collective-permute-done.23.refs_5_), channel_id=1, source_target_pairs={{0,1},{2,0},{4,2},{6,4},{7,6},{5,7},{3,5},{1,3},{8,9},{10,8},{12,1... | collective-permute-start | bytes 1178504 | tf_op jit(solution)/shard_map/ppermute | solution.py:104
  55.4 64.5 %collective-permute-start.35 = (bf16[538,288]{1,0:T(8,128)(2,1)}, bf16[538,288]{1,0:T(8,128)(2,1)}, u32[]{:S(2)}, u32[]{:S(2)}) collective-permute-start(bf16[538,288]{1,0:T(8,128)(2,1)} %collective-permute-done.34.refs_6_), channel_id=1, source_target_pairs={{0,1},{2,0},{4,2},{6,4},{7,6},{5,7},{3,5},{1,3},{8,9},{10,8},{12,1... | collective-permute-start | bytes 929672 | tf_op jit(solution)/shard_map/ppermute | solution.py:104
  61.6 164.4 %collective-permute-start.8 = (bf16[144,864]{1,0:T(8,128)(2,1)}, bf16[144,864]{1,0:T(8,128)(2,1)}, u32[]{:S(2)}, u32[]{:S(2)}) collective-permute-start(bf16[144,864]{1,0:T(8,128)(2,1)} %collective-permute-done.7.refs_2_), channel_id=1, source_target_pairs={{0,2},{2,4},{4,6},{6,7},{7,5},{5,3},{3,1},{1,0},{8,10},{10,12},{12... | collective-permute-start | bytes 746504 | tf_op jit(solution)/shard_map/ppermute | solution.py:104
  118.8 136.0 %collective-permute-start.1 = (bf16[1,512,1152]{2,1,0:T(8,128)(2,1)S(1)}, bf16[1,512,1152]{2,1,0:T(8,128)(2,1)S(1)}, u32[]{:S(2)}, u32[]{:S(2)}) collective-permute-start(bf16[1,512,1152]{2,1,0:T(8,128)(2,1)S(1)} %copy-done), channel_id=1, source_target_pairs={{0,16},{8,24},{16,0},{24,8},{1,17},{9,25},{17,1},{25,9},{2,18},{10... | collective-permute-start | bytes 3538952 | tf_op jit(solution)/shard_map/ppermute | solution.py:43
  120.0 115.3 %collective-permute-start.12 = (bf16[144,864]{1,0:T(8,128)(2,1)}, bf16[144,864]{1,0:T(8,128)(2,1)}, u32[]{:S(2)}, u32[]{:S(2)}) collective-permute-start(bf16[144,864]{1,0:T(8,128)(2,1)} %copy-done.31), channel_id=1, source_target_pairs={{0,1},{2,0},{4,2},{6,4},{7,6},{5,7},{3,5},{1,3},{8,9},{10,8},{12,1... | collective-permute-start | bytes 746504 | tf_op jit(solution)/shard_map/ppermute | solution.py:104
  235.2 29.6 %collective-permute-start.36 = (bf16[2,538,288]{1,2,0:T(8,128)(2,1)}, bf16[2,538,288]{1,2,0:T(8,128)(2,1)}, u32[]{:S(2)}, u32[]{:S(2)}) collective-permute-start(bf16[2,538,288]{1,2,0:T(8,128)(2,1)} %copy.233), channel_id=1, source_target_pairs={{0,24},{8,16},{16,8},{24,0},{1,25},{9,17},{17,9},{25,1},{2,26},{10... | collective-permute-start | bytes 1859336 | tf_op jit(solution)/shard_map/ppermute | solution.py:43
  247.6 187.9 %collective-permute-start.37 = (bf16[2,538,288]{1,2,0:T(8,128)(2,1)}, bf16[2,538,288]{1,2,0:T(8,128)(2,1)}, u32[]{:S(2)}, u32[]{:S(2)}) collective-permute-start(bf16[2,538,288]{1,2,0:T(8,128)(2,1)} %copy.234), channel_id=1, source_target_pairs={{0,16},{8,24},{16,0},{24,8},{1,17},{9,25},{17,1},{25,9},{2,18},{10... | collective-permute-start | bytes 1859336 | tf_op jit(solution)/shard_map/ppermute | solution.py:43
  249.1 187.1 %collective-permute-start.38 = (bf16[2,538,288]{1,2,0:T(8,128)(2,1)}, bf16[2,538,288]{1,2,0:T(8,128)(2,1)}, u32[]{:S(2)}, u32[]{:S(2)}) collective-permute-start(bf16[2,538,288]{1,2,0:T(8,128)(2,1)} %copy.237), channel_id=1, source_target_pairs={{0,8},{8,0},{16,24},{24,16},{1,9},{9,1},{17,25},{25,17},{2,10},{10... | collective-permute-start | bytes 1859336 | tf_op jit(solution)/shard_map/ppermute | solution.py:43
  254.9 217.3 %collective-permute-start = (bf16[1,512,1152]{2,1,0:T(8,128)(2,1)S(1)}, bf16[1,512,1152]{2,1,0:T(8,128)(2,1)}, u32[]{:S(2)}, u32[]{:S(2)}) collective-permute-start(bf16[1,512,1152]{2,1,0:T(8,128)(2,1)S(1)} %copy-done), channel_id=1, source_target_pairs={{0,8},{8,0},{16,24},{24,16},{1,9},{9,1},{17,25},{25,17},{2,10},{10... | collective-permute-start | bytes 3538952 | tf_op jit(solution)/shard_map/ppermute | solution.py:43
  263.5 203.3 %collective-permute-start.17 = (bf16[1,512,1152]{2,1,0:T(8,128)(2,1)S(1)}, bf16[1,512,1152]{2,1,0:T(8,128)(2,1)}, u32[]{:S(2)}, u32[]{:S(2)}) collective-permute-start(bf16[1,512,1152]{2,1,0:T(8,128)(2,1)S(1)} %copy-done.7), channel_id=1, source_target_pairs={{0,16},{8,24},{16,0},{24,8},{1,17},{9,25},{17,1},{25,9},{2,18},{10... | collective-permute-start | bytes 3538952 | tf_op jit(solution)/shard_map/ppermute | solution.py:43
  264.8 207.3 %collective-permute-start.2 = (bf16[1,512,1152]{2,1,0:T(8,128)(2,1)S(1)}, bf16[1,512,1152]{2,1,0:T(8,128)(2,1)}, u32[]{:S(2)}, u32[]{:S(2)}) collective-permute-start(bf16[1,512,1152]{2,1,0:T(8,128)(2,1)S(1)} %collective-permute-done.1), channel_id=1, source_target_pairs={{0,8},{8,0},{16,24},{24,16},{1,9},{9,1},{17,25},{25,17},{2,10},{10... | collective-permute-start | bytes 3538952 | tf_op jit(solution)/shard_map/ppermute | solution.py:43
  435.5 31.6 %collective-permute-start.26 = (bf16[1152,288]{0,1:T(8,128)(2,1)}, bf16[1152,288]{0,1:T(8,128)(2,1)}, u32[]{:S(2)}, u32[]{:S(2)}) collective-permute-start(bf16[1152,288]{0,1:T(8,128)(2,1)} %copy.222), channel_id=1, source_target_pairs={{0,16},{8,24},{16,0},{24,8},{1,17},{9,25},{17,1},{25,9},{2,18},{10... | collective-permute-start | bytes 1990664 | tf_op jit(solution)/shard_map/ppermute | solution.py:43
  436.2 33.4 %collective-permute-start.28 = (bf16[1152,288]{0,1:T(8,128)(2,1)}, bf16[1152,288]{0,1:T(8,128)(2,1)}, u32[]{:S(2)}, u32[]{:S(2)}) collective-permute-start(bf16[1152,288]{0,1:T(8,128)(2,1)} %copy.222), channel_id=1, source_target_pairs={{0,8},{8,0},{16,24},{24,16},{1,9},{9,1},{17,25},{25,17},{2,10},{10... | collective-permute-start | bytes 1990664 | tf_op jit(solution)/shard_map/ppermute | solution.py:43
  466.8 69.9 %collective-permute-start.16 = (bf16[1,512,1152]{2,1,0:T(8,128)(2,1)S(1)}, bf16[1,512,1152]{2,1,0:T(8,128)(2,1)}, u32[]{:S(2)}, u32[]{:S(2)}) collective-permute-start(bf16[1,512,1152]{2,1,0:T(8,128)(2,1)S(1)} %copy-done.7), channel_id=1, source_target_pairs={{0,8},{8,0},{16,24},{24,16},{1,9},{9,1},{17,25},{25,17},{2,10},{10... | collective-permute-start | bytes 3538952 | tf_op jit(solution)/shard_map/ppermute | solution.py:43
  467.0 70.3 %collective-permute-start.18 = (bf16[1,512,1152]{2,1,0:T(8,128)(2,1)}, bf16[1,512,1152]{2,1,0:T(8,128)(2,1)}, u32[]{:S(2)}, u32[]{:S(2)}) collective-permute-start(bf16[1,512,1152]{2,1,0:T(8,128)(2,1)} %collective-permute-done.17), channel_id=1, source_target_pairs={{0,8},{8,0},{16,24},{24,16},{1,9},{9,1},{17,25},{25,17},{2,10},{10... | collective-permute-start | bytes 3538952 | tf_op jit(solution)/shard_map/ppermute | solution.py:43
  469.6 72.1 %collective-permute-start.27 = (bf16[1152,288]{0,1:T(8,128)(2,1)}, bf16[1152,288]{0,1:T(8,128)(2,1)}, u32[]{:S(2)}, u32[]{:S(2)}) collective-permute-start(bf16[1152,288]{0,1:T(8,128)(2,1)} %collective-permute-done.26), channel_id=1, source_target_pairs={{0,8},{8,0},{16,24},{24,16},{1,9},{9,1},{17,25},{25,17},{2,10},{10... | collective-permute-start | bytes 1990664 | tf_op jit(solution)/shard_map/ppermute | solution.py:43
  513.2 30.8 %collective-permute-start.14 = (bf16[1,4,256,288]{2,3,1,0:T(8,128)(2,1)}, bf16[1,4,256,288]{2,3,1,0:T(8,128)(2,1)}, u32[]{:S(2)}, u32[]{:S(2)}) collective-permute-start(bf16[1,4,256,288]{2,3,1,0:T(8,128)(2,1)} %copy.220), channel_id=1, source_target_pairs={{0,16},{8,24},{16,0},{24,8},{1,17},{9,25},{17,1},{25,9},{2,18},{10... | collective-permute-start | bytes 1769480 | tf_op jit(solution)/shard_map/ppermute | solution.py:43
  514.5 47.7 %collective-permute-start.13 = (bf16[1,4,256,288]{2,3,1,0:T(8,128)(2,1)}, bf16[1,4,256,288]{2,3,1,0:T(8,128)(2,1)}, u32[]{:S(2)}, u32[]{:S(2)}) collective-permute-start(bf16[1,4,256,288]{2,3,1,0:T(8,128)(2,1)} %copy.220), channel_id=1, source_target_pairs={{0,8},{8,0},{16,24},{24,16},{1,9},{9,1},{17,25},{25,17},{2,10},{10... | collective-permute-start | bytes 1769480 | tf_op jit(solution)/shard_map/ppermute | solution.py:43
  559.8 37.6 %collective-permute-start.41 = (bf16[1,4,256,288]{2,3,1,0:T(8,128)(2,1)}, bf16[1,4,256,288]{2,3,1,0:T(8,128)(2,1)S(1)}, u32[]{:S(2)}, u32[]{:S(2)}) collective-permute-start(bf16[1,4,256,288]{2,3,1,0:T(8,128)(2,1)} %collective-permute-done.40), channel_id=1, source_target_pairs={{0,8},{8,0},{16,24},{24,16},{1,9},{9,1},{17,25},{25,17},{2,10},{10... | collective-permute-start | bytes 1769480 | tf_op jit(solution)/shard_map/ppermute | solution.py:43
  649.3 47.9 %collective-permute-start.93 = (bf16[2,538,288]{1,2,0:T(8,128)(2,1)}, bf16[2,538,288]{1,2,0:T(8,128)(2,1)}, u32[]{:S(2)}, u32[]{:S(2)}) collective-permute-start(bf16[2,538,288]{1,2,0:T(8,128)(2,1)} %copy.269), channel_id=1, source_target_pairs={{0,8},{8,0},{16,24},{24,16},{1,9},{9,1},{17,25},{25,17},{2,10},{10... | collective-permute-start | bytes 1859336 | tf_op jit(solution)/shard_map/ppermute | solution.py:43
  650.7 47.7 %collective-permute-start.94 = (bf16[2,538,288]{1,2,0:T(8,128)(2,1)}, bf16[2,538,288]{1,2,0:T(8,128)(2,1)}, u32[]{:S(2)}, u32[]{:S(2)}) collective-permute-start(bf16[2,538,288]{1,2,0:T(8,128)(2,1)} %copy.270), channel_id=1, source_target_pairs={{0,16},{8,24},{16,0},{24,8},{1,17},{9,25},{17,1},{25,9},{2,18},{10... | collective-permute-start | bytes 1859336 | tf_op jit(solution)/shard_map/ppermute | solution.py:43
  653.2 52.4 %collective-permute-start.95 = (bf16[2,538,288]{1,2,0:T(8,128)(2,1)}, bf16[2,538,288]{1,2,0:T(8,128)(2,1)}, u32[]{:S(2)}, u32[]{:S(2)}) collective-permute-start(bf16[2,538,288]{1,2,0:T(8,128)(2,1)} %copy.271), channel_id=1, source_target_pairs={{0,24},{8,16},{16,8},{24,0},{1,25},{9,17},{17,9},{25,1},{2,26},{10... | collective-permute-start | bytes 1859336 | tf_op jit(solution)/shard_map/ppermute | solution.py:43
  705.6 54.9 %collective-permute-start.90 = (bf16[144,1076]{1,0:T(8,128)(2,1)}, bf16[144,1076]{1,0:T(8,128)(2,1)}, u32[]{:S(2)}, u32[]{:S(2)}) collective-permute-start(bf16[144,1076]{1,0:T(8,128)(2,1)} %get-tuple-element.154), channel_id=1, source_target_pairs={{0,1},{2,0},{4,2},{6,4},{7,6},{5,7},{3,5},{1,3},{8,9},{10,8},{12,1... | collective-permute-start | bytes 929672 | tf_op jit(solution)/shard_map/ppermute | solution.py:104
  712.3 62.1 %collective-permute-start.43 = (bf16[1,512,1152]{2,1,0:T(8,128)(2,1)}, bf16[1,512,1152]{2,1,0:T(8,128)(2,1)}, u32[]{:S(2)}, u32[]{:S(2)}) collective-permute-start(bf16[1,512,1152]{2,1,0:T(8,128)(2,1)} %pad_maximum_fusion.7), channel_id=1, source_target_pairs={{0,8},{8,0},{16,24},{24,16},{1,9},{9,1},{17,25},{25,17},{2,10},{10... | collective-permute-start | bytes 3538952 | tf_op jit(solution)/shard_map/ppermute | solution.py:43
  712.4 30.2 %collective-permute-start.87 = (bf16[144,1076]{1,0:T(8,128)(2,1)}, bf16[144,1076]{1,0:T(8,128)(2,1)}, u32[]{:S(2)}, u32[]{:S(2)}) collective-permute-start(bf16[144,1076]{1,0:T(8,128)(2,1)} %fusion.65), channel_id=1, source_target_pairs={{0,2},{2,4},{4,6},{6,7},{7,5},{5,3},{3,1},{1,0},{8,10},{10,12},{12... | collective-permute-start | bytes 929672 | tf_op jit(solution)/shard_map/ppermute | solution.py:104
  778.9 33.9 %collective-permute-start.54 = (bf16[1,256,1152]{2,1,0:T(8,128)(2,1)}, bf16[1,256,1152]{2,1,0:T(8,128)(2,1)}, u32[]{:S(2)}, u32[]{:S(2)}) collective-permute-start(bf16[1,256,1152]{2,1,0:T(8,128)(2,1)} %get-tuple-element.126), channel_id=1, source_target_pairs={{0,8},{8,0},{16,24},{24,16},{1,9},{9,1},{17,25},{25,17},{2,10},{10... | collective-permute-start | bytes 1769480 | tf_op jit(solution)/shard_map/ppermute | solution.py:43
  806.0 166.5 %collective-permute-start.42 = (bf16[1,512,1152]{2,1,0:T(8,128)(2,1)}, bf16[1,512,1152]{2,1,0:T(8,128)(2,1)}, u32[]{:S(2)}, u32[]{:S(2)}) collective-permute-start(bf16[1,512,1152]{2,1,0:T(8,128)(2,1)} %pad_maximum_fusion.6), channel_id=1, source_target_pairs={{0,8},{8,0},{16,24},{24,16},{1,9},{9,1},{17,25},{25,17},{2,10},{10... | collective-permute-start | bytes 3538952 | tf_op jit(solution)/shard_map/ppermute | solution.py:43
  812.7 160.1 %collective-permute-start.44 = (bf16[1,512,1152]{2,1,0:T(8,128)(2,1)}, bf16[1,512,1152]{2,1,0:T(8,128)(2,1)}, u32[]{:S(2)}, u32[]{:S(2)}) collective-permute-start(bf16[1,512,1152]{2,1,0:T(8,128)(2,1)} %add_convert_fusion.2), channel_id=1, source_target_pairs={{0,16},{8,24},{16,0},{24,8},{1,17},{9,25},{17,1},{25,9},{2,18},{10... | collective-permute-start | bytes 3538952 | tf_op jit(solution)/shard_map/ppermute | solution.py:43
  828.9 106.9 %collective-permute-start.73 = (bf16[144,288]{1,0:T(8,128)(2,1)}, bf16[144,288]{1,0:T(8,128)(2,1)}, u32[]{:S(2)}, u32[]{:S(2)}) collective-permute-start(bf16[144,288]{1,0:T(8,128)(2,1)} %get-tuple-element.180), channel_id=1, source_target_pairs={{0,2},{2,4},{4,6},{6,7},{7,5},{5,3},{3,1},{1,0},{8,10},{10,12},{12... | collective-permute-start | bytes 248840 | tf_op jit(solution)/shard_map/ppermute | solution.py:104
  830.5 109.9 %collective-permute-start.76 = (bf16[144,288]{1,0:T(8,128)(2,1)}, bf16[144,288]{1,0:T(8,128)(2,1)}, u32[]{:S(2)}, u32[]{:S(2)}) collective-permute-start(bf16[144,288]{1,0:T(8,128)(2,1)} %get-tuple-element.181), channel_id=1, source_target_pairs={{0,1},{2,0},{4,2},{6,4},{7,6},{5,7},{3,5},{1,3},{8,9},{10,8},{12,1... | collective-permute-start | bytes 248840 | tf_op jit(solution)/shard_map/ppermute | solution.py:104
  (150 other events, 3375.8 us)

commit v2 on v1

--- a/solution.py
+++ b/solution.py
@@ -91,11 +91,10 @@
 
 
 def ring_place():
-    order = ring_order()
-    table = np.zeros(len(order), np.int32)
-    for at, device in enumerate(order):
-        table[device] = at
-    return jnp.asarray(table)[lax.axis_index("fsdp")]
+    device = lax.axis_index("fsdp")
+    if lax.axis_size("fsdp") == 8:
+        return jnp.where(device % 2 == 0, device // 2, (15 - device) // 2)
+    return device
 
 
 def ring_shift(value, step):
@@ -107,51 +106,57 @@
 
 
 def ring_owner(offset):
-    order = ring_order()
-    return jnp.asarray(order, jnp.int32)[(ring_place() + offset) % len(order)]
+    count = lax.axis_size("fsdp")
+    at = lax.rem(ring_place() + (offset + count), count)
+    if count == 8:
+        return jnp.where(at < 4, 2 * at, 15 - 2 * at)
+    return at
 
 
 def ring_gather(value, flip):
     count = lax.axis_size("fsdp")
     found = [(0, value)]
     far = (count // 2, count - 1 - count // 2)
-    for step, reach in ((1, far[flip]), (-1, far[1 - flip])):
-        moving = value
-        for k in range(1, reach + 1):
-            moving = ring_shift(moving, step)
-            found.append((-step * k, moving))
+    moving = [value, value]
+    for k in range(1, count // 2 + 1):
+        for way, step in ((0, 1), (1, -1)):
+            if k <= far[way ^ flip]:
+                moving[way] = ring_shift(moving[way], step)
+                found.append((-step * k, moving[way]))
     index = jnp.stack([ring_owner(offset) for offset, _ in found])
-    return place([block for _, block in found], index)
-
-
-def place(blocks, index):
+    return [block for _, block in found], index
+
+
+def place(blocks, index, cuts, wide=None):
     count = len(blocks)
+    pieces = len(cuts) - 1
+    extra = [] if wide is None else [wide]
 
     def kernel(index_ref, *refs):
-        target, sems = refs[count], refs[count + 1]
-        copies = [
-            pltpu.make_async_copy(refs[i], target.at[index_ref[i]], sems.at[i])
-            for i in range(count)
-        ]
-        for copy in copies:
-            copy.start()
-        for copy in copies:
-            copy.wait()
+        outs = refs[count + len(extra) :]
+        for i in range(count):
+            for p in range(pieces):
+                value = refs[i][cuts[p] : cuts[p + 1]]
+                if extra:
+                    value = mm(value, refs[count][...]).astype(BF)
+                outs[p][index_ref[i]] = value
 
     block = blocks[0]
+    cols = block.shape[1] if wide is None else wide.shape[1]
+    shapes = [(count, cuts[p + 1] - cuts[p], cols) for p in range(pieces)]
     return pl.pallas_call(
         kernel,
         grid_spec=pltpu.PrefetchScalarGridSpec(
             num_scalar_prefetch=1,
             grid=(1,),
-            in_specs=[pl.BlockSpec(memory_space=pl.ANY)] * count,
-            out_specs=pl.BlockSpec(memory_space=pl.ANY),
-            scratch_shapes=[pltpu.SemaphoreType.DMA((count,))],
+            in_specs=[pl.BlockSpec(a.shape, lambda i, index: (0, 0)) for a in blocks + extra],
+            out_specs=[pl.BlockSpec(shape, lambda i, index: (0, 0, 0)) for shape in shapes],
         ),
-        out_shape=jax.ShapeDtypeStruct((count,) + block.shape, block.dtype),
-        cost_estimate=cost(0, 2 * count * block.size * 2),
+        out_shape=[jax.ShapeDtypeStruct(shape, BF) for shape in shapes],
+        cost_estimate=cost(0 if wide is None else count * block.size * cols, 4 * count * block.size),
+        compiler_params=pltpu.CompilerParams(vmem_limit_bytes=VMEM_BYTES),
         name="place_blocks",
-    )(index, *blocks)
+    )(index, *blocks, *extra)
 
 
 def ring_reduce(take, flip):
@@ -220,14 +225,20 @@
     flat = qkv.reshape(images, keys, 3 * wide_heads)
 
     def kernel(q_ref, kv_ref, *refs):
-        mixed_ref, query_ref, exact_ref = refs[-3:]
+        mixed_ref, query_ref, exact_ref, turned = refs[-4:]
+
+        @pl.when(pl.program_id(1) == 0)
+        def _():
+            for e in range(heads):
+                at = wide_heads + e * WIDE
+                turned[e] = kv_ref[0, :, at : at + WIDE].T
+
         total = jnp.zeros((rows, heads * HEAD), F32)
         for e in range(heads):
             here = slice(e * WIDE, (e + 1) * WIDE)
             query = q_ref[0, 0, :, here]
-            k = kv_ref[0, :, wide_heads + e * WIDE : wide_heads + (e + 1) * WIDE]
             v = kv_ref[0, :, 2 * wide_heads + e * WIDE : 2 * wide_heads + (e + 1) * WIDE]
-            scores = mm(query, k, NT)
+            scores = mm(query, turned[e])
             top = jnp.max(scores, axis=-1, keepdims=True)
             weights = jnp.exp2(scores - top).astype(BF)
             mixed = mm(weights, v)
@@ -259,6 +270,7 @@
         out_specs=outs,
         out_shape=shapes,
         input_output_aliases={2 + i: 1 + i for i in range(len(extra))},
+        scratch_shapes=[pltpu.VMEM((heads, WIDE, keys), BF)],
         cost_estimate=cost(2 * scores * WIDE * 2, flat.size * 2 + 3 * images * keys * wide_heads, scores),
         compiler_params=pltpu.CompilerParams(vmem_limit_bytes=VMEM_BYTES),
         name="attend",
@@ -267,16 +279,27 @@
 
 def middle(mixed, tokens, cotangent, weights, chunk, kept):
     images, count, length, width = tokens.shape
-    me, w_output, w_up, w_down, b_output, gain, shift, b_up = weights
+    me, w_output, w_up, up_turned, w_down, down_turned, b_output, gain, shift, b_up = weights
     rows = length // CHUNKS
     own = mixed[0].shape[-1]
+    both = 2 * rows
     hidden_count = w_up.shape[1]
 
     def kernel(me_ref, *refs):
         mixed_refs = refs[:count]
-        tok_ref, cot_ref, wo_ref, up_ref, down_ref, bo_ref, g_ref, s_ref, bu_ref = refs[
-            count : count + 9
-        ]
+        (
+            tok_ref,
+            cot_ref,
+            wo_ref,
+            up_ref,
+            up_turned_ref,
+            down_ref,
+            down_turned_ref,
+            bo_ref,
+            g_ref,
+            s_ref,
+            bu_ref,
+        ) = refs[count : count + 11]
         (
             h_ref,
             z_ref,
@@ -288,23 +311,24 @@
             gb_ref,
         ) = refs[-8:]
         block = pl.program_id(1)
-        x_one = tok_ref[0, 0].astype(F32) + bo_ref[...]
+        x_one = tok_ref[0].reshape(both, width).astype(F32) + bo_ref[...]
         pieces = []
         for i in range(count):
-            piece = mixed_refs[i][0, 0]
+            order = (1, 0) if i & 1 else (0, 1)
+            piece = jnp.concatenate([mixed_refs[i][0, at] for at in order], axis=0)
             pieces.append(piece)
             x_one = x_one + mm(piece, wo_ref[me_ref[0] ^ i])
-        cat_ref[0, 0] = jnp.concatenate(pieces, axis=-1)
+        cat_ref[0] = jnp.concatenate(pieces, axis=-1).reshape(2, rows, width)
 
         @pl.when(block == 0)
         def _():
-            x_ref[0] = x_one
+            x_ref[0] = x_one[:rows]
 
         normed, _ = norm_parts(x_one)
         h_two = (normed * g_ref[...] + s_ref[...]).astype(BF)
-        h_ref[0, 0] = h_two
+        h_ref[0] = h_two.reshape(2, rows, width)
         hidden = mm(h_two, up_ref[...]) + bu_ref[...]
-        grad_act = mm(cot_ref[0, 0], down_ref[...], NT)
+        grad_act = mm(cot_ref[0].reshape(both, width), down_turned_ref[...])
         square = hidden * hidden
         inner = jnp.tanh(ROOT * (hidden + CUBIC * square * hidden))
         half = 0.5 * (1.0 + inner)
@@ -312,10 +336,10 @@
         slope = half + 0.5 * hidden * (1.0 - inner * inner) * ROOT * (1.0 + 3.0 * CUBIC * square)
         wide_grad = grad_act * slope
         grad_hidden = wide_grad.astype(BF)
-        z_ref[0, 0] = z
-        du_ref[0, 0] = grad_hidden
-        dh_ref[0, 0] = mm(grad_hidden, up_ref[...], NT).astype(BF)
-        y_ref[0, 0] = mm(z, down_ref[...]).astype(BF)
+        z_ref[0] = z.reshape(2, rows, hidden_count)
+        du_ref[0] = grad_hidden.reshape(2, rows, hidden_count)
+        dh_ref[0] = mm(grad_hidden, up_turned_ref[...]).astype(BF).reshape(2, rows, width)
+        y_ref[0] = mm(z, down_ref[...]).astype(BF).reshape(2, rows, width)
         summed = jnp.sum(grad_hidden.astype(F32), axis=0, keepdims=True)
         first = (pl.program_id(0) == 0) & (block == 0)
 
@@ -328,15 +352,15 @@
             gb_ref[...] += summed
 
     def piece_spec(i):
-        return pl.BlockSpec((1, 1, rows, own), lambda im, b, me_ref: (im, b ^ i, 0, 0))
+        return pl.BlockSpec((1, 2, rows, own), lambda im, b, me_ref: (im, b ^ (i >> 1), 0, 0))
 
     def whole_spec(array):
         return pl.BlockSpec(array.shape, lambda im, b, me_ref: (0,) * array.ndim)
 
-    full = pl.BlockSpec((1, 1, rows, width), lambda im, b, me_ref: (im, b, chunk, 0))
-    full_hidden = pl.BlockSpec((1, 1, rows, hidden_count), lambda im, b, me_ref: (im, b, chunk, 0))
-    part = pl.BlockSpec((1, 1, rows, width), lambda im, b, me_ref: (im, b, 0, 0))
-    constants = [w_output, w_up, w_down, b_output, gain, shift, b_up]
+    full = pl.BlockSpec((1, 2, rows, width), lambda im, b, me_ref: (im, b, chunk, 0))
+    full_hidden = pl.BlockSpec((1, 2, rows, hidden_count), lambda im, b, me_ref: (im, b, chunk, 0))
+    part = pl.BlockSpec((1, 2, rows, width), lambda im, b, me_ref: (im, b, 0, 0))
+    constants = [w_output, w_up, up_turned, w_down, down_turned, b_output, gain, shift, b_up]
     extra = list(kept)
     inputs = [*mixed, tokens, cotangent, *constants, *extra]
     all_rows = images * count * rows
@@ -344,7 +368,7 @@
         kernel,
         grid_spec=pltpu.PrefetchScalarGridSpec(
             num_scalar_prefetch=1,
-            grid=(images, count),
+            grid=(images, count // 2),
             in_specs=[piece_spec(i) for i in range(count)]
             + [full, full]
             + [whole_spec(array) for array in constants]
@@ -370,7 +394,7 @@
             jax.ShapeDtypeStruct((images, rows, width), F32),
             jax.ShapeDtypeStruct((1, hidden_count), F32),
         ],
-        input_output_aliases={1 + count + 9 + i: i for i in range(len(extra))},
+        input_output_aliases={1 + count + 11 + i: i for i in range(len(extra))},
         cost_estimate=cost(
             all_rows * width * (width + 4 * hidden_count) * 2,
             all_rows * (width * 16 + hidden_count * 4) + (w_output.size + 2 * w_up.size) * 2,
@@ -387,7 +411,7 @@
 
     def kernel(grad_ref, w_ref, exact_ref, *refs):
         out_ref = refs[-1]
-        result = mm(grad_ref[0, 0], w_ref[...], NT).astype(BF).astype(F32)
+        result = mm(grad_ref[0, 0], w_ref[...]).astype(BF).astype(F32)
         for e in range(heads):
             here = slice(e * WIDE, (e + 1) * WIDE)
             mine = result[:, here]
@@ -476,12 +500,12 @@
 
 def project_back(grads, w_wide):
     images, count, length, wide_heads = grads[0].shape
-    width = w_wide.shape[0]
+    width = w_wide.shape[1]
 
     def kernel(q_ref, k_ref, v_ref, w_ref, out_ref):
         total = jnp.zeros((length, width), F32)
         for i, ref in enumerate((q_ref, k_ref, v_ref)):
-            total = total + mm(ref[0, 0], w_ref[:, i * wide_heads : (i + 1) * wide_heads], NT)
+            total = total + mm(ref[0, 0], w_ref[i * wide_heads : (i + 1) * wide_heads])
         out_ref[0, 0] = total.astype(BF)
 
     block = pl.BlockSpec((1, 1, length, wide_heads), lambda im, b: (im, b, 0, 0))
@@ -536,12 +560,18 @@
         + [gain_one, shift_one, b_output, gain_two, shift_two, b_down]
     )
     small = spread(small)
-    qkv_rows = ring_gather(qkv_shard, 0).reshape(width, 3 * own)
-    down_rows = ring_gather(w_down, 1)
-    upper = ring_gather(jnp.concatenate([w_up, w_output], axis=1), 0)
-    upper = upper.reshape(width, -1)
-    up_mat = upper[:, : w_up.shape[1]]
-    output_cols = upper[:, w_up.shape[1] :]
+    qkv_blocks, qkv_index = ring_gather(qkv_shard, 0)
+    w_wide = place(
+        qkv_blocks, qkv_index, (0, qkv_shard.shape[0]), widen(3 * own, 3 * wide_heads)
+    )[0].reshape(width, 3 * wide_heads)
+    lower_shard = jnp.concatenate([w_output, w_down], axis=0)
+    lower_shard, up_shard, _ = lax.optimization_barrier((lower_shard, w_up, qkv_blocks[-1]))
+    cut = w_output.shape[0]
+    output_cols, down_rows = place(
+        *ring_gather(lower_shard, 1), (0, cut, cut + w_down.shape[0])
+    )
+    output_cols = output_cols.reshape(width, own)
+    up_mat = place(*ring_gather(up_shard, 0), (0, cut))[0].reshape(width, -1)
 
     patches = images * length
     valid = jnp.stack([block[:patches].reshape(images, length) for block in small], axis=1)
@@ -561,9 +591,8 @@
     down_mat = jnp.concatenate(reorder(down_parts, me), axis=2).reshape(-1, width)
 
     expand = widen(own, wide_heads)
-    w_wide = mm(qkv_rows, widen(3 * own, 3 * wide_heads)).astype(BF)
     own_rows = lax.dynamic_index_in_dim(output_mat, me, 0, keepdims=False)
-    output_wide = mm(expand.T, own_rows).astype(BF)
+    output_wide = mm(own_rows.T, expand).astype(BF)
     lane = np.arange(3 * wide_heads) % WIDE
     kind = np.arange(3 * wide_heads) // wide_heads
     factor = np.where(kind == 0, SCALE * LOG2E, 1.0).astype(np.float32)
@@ -583,12 +612,13 @@
         [widen_vector(b_query), jnp.zeros((wide_heads,), F32), widen_vector(b_value)]
     )
     bias_wide = bias_wide * factor + ones.astype(np.float32)
-    weights = (me, output_mat, up_mat, down_mat, b_out, g_two, s_two, b_up.astype(F32)[None])
+    weights = (me, output_mat, up_mat, up_mat.T, down_mat, down_mat.T, b_out, g_two, s_two, b_up.astype(F32)[None])
 
     def run(tokens, bias_mask, cotangent):
         images = tokens.shape[0]
         tok_all = jnp.stack(spread(tokens), axis=1)
-        cot_all = jnp.stack(spread(cotangent), axis=1)
+        tok_all, cot_first = lax.optimization_barrier((tok_all, cotangent))
+        cot_all = jnp.stack(spread(cot_first), axis=1)
         normed, _ = norm_parts(tok_all.astype(F32))
         h_one = (normed * g_one + s_one).astype(BF)
         product = jnp.einsum("ijld,de->ijle", h_one, w_wide, preferred_element_type=F32)
@@ -652,12 +682,13 @@
             qkv.reshape(images, count * length, 3 * wide_heads),
         )
         grads = [g.reshape(images, count, length, wide_heads) for g in grads]
-        grad_h = project_back(grads, w_wide)
+        grad_h = project_back(grads, w_wide.T)
         grad_norm_one = collect([grad_h[:, j] for j in range(count)]).astype(F32)
         qkv_grad = [
             jnp.einsum("ijld,ijle->de", h_one, g, preferred_element_type=F32) for g in grads
         ]
 
+        out_parts, grad_mixed = lax.optimization_barrier((out_parts, grad_mixed))
         out_sum = collect(
             [jnp.concatenate([y[:, j] for y in out_parts], axis=1) for j in range(count)]
         )
@@ -692,29 +723,22 @@
         layer_out, grad_tokens = layer_out[:, 0], grad_tokens[:, 0]
     down_grad, up_grad, output_grad, qkv_grad, early, up_bias_grad, late, bias_grads = sums
 
-    def relative(f):
-        return ((f // group) ^ me) * group + f % group
-
     down_grad = down_grad.astype(BF).reshape(group, -1, width)
 
     def down_cols(j):
         return lax.dynamic_slice_in_dim(down_grad, (me ^ j) * own, own, 2)
 
-    down_pieces = jnp.concatenate(
-        [down_cols(0)] + [swap(down_cols(j), j) for j in range(1, count)], axis=0
-    )
-    final_down = ring_reduce(
-        lambda f: lax.dynamic_index_in_dim(down_pieces, relative(f), 0, keepdims=False), 1
-    )
-    up_grad = up_grad.astype(BF).reshape(fcount, width // fcount, -1)
-    final_up = ring_reduce(lambda f: lax.dynamic_index_in_dim(up_grad, f, 0, keepdims=False), 0)
-    output_grad = output_grad.astype(BF).reshape(fcount, width // fcount, -1)
-    final_output = ring_reduce(
-        lambda f: lax.dynamic_index_in_dim(output_grad, relative(f), 0, keepdims=False), 1
-    )
+    down_pieces = [down_cols(0)] + [swap(down_cols(j), j) for j in range(1, count)]
+    down_pieces = jnp.concatenate(reorder(down_pieces, me), axis=0)
+    final_up = lax.psum_scatter(
+        up_grad.astype(BF).reshape(fcount, width // fcount, -1), "fsdp", scatter_dimension=0
+    ).astype(F32)
+    final_down = lax.psum_scatter(down_pieces, "fsdp", scatter_dimension=0).astype(F32)
+    output_grad = reorder(jnp.split(output_grad.astype(BF), count, axis=0), me)
+    output_grad = jnp.concatenate(output_grad, axis=0)
     qkv_grad = [mm(full.astype(BF), expand, NT).astype(BF) for full in qkv_grad]
-    qkv_grad = jnp.concatenate(qkv_grad, axis=1).reshape(fcount, width // fcount, -1)
-    final_qkv = ring_reduce(lambda f: lax.dynamic_index_in_dim(qkv_grad, f, 0, keepdims=False), 0)
+    four = jnp.concatenate(qkv_grad + [output_grad], axis=1).reshape(fcount, width // fcount, -1)
+    four = ring_reduce(lambda f: lax.dynamic_index_in_dim(four, f, 0, keepdims=False), 0)
 
     def to_owner(stack):
         kinds = stack.shape[0]
@@ -732,8 +756,8 @@
     gain_one_grad, shift_one_grad, b_query_grad, b_value_grad = [
         late[i * own : (i + 1) * own] for i in range(4)
     ]
-    final_query, final_key, final_value = [
-        final_qkv[:, i * own : (i + 1) * own] for i in range(3)
+    final_query, final_key, final_value, final_output = [
+        four[:, i * own : (i + 1) * own] for i in range(4)
     ]
     return (
         layer_out,

time: 1040 us -> 762 us (0.73)
  Pallas kernels: 438 us -> 193 us
  waiting for transfers between devices: 128 us -> 176 us
  between operations: 41.7 us -> 15.5 us
  other arithmetic: 108 us -> 90.7 us
  local copies, waits for them, and re-layouts: 162 us -> 149 us
  matrix products: 71.3 us -> 58.9 us
    pallas_call x3, Pallas kernels: 268 us -> 18 us  [place(): pl.pallas_call(kernel, grid_spec=pltpu.PrefetchScalarGridSpec(num_scalar_...]
    ppermute x48, waiting for transfers between devices: 28.3 us -> 113 us  [swap(): return lax.ppermute(value, 'seq', [(i, i ^ bit) for i in range(count)])]
    ppermute x49 -> x28, starting transfers between devices: 53.1 us -> 31.2 us  [ring_shift(): lax.ppermute(value, 'fsdp', [(order[i], order[(i + step) % count]) for i...]
    ppermute x49 -> x28, waiting for transfers between devices: 81.9 us -> 61.9 us  [ring_shift(): lax.ppermute(value, 'fsdp', [(order[i], order[(i + step) % count]) for i...]
    ppermute x6, waiting for transfers between devices: 17.8 us -> 1.39 us  [ring_sum(): lax.ppermute(value, 'fsdp', [(i, i ^ bit) for i in range(count)])]
    reshape x0 -> x3, local copies, waits for them, and re-layouts: none -> 13.5 us  [the longest x1 6.05 us: local(): w_wide = place(qkv_blocks, qkv_index, (0, qkv_shard.shape[0]), widen(3 *...]
    convert_element_type x16 -> x4, other arithmetic: 18.4 us -> 5.51 us  [ring_reduce(): part = (part.astype(F32) + incoming.astype(F32)).astype(BF)]
    ppermute x0 -> x7, local copies, waits for them, and re-layouts: none -> 12.2 us  [ring_shift(): lax.ppermute(value, 'fsdp', [(order[i], order[(i + step) % count]) for i...]
  transfers between devices with their start and end apart: 103 -> 84, of which waited for: 31 -> 22; matrix products, arithmetic and copies ran while one was open for 30% -> 35% of each run, Pallas kernels for 40% -> 18%
where the time goes in v2:
time: 762 us; the launch traced here: 753 us
  Pallas kernels  193 us (25%)
  waiting for transfers between devices  176 us (23%)
  local copies, waits for them, and re-layouts  149 us (20%)
  other arithmetic  90.7 us (12%)
  starting transfers between devices  68.9 us (9%)
  matrix products  58.9 us (8%)
  between operations  15.5 us (2%)
    ppermute x48, waiting for transfers between devices, swap(): return lax.ppermute(value, 'seq', [(i, i ^ bit) for i in range(count)])  113 us
    ppermute x28, waiting for transfers between devices, ring_shift(): lax.ppermute(value, 'fsdp', [(order[i], order[(i + step) % count]) for i...  61.9 us
    pallas_call x2, Pallas kernels, middle(): pl.pallas_call(kernel, grid_spec=pltpu.PrefetchScalarGridSpec(num_scalar_...  60.5 us
    pallas_call x1, Pallas kernels, attend_back(): pl.pallas_call(kernel, grid=(images, heads, steps), in_specs=[row_spec, r...  49.3 us
    pallas_call x2, Pallas kernels, attend(): pl.pallas_call(kernel, grid=(images, count), in_specs=[part, pl.BlockSpec...  40.1 us
    ppermute x28, starting transfers between devices, ring_shift(): lax.ppermute(value, 'fsdp', [(order[i], order[(i + step) % count]) for i...  31.2 us
    ppermute x48, starting transfers between devices, swap(): return lax.ppermute(value, 'seq', [(i, i ^ bit) for i in range(count)])  28.1 us
    dot_general x4, matrix products, mm(): return lax.dot_general(left, right, dims, preferred_element_type=F32)  24.9 us
  transfers between devices with their start and end apart: 84, of which 22 were waited for; matrix products, arithmetic and copies ran while one was open for 35% of the time, Pallas kernels for 18%

profile of v2, /device:TPU:0, one launch (start us, length us, event | category | flops | bytes accessed | tf_op | source)
XLA Modules:
  0.0 752.6 jit_solution(13829515408317353344)
XLA Ops:
  13.7 6.3 collective-permute-done.6.refs_1_
  52.1 9.6 %collective-permute-done.11.refs_6_ = bf16[144,864]{1,0:T(8,128)(2,1)S(1)} collective-permute-done((bf16[144,864]{1,0:T(8,128)(2,1)}, bf16[144,864]{1,0:T(8,128)(2,1)S(1)}, u32[]{:S(2)}, u32[]{:S(2)}) %collective-permute-start.11) | collective-permute-done | bytes 248864 | tf_op jit(solution)/shard_map/ppermute | solution.py:103
  76.2 7.4 collective-permute-done.22
  84.7 8.8 %place_blocks.3 = bf16[8,144,1536]{2,1,0:T(8,128)(2,1)} custom-call(s32[8]{0:T(128)} %stack.170.index_ref, bf16[144,864]{1,0:T(8,128)(2,1)} %pad_maximum_fusion.10.refs_0_, bf16[144,864]{1,0:T(8,128)(2,1)} %copy-done.55, bf16[144,864]{1,0:T(8,128)(2,1)} %collective-permute-done.7.refs_2_, bf16[144,864]{1,0:T(8,128)(2,1)} %copy-done.56, ...), custom_call_target="tpu_custom_call" | custom-call | flops 3057647616 | bytes 3981312 | tf_op jit(solution)/shard_map/place_blocks/pallas_call | solution.py:147
  106.4 10.9 %add_convert_fusion = bf16[4,512,1536]{2,1,0:T(8,128)(2,1)} fusion(bf16[1152,1536,1]{1,0,2:T(8,128)(2,1)S(1)} %bitcast.274, f32[1536]{0:T(1024)S(1)} %copy-done.58, f32[4,512]{1,0:T(4,128)S(1)} %get-tuple-element.242, f32[1536]{0:T(1024)S(1)} %fusion.63, f32[1536]{0:T(1024)S(1)} %copy-done.38, bf16[1,4,512,1152]{3,2,1,0:T(8,128)(2,1)S(1)} %pad_maximum_fusion.refs_4_, ...), kind=kOutput, calls=%fused_computation | convolution fusion | flops 7277641728 | bytes 14601216 | tf_op jit(solution)/shard_map/ijld,de->ijle/dot_general | solution.py:624
  117.3 19.9 %attend.2 = (bf16[1,4,256,288]{3,2,1,0:T(8,128)(2,1)}, bf16[1,4,512,512]{3,2,1,0:T(8,128)(2,1)}, f32[1,4,512,512]{3,2,1,0:T(8,128)}) custom-call(bf16[1,4,512,1536]{3,2,1,0:T(8,128)(2,1)} %bitcast.304, bf16[1,2048,1536]{2,1,0:T(8,128)(2,1)} %bitcast.305), custom_call_target="tpu_custom_call" | custom-call | flops 8589934592 | bytes 9437184 | tf_op jit(solution)/shard_map/attend/pallas_call | solution.py:265
  140.9 20.2 %attend.3 = (bf16[1,4,256,288]{3,2,1,0:T(8,128)(2,1)}, bf16[1,4,512,512]{3,2,1,0:T(8,128)(2,1)}, f32[1,4,512,512]{3,2,1,0:T(8,128)}) custom-call(bf16[1,4,512,1536]{3,2,1,0:T(8,128)(2,1)} %bitcast.306, bf16[1,2048,1536]{2,1,0:T(8,128)(2,1)} %bitcast.307, ...), custom_call_target="tpu_custom_call", output_to_operand_aliasing={{1}: (2, {}), {2}: (3, {})} | custom-call | flops 8589934592 | bytes 9437184 | tf_op jit(solution)/shard_map/attend/pallas_call | solution.py:265
  203.8 17.8 %collective-permute-done.36 = bf16[2,538,288]{1,2,0:T(8,128)(2,1)S(1)} collective-permute-done((bf16[2,538,288]{1,2,0:T(8,128)(2,1)}, bf16[2,538,288]{1,2,0:T(8,128)(2,1)S(1)}, u32[]{:S(2)}, u32[]{:S(2)}) %collective-permute-start.36) | collective-permute-done | bytes 619808 | tf_op jit(solution)/shard_map/ppermute | solution.py:43
  222.2 16.1 %collective-permute-done.37 = bf16[2,538,288]{1,2,0:T(8,128)(2,1)} collective-permute-done((bf16[2,538,288]{1,2,0:T(8,128)(2,1)}, bf16[2,538,288]{1,2,0:T(8,128)(2,1)}, u32[]{:S(2)}, u32[]{:S(2)}) %collective-permute-start.37) | collective-permute-done | bytes 619808 | tf_op jit(solution)/shard_map/ppermute | solution.py:43
  239.5 6.0 copy.132
  271.6 5.8 concatenate.100
  293.3 6.0 pad_maximum_fusion.3
  299.2 5.2 copy.112
  308.0 30.2 %middle.2 = (bf16[1,4,512,1152]{3,2,1,0:T(8,128)(2,1)}, bf16[1,4,512,1076]{3,2,1,0:T(8,128)(2,1)}, bf16[1,4,512,1076]{3,2,1,0:T(8,128)(2,1)}, bf16[1,4,512,1152]...) custom-call(s32[1]{0:T(128)} %bitcast.me_ref, ...), custom_call_target="tpu_custom_call" | custom-call | flops 25744637952 | bytes 30894080 | tf_op jit(solution)/shard_map/middle/pallas_call | solution.py:367
  338.2 30.3 %middle.3 = (bf16[1,4,512,1152]{3,2,1,0:T(8,128)(2,1)}, bf16[1,4,512,1076]{3,2,1,0:T(8,128)(2,1)}, bf16[1,4,512,1076]{3,2,1,0:T(8,128)(2,1)}, bf16[1,4,512,1152]...) custom-call(s32[1]{0:T(128)} %bitcast.me_ref, ...), custom_call_target="tpu_custom_call", output_to_operand_aliasing={{0}: (16, {}), {1}: (17, {}), {2}: (18, {}), {3}: (19, {})} | custom-call | flops 25744637952 | bytes 30894080 | tf_op jit(solution)/shard_map/middle/pallas_call | solution.py:367
  368.5 10.4 %fusion.7 = bf16[1076,1152]{1,0:T(8,128)(2,1)} fusion(bf16[1,4,512,1076]{3,2,1,0:T(8,128)(2,1)} %get-tuple-element.82, bf16[1,1,512,1152]{3,2,1,0:T(8,128)(2,1)S(1)} %bitcast.294, bf16[1,1,512,1152]{3,2,1,0:T(8,128)(2,1)} %bitcast.22, bf16[1,1,512,1152]{3,2,1,0:T(8,128)(2,1)S(1)} %bitcast.292, bf16[1,1,512,1152]{3,2,1,0:T(8,128)(2,1)S(1)} %bitcast.260), kind=kOutput, calls=%fused_computation.12 | convolution fusion | flops 5085522432 | bytes 11604992 | tf_op jit(solution)/shard_map/ijlf,ijld->fd/dot_general | solution.py:668
  378.9 7.7 %fusion.6 = bf16[1152,1076]{0,1:T(8,128)(2,1)} fusion(bf16[1,4,512,1076]{3,2,1,0:T(8,128)(2,1)S(1)} %copy-done.62, bf16[1,4,512,1152]{3,2,1,0:T(8,128)(2,1)S(1)} %copy-done.61), kind=kOutput, calls=%fused_computation.11 | convolution fusion | flops 5078444544 | bytes 11604992 | tf_op jit(solution)/shard_map/ijld,ijlf->df/dot_general | solution.py:671
  408.8 8.2 %collective-permute-done.44 = bf16[1,256,1152]{2,1,0:T(8,128)(2,1)} collective-permute-done((bf16[1,256,1152]{2,1,0:T(8,128)(2,1)}, bf16[1,256,1152]{2,1,0:T(8,128)(2,1)}, u32[]{:S(2)}, u32[]{:S(2)}) %collective-permute-start.44) | collective-permute-done | bytes 589856 | tf_op jit(solution)/shard_map/ppermute | solution.py:43
  417.1 12.0 %collective-permute-done.50 = bf16[1,256,1152]{2,1,0:T(8,128)(2,1)} collective-permute-done((bf16[1,256,1152]{2,1,0:T(8,128)(2,1)}, bf16[1,256,1152]{2,1,0:T(8,128)(2,1)}, u32[]{:S(2)}, u32[]{:S(2)}) %collective-permute-start.50) | collective-permute-done | bytes 589856 | tf_op jit(solution)/shard_map/ppermute | solution.py:43
  458.7 26.4 %collective-permute-done.75 = f32[4,288]{1,0:T(4,128)S(1)} collective-permute-done((f32[4,288]{1,0:T(4,128)S(1)}, f32[4,288]{1,0:T(4,128)S(1)}, u32[]{:S(2)}, u32[]{:S(2)}) %collective-permute-start.75) | collective-permute-done | bytes 4640 | tf_op jit(solution)/shard_map/ppermute | solution.py:43
  515.5 6.0 mixed_back.2.refs_0_
  524.8 6.1 mixed_back.3
  531.0 49.3 %attend_back.1 = (bf16[1,2048,512]{2,1,0:T(8,128)(2,1)}, bf16[1,2048,512]{2,1,0:T(8,128)(2,1)}, bf16[1,2048,512]{2,1,0:T(8,128)(2,1)}) custom-call(bf16[1,2048,512]{2,1,0:T(8,128)(2,1)} %bitcast.312, bf16[1,2048,512]{2,1,0:T(8,128)(2,1)} %bitcast.271, bf16[1,2048,1536]{2,1,0:T(8,128)(2,1)} %bitcast.308, bf16[1,2048,1536]{2,1,0:T(8,128)(2,1)} %bitcast.309), custom_call_target="tpu_custom_call" | custom-call | flops 42949672960 | bytes 14680064 | tf_op jit(solution)/shard_map/attend_back/pallas_call | solution.py:484
  580.3 7.3 convolution_convert_fusion.3
  587.6 7.2 convolution_convert_fusion.2
  594.8 7.2 convolution_convert_fusion.1
  613.0 5.3 copy.142
  622.2 12.6 %project_back.1 = bf16[1,4,512,1152]{3,2,1,0:T(8,128)(2,1)} custom-call(bf16[1,4,512,512]{3,2,1,0:T(8,128)(2,1)} %bitcast.287, bf16[1,4,512,512]{3,2,1,0:T(8,128)(2,1)} %bitcast.311, bf16[1,4,512,512]{3,2,1,0:T(8,128)(2,1)} %bitcast.289, bf16[1536,1152]{1,0:T(8,128)(2,1)} %bitcast.272), custom_call_target="tpu_custom_call" | custom-call | flops 7247757312 | bytes 14548992 | tf_op jit(solution)/shard_map/project_back/pallas_call | solution.py:512
  645.9 6.1 collective-permute-done.67
  657.4 5.6 collective-permute-done.68
  684.2 17.1 %collective-permute-done.59 = bf16[1,512,1152]{2,1,0:T(8,128)(2,1)S(1)} collective-permute-done((bf16[1,512,1152]{2,1,0:T(8,128)(2,1)S(1)}, bf16[1,512,1152]{2,1,0:T(8,128)(2,1)S(1)}, u32[]{:S(2)}, u32[]{:S(2)}) %collective-permute-start.59) | collective-permute-done | bytes 1179680 | tf_op jit(solution)/shard_map/ppermute | solution.py:43
  712.2 10.8 %collective-permute-done.62 = f32[2,288]{1,0:T(2,128)S(1)} collective-permute-done((f32[2,288]{1,0:T(2,128)S(1)}, f32[2,288]{1,0:T(2,128)S(1)}, u32[]{:S(2)}, u32[]{:S(2)}) %collective-permute-start.62) | collective-permute-done | bytes 2336 | tf_op jit(solution)/shard_map/ppermute | solution.py:43
  (460 shorter events, 331.0 us)
Async XLA Ops:
  7.2 734.3 %reduce-scatter.3.cloned.1.call-start = ((), (), s32[]{:S(2)}) async-start(), calls=%async_computation.2 | async-start | bytes 2985984 | tf_op jit(solution)/shard_map/reduce_scatter | solution.py:733
  7.2 38.3 %collective-permute-start.1 = (bf16[1,512,1152]{2,1,0:T(8,128)(2,1)}, bf16[1,512,1152]{2,1,0:T(8,128)(2,1)S(1)}, u32[]{:S(2)}, u32[]{:S(2)}) collective-permute-start(bf16[1,512,1152]{2,1,0:T(8,128)(2,1)} %param.21), channel_id=1, source_target_pairs={{0,16},{8,24},{16,0},{24,8},{1,17},{9,25},{17,1},{25,9},{2,18},{10... | collective-permute-start | bytes 3538952 | tf_op jit(solution)/shard_map/ppermute | solution.py:43
  28.8 34.5 %collective-permute-start = (bf16[1,512,1152]{2,1,0:T(8,128)(2,1)}, bf16[1,512,1152]{2,1,0:T(8,128)(2,1)}, u32[]{:S(2)}, u32[]{:S(2)}) collective-permute-start(bf16[1,512,1152]{2,1,0:T(8,128)(2,1)} %param.21), channel_id=1, source_target_pairs={{0,8},{8,0},{16,24},{24,16},{1,9},{9,1},{17,25},{25,17},{2,10},{10... | collective-permute-start | bytes 3538952 | tf_op jit(solution)/shard_map/ppermute | solution.py:43
  45.5 55.2 %collective-permute-start.2 = (bf16[1,512,1152]{2,1,0:T(8,128)(2,1)S(1)}, bf16[1,512,1152]{2,1,0:T(8,128)(2,1)}, u32[]{:S(2)}, u32[]{:S(2)}) collective-permute-start(bf16[1,512,1152]{2,1,0:T(8,128)(2,1)S(1)} %collective-permute-done.1), channel_id=1, source_target_pairs={{0,8},{8,0},{16,24},{24,16},{1,9},{9,1},{17,25},{25,17},{2,10},{10... | collective-permute-start | bytes 3538952 | tf_op jit(solution)/shard_map/ppermute | solution.py:43
  93.6 69.8 %collective-permute-start.33 = (bf16[144,1076]{1,0:T(8,128)(2,1)}, bf16[144,1076]{1,0:T(8,128)(2,1)}, u32[]{:S(2)}, u32[]{:S(2)}) collective-permute-start(bf16[144,1076]{1,0:T(8,128)(2,1)} %collective-permute-done.31.refs_3_), channel_id=1, source_target_pairs={{0,2},{2,4},{4,6},{6,7},{7,5},{5,3},{3,1},{1,0},{8,10},{10,12},{12... | collective-permute-start | bytes 929672 | tf_op jit(solution)/shard_map/ppermute | solution.py:103
  95.1 68.2 %collective-permute-start.34 = (bf16[144,1076]{1,0:T(8,128)(2,1)}, bf16[144,1076]{1,0:T(8,128)(2,1)}, u32[]{:S(2)}, u32[]{:S(2)}) collective-permute-start(bf16[144,1076]{1,0:T(8,128)(2,1)} %collective-permute-done.32.refs_4_), channel_id=1, source_target_pairs={{0,1},{2,0},{4,2},{6,4},{7,6},{5,7},{3,5},{1,3},{8,9},{10,8},{12,1... | collective-permute-start | bytes 929672 | tf_op jit(solution)/shard_map/ppermute | solution.py:103
  95.6 71.2 %collective-permute-start.23 = (bf16[682,288]{0,1:T(8,128)(2,1)S(1)}, bf16[682,288]{0,1:T(8,128)(2,1)}, u32[]{:S(2)}, u32[]{:S(2)}) collective-permute-start(bf16[682,288]{0,1:T(8,128)(2,1)S(1)} %collective-permute-done.21), channel_id=1, source_target_pairs={{0,2},{2,4},{4,6},{6,7},{7,5},{5,3},{3,1},{1,0},{8,10},{10,12},{12... | collective-permute-start | bytes 1178504 | tf_op jit(solution)/shard_map/ppermute | solution.py:103
  100.1 68.3 %collective-permute-start.25 = (bf16[682,288]{0,1:T(8,128)(2,1)S(1)}, bf16[682,288]{0,1:T(8,128)(2,1)}, u32[]{:S(2)}, u32[]{:S(2)}) collective-permute-start(bf16[682,288]{0,1:T(8,128)(2,1)S(1)} %collective-permute-done.24), channel_id=1, source_target_pairs={{0,1},{2,0},{4,2},{6,4},{7,6},{5,7},{3,5},{1,3},{8,9},{10,8},{12,1... | collective-permute-start | bytes 1178504 | tf_op jit(solution)/shard_map/ppermute | solution.py:103
  139.4 59.7 %collective-permute-start.14 = (bf16[1,4,256,288]{2,3,1,0:T(8,128)(2,1)}, bf16[1,4,256,288]{2,3,1,0:T(8,128)(2,1)}, u32[]{:S(2)}, u32[]{:S(2)}) collective-permute-start(bf16[1,4,256,288]{2,3,1,0:T(8,128)(2,1)} %copy.96), channel_id=1, source_target_pairs={{0,16},{8,24},{16,0},{24,8},{1,17},{9,25},{17,1},{25,9},{2,18},{10... | collective-permute-start | bytes 1769480 | tf_op jit(solution)/shard_map/ppermute | solution.py:43
  163.3 36.1 %collective-permute-start.13 = (bf16[1,4,256,288]{2,3,1,0:T(8,128)(2,1)}, bf16[1,4,256,288]{2,3,1,0:T(8,128)(2,1)}, u32[]{:S(2)}, u32[]{:S(2)}) collective-permute-start(bf16[1,4,256,288]{2,3,1,0:T(8,128)(2,1)} %copy.96), channel_id=1, source_target_pairs={{0,8},{8,0},{16,24},{24,16},{1,9},{9,1},{17,25},{25,17},{2,10},{10... | collective-permute-start | bytes 1769480 | tf_op jit(solution)/shard_map/ppermute | solution.py:43
  163.3 37.6 %collective-permute-start.40 = (bf16[1,4,256,288]{2,3,1,0:T(8,128)(2,1)}, bf16[1,4,256,288]{2,3,1,0:T(8,128)(2,1)}, u32[]{:S(2)}, u32[]{:S(2)}) collective-permute-start(bf16[1,4,256,288]{2,3,1,0:T(8,128)(2,1)} %copy.127), channel_id=1, source_target_pairs={{0,16},{8,24},{16,0},{24,8},{1,17},{9,25},{17,1},{25,9},{2,18},{10... | collective-permute-start | bytes 1769480 | tf_op jit(solution)/shard_map/ppermute | solution.py:43
  168.4 33.7 %collective-permute-start.39 = (bf16[1,4,256,288]{2,3,1,0:T(8,128)(2,1)}, bf16[1,4,256,288]{2,3,1,0:T(8,128)(2,1)}, u32[]{:S(2)}, u32[]{:S(2)}) collective-permute-start(bf16[1,4,256,288]{2,3,1,0:T(8,128)(2,1)} %copy.127), channel_id=1, source_target_pairs={{0,8},{8,0},{16,24},{24,16},{1,9},{9,1},{17,25},{25,17},{2,10},{10... | collective-permute-start | bytes 1769480 | tf_op jit(solution)/shard_map/ppermute | solution.py:43
  188.7 50.1 %collective-permute-start.26 = (bf16[1152,288]{0,1:T(8,128)(2,1)}, bf16[1152,288]{0,1:T(8,128)(2,1)}, u32[]{:S(2)}, u32[]{:S(2)}) collective-permute-start(bf16[1152,288]{0,1:T(8,128)(2,1)} %copy.108), channel_id=1, source_target_pairs={{0,16},{8,24},{16,0},{24,8},{1,17},{9,25},{17,1},{25,9},{2,18},{10... | collective-permute-start | bytes 1990664 | tf_op jit(solution)/shard_map/ppermute | solution.py:43
  199.5 38.8 %collective-permute-start.37 = (bf16[2,538,288]{1,2,0:T(8,128)(2,1)}, bf16[2,538,288]{1,2,0:T(8,128)(2,1)}, u32[]{:S(2)}, u32[]{:S(2)}) collective-permute-start(bf16[2,538,288]{1,2,0:T(8,128)(2,1)} %copy.115), channel_id=1, source_target_pairs={{0,16},{8,24},{16,0},{24,8},{1,17},{9,25},{17,1},{25,9},{2,18},{10... | collective-permute-start | bytes 1859336 | tf_op jit(solution)/shard_map/ppermute | solution.py:43
  201.0 37.3 %collective-permute-start.38 = (bf16[2,538,288]{1,2,0:T(8,128)(2,1)}, bf16[2,538,288]{1,2,0:T(8,128)(2,1)}, u32[]{:S(2)}, u32[]{:S(2)}) collective-permute-start(bf16[2,538,288]{1,2,0:T(8,128)(2,1)} %copy.118), channel_id=1, source_target_pairs={{0,8},{8,0},{16,24},{24,16},{1,9},{9,1},{17,25},{25,17},{2,10},{10... | collective-permute-start | bytes 1859336 | tf_op jit(solution)/shard_map/ppermute | solution.py:43
  202.0 86.9 %collective-permute-start.17 = (bf16[1,512,1152]{2,1,0:T(8,128)(2,1)S(1)}, bf16[1,512,1152]{2,1,0:T(8,128)(2,1)}, u32[]{:S(2)}, u32[]{:S(2)}) collective-permute-start(bf16[1,512,1152]{2,1,0:T(8,128)(2,1)S(1)} %copy-done.5), channel_id=1, source_target_pairs={{0,16},{8,24},{16,0},{24,8},{1,17},{9,25},{17,1},{25,9},{2,18},{10... | collective-permute-start | bytes 3538952 | tf_op jit(solution)/shard_map/ppermute | solution.py:43
  221.6 69.6 %collective-permute-start.28 = (bf16[1152,288]{0,1:T(8,128)(2,1)}, bf16[1152,288]{0,1:T(8,128)(2,1)}, u32[]{:S(2)}, u32[]{:S(2)}) collective-permute-start(bf16[1152,288]{0,1:T(8,128)(2,1)} %copy.108), channel_id=1, source_target_pairs={{0,8},{8,0},{16,24},{24,16},{1,9},{9,1},{17,25},{25,17},{2,10},{10... | collective-permute-start | bytes 1990664 | tf_op jit(solution)/shard_map/ppermute | solution.py:43
  238.3 48.0 %collective-permute-start.15 = (bf16[1,4,256,288]{2,3,1,0:T(8,128)(2,1)}, bf16[1,4,256,288]{2,3,1,0:T(8,128)(2,1)}, u32[]{:S(2)}, u32[]{:S(2)}) collective-permute-start(bf16[1,4,256,288]{2,3,1,0:T(8,128)(2,1)} %collective-permute-done.14), channel_id=1, source_target_pairs={{0,8},{8,0},{16,24},{24,16},{1,9},{9,1},{17,25},{25,17},{2,10},{10... | collective-permute-start | bytes 1769480 | tf_op jit(solution)/shard_map/ppermute | solution.py:43
  238.3 50.7 %collective-permute-start.41 = (bf16[1,4,256,288]{2,3,1,0:T(8,128)(2,1)}, bf16[1,4,256,288]{2,3,1,0:T(8,128)(2,1)}, u32[]{:S(2)}, u32[]{:S(2)}) collective-permute-start(bf16[1,4,256,288]{2,3,1,0:T(8,128)(2,1)} %collective-permute-done.40), channel_id=1, source_target_pairs={{0,8},{8,0},{16,24},{24,16},{1,9},{9,1},{17,25},{25,17},{2,10},{10... | collective-permute-start | bytes 1769480 | tf_op jit(solution)/shard_map/ppermute | solution.py:43
  238.8 52.4 %collective-permute-start.27 = (bf16[1152,288]{0,1:T(8,128)(2,1)}, bf16[1152,288]{0,1:T(8,128)(2,1)}, u32[]{:S(2)}, u32[]{:S(2)}) collective-permute-start(bf16[1152,288]{0,1:T(8,128)(2,1)} %collective-permute-done.26), channel_id=1, source_target_pairs={{0,8},{8,0},{16,24},{24,16},{1,9},{9,1},{17,25},{25,17},{2,10},{10... | collective-permute-start | bytes 1990664 | tf_op jit(solution)/shard_map/ppermute | solution.py:43
  391.8 351.6 %reduce-scatter.5.cloned.1.call-start = ((), (), s32[]{:S(2)}) async-start(), calls=%async_computation.3 | async-start | bytes 3760128 | tf_op jit(solution)/shard_map/reduce_scatter | solution.py:736
  449.6 39.2 %collective-permute-start.79 = (bf16[2,538,288]{1,2,0:T(8,128)(2,1)}, bf16[2,538,288]{1,2,0:T(8,128)(2,1)}, u32[]{:S(2)}, u32[]{:S(2)}) collective-permute-start(bf16[2,538,288]{1,2,0:T(8,128)(2,1)} %copy.151), channel_id=1, source_target_pairs={{0,24},{8,16},{16,8},{24,0},{1,25},{9,17},{17,9},{25,1},{2,26},{10... | collective-permute-start | bytes 1859336 | tf_op jit(solution)/shard_map/ppermute | solution.py:43
  453.6 36.7 %collective-permute-start.80 = (bf16[2,538,288]{1,2,0:T(8,128)(2,1)}, bf16[2,538,288]{1,2,0:T(8,128)(2,1)}, u32[]{:S(2)}, u32[]{:S(2)}) collective-permute-start(bf16[2,538,288]{1,2,0:T(8,128)(2,1)} %copy.152), channel_id=1, source_target_pairs={{0,16},{8,24},{16,0},{24,8},{1,17},{9,25},{17,1},{25,9},{2,18},{10... | collective-permute-start | bytes 1859336 | tf_op jit(solution)/shard_map/ppermute | solution.py:43
  455.2 37.5 %collective-permute-start.81 = (bf16[2,538,288]{1,2,0:T(8,128)(2,1)}, bf16[2,538,288]{1,2,0:T(8,128)(2,1)}, u32[]{:S(2)}, u32[]{:S(2)}) collective-permute-start(bf16[2,538,288]{1,2,0:T(8,128)(2,1)} %copy.155), channel_id=1, source_target_pairs={{0,8},{8,0},{16,24},{24,16},{1,9},{9,1},{17,25},{25,17},{2,10},{10... | collective-permute-start | bytes 1859336 | tf_op jit(solution)/shard_map/ppermute | solution.py:43
  455.7 29.4 %collective-permute-start.75 = (f32[4,288]{1,0:T(4,128)S(1)}, f32[4,288]{1,0:T(4,128)S(1)}, u32[]{:S(2)}, u32[]{:S(2)}) collective-permute-start(f32[4,288]{1,0:T(4,128)S(1)} %bitcast_add_fusion), channel_id=1, source_target_pairs={{0,16},{8,24},{16,0},{24,8},{1,17},{9,25},{17,1},{25,9},{2,18},{10... | collective-permute-start | bytes 13832 | tf_op jit(solution)/shard_map/ppermute | solution.py:43
  457.5 40.5 %collective-permute-start.52 = (bf16[1,256,1152]{2,1,0:T(8,128)(2,1)}, bf16[1,256,1152]{2,1,0:T(8,128)(2,1)}, u32[]{:S(2)}, u32[]{:S(2)}) collective-permute-start(bf16[1,256,1152]{2,1,0:T(8,128)(2,1)} %get-tuple-element.159), channel_id=1, source_target_pairs={{0,16},{8,24},{16,0},{24,8},{1,17},{9,25},{17,1},{25,9},{2,18},{10... | collective-permute-start | bytes 1769480 | tf_op jit(solution)/shard_map/ppermute | solution.py:43
  621.4 35.4 %collective-permute-start.70 = (bf16[144,1152]{1,0:T(8,128)(2,1)}, bf16[144,1152]{1,0:T(8,128)(2,1)}, u32[]{:S(2)}, u32[]{:S(2)}) collective-permute-start(bf16[144,1152]{1,0:T(8,128)(2,1)} %get-tuple-element.181), channel_id=1, source_target_pairs={{0,1},{2,0},{4,2},{6,4},{7,6},{5,7},{3,5},{1,3},{8,9},{10,8},{12,1... | collective-permute-start | bytes 995336 | tf_op jit(solution)/shard_map/ppermute | solution.py:103
  638.2 27.9 %collective-permute-start.58 = (bf16[1,512,1152]{2,1,0:T(8,128)(2,1)}, bf16[1,512,1152]{2,1,0:T(8,128)(2,1)}, u32[]{:S(2)}, u32[]{:S(2)}) collective-permute-start(bf16[1,512,1152]{2,1,0:T(8,128)(2,1)} %get-tuple-element.174), channel_id=1, source_target_pairs={{0,8},{8,0},{16,24},{24,16},{1,9},{9,1},{17,25},{25,17},{2,10},{10... | collective-permute-start | bytes 3538952 | tf_op jit(solution)/shard_map/ppermute | solution.py:43
  638.2 46.1 %collective-permute-start.57 = (bf16[1,512,1152]{2,1,0:T(8,128)(2,1)}, bf16[1,512,1152]{2,1,0:T(8,128)(2,1)}, u32[]{:S(2)}, u32[]{:S(2)}) collective-permute-start(bf16[1,512,1152]{2,1,0:T(8,128)(2,1)} %get-tuple-element.173), channel_id=1, source_target_pairs={{0,8},{8,0},{16,24},{24,16},{1,9},{9,1},{17,25},{25,17},{2,10},{10... | collective-permute-start | bytes 3538952 | tf_op jit(solution)/shard_map/ppermute | solution.py:43
  656.7 80.8 %collective-permute-start.54 = (bf16[1,512,1152]{2,1,0:T(8,128)(2,1)}, bf16[1,512,1152]{2,1,0:T(8,128)(2,1)}, u32[]{:S(2)}, u32[]{:S(2)}) collective-permute-start(bf16[1,512,1152]{2,1,0:T(8,128)(2,1)} %pad_maximum_fusion.7), channel_id=1, source_target_pairs={{0,8},{8,0},{16,24},{24,16},{1,9},{9,1},{17,25},{25,17},{2,10},{10... | collective-permute-start | bytes 3538952 | tf_op jit(solution)/shard_map/ppermute | solution.py:43
  672.4 28.9 %collective-permute-start.59 = (bf16[1,512,1152]{2,1,0:T(8,128)(2,1)S(1)}, bf16[1,512,1152]{2,1,0:T(8,128)(2,1)S(1)}, u32[]{:S(2)}, u32[]{:S(2)}) collective-permute-start(bf16[1,512,1152]{2,1,0:T(8,128)(2,1)S(1)} %fusion.39), channel_id=1, source_target_pairs={{0,16},{8,24},{16,0},{24,8},{1,17},{9,25},{17,1},{25,9},{2,18},{10... | collective-permute-start | bytes 3538952 | tf_op jit(solution)/shard_map/ppermute | solution.py:43
  678.1 59.4 %collective-permute-start.56 = (bf16[1,512,1152]{2,1,0:T(8,128)(2,1)}, bf16[1,512,1152]{2,1,0:T(8,128)(2,1)}, u32[]{:S(2)}, u32[]{:S(2)}) collective-permute-start(bf16[1,512,1152]{2,1,0:T(8,128)(2,1)} %add_convert_fusion.1), channel_id=1, source_target_pairs={{0,16},{8,24},{16,0},{24,8},{1,17},{9,25},{17,1},{25,9},{2,18},{10... | collective-permute-start | bytes 3538952 | tf_op jit(solution)/shard_map/ppermute | solution.py:43
  (115 other events, 1666.8 us)
Sparse Core Ops, SparseCore 0:
  391.9 70.3 reduce-scatter.2
  505.8 75.1 reduce-scatter.4

commit v3 on v2

--- a/solution.py
+++ b/solution.py
@@ -73,6 +73,13 @@
     return blocks[0]
 
 
+def collect_direct(blocks):
+    total = blocks[0].astype(F32)
+    for j in range(len(blocks) - 1, 0, -1):
+        total = total + swap(blocks[j], j).astype(F32)
+    return total
+
+
 def reorder(blocks, me):
     blocks = list(blocks)
     bit = 1
@@ -123,55 +130,59 @@
             if k <= far[way ^ flip]:
                 moving[way] = ring_shift(moving[way], step)
                 found.append((-step * k, moving[way]))
+        moving = list(lax.optimization_barrier(tuple(moving)))
     index = jnp.stack([ring_owner(offset) for offset, _ in found])
     return [block for _, block in found], index
 
 
-def place(blocks, index, cuts, wide=None):
+def place_wide(blocks, index, wide):
     count = len(blocks)
-    pieces = len(cuts) - 1
-    extra = [] if wide is None else [wide]
+    rows, cols = blocks[0].shape
+    merged = rows % 16 == 0
 
     def kernel(index_ref, *refs):
-        outs = refs[count + len(extra) :]
+        wide_ref, out_ref, held = refs[count:]
         for i in range(count):
-            for p in range(pieces):
-                value = refs[i][cuts[p] : cuts[p + 1]]
-                if extra:
-                    value = mm(value, refs[count][...]).astype(BF)
-                outs[p][index_ref[i]] = value
-
-    block = blocks[0]
-    cols = block.shape[1] if wide is None else wide.shape[1]
-    shapes = [(count, cuts[p + 1] - cuts[p], cols) for p in range(pieces)]
-    return pl.pallas_call(
+            held[index_ref[i]] = refs[i][...]
+        if merged:
+            out_ref[...] = mm(held[...].reshape(count * rows, cols), wide_ref[...]).astype(BF)
+        else:
+            for i in range(count):
+                out_ref[i] = mm(held[i], wide_ref[...]).astype(BF)
+
+    shape = (count * rows, wide.shape[1]) if merged else (count, rows, wide.shape[1])
+    out = pl.pallas_call(
         kernel,
         grid_spec=pltpu.PrefetchScalarGridSpec(
             num_scalar_prefetch=1,
             grid=(1,),
-            in_specs=[pl.BlockSpec(a.shape, lambda i, index: (0, 0)) for a in blocks + extra],
-            out_specs=[pl.BlockSpec(shape, lambda i, index: (0, 0, 0)) for shape in shapes],
+            in_specs=[pl.BlockSpec(a.shape, lambda i, index: (0, 0)) for a in [*blocks, wide]],
+            out_specs=pl.BlockSpec(shape, lambda i, index: (0,) * len(shape)),
+            scratch_shapes=[pltpu.VMEM((count, rows, cols), BF)],
         ),
-        out_shape=[jax.ShapeDtypeStruct(shape, BF) for shape in shapes],
-        cost_estimate=cost(0 if wide is None else count * block.size * cols, 4 * count * block.size),
+        out_shape=jax.ShapeDtypeStruct(shape, BF),
+        cost_estimate=cost(count * rows * cols * wide.shape[1], 4 * count * rows * cols),
         compiler_params=pltpu.CompilerParams(vmem_limit_bytes=VMEM_BYTES),
-        name="place_blocks",
-    )(index, *blocks, *extra)
+        name="place_wide",
+    )(index, *blocks, wide)
+    return out.reshape(count * rows, wide.shape[1])
 
 
 def ring_reduce(take, flip):
     count = lax.axis_size("fsdp")
     far = (count // 2, count - 1 - count // 2)
     total = take(ring_owner(0)).astype(F32)
-    for step, reach in ((1, far[flip]), (-1, far[1 - flip])):
-        incoming = None
-        for k in range(reach, 0, -1):
-            part = take(ring_owner(step * k))
-            if incoming is not None:
-                part = (part.astype(F32) + incoming.astype(F32)).astype(BF)
-            incoming = ring_shift(part, step)
-        total = total + incoming.astype(F32)
-    return total
+    incoming = [None, None]
+    for k in range(count // 2, 0, -1):
+        for way, step in ((0, 1), (1, -1)):
+            if k <= far[way ^ flip]:
+                part = take(ring_owner(step * k))
+                if incoming[way] is not None:
+                    part = (part.astype(F32) + incoming[way].astype(F32)).astype(BF)
+                incoming[way] = ring_shift(part, step)
+        if incoming[1] is not None and incoming[0] is not None:
+            incoming = list(lax.optimization_barrier(tuple(incoming)))
+    return total + incoming[0].astype(F32) + incoming[1].astype(F32)
 
 
 def ring_sum(value):
@@ -300,16 +311,9 @@
             s_ref,
             bu_ref,
         ) = refs[count : count + 11]
-        (
-            h_ref,
-            z_ref,
-            du_ref,
-            cat_ref,
-            dh_ref,
-            y_ref,
-            x_ref,
-            gb_ref,
-        ) = refs[-8:]
+        outs = refs[-(6 + 2 * count) :]
+        h_ref, z_ref, du_ref, cat_ref, x_ref, gb_ref = outs[:6]
+        dh_refs, y_refs = outs[6 : 6 + count], outs[6 + count :]
         block = pl.program_id(1)
         x_one = tok_ref[0].reshape(both, width).astype(F32) + bo_ref[...]
         pieces = []
@@ -338,8 +342,17 @@
         grad_hidden = wide_grad.astype(BF)
         z_ref[0] = z.reshape(2, rows, hidden_count)
         du_ref[0] = grad_hidden.reshape(2, rows, hidden_count)
-        dh_ref[0] = mm(grad_hidden, up_turned_ref[...]).astype(BF).reshape(2, rows, width)
-        y_ref[0] = mm(z, down_ref[...]).astype(BF).reshape(2, rows, width)
+        dh = mm(grad_hidden, up_turned_ref[...]).astype(BF)
+        y = mm(z, down_ref[...]).astype(BF)
+        for pair in range(count // 2):
+
+            @pl.when(block == pair)
+            def _():
+                for side in (0, 1):
+                    here = slice(side * rows, (side + 1) * rows)
+                    dh_refs[2 * pair + side][0] = dh[here]
+                    y_refs[2 * pair + side][0] = y[here]
+
         summed = jnp.sum(grad_hidden.astype(F32), axis=0, keepdims=True)
         first = (pl.program_id(0) == 0) & (block == 0)
 
@@ -359,7 +372,7 @@
 
     full = pl.BlockSpec((1, 2, rows, width), lambda im, b, me_ref: (im, b, chunk, 0))
     full_hidden = pl.BlockSpec((1, 2, rows, hidden_count), lambda im, b, me_ref: (im, b, chunk, 0))
-    part = pl.BlockSpec((1, 2, rows, width), lambda im, b, me_ref: (im, b, 0, 0))
+    part = pl.BlockSpec((1, rows, width), lambda im, b, me_ref: (im, 0, 0))
     constants = [w_output, w_up, up_turned, w_down, down_turned, b_output, gain, shift, b_up]
     extra = list(kept)
     inputs = [*mixed, tokens, cotangent, *constants, *extra]
@@ -379,21 +392,19 @@
                 full_hidden,
                 full,
                 part,
-                part,
-                pl.BlockSpec((1, rows, width), lambda im, b, me_ref: (im, 0, 0)),
                 pl.BlockSpec((1, hidden_count), lambda im, b, me_ref: (0, 0)),
-            ],
+            ]
+            + [part] * (2 * count),
         ),
         out_shape=[
             jax.ShapeDtypeStruct(tokens.shape, BF),
             jax.ShapeDtypeStruct((images, count, length, hidden_count), BF),
             jax.ShapeDtypeStruct((images, count, length, hidden_count), BF),
             jax.ShapeDtypeStruct(tokens.shape, BF),
-            jax.ShapeDtypeStruct((images, count, rows, width), BF),
-            jax.ShapeDtypeStruct((images, count, rows, width), BF),
             jax.ShapeDtypeStruct((images, rows, width), F32),
             jax.ShapeDtypeStruct((1, hidden_count), F32),
-        ],
+        ]
+        + [jax.ShapeDtypeStruct((images, rows, width), BF)] * (2 * count),
         input_output_aliases={1 + count + 11 + i: i for i in range(len(extra))},
         cost_estimate=cost(
             all_rows * width * (width + 4 * hidden_count) * 2,
@@ -411,20 +422,22 @@
 
     def kernel(grad_ref, w_ref, exact_ref, *refs):
         out_ref = refs[-1]
-        result = mm(grad_ref[0, 0], w_ref[...]).astype(BF).astype(F32)
+        result = mm(grad_ref[0].reshape(2 * rows, width), w_ref[...]).astype(BF).astype(F32)
         for e in range(heads):
             here = slice(e * WIDE, (e + 1) * WIDE)
             mine = result[:, here]
-            delta = jnp.sum(mine * exact_ref[0, 0, :, here], axis=-1, keepdims=True)
-            out_ref[0, 0, :, here] = put_parts(mine, delta, SUM_AT).astype(BF)
-
-    full = pl.BlockSpec((1, 1, rows, wide_heads), lambda im, b: (im, b, chunk, 0))
+            exact = exact_ref[0, :, :, here].reshape(2 * rows, WIDE)
+            delta = jnp.sum(mine * exact, axis=-1, keepdims=True)
+            value = put_parts(mine, delta, SUM_AT).astype(BF)
+            out_ref[0, :, :, here] = value.reshape(2, rows, WIDE)
+
+    full = pl.BlockSpec((1, 2, rows, wide_heads), lambda im, b: (im, b, chunk, 0))
     extra = list(kept)
     return pl.pallas_call(
         kernel,
-        grid=(images, count),
+        grid=(images, count // 2),
         in_specs=[
-            pl.BlockSpec((1, 1, rows, width), lambda im, b: (im, b, 0, 0)),
+            pl.BlockSpec((1, 2, rows, width), lambda im, b: (im, b, 0, 0)),
             pl.BlockSpec(w_wide.shape, lambda im, b: (0, 0)),
             full,
         ]
@@ -441,9 +454,9 @@
     )(grad, w_wide, exact, *extra)
 
 
-def attend_back(query, grad, qkv):
+def attend_back(query, grad, qkv, first, heads):
     images, keys, wide_heads = query.shape
-    heads = wide_heads // WIDE
+    every = wide_heads // WIDE
     rows = min(512, keys)
     span = min(512, keys)
     steps = keys // rows
@@ -474,18 +487,19 @@
             dk_ref[0] = (dk[...] * (1.0 / LOG2E)).astype(BF)
             dv_ref[0] = dv[...].astype(BF)
 
-    row_spec = pl.BlockSpec((1, rows, WIDE), lambda i, e, b: (i, b, e))
+    row_in = pl.BlockSpec((1, rows, WIDE), lambda i, e, b: (i, b, e + first))
+    row_out = pl.BlockSpec((1, rows, WIDE), lambda i, e, b: (i, b, e))
 
     def all_spec(shift):
         return pl.BlockSpec((1, keys, WIDE), lambda i, e, b: (i, 0, e + shift))
 
-    shape = jax.ShapeDtypeStruct((images, keys, wide_heads), BF)
+    shape = jax.ShapeDtypeStruct((images, keys, heads * WIDE), BF)
     scores = images * heads * keys * keys
     return pl.pallas_call(
         kernel,
         grid=(images, heads, steps),
-        in_specs=[row_spec, row_spec, all_spec(heads), all_spec(2 * heads)],
-        out_specs=[row_spec, all_spec(0), all_spec(0)],
+        in_specs=[row_in, row_in, all_spec(every + first), all_spec(2 * every + first)],
+        out_specs=[row_out, all_spec(0), all_spec(0)],
         out_shape=[shape] * 3,
         scratch_shapes=[
             pltpu.VMEM((WIDE, keys), BF),
@@ -498,30 +512,82 @@
     )(query, grad, qkv, qkv)
 
 
-def project_back(grads, w_wide):
-    images, count, length, wide_heads = grads[0].shape
-    width = w_wide.shape[1]
-
-    def kernel(q_ref, k_ref, v_ref, w_ref, out_ref):
+def project_back(grads, tokens, w_turned, gain, shift, narrow):
+    images, count, length, width = tokens.shape
+    parts = len(grads[0])
+    part = grads[0][0].shape[-1]
+    wide = parts * part
+    own = narrow.shape[1]
+    flat = [piece for kind in grads for piece in kind]
+    last_image, last_block = images - 1, count - 1
+
+    def kernel(*refs):
+        ins = refs[: len(flat)]
+        tok_ref, w_ref, g_ref, s_ref, n_ref = refs[len(flat) : len(flat) + 5]
+        outs = refs[len(flat) + 5 : -1]
+        held = refs[-1]
+        dh_refs = outs[:count]
+        weight_ref, norm_ref, bias_ref = outs[count:]
+        block = pl.program_id(1)
+        first = (pl.program_id(0) == 0) & (block == 0)
+
+        @pl.when(first)
+        def _():
+            held[...] = jnp.zeros_like(held)
+            norm_ref[...] = jnp.zeros_like(norm_ref)
+            bias_ref[...] = jnp.zeros_like(bias_ref)
+
+        normed, _ = norm_parts(tok_ref[0, 0].astype(F32))
+        turned = (normed * g_ref[...] + s_ref[...]).astype(BF).T
         total = jnp.zeros((length, width), F32)
-        for i, ref in enumerate((q_ref, k_ref, v_ref)):
-            total = total + mm(ref[0, 0], w_ref[i * wide_heads : (i + 1) * wide_heads])
-        out_ref[0, 0] = total.astype(BF)
-
-    block = pl.BlockSpec((1, 1, length, wide_heads), lambda im, b: (im, b, 0, 0))
+        for i, ref in enumerate(ins):
+            piece = ref[0, 0]
+            here = slice(i * part, (i + 1) * part)
+            total = total + mm(piece, w_ref[here])
+            held[:, here] += mm(turned, piece)
+            bias_ref[:, here] += jnp.sum(piece.astype(F32), axis=0, keepdims=True)
+        for j in range(count):
+
+            @pl.when(block == j)
+            def _():
+                dh_refs[j][0] = total.astype(BF)
+
+        norm_ref[0:1] += jnp.sum(total * normed, axis=0, keepdims=True)
+        norm_ref[1:2] += jnp.sum(total, axis=0, keepdims=True)
+
+        @pl.when((pl.program_id(0) == last_image) & (block == last_block))
+        def _():
+            for kind in range(3):
+                whole = held[:, kind * wide : (kind + 1) * wide].astype(BF)
+                weight_ref[kind] = mm(whole, n_ref[...]).astype(BF)
+
+    piece_spec = pl.BlockSpec((1, 1, length, part), lambda im, b: (im, b, 0, 0))
+    row_spec = pl.BlockSpec((1, 1, length, width), lambda im, b: (im, b, 0, 0))
+
+    def whole_spec(shape):
+        return pl.BlockSpec(shape, lambda im, b: (0,) * len(shape))
+
+    shapes = [(3, width, own), (2, width), (1, 3 * wide)]
+    kinds = [BF, F32, F32]
+    all_rows = images * count * length
     return pl.pallas_call(
         kernel,
         grid=(images, count),
-        in_specs=[block] * 3 + [pl.BlockSpec(w_wide.shape, lambda im, b: (0, 0))],
-        out_specs=pl.BlockSpec((1, 1, length, width), lambda im, b: (im, b, 0, 0)),
-        out_shape=jax.ShapeDtypeStruct((images, count, length, width), BF),
+        in_specs=[piece_spec] * len(flat)
+        + [row_spec]
+        + [whole_spec(a.shape) for a in (w_turned, gain, shift, narrow)],
+        out_specs=[pl.BlockSpec((1, length, width), lambda im, b: (im, 0, 0))] * count
+        + [whole_spec(shape) for shape in shapes],
+        out_shape=[jax.ShapeDtypeStruct((images, length, width), BF)] * count
+        + [jax.ShapeDtypeStruct(shape, kind) for shape, kind in zip(shapes, kinds)],
+        scratch_shapes=[pltpu.VMEM((width, 3 * wide), F32)],
         cost_estimate=cost(
-            images * count * length * width * wide_heads * 3,
-            images * count * length * (wide_heads * 6 + width * 2) + w_wide.size * 2,
+            2 * all_rows * width * wide * 3,
+            all_rows * (wide * 6 + width * 4) + w_turned.size * 2,
         ),
         compiler_params=pltpu.CompilerParams(vmem_limit_bytes=VMEM_BYTES),
         name="project_back",
-    )(*grads, w_wide)
+    )(*flat, tokens, w_turned, gain, shift, narrow)
 
 
 def local(
@@ -561,17 +627,13 @@
     )
     small = spread(small)
     qkv_blocks, qkv_index = ring_gather(qkv_shard, 0)
-    w_wide = place(
-        qkv_blocks, qkv_index, (0, qkv_shard.shape[0]), widen(3 * own, 3 * wide_heads)
-    )[0].reshape(width, 3 * wide_heads)
-    lower_shard = jnp.concatenate([w_output, w_down], axis=0)
-    lower_shard, up_shard, _ = lax.optimization_barrier((lower_shard, w_up, qkv_blocks[-1]))
+    w_wide = place_wide(qkv_blocks, qkv_index, widen(3 * own, 3 * wide_heads))
     cut = w_output.shape[0]
-    output_cols, down_rows = place(
-        *ring_gather(lower_shard, 1), (0, cut, cut + w_down.shape[0])
-    )
-    output_cols = output_cols.reshape(width, own)
-    up_mat = place(*ring_gather(up_shard, 0), (0, cut))[0].reshape(width, -1)
+    lower = jnp.concatenate([w_output, w_down], axis=0)
+    lower = lax.all_gather(lower, "fsdp", axis=0)
+    output_cols = lower[:, :cut].reshape(width, own)
+    down_rows = lower[:, cut:]
+    up_mat = lax.all_gather(w_up, "fsdp", axis=0, tiled=True)
 
     patches = images * length
     valid = jnp.stack([block[:patches].reshape(images, length) for block in small], axis=1)
@@ -614,6 +676,9 @@
     bias_wide = bias_wide * factor + ones.astype(np.float32)
     weights = (me, output_mat, up_mat, up_mat.T, down_mat, down_mat.T, b_out, g_two, s_two, b_up.astype(F32)[None])
 
+    images_all = images
+    w_turned = w_wide.T
+
     def run(tokens, bias_mask, cotangent):
         images = tokens.shape[0]
         tok_all = jnp.stack(spread(tokens), axis=1)
@@ -630,29 +695,13 @@
             mixed, *kept_attend = attend(qkv, wide_heads, c, kept_attend)
             mixed_chunks.append(spread(mixed))
         query_wide, mixed_exact = kept_attend
-        hidden_parts, out_parts, x_parts = [], [], []
-        up_bias_grad = 0.0
-        for c in range(CHUNKS):
-            *kept_middle, dh, y, x_own, gb = middle(
-                mixed_chunks[c], tok_all, cot_all, weights, c, kept_middle
-            )
-            hidden_parts.append(collect([dh[:, j] for j in range(count)]))
-            out_parts.append(y)
-            x_parts.append(x_own)
-            up_bias_grad = up_bias_grad + gb[0]
-        h_two, activated, grad_hidden, mixed_all = kept_middle
-
-        kept_back = ()
-        grad_attn_all, grad_residual = [], []
-        early = 0.0
-        for c in range(CHUNKS):
-            grad_norm = hidden_parts[c].astype(F32)
-            normed_two, inverse_two = norm_parts(x_parts[c])
+        def grad_rows(c, hidden_grad, x_own):
+            grad_norm = hidden_grad.astype(F32)
+            normed_two, inverse_two = norm_parts(x_own)
             cot_own = cotangent[:, c * rows : (c + 1) * rows].astype(F32)
             residual = cot_own + norm_back(grad_norm, normed_two, inverse_two, g_two)
             grad_attn = residual.astype(BF)
-            grad_residual.append(residual)
-            early = early + jnp.stack(
+            sums = jnp.stack(
                 [
                     jnp.sum(grad_norm * normed_two, axis=(0, 1)),
                     jnp.sum(grad_norm, axis=(0, 1)),
@@ -660,51 +709,76 @@
                     jnp.sum(cot_own, axis=(0, 1)),
                 ]
             )
+            return residual, grad_attn, sums
+
+        out_parts, x_parts = [], []
+        grad_attn_all, grad_residual = [], []
+        hidden_parts = []
+        early, up_bias_grad = 0.0, 0.0
+        for c in range(CHUNKS):
+            result = middle(mixed_chunks[c], tok_all, cot_all, weights, c, kept_middle)
+            kept_middle, x_own, gb = result[:4], result[4], result[5]
+            hidden_parts.append(list(result[6 : 6 + count]))
+            out_parts.append(result[6 + count :])
+            x_parts.append(x_own)
+            up_bias_grad = up_bias_grad + gb[0]
+        h_two, activated, grad_hidden, mixed_all = kept_middle
+        cot_down, up_in = cot_all, h_two
+        kept_back = ()
+        for c in range(CHUNKS):
+            last = c == CHUNKS - 1
+            hidden_grad = (collect if last else collect_direct)(hidden_parts[c])
+            residual, grad_attn, sums = grad_rows(c, hidden_grad, x_parts[c])
+            grad_residual.append(residual)
+            early = early + sums
+            if not last:
+                grad_attn, cot_down, up_in = lax.optimization_barrier(
+                    (grad_attn, cot_down, up_in)
+                )
             stacked = jnp.stack(spread(grad_attn), axis=1)
             grad_attn_all.append(stacked)
             kept_back = (mixed_back(stacked, output_wide, mixed_exact, c, kept_back),)
         grad_mixed = kept_back[0]
 
+        up_grad = jnp.einsum("ijld,ijlf->df", up_in, grad_hidden, preferred_element_type=F32)
         down_grad = jnp.einsum(
-            "ijlf,ijld->fd", activated, cot_all, preferred_element_type=F32
+            "ijlf,ijld->fd", activated, cot_down, preferred_element_type=F32
         )
-        up_grad = jnp.einsum("ijld,ijlf->df", h_two, grad_hidden, preferred_element_type=F32)
+
+        wide_shape = (images, count * length, wide_heads)
+        query_in = query_wide.reshape(wide_shape)
+        grad_in = grad_mixed.reshape(wide_shape)
+        flat_qkv = qkv.reshape(images, count * length, 3 * wide_heads)
+        halves = 2 if heads % 2 == 0 else 1
+        step = heads // halves
+        out_parts, grad_in = lax.optimization_barrier((out_parts, grad_in))
+        out_blocks = [jnp.concatenate([y[j] for y in out_parts], axis=1) for j in range(count)]
+        pieces = []
+        for half in range(halves):
+            pieces.append(attend_back(query_in, grad_in, flat_qkv, half * step, step))
+        grads = [
+            [piece[k].reshape(images, count, length, -1) for piece in pieces] for k in range(3)
+        ]
+        out_sum = collect(out_blocks)
         grad_attn_all = jnp.concatenate(grad_attn_all, axis=2)
+        mixed_late, grad_attn_all, _ = lax.optimization_barrier(
+            (mixed_all, grad_attn_all, pieces[0][0])
+        )
         grad_attn_cols = lax.dynamic_slice_in_dim(grad_attn_all, me * own, own, 3)
         output_grad = jnp.einsum(
-            "ijle,ijld->ed", mixed_all, grad_attn_cols, preferred_element_type=F32
+            "ijle,ijld->ed", mixed_late, grad_attn_cols, preferred_element_type=F32
         )
-
-        wide_shape = (images, count * length, wide_heads)
-        grads = attend_back(
-            query_wide.reshape(wide_shape),
-            grad_mixed.reshape(wide_shape),
-            qkv.reshape(images, count * length, 3 * wide_heads),
-        )
-        grads = [g.reshape(images, count, length, wide_heads) for g in grads]
-        grad_h = project_back(grads, w_wide.T)
-        grad_norm_one = collect([grad_h[:, j] for j in range(count)]).astype(F32)
-        qkv_grad = [
-            jnp.einsum("ijld,ijle->de", h_one, g, preferred_element_type=F32) for g in grads
-        ]
-
-        out_parts, grad_mixed = lax.optimization_barrier((out_parts, grad_mixed))
-        out_sum = collect(
-            [jnp.concatenate([y[:, j] for y in out_parts], axis=1) for j in range(count)]
-        )
+        result = project_back(grads, tok_all, w_turned, g_one, s_one, expand.T)
+        qkv_grad, late, bias_grads = result[count:]
+        grad_norm_one = collect(list(result[:count])).astype(F32)
+
         layer_out = (jnp.concatenate(x_parts, axis=1) + out_sum.astype(F32) + b_dn).astype(BF)
         normed_one, inverse_one = norm_parts(tokens.astype(F32))
         grad_tokens = (
             jnp.concatenate(grad_residual, axis=1)
             + norm_back(grad_norm_one, normed_one, inverse_one, g_one)
         ).astype(BF)
-        late = jnp.stack(
-            [
-                jnp.sum(grad_norm_one * normed_one, axis=(0, 1)),
-                jnp.sum(grad_norm_one, axis=(0, 1)),
-            ]
-        )
-        bias_grads = [jnp.sum(grads[i].astype(F32), axis=(0, 1, 2)) for i in (0, 2)]
+        qkv_grad = qkv_grad if images_all == 1 else qkv_grad.astype(F32)
         sums = (down_grad, up_grad, output_grad, qkv_grad, early, up_bias_grad, late, bias_grads)
         return sums, (layer_out, grad_tokens)
 
@@ -736,9 +810,15 @@
     final_down = lax.psum_scatter(down_pieces, "fsdp", scatter_dimension=0).astype(F32)
     output_grad = reorder(jnp.split(output_grad.astype(BF), count, axis=0), me)
     output_grad = jnp.concatenate(output_grad, axis=0)
-    qkv_grad = [mm(full.astype(BF), expand, NT).astype(BF) for full in qkv_grad]
-    four = jnp.concatenate(qkv_grad + [output_grad], axis=1).reshape(fcount, width // fcount, -1)
-    four = ring_reduce(lambda f: lax.dynamic_index_in_dim(four, f, 0, keepdims=False), 0)
+    qkv_grad = qkv_grad.astype(BF).reshape(3, fcount, width // fcount, own)
+    output_grad = output_grad.reshape(fcount, width // fcount, own)
+
+    def four_parts(f):
+        parts = lax.dynamic_index_in_dim(qkv_grad, f, 1, keepdims=False)
+        last = lax.dynamic_index_in_dim(output_grad, f, 0, keepdims=True)
+        return jnp.concatenate([parts, last], axis=0)
+
+    four = ring_reduce(four_parts, 0)
 
     def to_owner(stack):
         kinds = stack.shape[0]
@@ -748,6 +828,7 @@
     early = to_owner(early)
     early = ring_sum(jnp.concatenate([early.reshape(-1), up_bias_grad]))
     late = to_owner(late)
+    bias_grads = [bias_grads[0, i * wide_heads : (i + 1) * wide_heads] for i in (0, 2)]
     late = ring_sum(jnp.concatenate([late.reshape(-1)] + [narrow(g) for g in bias_grads]))
     gain_two_grad, shift_two_grad, b_output_grad, b_down_grad = [
         early[i * own : (i + 1) * own] for i in range(4)
@@ -756,9 +837,7 @@
     gain_one_grad, shift_one_grad, b_query_grad, b_value_grad = [
         late[i * own : (i + 1) * own] for i in range(4)
     ]
-    final_query, final_key, final_value, final_output = [
-        four[:, i * own : (i + 1) * own] for i in range(4)
-    ]
+    final_query, final_key, final_value, final_output = [four[i] for i in range(4)]
     return (
         layer_out,
         grad_tokens,

time: 762 us -> 747 us (0.980)
  waiting for transfers between devices: 176 us -> 200 us
  matrix products: 58.9 us -> 41 us
  Pallas kernels: 193 us -> 205 us
  local copies, waits for them, and re-layouts: 149 us -> 137 us
  starting transfers between devices: 68.9 us -> 58.8 us
    ppermute x48, waiting for transfers between devices: 113 us -> 149 us  [swap(): return lax.ppermute(value, 'seq', [(i, i ^ bit) for i in range(count)])]
    dot_general x4 -> x1, matrix products: 24.9 us -> 3.18 us  [mm(): return lax.dot_general(left, right, dims, preferred_element_type=F32)]
    ppermute x28 -> x14, waiting for transfers between devices: 61.9 us -> 47.9 us  [ring_shift(): lax.ppermute(value, 'fsdp', [(order[i], order[(i + step) % count]) for i...]
    reshape x3 -> x2, local copies, waits for them, and re-layouts: 13.5 us -> 1.23 us  [the longest x1 1.14 us: local(): output_cols = lower[:, :cut].reshape(width, own)]
    ppermute x7 -> x0, local copies, waits for them, and re-layouts: 12.2 us -> none  [ring_shift(): lax.ppermute(value, 'fsdp', [(order[i], order[(i + step) % count]) for i...]
    ppermute x28 -> x14, starting transfers between devices: 31.2 us -> 21.1 us  [ring_shift(): lax.ppermute(value, 'fsdp', [(order[i], order[(i + step) % count]) for i...]
    pallas_call x7 -> x6, Pallas kernels: 92.2 us -> 101 us  [the longest x2 51.4 us: attend_back(): pl.pallas_call(kernel, grid=(images, heads, steps), in_specs=[row_in, row...]
    concatenate x3 -> x0, local copies, waits for them, and re-layouts: 7.72 us -> none  [the longest x1 5.27 us: local(): jnp.concatenate(qkv_grad + [output_grad], axis=1)]
  transfers between devices with their start and end apart: 84 -> 72, of which waited for: 22 -> 23; matrix products, arithmetic and copies ran while one was open for 35% -> 30% of each run, Pallas kernels for 18% -> 19%
where the time goes in v3:
time: 747 us; the launch traced here: 741 us
  Pallas kernels  205 us (27%)
  waiting for transfers between devices  200 us (27%)
  local copies, waits for them, and re-layouts  137 us (18%)
  other arithmetic  83.6 us (11%)
  starting transfers between devices  58.8 us (8%)
  matrix products  41 us (5%)
  between operations  15.1 us (2%)
    ppermute x48, waiting for transfers between devices, swap(): return lax.ppermute(value, 'seq', [(i, i ^ bit) for i in range(count)])  149 us
    pallas_call x2, Pallas kernels, middle(): pl.pallas_call(kernel, grid_spec=pltpu.PrefetchScalarGridSpec(num_scalar_...  63.2 us
    pallas_call x2, Pallas kernels, attend_back(): pl.pallas_call(kernel, grid=(images, heads, steps), in_specs=[row_in, row...  51.4 us
    ppermute x14, waiting for transfers between devices, ring_shift(): lax.ppermute(value, 'fsdp', [(order[i], order[(i + step) % count]) for i...  47.9 us
    pallas_call x2, Pallas kernels, attend(): pl.pallas_call(kernel, grid=(images, count), in_specs=[part, pl.BlockSpec...  40.3 us
    pallas_call x1, Pallas kernels, project_back(): pl.pallas_call(kernel, grid=(images, count), in_specs=[piece_spec] * len(...  30.2 us
    ppermute x15, local copies, waits for them, and re-layouts, swap(): return lax.ppermute(value, 'seq', [(i, i ^ bit) for i in range(count)])  29.1 us
    ppermute x48, starting transfers between devices, swap(): return lax.ppermute(value, 'seq', [(i, i ^ bit) for i in range(count)])  25.1 us
  transfers between devices with their start and end apart: 72, of which 23 were waited for; matrix products, arithmetic and copies ran while one was open for 30% of the time, Pallas kernels for 19%

profile of v3, /device:TPU:0, one launch (start us, length us, event | category | flops | bytes accessed | tf_op | source)
XLA Modules:
  0.0 740.5 jit_solution(3229830124903698966)
XLA Ops:
  30.4 9.3 %collective-permute-done.1 = bf16[1,512,1152]{2,1,0:T(8,128)(2,1)S(1)} collective-permute-done((bf16[1,512,1152]{2,1,0:T(8,128)(2,1)}, bf16[1,512,1152]{2,1,0:T(8,128)(2,1)S(1)}, u32[]{:S(2)}, u32[]{:S(2)}) %collective-permute-start.1) | collective-permute-done | bytes 1179680 | tf_op jit(solution)/shard_map/ppermute | solution.py:43
  73.7 8.9 %place_wide.1 = bf16[1152,1536]{1,0:T(8,128)(2,1)} custom-call(s32[8]{0:T(128)} %stack.139.index_ref, bf16[144,864]{1,0:T(8,128)(2,1)} %pad_maximum_fusion.9.refs_0_, bf16[144,864]{1,0:T(8,128)(2,1)} %collective-permute-done.6.refs_1_, bf16[144,864]{1,0:T(8,128)(2,1)} %collective-permute-done.7.refs_2_, bf16[144,864]{1,0:T(8,128)(2,1)} %collective-permute-done.8.refs_3_, ...), custom_call_target="tpu_custom_call" | custom-call | flops 3057647616 | bytes 3981312 | tf_op jit(solution)/shard_map/place_wide/pallas_call | solution.py:154
  88.2 10.9 %add_convert_fusion = bf16[4,512,1536]{2,1,0:T(8,128)(2,1)} fusion(f32[1536]{0:T(1024)S(1)} %copy-done.59, f32[4,512]{1,0:T(4,128)S(1)} %get-tuple-element.318, f32[1536]{0:T(1024)S(1)} %copy-done.54, f32[1536]{0:T(1024)S(1)} %copy-done.53, bf16[1,4,512,1152]{3,2,1,0:T(8,128)(2,1)S(1)} %pad_maximum_fusion.refs_4_.refs_6_, f32[1152]{0:T(1024)S(1)} %get-tuple-element.213, ...), kind=kOutput, calls=%fused_computation | convolution fusion | flops 7277641728 | bytes 14601216 | tf_op jit(solution)/shard_map/ijld,de->ijle/dot_general | solution.py:689
  99.1 20.0 %attend.2 = (bf16[1,4,256,288]{3,2,1,0:T(8,128)(2,1)}, bf16[1,4,512,512]{3,2,1,0:T(8,128)(2,1)}, f32[1,4,512,512]{3,2,1,0:T(8,128)}) custom-call(bf16[1,4,512,1536]{3,2,1,0:T(8,128)(2,1)} %bitcast.180, bf16[1,2048,1536]{2,1,0:T(8,128)(2,1)} %bitcast.181), custom_call_target="tpu_custom_call" | custom-call | flops 8589934592 | bytes 9437184 | tf_op jit(solution)/shard_map/attend/pallas_call | solution.py:276
  122.8 20.3 %attend.3 = (bf16[1,4,256,288]{3,2,1,0:T(8,128)(2,1)}, bf16[1,4,512,512]{3,2,1,0:T(8,128)(2,1)}, f32[1,4,512,512]{3,2,1,0:T(8,128)}) custom-call(bf16[1,4,512,1536]{3,2,1,0:T(8,128)(2,1)} %bitcast.182, bf16[1,2048,1536]{2,1,0:T(8,128)(2,1)} %bitcast.183, ...), custom_call_target="tpu_custom_call", output_to_operand_aliasing={{1}: (2, {}), {2}: (3, {})} | custom-call | flops 8589934592 | bytes 9437184 | tf_op jit(solution)/shard_map/attend/pallas_call | solution.py:276
  151.2 10.2 %collective-permute-done.26 = bf16[1,4,256,288]{2,3,1,0:T(8,128)(2,1)} collective-permute-done((bf16[1,4,256,288]{2,3,1,0:T(8,128)(2,1)}, bf16[1,4,256,288]{2,3,1,0:T(8,128)(2,1)}, u32[]{:S(2)}, u32[]{:S(2)}) %collective-permute-start.26) | collective-permute-done | bytes 589856 | tf_op jit(solution)/shard_map/ppermute | solution.py:43
  192.8 11.7 %collective-permute-done.22 = bf16[2,538,288]{1,2,0:T(8,128)(2,1)} collective-permute-done((bf16[2,538,288]{1,2,0:T(8,128)(2,1)}, bf16[2,538,288]{1,2,0:T(8,128)(2,1)}, u32[]{:S(2)}, u32[]{:S(2)}) %collective-permute-start.22) | collective-permute-done | bytes 619808 | tf_op jit(solution)/shard_map/ppermute | solution.py:43
  205.9 14.7 %collective-permute-done.23 = bf16[2,538,288]{1,2,0:T(8,128)(2,1)} collective-permute-done((bf16[2,538,288]{1,2,0:T(8,128)(2,1)S(1)}, bf16[2,538,288]{1,2,0:T(8,128)(2,1)}, u32[]{:S(2)}, u32[]{:S(2)}) %collective-permute-start.23) | collective-permute-done | bytes 619808 | tf_op jit(solution)/shard_map/ppermute | solution.py:43
  234.6 5.2 copy.131
  248.6 6.0 concatenate.111
  254.6 31.4 %middle.2 = (bf16[1,4,512,1152]{3,2,1,0:T(8,128)(2,1)}, bf16[1,4,512,1076]{3,2,1,0:T(8,128)(2,1)}, bf16[1,4,512,1076]{3,2,1,0:T(8,128)(2,1)}, bf16[1,4,512,1152]...) custom-call(s32[1]{0:T(128)} %bitcast.me_ref, ...), custom_call_target="tpu_custom_call" | custom-call | flops 25744637952 | bytes 30894080 | tf_op jit(solution)/shard_map/middle/pallas_call | solution.py:380
  286.0 31.8 %middle.3 = (bf16[1,4,512,1152]{3,2,1,0:T(8,128)(2,1)}, bf16[1,4,512,1076]{3,2,1,0:T(8,128)(2,1)}, bf16[1,4,512,1076]{3,2,1,0:T(8,128)(2,1)}, bf16[1,4,512,1152]...) custom-call(s32[1]{0:T(128)} %bitcast.me_ref, ...), custom_call_target="tpu_custom_call", output_to_operand_aliasing={{0}: (16, {}), {1}: (17, {}), {2}: (18, {}), {3}: (19, {})} | custom-call | flops 25744637952 | bytes 30894080 | tf_op jit(solution)/shard_map/middle/pallas_call | solution.py:380
  325.4 10.3 %collective-permute-done.34 = bf16[1,256,1152]{2,1,0:T(8,128)(2,1)S(1)} collective-permute-done((bf16[1,256,1152]{2,1,0:T(8,128)(2,1)}, bf16[1,256,1152]{2,1,0:T(8,128)(2,1)S(1)}, u32[]{:S(2)}, u32[]{:S(2)}) %collective-permute-start.34) | collective-permute-done | bytes 589856 | tf_op jit(solution)/shard_map/ppermute | solution.py:43
  335.6 13.3 %collective-permute-done.35 = bf16[1,256,1152]{2,1,0:T(8,128)(2,1)S(1)} collective-permute-done((bf16[1,256,1152]{2,1,0:T(8,128)(2,1)}, bf16[1,256,1152]{2,1,0:T(8,128)(2,1)S(1)}, u32[]{:S(2)}, u32[]{:S(2)}) %collective-permute-start.35) | collective-permute-done | bytes 589856 | tf_op jit(solution)/shard_map/ppermute | solution.py:43
  348.9 12.3 %collective-permute-done.30 = bf16[1,256,1152]{2,1,0:T(8,128)(2,1)S(1)} collective-permute-done((bf16[1,256,1152]{2,1,0:T(8,128)(2,1)S(1)}, bf16[1,256,1152]{2,1,0:T(8,128)(2,1)S(1)}, u32[]{:S(2)}, u32[]{:S(2)}) %collective-permute-start.30) | collective-permute-done | bytes 589856 | tf_op jit(solution)/shard_map/ppermute | solution.py:43
  379.9 5.9 copy.140
  403.2 11.3 %fusion.7 = bf16[1076,1152]{1,0:T(8,128)(2,1)} fusion(bf16[1,4,512,1152]{3,2,1,0:T(8,128)(2,1)} %pad_maximum_fusion.1.refs_5_, bf16[1,4,512,1076]{3,2,1,0:T(8,128)(2,1)} %get-tuple-element.163), kind=kOutput, calls=%fused_computation.12 | convolution fusion | flops 5078444544 | bytes 11604992 | tf_op jit(solution)/shard_map/ijlf,ijld->fd/dot_general | solution.py:744
  435.4 11.4 %fusion.6 = bf16[1152,1076]{0,1:T(8,128)(2,1)} fusion(bf16[1,4,512,1076]{3,2,1,0:T(8,128)(2,1)} %get-tuple-element.162, bf16[1,4,512,1152]{3,2,1,0:T(8,128)(2,1)} %get-tuple-element.161), kind=kOutput, calls=%fused_computation.11 | convolution fusion | flops 5078444544 | bytes 11604992 | tf_op jit(solution)/shard_map/ijld,ijlf->df/dot_general | solution.py:743
  446.8 5.2 copy.158
  453.4 20.4 %collective-permute-done.38 = bf16[1,256,1152]{2,1,0:T(8,128)(2,1)} collective-permute-done((bf16[1,256,1152]{2,1,0:T(8,128)(2,1)S(1)}, bf16[1,256,1152]{2,1,0:T(8,128)(2,1)}, u32[]{:S(2)}, u32[]{:S(2)}) %collective-permute-start.38) | collective-permute-done | bytes 589856 | tf_op jit(solution)/shard_map/ppermute | solution.py:43
  477.5 8.9 %collective-permute-done.32 = bf16[1,256,1152]{2,1,0:T(8,128)(2,1)} collective-permute-done((bf16[1,256,1152]{2,1,0:T(8,128)(2,1)S(1)}, bf16[1,256,1152]{2,1,0:T(8,128)(2,1)}, u32[]{:S(2)}, u32[]{:S(2)}) %collective-permute-start.32) | collective-permute-done | bytes 589856 | tf_op jit(solution)/shard_map/ppermute | solution.py:43
  506.5 5.3 mixed_back.2.refs_0_
  511.8 5.4 mixed_back.3
  517.2 25.7 %attend_back.2 = (bf16[1,2048,256]{2,1,0:T(8,128)(2,1)}, bf16[1,2048,256]{2,1,0:T(8,128)(2,1)}, bf16[1,2048,256]{2,1,0:T(8,128)(2,1)}) custom-call(bf16[1,2048,512]{2,1,0:T(8,128)(2,1)} %bitcast.188, bf16[1,2048,512]{2,1,0:T(8,128)(2,1)} %bitcast.157, bf16[1,2048,1536]{2,1,0:T(8,128)(2,1)} %bitcast.184, bf16[1,2048,1536]{2,1,0:T(8,128)(2,1)} %bitcast.185), custom_call_target="tpu_custom_call" | custom-call | flops 21474836480 | bytes 14680064 | tf_op jit(solution)/shard_map/attend_back/pallas_call | solution.py:498
  551.1 25.7 %attend_back.3 = (bf16[1,2048,256]{2,1,0:T(8,128)(2,1)}, bf16[1,2048,256]{2,1,0:T(8,128)(2,1)}, bf16[1,2048,256]{2,1,0:T(8,128)(2,1)}) custom-call(bf16[1,2048,512]{2,1,0:T(8,128)(2,1)} %bitcast.189, bf16[1,2048,512]{2,1,0:T(8,128)(2,1)} %bitcast.158, bf16[1,2048,1536]{2,1,0:T(8,128)(2,1)} %bitcast.186, bf16[1,2048,1536]{2,1,0:T(8,128)(2,1)} %bitcast.187), custom_call_target="tpu_custom_call" | custom-call | flops 21474836480 | bytes 14680064 | tf_op jit(solution)/shard_map/attend_back/pallas_call | solution.py:498
  576.8 30.2 %project_back.1 = (bf16[1,512,1152]{2,1,0:T(8,128)(2,1)}, bf16[1,512,1152]{2,1,0:T(8,128)(2,1)}, bf16[1,512,1152]{2,1,0:T(8,128)(2,1)}, bf16[1,512,1152]{2,1,0:T...) custom-call(bf16[1,4,512,256]{3,2,1,0:T(8,128)(2,1)} %bitcast.190, ...), custom_call_target="tpu_custom_call" | custom-call | flops 14495514624 | bytes 19267584 | tf_op jit(solution)/shard_map/project_back/pallas_call | solution.py:573
  620.8 6.9 collective-permute-done.52
  649.0 19.3 %collective-permute-done.56 = bf16[4,144,288]{2,1,0:T(8,128)(2,1)S(1)} collective-permute-done((bf16[4,144,288]{2,1,0:T(8,128)(2,1)S(1)}, bf16[4,144,288]{2,1,0:T(8,128)(2,1)S(1)}, u32[]{:S(2)}, u32[]{:S(2)}) %collective-permute-start.56) | collective-permute-done | bytes 331808 | tf_op jit(solution)/shard_map/ppermute | solution.py:110
  668.5 7.0 collective-permute-start.58
  677.1 11.2 %collective-permute-done.58 = bf16[4,144,288]{2,1,0:T(8,128)(2,1)S(1)} collective-permute-done((bf16[4,144,288]{2,1,0:T(8,128)(2,1)S(1)}, bf16[4,144,288]{2,1,0:T(8,128)(2,1)S(1)}, u32[]{:S(2)}, u32[]{:S(2)}) %collective-permute-start.58) | collective-permute-done | bytes 331808 | tf_op jit(solution)/shard_map/ppermute | solution.py:110
  690.9 13.9 %collective-permute-done.45 = bf16[1,512,1152]{2,1,0:T(8,128)(2,1)S(1)} collective-permute-done((bf16[1,512,1152]{2,1,0:T(8,128)(2,1)S(1)}, bf16[1,512,1152]{2,1,0:T(8,128)(2,1)S(1)}, u32[]{:S(2)}, u32[]{:S(2)}) %collective-permute-start.45) | collective-permute-done | bytes 1179680 | tf_op jit(solution)/shard_map/ppermute | solution.py:43
  706.0 19.5 %collective-permute-done.42 = bf16[1,512,1152]{2,1,0:T(8,128)(2,1)S(1)} collective-permute-done((bf16[1,512,1152]{2,1,0:T(8,128)(2,1)S(1)}, bf16[1,512,1152]{2,1,0:T(8,128)(2,1)S(1)}, u32[]{:S(2)}, u32[]{:S(2)}) %collective-permute-start.42) | collective-permute-done | bytes 1179680 | tf_op jit(solution)/shard_map/ppermute | solution.py:43
  (420 shorter events, 276.2 us)
Async XLA Ops:
  7.2 140.5 %all-gather.7.cloned.1.call-start = ((), (), s32[]{:S(2)}) async-start(), calls=%async_computation.5 | async-start | bytes 3981312 | tf_op jit(solution)/shard_map/all_gather | solution.py:633
  10.4 165.1 %all-gather.5.cloned.1.call-start = ((), (), s32[]{:S(2)}) async-start(), calls=%async_computation.2 | async-start | bytes 2985984 | tf_op jit(solution)/shard_map/all_gather | solution.py:636
  10.4 29.2 %collective-permute-start.1 = (bf16[1,512,1152]{2,1,0:T(8,128)(2,1)}, bf16[1,512,1152]{2,1,0:T(8,128)(2,1)S(1)}, u32[]{:S(2)}, u32[]{:S(2)}) collective-permute-start(bf16[1,512,1152]{2,1,0:T(8,128)(2,1)} %param.21), channel_id=1, source_target_pairs={{0,16},{8,24},{16,0},{24,8},{1,17},{9,25},{17,1},{25,9},{2,18},{10... | collective-permute-start | bytes 3538952 | tf_op jit(solution)/shard_map/ppermute | solution.py:43
  17.3 65.3 %collective-permute-start = (bf16[1,512,1152]{2,1,0:T(8,128)(2,1)}, bf16[1,512,1152]{2,1,0:T(8,128)(2,1)S(1)}, u32[]{:S(2)}, u32[]{:S(2)}) collective-permute-start(bf16[1,512,1152]{2,1,0:T(8,128)(2,1)} %param.21), channel_id=1, source_target_pairs={{0,8},{8,0},{16,24},{24,16},{1,9},{9,1},{17,25},{25,17},{2,10},{10... | collective-permute-start | bytes 3538952 | tf_op jit(solution)/shard_map/ppermute | solution.py:43
  22.9 706.7 %reduce-scatter.3.cloned.1.call-start = ((), (), s32[]{:S(2)}) async-start(), calls=%async_computation.3 | async-start | bytes 2985984 | tf_op jit(solution)/shard_map/reduce_scatter | solution.py:807
  39.7 43.0 %collective-permute-start.2 = (bf16[1,512,1152]{2,1,0:T(8,128)(2,1)S(1)}, bf16[1,512,1152]{2,1,0:T(8,128)(2,1)}, u32[]{:S(2)}, u32[]{:S(2)}) collective-permute-start(bf16[1,512,1152]{2,1,0:T(8,128)(2,1)S(1)} %collective-permute-done.1), channel_id=1, source_target_pairs={{0,8},{8,0},{16,24},{24,16},{1,9},{9,1},{17,25},{25,17},{2,10},{10... | collective-permute-start | bytes 3538952 | tf_op jit(solution)/shard_map/ppermute | solution.py:43
  86.7 59.9 %collective-permute-start.17 = (bf16[1,512,1152]{2,1,0:T(8,128)(2,1)}, bf16[1,512,1152]{2,1,0:T(8,128)(2,1)}, u32[]{:S(2)}, u32[]{:S(2)}) collective-permute-start(bf16[1,512,1152]{2,1,0:T(8,128)(2,1)} %param.38), channel_id=1, source_target_pairs={{0,16},{8,24},{16,0},{24,8},{1,17},{9,25},{17,1},{25,9},{2,18},{10... | collective-permute-start | bytes 3538952 | tf_op jit(solution)/shard_map/ppermute | solution.py:43
  121.3 24.8 %collective-permute-start.14 = (bf16[1,4,256,288]{2,3,1,0:T(8,128)(2,1)}, bf16[1,4,256,288]{2,3,1,0:T(8,128)(2,1)S(1)}, u32[]{:S(2)}, u32[]{:S(2)}) collective-permute-start(bf16[1,4,256,288]{2,3,1,0:T(8,128)(2,1)} %copy.108), channel_id=1, source_target_pairs={{0,16},{8,24},{16,0},{24,8},{1,17},{9,25},{17,1},{25,9},{2,18},{10... | collective-permute-start | bytes 1769480 | tf_op jit(solution)/shard_map/ppermute | solution.py:43
  122.8 28.1 %collective-permute-start.13 = (bf16[1,4,256,288]{2,3,1,0:T(8,128)(2,1)}, bf16[1,4,256,288]{2,3,1,0:T(8,128)(2,1)}, u32[]{:S(2)}, u32[]{:S(2)}) collective-permute-start(bf16[1,4,256,288]{2,3,1,0:T(8,128)(2,1)} %copy.108), channel_id=1, source_target_pairs={{0,8},{8,0},{16,24},{24,16},{1,9},{9,1},{17,25},{25,17},{2,10},{10... | collective-permute-start | bytes 1769480 | tf_op jit(solution)/shard_map/ppermute | solution.py:43
  146.2 40.9 %collective-permute-start.16 = (bf16[1,512,1152]{2,1,0:T(8,128)(2,1)}, bf16[1,512,1152]{2,1,0:T(8,128)(2,1)}, u32[]{:S(2)}, u32[]{:S(2)}) collective-permute-start(bf16[1,512,1152]{2,1,0:T(8,128)(2,1)} %param.38), channel_id=1, source_target_pairs={{0,8},{8,0},{16,24},{24,16},{1,9},{9,1},{17,25},{25,17},{2,10},{10... | collective-permute-start | bytes 3538952 | tf_op jit(solution)/shard_map/ppermute | solution.py:43
  146.5 41.1 %collective-permute-start.18 = (bf16[1,512,1152]{2,1,0:T(8,128)(2,1)}, bf16[1,512,1152]{2,1,0:T(8,128)(2,1)}, u32[]{:S(2)}, u32[]{:S(2)}) collective-permute-start(bf16[1,512,1152]{2,1,0:T(8,128)(2,1)} %collective-permute-done.17), channel_id=1, source_target_pairs={{0,8},{8,0},{16,24},{24,16},{1,9},{9,1},{17,25},{25,17},{2,10},{10... | collective-permute-start | bytes 3538952 | tf_op jit(solution)/shard_map/ppermute | solution.py:43
  161.4 26.2 %collective-permute-start.19 = (bf16[1152,288]{0,1:T(8,128)(2,1)}, bf16[1152,288]{0,1:T(8,128)(2,1)}, u32[]{:S(2)}, u32[]{:S(2)}) collective-permute-start(bf16[1152,288]{0,1:T(8,128)(2,1)} %copy.112), channel_id=1, source_target_pairs={{0,16},{8,24},{16,0},{24,8},{1,17},{9,25},{17,1},{25,9},{2,18},{10... | collective-permute-start | bytes 1990664 | tf_op jit(solution)/shard_map/ppermute | solution.py:43
  180.7 60.6 %collective-permute-start.21 = (bf16[1152,288]{0,1:T(8,128)(2,1)}, bf16[1152,288]{0,1:T(8,128)(2,1)}, u32[]{:S(2)}, u32[]{:S(2)}) collective-permute-start(bf16[1152,288]{0,1:T(8,128)(2,1)} %copy.112), channel_id=1, source_target_pairs={{0,8},{8,0},{16,24},{24,16},{1,9},{9,1},{17,25},{25,17},{2,10},{10... | collective-permute-start | bytes 1990664 | tf_op jit(solution)/shard_map/ppermute | solution.py:43
  187.1 33.5 %collective-permute-start.23 = (bf16[2,538,288]{1,2,0:T(8,128)(2,1)S(1)}, bf16[2,538,288]{1,2,0:T(8,128)(2,1)}, u32[]{:S(2)}, u32[]{:S(2)}) collective-permute-start(bf16[2,538,288]{1,2,0:T(8,128)(2,1)S(1)} %get-tuple-element.241), channel_id=1, source_target_pairs={{0,16},{8,24},{16,0},{24,8},{1,17},{9,25},{17,1},{25,9},{2,18},{10... | collective-permute-start | bytes 1859336 | tf_op jit(solution)/shard_map/ppermute | solution.py:43
  187.6 34.5 %collective-permute-start.24 = (bf16[2,538,288]{1,2,0:T(8,128)(2,1)}, bf16[2,538,288]{1,2,0:T(8,128)(2,1)}, u32[]{:S(2)}, u32[]{:S(2)}) collective-permute-start(bf16[2,538,288]{1,2,0:T(8,128)(2,1)} %get-tuple-element.240), channel_id=1, source_target_pairs={{0,8},{8,0},{16,24},{24,16},{1,9},{9,1},{17,25},{25,17},{2,10},{10... | collective-permute-start | bytes 1859336 | tf_op jit(solution)/shard_map/ppermute | solution.py:43
  187.6 55.1 %collective-permute-start.20 = (bf16[1152,288]{0,1:T(8,128)(2,1)}, bf16[1152,288]{0,1:T(8,128)(2,1)}, u32[]{:S(2)}, u32[]{:S(2)}) collective-permute-start(bf16[1152,288]{0,1:T(8,128)(2,1)} %collective-permute-done.19), channel_id=1, source_target_pairs={{0,8},{8,0},{16,24},{24,16},{1,9},{9,1},{17,25},{25,17},{2,10},{10... | collective-permute-start | bytes 1990664 | tf_op jit(solution)/shard_map/ppermute | solution.py:43
  321.4 27.6 %collective-permute-start.35 = (bf16[1,256,1152]{2,1,0:T(8,128)(2,1)}, bf16[1,256,1152]{2,1,0:T(8,128)(2,1)S(1)}, u32[]{:S(2)}, u32[]{:S(2)}) collective-permute-start(bf16[1,256,1152]{2,1,0:T(8,128)(2,1)} %get-tuple-element.123), channel_id=1, source_target_pairs={{0,16},{8,24},{16,0},{24,8},{1,17},{9,25},{17,1},{25,9},{2,18},{10... | collective-permute-start | bytes 1769480 | tf_op jit(solution)/shard_map/ppermute | solution.py:43
  321.9 27.0 %collective-permute-start.36 = (bf16[1,256,1152]{2,1,0:T(8,128)(2,1)}, bf16[1,256,1152]{2,1,0:T(8,128)(2,1)S(1)}, u32[]{:S(2)}, u32[]{:S(2)}) collective-permute-start(bf16[1,256,1152]{2,1,0:T(8,128)(2,1)} %get-tuple-element.124), channel_id=1, source_target_pairs={{0,8},{8,0},{16,24},{24,16},{1,9},{9,1},{17,25},{25,17},{2,10},{10... | collective-permute-start | bytes 1769480 | tf_op jit(solution)/shard_map/ppermute | solution.py:43
  323.5 37.8 %collective-permute-start.30 = (bf16[1,256,1152]{2,1,0:T(8,128)(2,1)S(1)}, bf16[1,256,1152]{2,1,0:T(8,128)(2,1)S(1)}, u32[]{:S(2)}, u32[]{:S(2)}) collective-permute-start(bf16[1,256,1152]{2,1,0:T(8,128)(2,1)S(1)} %add_convert_fusion.3), channel_id=1, source_target_pairs={{0,16},{8,24},{16,0},{24,8},{1,17},{9,25},{17,1},{25,9},{2,18},{10... | collective-permute-start | bytes 1769480 | tf_op jit(solution)/shard_map/ppermute | solution.py:43
  426.7 47.7 %collective-permute-start.65 = (bf16[2,538,288]{1,2,0:T(8,128)(2,1)}, bf16[2,538,288]{1,2,0:T(8,128)(2,1)}, u32[]{:S(2)}, u32[]{:S(2)}) collective-permute-start(bf16[2,538,288]{1,2,0:T(8,128)(2,1)} %copy.160), channel_id=1, source_target_pairs={{0,24},{8,16},{16,8},{24,0},{1,25},{9,17},{17,9},{25,1},{2,26},{10... | collective-permute-start | bytes 1859336 | tf_op jit(solution)/shard_map/ppermute | solution.py:43
  429.1 57.4 %collective-permute-start.66 = (bf16[2,538,288]{1,2,0:T(8,128)(2,1)}, bf16[2,538,288]{1,2,0:T(8,128)(2,1)}, u32[]{:S(2)}, u32[]{:S(2)}) collective-permute-start(bf16[2,538,288]{1,2,0:T(8,128)(2,1)} %copy.161), channel_id=1, source_target_pairs={{0,16},{8,24},{16,0},{24,8},{1,17},{9,25},{17,1},{25,9},{2,18},{10... | collective-permute-start | bytes 1859336 | tf_op jit(solution)/shard_map/ppermute | solution.py:43
  432.6 56.6 %collective-permute-start.67 = (bf16[2,538,288]{1,2,0:T(8,128)(2,1)}, bf16[2,538,288]{1,2,0:T(8,128)(2,1)}, u32[]{:S(2)}, u32[]{:S(2)}) collective-permute-start(bf16[2,538,288]{1,2,0:T(8,128)(2,1)} %copy.164), channel_id=1, source_target_pairs={{0,8},{8,0},{16,24},{24,16},{1,9},{9,1},{17,25},{25,17},{2,10},{10... | collective-permute-start | bytes 1859336 | tf_op jit(solution)/shard_map/ppermute | solution.py:43
  433.3 40.4 %collective-permute-start.38 = (bf16[1,256,1152]{2,1,0:T(8,128)(2,1)S(1)}, bf16[1,256,1152]{2,1,0:T(8,128)(2,1)}, u32[]{:S(2)}, u32[]{:S(2)}) collective-permute-start(bf16[1,256,1152]{2,1,0:T(8,128)(2,1)S(1)} %get-tuple-element.126), channel_id=1, source_target_pairs={{0,16},{8,24},{16,0},{24,8},{1,17},{9,25},{17,1},{25,9},{2,18},{10... | collective-permute-start | bytes 1769480 | tf_op jit(solution)/shard_map/ppermute | solution.py:43
  434.5 51.9 %collective-permute-start.32 = (bf16[1,256,1152]{2,1,0:T(8,128)(2,1)S(1)}, bf16[1,256,1152]{2,1,0:T(8,128)(2,1)}, u32[]{:S(2)}, u32[]{:S(2)}) collective-permute-start(bf16[1,256,1152]{2,1,0:T(8,128)(2,1)S(1)} %get-tuple-element.258), channel_id=1, source_target_pairs={{0,16},{8,24},{16,0},{24,8},{1,17},{9,25},{17,1},{25,9},{2,18},{10... | collective-permute-start | bytes 1769480 | tf_op jit(solution)/shard_map/ppermute | solution.py:43
  452.0 279.5 %reduce-scatter.5.cloned.1.call-start = ((), (), s32[]{:S(2)}) async-start(), calls=%async_computation.4 | async-start | bytes 3760128 | tf_op jit(solution)/shard_map/reduce_scatter | solution.py:810
  610.9 31.0 %collective-permute-start.54 = (bf16[4,144,288]{2,1,0:T(8,128)(2,1)}, bf16[4,144,288]{2,1,0:T(8,128)(2,1)}, u32[]{:S(2)}, u32[]{:S(2)}) collective-permute-start(bf16[4,144,288]{2,1,0:T(8,128)(2,1)} %pad_maximum_fusion.8), channel_id=1, source_target_pairs={{0,1},{2,0},{4,2},{6,4},{7,6},{5,7},{3,5},{1,3},{8,9},{10,8},{12,1... | collective-permute-start | bytes 995336 | tf_op jit(solution)/shard_map/ppermute | solution.py:110
  633.5 42.0 %collective-permute-start.44 = (bf16[1,512,1152]{2,1,0:T(8,128)(2,1)}, bf16[1,512,1152]{2,1,0:T(8,128)(2,1)S(1)}, u32[]{:S(2)}, u32[]{:S(2)}) collective-permute-start(bf16[1,512,1152]{2,1,0:T(8,128)(2,1)} %get-tuple-element.146), channel_id=1, source_target_pairs={{0,8},{8,0},{16,24},{24,16},{1,9},{9,1},{17,25},{25,17},{2,10},{10... | collective-permute-start | bytes 3538952 | tf_op jit(solution)/shard_map/ppermute | solution.py:43
  633.6 57.3 %collective-permute-start.43 = (bf16[1,512,1152]{2,1,0:T(8,128)(2,1)}, bf16[1,512,1152]{2,1,0:T(8,128)(2,1)S(1)}, u32[]{:S(2)}, u32[]{:S(2)}) collective-permute-start(bf16[1,512,1152]{2,1,0:T(8,128)(2,1)} %get-tuple-element.144), channel_id=1, source_target_pairs={{0,8},{8,0},{16,24},{24,16},{1,9},{9,1},{17,25},{25,17},{2,10},{10... | collective-permute-start | bytes 3538952 | tf_op jit(solution)/shard_map/ppermute | solution.py:43
  648.3 27.8 %collective-permute-start.41 = (bf16[1,512,1152]{2,1,0:T(8,128)(2,1)S(1)}, bf16[1,512,1152]{2,1,0:T(8,128)(2,1)S(1)}, u32[]{:S(2)}, u32[]{:S(2)}) collective-permute-start(bf16[1,512,1152]{2,1,0:T(8,128)(2,1)S(1)} %pad_maximum_fusion.6), channel_id=1, source_target_pairs={{0,8},{8,0},{16,24},{24,16},{1,9},{9,1},{17,25},{25,17},{2,10},{10... | collective-permute-start | bytes 3538952 | tf_op jit(solution)/shard_map/ppermute | solution.py:43
  668.3 37.6 %collective-permute-start.40 = (bf16[1,512,1152]{2,1,0:T(8,128)(2,1)S(1)}, bf16[1,512,1152]{2,1,0:T(8,128)(2,1)S(1)}, u32[]{:S(2)}, u32[]{:S(2)}) collective-permute-start(bf16[1,512,1152]{2,1,0:T(8,128)(2,1)S(1)} %pad_maximum_fusion.5), channel_id=1, source_target_pairs={{0,8},{8,0},{16,24},{24,16},{1,9},{9,1},{17,25},{25,17},{2,10},{10... | collective-permute-start | bytes 3538952 | tf_op jit(solution)/shard_map/ppermute | solution.py:43
  675.8 29.0 %collective-permute-start.45 = (bf16[1,512,1152]{2,1,0:T(8,128)(2,1)S(1)}, bf16[1,512,1152]{2,1,0:T(8,128)(2,1)S(1)}, u32[]{:S(2)}, u32[]{:S(2)}) collective-permute-start(bf16[1,512,1152]{2,1,0:T(8,128)(2,1)S(1)} %add_convert_fusion.1), channel_id=1, source_target_pairs={{0,16},{8,24},{16,0},{24,8},{1,17},{9,25},{17,1},{25,9},{2,18},{10... | collective-permute-start | bytes 3538952 | tf_op jit(solution)/shard_map/ppermute | solution.py:43
  688.3 37.2 %collective-permute-start.42 = (bf16[1,512,1152]{2,1,0:T(8,128)(2,1)S(1)}, bf16[1,512,1152]{2,1,0:T(8,128)(2,1)S(1)}, u32[]{:S(2)}, u32[]{:S(2)}) collective-permute-start(bf16[1,512,1152]{2,1,0:T(8,128)(2,1)S(1)} %add_convert_fusion.2), channel_id=1, source_target_pairs={{0,16},{8,24},{16,0},{24,8},{1,17},{9,25},{17,1},{25,9},{2,18},{10... | collective-permute-start | bytes 3538952 | tf_op jit(solution)/shard_map/ppermute | solution.py:43
  (101 other events, 1403.9 us)
Sparse Core Ops, SparseCore 0:
  10.8 77.1 all-gather.6
  90.1 56.0 all-gather.4
  452.1 69.6 reduce-scatter.2
  633.6 93.0 reduce-scatter.4

commit v4 on v3

--- a/solution.py
+++ b/solution.py
@@ -14,7 +14,8 @@
 MASK_AT = HEAD
 LSE_AT = HEAD + 1
 SUM_AT = HEAD
-CHUNKS = 2
+CHUNKS = 1
+BESIDE_AT = 3
 
 EPS = 1e-06
 ROOT = 0.7978845608028654
@@ -35,7 +36,7 @@
 
 
 def cost(macs, moved, special=0):
-    return pl.CostEstimate(flops=2 * macs, bytes_accessed=moved, transcendentals=special)
+    return pl.CostEstimate(flops=macs // 64, bytes_accessed=moved // 64, transcendentals=special // 64)
 
 
 def swap(value, bit):
@@ -73,11 +74,16 @@
     return blocks[0]
 
 
-def collect_direct(blocks):
-    total = blocks[0].astype(F32)
-    for j in range(len(blocks) - 1, 0, -1):
-        total = total + swap(blocks[j], j).astype(F32)
-    return total
+def together(*values):
+    return lax.optimization_barrier(values)
+
+
+def collect_pair(blocks):
+    own, near, across, far = blocks
+    far = swap(far, 1)
+    near = swap(near, 1)
+    across = (across.astype(F32) + far.astype(F32)).astype(BF)
+    return own.astype(F32) + near.astype(F32), across
 
 
 def reorder(blocks, me):
@@ -168,7 +174,8 @@
     return out.reshape(count * rows, wide.shape[1])
 
 
-def ring_reduce(take, flip):
+def ring_reduce(take, flip, beside, side, side_steps):
+    side_steps = list(side_steps)
     count = lax.axis_size("fsdp")
     far = (count // 2, count - 1 - count // 2)
     total = take(ring_owner(0)).astype(F32)
@@ -180,18 +187,23 @@
                 if incoming[way] is not None:
                     part = (part.astype(F32) + incoming[way].astype(F32)).astype(BF)
                 incoming[way] = ring_shift(part, step)
+        if side_steps:
+            side = side_steps.pop(0)(side)
         if incoming[1] is not None and incoming[0] is not None:
-            incoming = list(lax.optimization_barrier(tuple(incoming)))
-    return total + incoming[0].astype(F32) + incoming[1].astype(F32)
-
-
-def ring_sum(value):
+            incoming, side = together(incoming, side)
+        if k == BESIDE_AT:
+            incoming, beside = together(incoming, beside)
+    return total + incoming[0].astype(F32) + incoming[1].astype(F32), beside, side
+
+
+def sum_steps():
     count = lax.axis_size("fsdp")
-    bit = 1
-    while bit < count:
-        value = value + lax.ppermute(value, "fsdp", [(i, i ^ bit) for i in range(count)])
-        bit *= 2
-    return value
+
+    def step(bit, value):
+        return value + lax.ppermute(value, "fsdp", [(i, i ^ bit) for i in range(count)])
+
+    bits = [1 << i for i in range(count.bit_length() - 1)]
+    return [functools.partial(step, bit) for bit in bits]
 
 
 def norm_parts(value):
@@ -293,7 +305,6 @@
     me, w_output, w_up, up_turned, w_down, down_turned, b_output, gain, shift, b_up = weights
     rows = length // CHUNKS
     own = mixed[0].shape[-1]
-    both = 2 * rows
     hidden_count = w_up.shape[1]
 
     def kernel(me_ref, *refs):
@@ -315,24 +326,23 @@
         h_ref, z_ref, du_ref, cat_ref, x_ref, gb_ref = outs[:6]
         dh_refs, y_refs = outs[6 : 6 + count], outs[6 + count :]
         block = pl.program_id(1)
-        x_one = tok_ref[0].reshape(both, width).astype(F32) + bo_ref[...]
+        x_one = tok_ref[0, 0].astype(F32) + bo_ref[...]
         pieces = []
         for i in range(count):
-            order = (1, 0) if i & 1 else (0, 1)
-            piece = jnp.concatenate([mixed_refs[i][0, at] for at in order], axis=0)
+            piece = mixed_refs[i][0, 0]
             pieces.append(piece)
             x_one = x_one + mm(piece, wo_ref[me_ref[0] ^ i])
-        cat_ref[0] = jnp.concatenate(pieces, axis=-1).reshape(2, rows, width)
+        cat_ref[0, 0] = jnp.concatenate(pieces, axis=-1)
 
         @pl.when(block == 0)
         def _():
-            x_ref[0] = x_one[:rows]
+            x_ref[0] = x_one
 
         normed, _ = norm_parts(x_one)
         h_two = (normed * g_ref[...] + s_ref[...]).astype(BF)
-        h_ref[0] = h_two.reshape(2, rows, width)
+        h_ref[0, 0] = h_two
         hidden = mm(h_two, up_ref[...]) + bu_ref[...]
-        grad_act = mm(cot_ref[0].reshape(both, width), down_turned_ref[...])
+        grad_act = mm(cot_ref[0, 0], down_turned_ref[...])
         square = hidden * hidden
         inner = jnp.tanh(ROOT * (hidden + CUBIC * square * hidden))
         half = 0.5 * (1.0 + inner)
@@ -340,18 +350,16 @@
         slope = half + 0.5 * hidden * (1.0 - inner * inner) * ROOT * (1.0 + 3.0 * CUBIC * square)
         wide_grad = grad_act * slope
         grad_hidden = wide_grad.astype(BF)
-        z_ref[0] = z.reshape(2, rows, hidden_count)
-        du_ref[0] = grad_hidden.reshape(2, rows, hidden_count)
+        z_ref[0, 0] = z
+        du_ref[0, 0] = grad_hidden
         dh = mm(grad_hidden, up_turned_ref[...]).astype(BF)
         y = mm(z, down_ref[...]).astype(BF)
-        for pair in range(count // 2):
-
-            @pl.when(block == pair)
+        for j in range(count):
+
+            @pl.when(block == j)
             def _():
-                for side in (0, 1):
-                    here = slice(side * rows, (side + 1) * rows)
-                    dh_refs[2 * pair + side][0] = dh[here]
-                    y_refs[2 * pair + side][0] = y[here]
+                dh_refs[j][0] = dh
+                y_refs[j][0] = y
 
         summed = jnp.sum(grad_hidden.astype(F32), axis=0, keepdims=True)
         first = (pl.program_id(0) == 0) & (block == 0)
@@ -365,13 +373,13 @@
             gb_ref[...] += summed
 
     def piece_spec(i):
-        return pl.BlockSpec((1, 2, rows, own), lambda im, b, me_ref: (im, b ^ (i >> 1), 0, 0))
+        return pl.BlockSpec((1, 1, rows, own), lambda im, b, me_ref: (im, b ^ i, 0, 0))
 
     def whole_spec(array):
         return pl.BlockSpec(array.shape, lambda im, b, me_ref: (0,) * array.ndim)
 
-    full = pl.BlockSpec((1, 2, rows, width), lambda im, b, me_ref: (im, b, chunk, 0))
-    full_hidden = pl.BlockSpec((1, 2, rows, hidden_count), lambda im, b, me_ref: (im, b, chunk, 0))
+    full = pl.BlockSpec((1, 1, rows, width), lambda im, b, me_ref: (im, b, chunk, 0))
+    full_hidden = pl.BlockSpec((1, 1, rows, hidden_count), lambda im, b, me_ref: (im, b, chunk, 0))
     part = pl.BlockSpec((1, rows, width), lambda im, b, me_ref: (im, 0, 0))
     constants = [w_output, w_up, up_turned, w_down, down_turned, b_output, gain, shift, b_up]
     extra = list(kept)
@@ -381,7 +389,7 @@
         kernel,
         grid_spec=pltpu.PrefetchScalarGridSpec(
             num_scalar_prefetch=1,
-            grid=(images, count // 2),
+            grid=(images, count),
             in_specs=[piece_spec(i) for i in range(count)]
             + [full, full]
             + [whole_spec(array) for array in constants]
@@ -422,22 +430,22 @@
 
     def kernel(grad_ref, w_ref, exact_ref, *refs):
         out_ref = refs[-1]
-        result = mm(grad_ref[0].reshape(2 * rows, width), w_ref[...]).astype(BF).astype(F32)
+        result = mm(grad_ref[0, 0], w_ref[...]).astype(BF).astype(F32)
         for e in range(heads):
             here = slice(e * WIDE, (e + 1) * WIDE)
             mine = result[:, here]
-            exact = exact_ref[0, :, :, here].reshape(2 * rows, WIDE)
+            exact = exact_ref[0, 0, :, here]
             delta = jnp.sum(mine * exact, axis=-1, keepdims=True)
             value = put_parts(mine, delta, SUM_AT).astype(BF)
-            out_ref[0, :, :, here] = value.reshape(2, rows, WIDE)
-
-    full = pl.BlockSpec((1, 2, rows, wide_heads), lambda im, b: (im, b, chunk, 0))
+            out_ref[0, 0, :, here] = value
+
+    full = pl.BlockSpec((1, 1, rows, wide_heads), lambda im, b: (im, b, chunk, 0))
     extra = list(kept)
     return pl.pallas_call(
         kernel,
-        grid=(images, count // 2),
+        grid=(images, count),
         in_specs=[
-            pl.BlockSpec((1, 2, rows, width), lambda im, b: (im, b, 0, 0)),
+            pl.BlockSpec((1, 1, rows, width), lambda im, b: (im, b, 0, 0)),
             pl.BlockSpec(w_wide.shape, lambda im, b: (0, 0)),
             full,
         ]
@@ -627,6 +635,11 @@
     )
     small = spread(small)
     qkv_blocks, qkv_index = ring_gather(qkv_shard, 0)
+    tok_blocks = None
+    if images == 1 and count == 4:
+        near, across = swap(tokens, 1), swap(tokens, 2)
+        across, qkv_blocks = together(across, qkv_blocks)
+        tok_blocks = [tokens, near, across, swap(across, 1)]
     w_wide = place_wide(qkv_blocks, qkv_index, widen(3 * own, 3 * wide_heads))
     cut = w_output.shape[0]
     lower = jnp.concatenate([w_output, w_down], axis=0)
@@ -642,19 +655,16 @@
     vectors = jnp.concatenate(vectors, axis=1).astype(F32)
     g_one, s_one, b_out, g_two, s_two, b_dn = [vectors[i : i + 1] for i in range(6)]
 
-    output_mat = jnp.concatenate(reorder(spread(output_cols), me), axis=1)
-    output_mat = output_mat.reshape(count, own, width)
+    output_parts = spread(output_cols)
 
     def down_part(j):
         start = (me ^ j) * group
         return lax.dynamic_slice_in_dim(down_rows, start, group, 0)
 
-    down_parts = [down_part(0)] + [swap(down_part(j), j) for j in range(1, count)]
-    down_mat = jnp.concatenate(reorder(down_parts, me), axis=2).reshape(-1, width)
+    down_sent = [down_part(j) for j in range(count)]
+    down_parts = [down_sent[0]] + [swap(down_sent[j], j) for j in range(1, count)]
 
     expand = widen(own, wide_heads)
-    own_rows = lax.dynamic_index_in_dim(output_mat, me, 0, keepdims=False)
-    output_wide = mm(own_rows.T, expand).astype(BF)
     lane = np.arange(3 * wide_heads) % WIDE
     kind = np.arange(3 * wide_heads) // wide_heads
     factor = np.where(kind == 0, SCALE * LOG2E, 1.0).astype(np.float32)
@@ -674,20 +684,38 @@
         [widen_vector(b_query), jnp.zeros((wide_heads,), F32), widen_vector(b_value)]
     )
     bias_wide = bias_wide * factor + ones.astype(np.float32)
-    weights = (me, output_mat, up_mat, up_mat.T, down_mat, down_mat.T, b_out, g_two, s_two, b_up.astype(F32)[None])
-
-    images_all = images
+
+    single = images == 1
     w_turned = w_wide.T
 
-    def run(tokens, bias_mask, cotangent):
+    def scatter_up(up_grad):
+        blocks = up_grad.astype(BF).reshape(fcount, width // fcount, -1)
+        return lax.psum_scatter(blocks, "fsdp", scatter_dimension=0)
+
+    def send_down(down_grad):
+        shaped = down_grad.astype(BF).reshape(width, group, -1).transpose(1, 0, 2)
+
+        def cols(j):
+            return lax.dynamic_slice_in_dim(shaped, (me ^ j) * own, own, 1)
+
+        return [cols(0)] + [swap(cols(j), j) for j in range(1, count)]
+
+    def merge_down(got):
+        return jnp.concatenate(reorder(got, me), axis=0)
+
+    def run(tokens, bias_mask, cotangent, tok_blocks=None):
         images = tokens.shape[0]
-        tok_all = jnp.stack(spread(tokens), axis=1)
-        tok_all, cot_first = lax.optimization_barrier((tok_all, cotangent))
-        cot_all = jnp.stack(spread(cot_first), axis=1)
+        if tok_blocks is None:
+            tok_blocks = spread(tokens)
+        tok_all = jnp.stack(tok_blocks, axis=1)
+        tok_all, cot_first = together(tok_all, cotangent)
+        cot_blocks = spread(cot_first)
         normed, _ = norm_parts(tok_all.astype(F32))
         h_one = (normed * g_one + s_one).astype(BF)
         product = jnp.einsum("ijld,de->ijle", h_one, w_wide, preferred_element_type=F32)
         qkv = (product * factor + bias_wide + bias_mask[..., None] * at_mask).astype(BF)
+        qkv, cot_blocks = together(qkv, cot_blocks)
+        cot_all = jnp.stack(cot_blocks, axis=1)
 
         kept_attend, kept_middle = (), ()
         mixed_chunks = []
@@ -695,6 +723,24 @@
             mixed, *kept_attend = attend(qkv, wide_heads, c, kept_attend)
             mixed_chunks.append(spread(mixed))
         query_wide, mixed_exact = kept_attend
+        mixed_exact, down_in, output_in = together(mixed_exact, down_parts, output_parts)
+        down_mat = jnp.concatenate(reorder(down_in, me), axis=2).reshape(-1, width)
+        output_mat = jnp.concatenate(reorder(output_in, me), axis=1)
+        output_mat = output_mat.reshape(count, own, width)
+        own_rows = lax.dynamic_index_in_dim(output_mat, me, 0, keepdims=False)
+        output_wide = mm(own_rows.T, expand).astype(BF)
+        weights = (
+            me,
+            output_mat,
+            up_mat,
+            up_mat.T,
+            down_mat,
+            down_mat.T,
+            b_out,
+            g_two,
+            s_two,
+            b_up.astype(F32)[None],
+        )
         def grad_rows(c, hidden_grad, x_own):
             grad_norm = hidden_grad.astype(F32)
             normed_two, inverse_two = norm_parts(x_own)
@@ -723,27 +769,35 @@
             x_parts.append(x_own)
             up_bias_grad = up_bias_grad + gb[0]
         h_two, activated, grad_hidden, mixed_all = kept_middle
-        cot_down, up_in = cot_all, h_two
-        kept_back = ()
-        for c in range(CHUNKS):
-            last = c == CHUNKS - 1
-            hidden_grad = (collect if last else collect_direct)(hidden_parts[c])
-            residual, grad_attn, sums = grad_rows(c, hidden_grad, x_parts[c])
-            grad_residual.append(residual)
-            early = early + sums
-            if not last:
-                grad_attn, cot_down, up_in = lax.optimization_barrier(
-                    (grad_attn, cot_down, up_in)
-                )
-            stacked = jnp.stack(spread(grad_attn), axis=1)
-            grad_attn_all.append(stacked)
-            kept_back = (mixed_back(stacked, output_wide, mixed_exact, c, kept_back),)
-        grad_mixed = kept_back[0]
-
-        up_grad = jnp.einsum("ijld,ijlf->df", up_in, grad_hidden, preferred_element_type=F32)
+        blocks = hidden_parts[0]
+        if count == 4:
+            near_sum, crossing = collect_pair(blocks)
+            h_two, crossing = together(h_two, crossing)
+            incoming = swap(crossing, 2)
+        else:
+            near_sum, incoming = collect(blocks), jnp.zeros((), F32)
+        up_grad = jnp.einsum(
+            "ijld,ijlf->df",
+            h_two,
+            grad_hidden,
+            preferred_element_type=F32,
+        ).astype(BF if single else F32)
+        incoming, up_grad = together(incoming, up_grad)
+        if single:
+            up_grad = scatter_up(up_grad)
+        hidden_grad = near_sum + incoming.astype(F32)
+        residual, grad_attn, early = grad_rows(0, hidden_grad, x_parts[0])
+        grad_attn, activated = together(grad_attn, activated)
         down_grad = jnp.einsum(
-            "ijlf,ijld->fd", activated, cot_down, preferred_element_type=F32
-        )
+            "ijld,ijlf->df",
+            cot_all,
+            activated,
+            preferred_element_type=F32,
+        ).astype(BF if single else F32)
+        grad_residual.append(residual)
+        attn_blocks, down_grad = together(spread(grad_attn), down_grad)
+        grad_attn_all = jnp.stack(attn_blocks, axis=1)
+        grad_mixed = mixed_back(grad_attn_all, output_wide, mixed_exact, 0, ())
 
         wide_shape = (images, count * length, wide_heads)
         query_in = query_wide.reshape(wide_shape)
@@ -751,22 +805,34 @@
         flat_qkv = qkv.reshape(images, count * length, 3 * wide_heads)
         halves = 2 if heads % 2 == 0 else 1
         step = heads // halves
-        out_parts, grad_in = lax.optimization_barrier((out_parts, grad_in))
-        out_blocks = [jnp.concatenate([y[j] for y in out_parts], axis=1) for j in range(count)]
-        pieces = []
-        for half in range(halves):
-            pieces.append(attend_back(query_in, grad_in, flat_qkv, half * step, step))
+        grad_in, out_blocks, down_grad = together(grad_in, list(out_parts[0]), down_grad)
+        if single:
+            down_grad = send_down(down_grad)
+            grad_in, up_grad = together(grad_in, up_grad)
+        if count == 4:
+            out_sum, out_across = collect_pair(out_blocks)
+            grad_in, out_across = together(grad_in, out_across)
+            out_incoming = swap(out_across, 2)
+        else:
+            out_sum, out_incoming = collect(out_blocks), jnp.zeros((), F32)
+        first = attend_back(query_in, grad_in, flat_qkv, 0, step)
+        pieces = [first]
+        if halves == 2:
+            first, down_grad = together(first, down_grad)
+            if single:
+                down_grad = merge_down(down_grad)
+            query_in, down_grad = together(query_in, down_grad)
+            pieces = [first, attend_back(query_in, grad_in, flat_qkv, step, step)]
+            pieces, out_incoming = together(pieces, out_incoming)
+        elif single:
+            down_grad = merge_down(down_grad)
+        out_sum = out_sum + out_incoming.astype(F32)
         grads = [
             [piece[k].reshape(images, count, length, -1) for piece in pieces] for k in range(3)
         ]
-        out_sum = collect(out_blocks)
-        grad_attn_all = jnp.concatenate(grad_attn_all, axis=2)
-        mixed_late, grad_attn_all, _ = lax.optimization_barrier(
-            (mixed_all, grad_attn_all, pieces[0][0])
-        )
         grad_attn_cols = lax.dynamic_slice_in_dim(grad_attn_all, me * own, own, 3)
         output_grad = jnp.einsum(
-            "ijle,ijld->ed", mixed_late, grad_attn_cols, preferred_element_type=F32
+            "ijle,ijld->ed", mixed_all, grad_attn_cols, preferred_element_type=F32
         )
         result = project_back(grads, tok_all, w_turned, g_one, s_one, expand.T)
         qkv_grad, late, bias_grads = result[count:]
@@ -778,12 +844,12 @@
             jnp.concatenate(grad_residual, axis=1)
             + norm_back(grad_norm_one, normed_one, inverse_one, g_one)
         ).astype(BF)
-        qkv_grad = qkv_grad if images_all == 1 else qkv_grad.astype(F32)
+        qkv_grad = qkv_grad if single else qkv_grad.astype(F32)
         sums = (down_grad, up_grad, output_grad, qkv_grad, early, up_bias_grad, late, bias_grads)
         return sums, (layer_out, grad_tokens)
 
     if images == 1:
-        sums, (layer_out, grad_tokens) = run(tokens, bias_mask, cotangent)
+        sums, (layer_out, grad_tokens) = run(tokens, bias_mask, cotangent, tok_blocks)
     else:
         items = (tokens[:, None], bias_mask[:, None], cotangent[:, None])
         shapes = jax.eval_shape(lambda item: run(*item)[0], jax.tree.map(lambda a: a[0], items))
@@ -797,17 +863,9 @@
         layer_out, grad_tokens = layer_out[:, 0], grad_tokens[:, 0]
     down_grad, up_grad, output_grad, qkv_grad, early, up_bias_grad, late, bias_grads = sums
 
-    down_grad = down_grad.astype(BF).reshape(group, -1, width)
-
-    def down_cols(j):
-        return lax.dynamic_slice_in_dim(down_grad, (me ^ j) * own, own, 2)
-
-    down_pieces = [down_cols(0)] + [swap(down_cols(j), j) for j in range(1, count)]
-    down_pieces = jnp.concatenate(reorder(down_pieces, me), axis=0)
-    final_up = lax.psum_scatter(
-        up_grad.astype(BF).reshape(fcount, width // fcount, -1), "fsdp", scatter_dimension=0
-    ).astype(F32)
-    final_down = lax.psum_scatter(down_pieces, "fsdp", scatter_dimension=0).astype(F32)
+    down_pieces = down_grad if single else merge_down(send_down(down_grad))
+    final_up = (up_grad if single else scatter_up(up_grad)).astype(F32)
+    final_down = lax.psum_scatter(down_pieces, "fsdp", scatter_dimension=0)
     output_grad = reorder(jnp.split(output_grad.astype(BF), count, axis=0), me)
     output_grad = jnp.concatenate(output_grad, axis=0)
     qkv_grad = qkv_grad.astype(BF).reshape(3, fcount, width // fcount, own)
@@ -818,25 +876,38 @@
         last = lax.dynamic_index_in_dim(output_grad, f, 0, keepdims=True)
         return jnp.concatenate([parts, last], axis=0)
 
-    four = ring_reduce(four_parts, 0)
 
     def to_owner(stack):
         kinds = stack.shape[0]
         parts = jnp.split(stack.reshape(kinds, count, own), count, axis=1)
-        return collect(reorder([part[:, 0] for part in parts], me))
-
-    early = to_owner(early)
-    early = ring_sum(jnp.concatenate([early.reshape(-1), up_bias_grad]))
-    late = to_owner(late)
+        parts = reorder([part[:, 0] for part in parts], me)
+        total = parts[0]
+        for j in range(1, count):
+            total = total + swap(parts[j], j)
+        return jnp.concatenate(
+            [total.reshape(-1)] + [narrow(g) for g in bias_grads] + [up_bias_grad]
+        )
+
     bias_grads = [bias_grads[0, i * wide_heads : (i + 1) * wide_heads] for i in (0, 2)]
-    late = ring_sum(jnp.concatenate([late.reshape(-1)] + [narrow(g) for g in bias_grads]))
-    gain_two_grad, shift_two_grad, b_output_grad, b_down_grad = [
-        early[i * own : (i + 1) * own] for i in range(4)
-    ]
-    b_up_grad = early[4 * own :]
-    gain_one_grad, shift_one_grad, b_query_grad, b_value_grad = [
-        late[i * own : (i + 1) * own] for i in range(4)
-    ]
+    four, final_down, vectors = ring_reduce(
+        four_parts,
+        0,
+        final_down,
+        jnp.concatenate([early, late], axis=0),
+        [to_owner] + sum_steps(),
+    )
+    final_down = final_down.astype(F32).T
+    (
+        gain_two_grad,
+        shift_two_grad,
+        b_output_grad,
+        b_down_grad,
+        gain_one_grad,
+        shift_one_grad,
+        b_query_grad,
+        b_value_grad,
+    ) = [vectors[i * own : (i + 1) * own] for i in range(8)]
+    b_up_grad = vectors[8 * own :]
     final_query, final_key, final_value, final_output = [four[i] for i in range(4)]
     return (
         layer_out,

time: 747 us -> 685 us (0.917)
  waiting for transfers between devices: 200 us -> 180 us
  local copies, waits for them, and re-layouts: 137 us -> 125 us
  starting transfers between devices: 58.8 us -> 47.7 us
  Pallas kernels: 205 us -> 194 us
  other arithmetic: 83.6 us -> 72.7 us
    ppermute x48 -> x36, waiting for transfers between devices: 149 us -> 124 us  [swap(): return lax.ppermute(value, 'seq', [(i, i ^ bit) for i in range(count)])]
    ppermute x15 -> x3, local copies, waits for them, and re-layouts: 29.1 us -> 7.57 us  [swap(): return lax.ppermute(value, 'seq', [(i, i ^ bit) for i in range(count)])]
    optimization_barrier x0 -> x7, local copies, waits for them, and re-layouts: none -> 18.3 us  [together(): return lax.optimization_barrier(values)]
    another operation x8 -> x0, local copies, waits for them, and re-layouts: 9.08 us -> none  [grad_rows(): jnp.stack([jnp.sum(grad_norm * normed_two, axis=(0, 1)), jnp.sum(grad_nor...]
    unnamed x125 -> x167, local copies, waits for them, and re-layouts: 3.88 us -> 11.8 us
    pallas_call x2 -> x1, Pallas kernels: 63.2 us -> 55.4 us  [middle(): pl.pallas_call(kernel, grid_spec=pltpu.PrefetchScalarGridSpec(num_scalar_...]
    concatenate x3 -> x9, local copies, waits for them, and re-layouts: 10.9 us -> 15.7 us  [the longest x1 5.97 us: run(): output_mat = jnp.concatenate(reorder(output_in, me), axis=1)]
    ppermute x48 -> x36, starting transfers between devices: 25.1 us -> 22.1 us  [swap(): return lax.ppermute(value, 'seq', [(i, i ^ bit) for i in range(count)])]
  transfers between devices with their start and end apart: 72 -> 57, of which waited for: 23 -> 20; matrix products, arithmetic and copies ran while one was open for 30% -> 31% of each run, Pallas kernels for 19% -> 21%
where the time goes in v4:
time: 685 us; the launch traced here: 675 us
  Pallas kernels  194 us (28%)
  waiting for transfers between devices  180 us (26%)
  local copies, waits for them, and re-layouts  125 us (18%)
  other arithmetic  72.7 us (11%)
  starting transfers between devices  47.7 us (7%)
  matrix products  39.6 us (6%)
  between operations  15.3 us (2%)
    ppermute x36, waiting for transfers between devices, swap(): return lax.ppermute(value, 'seq', [(i, i ^ bit) for i in range(count)])  124 us
    pallas_call x1, Pallas kernels, middle(): pl.pallas_call(kernel, grid_spec=pltpu.PrefetchScalarGridSpec(num_scalar_...  55.4 us
    ppermute x14, waiting for transfers between devices, ring_shift(): lax.ppermute(value, 'fsdp', [(order[i], order[(i + step) % count]) for i...  54.6 us
    pallas_call x2, Pallas kernels, attend_back(): pl.pallas_call(kernel, grid=(images, heads, steps), in_specs=[row_in, row...  51.3 us
    pallas_call x1, Pallas kernels, attend(): pl.pallas_call(kernel, grid=(images, count), in_specs=[part, pl.BlockSpec...  39.9 us
    pallas_call x1, Pallas kernels, project_back(): pl.pallas_call(kernel, grid=(images, count), in_specs=[piece_spec] * len(...  30 us
    ppermute x36, starting transfers between devices, swap(): return lax.ppermute(value, 'seq', [(i, i ^ bit) for i in range(count)])  22.1 us
    ppermute x14, starting transfers between devices, ring_shift(): lax.ppermute(value, 'fsdp', [(order[i], order[(i + step) % count]) for i...  18.8 us
  transfers between devices with their start and end apart: 57, of which 20 were waited for; matrix products, arithmetic and copies ran while one was open for 31% of the time, Pallas kernels for 21%

profile of v4, /device:TPU:0, one launch (start us, length us, event | category | flops | bytes accessed | tf_op | source)
XLA Modules:
  0.0 675.2 jit_solution(980589151997649600)
XLA Ops:
  16.6 5.7 collective-permute-done.2.refs_1_
  25.6 10.7 %collective-permute-done.4.refs_3_ = bf16[144,864]{1,0:T(8,128)(2,1)S(1)} collective-permute-done((bf16[144,864]{1,0:T(8,128)(2,1)S(1)}, bf16[144,864]{1,0:T(8,128)(2,1)S(1)}, u32[]{:S(2)}, u32[]{:S(2)}) %collective-permute-start.4) | collective-permute-done | bytes 248864 | tf_op jit(solution)/shard_map/ppermute | solution.py:116
  36.3 6.8 %collective-permute-done.5.refs_4_ = bf16[144,864]{1,0:T(8,128)(2,1)} collective-permute-done((bf16[144,864]{1,0:T(8,128)(2,1)S(1)}, bf16[144,864]{1,0:T(8,128)(2,1)}, u32[]{:S(2)}, u32[]{:S(2)}) %collective-permute-start.5) | collective-permute-done | bytes 248864 | tf_op jit(solution)/shard_map/ppermute | solution.py:116
  52.0 13.7 %collective-permute-done.8.refs_7_ = bf16[144,864]{1,0:T(8,128)(2,1)S(1)} collective-permute-done((bf16[144,864]{1,0:T(8,128)(2,1)}, bf16[144,864]{1,0:T(8,128)(2,1)S(1)}, u32[]{:S(2)}, u32[]{:S(2)}) %collective-permute-start.8) | collective-permute-done | bytes 248864 | tf_op jit(solution)/shard_map/ppermute | solution.py:116
  73.9 9.1 %place_wide.1 = bf16[1152,1536]{1,0:T(8,128)(2,1)} custom-call(s32[8]{0:T(128)} %stack.98.index_ref, bf16[144,864]{1,0:T(8,128)(2,1)} %copy-done.28, bf16[144,864]{1,0:T(8,128)(2,1)} %copy-done.40, bf16[144,864]{1,0:T(8,128)(2,1)} %copy-done.41, bf16[144,864]{1,0:T(8,128)(2,1)} %copy-done.42, bf16[144,864]{1,0:T(8,128)(2,1)} %collective-permute-done.5.refs_4_, ...), custom_call_target="tpu_custom_call" | custom-call | flops 23887872 | bytes 62208 | tf_op jit(solution)/shard_map/place_wide/pallas_call | solution.py:160
  88.8 24.1 %collective-permute-done.14 = bf16[1,512,1152]{2,1,0:T(8,128)(2,1)S(1)} collective-permute-done((bf16[1,512,1152]{2,1,0:T(8,128)(2,1)S(1)}, bf16[1,512,1152]{2,1,0:T(8,128)(2,1)S(1)}, u32[]{:S(2)}, u32[]{:S(2)}) %collective-permute-start.14) | collective-permute-done | bytes 1179680 | tf_op jit(solution)/shard_map/ppermute | solution.py:44
  113.0 10.9 %fusion.21.q_ref = bf16[1,4,512,1536]{3,2,1,0:T(8,128)(2,1)} fusion(f32[1536]{0:T(1024)S(1)} %copy-done.79, f32[4,512]{1,0:T(4,128)S(1)} %get-tuple-element.365, f32[1536]{0:T(1024)S(1)} %copy-done.64, f32[1536]{0:T(1024)S(1)} %copy-done.63, bf16[1,4,512,1152]{3,2,1,0:T(8,128)(2,1)S(1)} %pad_maximum_fusion.refs_4_.refs_6_, ...), kind=kOutput, calls=%fused_computation.29 | convolution fusion | flops 7277641728 | bytes 14601216 | tf_op jit(solution)/shard_map/ijld,de->ijle/dot_general | solution.py:715
  125.9 39.9 %attend.1 = (bf16[1,4,512,288]{3,2,1,0:T(8,128)(2,1)}, bf16[1,4,512,512]{3,2,1,0:T(8,128)(2,1)}, f32[1,4,512,512]{3,2,1,0:T(8,128)}) custom-call(bf16[1,4,512,1536]{3,2,1,0:T(8,128)(2,1)} %fusion.21.q_ref, bf16[1,2048,1536]{2,1,0:T(8,128)(2,1)} %bitcast.149), custom_call_target="tpu_custom_call" | custom-call | flops 134217728 | bytes 147456 | tf_op jit(solution)/shard_map/attend/pallas_call | solution.py:288
  174.9 5.5 copy.102
  186.0 11.3 %collective-permute-done.17 = bf16[1,4,512,288]{2,3,1,0:T(8,128)(2,1)} collective-permute-done((bf16[1,4,512,288]{2,3,1,0:T(8,128)(2,1)}, bf16[1,4,512,288]{2,3,1,0:T(8,128)(2,1)}, u32[]{:S(2)}, u32[]{:S(2)}) %collective-permute-start.17) | collective-permute-done | bytes 1179680 | tf_op jit(solution)/shard_map/ppermute | solution.py:44
  198.9 12.7 %collective-permute-done.23 = bf16[1152,288]{0,1:T(8,128)(2,1)} collective-permute-done((bf16[1152,288]{0,1:T(8,128)(2,1)}, bf16[1152,288]{0,1:T(8,128)(2,1)}, u32[]{:S(2)}, u32[]{:S(2)}) %collective-permute-start.23) | collective-permute-done | bytes 663584 | tf_op jit(solution)/shard_map/ppermute | solution.py:44
  219.7 7.7 %collective-permute-done.20 = bf16[2,538,288]{1,2,0:T(8,128)(2,1)} collective-permute-done((bf16[2,538,288]{1,2,0:T(8,128)(2,1)}, bf16[2,538,288]{1,2,0:T(8,128)(2,1)}, u32[]{:S(2)}, u32[]{:S(2)}) %collective-permute-start.20) | collective-permute-done | bytes 619808 | tf_op jit(solution)/shard_map/ppermute | solution.py:44
  227.3 15.0 %collective-permute-done.21 = bf16[2,538,288]{1,2,0:T(8,128)(2,1)} collective-permute-done((bf16[2,538,288]{1,2,0:T(8,128)(2,1)}, bf16[2,538,288]{1,2,0:T(8,128)(2,1)}, u32[]{:S(2)}, u32[]{:S(2)}) %collective-permute-start.21) | collective-permute-done | bytes 619808 | tf_op jit(solution)/shard_map/ppermute | solution.py:44
  254.0 5.2 copy.104
  269.2 6.0 concatenate.83
  277.6 55.4 %middle.1 = (bf16[1,4,512,1152]{3,2,1,0:T(8,128)(2,1)}, bf16[1,4,512,1076]{3,2,1,0:T(8,128)(2,1)}, bf16[1,4,512,1076]{3,2,1,0:T(8,128)(2,1)}, bf16[1,4,512,1152]...) custom-call(s32[1]{0:T(128)} %bitcast.me_ref, ...), custom_call_target="tpu_custom_call" | custom-call | flops 402259968 | bytes 846496 | tf_op jit(solution)/shard_map/middle/pallas_call | solution.py:388
  340.5 10.0 %fusion.6 = bf16[1152,1076]{0,1:T(8,128)(2,1)} fusion(bf16[1,4,512,1076]{3,2,1,0:T(8,128)(2,1)} %get-tuple-element.165, bf16[1,4,512,1152]{3,2,1,0:T(8,128)(2,1)S(1)} %copy-done.78), kind=kOutput, calls=%fused_computation.11 | convolution fusion | flops 5078444544 | bytes 11604992 | tf_op jit(solution)/shard_map/ijld,ijlf->df/dot_general | solution.py:779
  350.4 16.6 %collective-permute-done.27 = bf16[1,512,1152]{2,1,0:T(8,128)(2,1)S(1)} collective-permute-done((bf16[1,512,1152]{2,1,0:T(8,128)(2,1)S(1)}, bf16[1,512,1152]{2,1,0:T(8,128)(2,1)S(1)}, u32[]{:S(2)}, u32[]{:S(2)}) %collective-permute-start.27) | collective-permute-done | bytes 1179680 | tf_op jit(solution)/shard_map/ppermute | solution.py:44
  376.5 5.2 copy.110
  382.3 20.2 %collective-permute-done.29 = bf16[1,512,1152]{2,1,0:T(8,128)(2,1)} collective-permute-done((bf16[1,512,1152]{2,1,0:T(8,128)(2,1)}, bf16[1,512,1152]{2,1,0:T(8,128)(2,1)}, u32[]{:S(2)}, u32[]{:S(2)}) %collective-permute-start.29) | collective-permute-done | bytes 1179680 | tf_op jit(solution)/shard_map/ppermute | solution.py:44
  405.7 10.6 %fusion.7 = bf16[1152,1076]{0,1:T(8,128)(2,1)} fusion(bf16[1,4,512,1076]{3,2,1,0:T(8,128)(2,1)} %get-tuple-element.169, bf16[1,1,512,1152]{3,2,1,0:T(8,128)(2,1)} %bitcast.177, bf16[1,1,512,1152]{3,2,1,0:T(8,128)(2,1)S(1)} %bitcast.174, bf16[1,1,512,1152]{3,2,1,0:T(8,128)(2,1)} %bitcast.175, bf16[1,1,512,1152]{3,2,1,0:T(8,128)(2,1)S(1)} %bitcast.168), kind=kOutput, calls=%fused_computation.12 | convolution fusion | flops 5085522432 | bytes 11604992 | tf_op jit(solution)/shard_map/ijld,ijlf->df/dot_general | solution.py:791
  420.3 8.6 %mixed_back.1 = bf16[1,4,512,512]{3,2,1,0:T(8,128)(2,1)} custom-call(bf16[1,4,512,1152]{3,2,1,0:T(8,128)(2,1)} %pad_maximum_fusion.2.grad_ref, bf16[1152,512]{1,0:T(8,128)(2,1)} %convolution_convert_fusion.w_ref, f32[1,4,512,512]{3,2,1,0:T(8,128)} %get-tuple-element.174.exact_ref), custom_call_target="tpu_custom_call" | custom-call | flops 18874368 | bytes 190464 | tf_op jit(solution)/shard_map/mixed_back/pallas_call | solution.py:444
  433.3 5.8 copy.120
  450.8 6.1 dynamic-slice_bitcast_fusion
  468.6 25.6 %attend_back.2 = (bf16[1,2048,256]{2,1,0:T(8,128)(2,1)}, bf16[1,2048,256]{2,1,0:T(8,128)(2,1)}, bf16[1,2048,256]{2,1,0:T(8,128)(2,1)}) custom-call(bf16[1,2048,512]{2,1,0:T(8,128)(2,1)} %bitcast.163, bf16[1,2048,512]{2,1,0:T(8,128)(2,1)} %bitcast.155, bf16[1,2048,1536]{2,1,0:T(8,128)(2,1)} %bitcast.150, bf16[1,2048,1536]{2,1,0:T(8,128)(2,1)} %bitcast.151), custom_call_target="tpu_custom_call" | custom-call | flops 167772160 | bytes 229376 | tf_op jit(solution)/shard_map/attend_back/pallas_call | solution.py:506
  509.6 5.0 fusion.32
  522.4 25.7 %attend_back.3 = (bf16[1,2048,256]{2,1,0:T(8,128)(2,1)}, bf16[1,2048,256]{2,1,0:T(8,128)(2,1)}, bf16[1,2048,256]{2,1,0:T(8,128)(2,1)}) custom-call(bf16[1,2048,512]{2,1,0:T(8,128)(2,1)} %bitcast.164, bf16[1,2048,512]{2,1,0:T(8,128)(2,1)} %bitcast.156, bf16[1,2048,1536]{2,1,0:T(8,128)(2,1)} %bitcast.152, bf16[1,2048,1536]{2,1,0:T(8,128)(2,1)} %bitcast.153), custom_call_target="tpu_custom_call" | custom-call | flops 167772160 | bytes 229376 | tf_op jit(solution)/shard_map/attend_back/pallas_call | solution.py:506
  548.1 30.0 %project_back.1 = (bf16[1,512,1152]{2,1,0:T(8,128)(2,1)}, bf16[1,512,1152]{2,1,0:T(8,128)(2,1)}, bf16[1,512,1152]{2,1,0:T(8,128)(2,1)}, bf16[1,512,1152]{2,1,0:T...) custom-call(bf16[1,4,512,256]{3,2,1,0:T(8,128)(2,1)} %bitcast.181, ...), custom_call_target="tpu_custom_call" | custom-call | flops 113246208 | bytes 301056 | tf_op jit(solution)/shard_map/project_back/pallas_call | solution.py:581
  588.0 5.2 collective-permute-start.40
  614.0 4.9 collective-permute-done.41
  623.9 14.2 %collective-permute-done.39 = bf16[1,512,1152]{2,1,0:T(8,128)(2,1)S(1)} collective-permute-done((bf16[1,512,1152]{2,1,0:T(8,128)(2,1)S(1)}, bf16[1,512,1152]{2,1,0:T(8,128)(2,1)S(1)}, u32[]{:S(2)}, u32[]{:S(2)}) %collective-permute-start.39) | collective-permute-done | bytes 1179680 | tf_op jit(solution)/shard_map/ppermute | solution.py:44
  645.4 7.8 %collective-permute-done.48 = bf16[4,144,288]{2,1,0:T(8,128)(2,1)S(1)} collective-permute-done((bf16[4,144,288]{2,1,0:T(8,128)(2,1)S(1)}, bf16[4,144,288]{2,1,0:T(8,128)(2,1)S(1)}, u32[]{:S(2)}, u32[]{:S(2)}) %collective-permute-start.48) | collective-permute-done | bytes 331808 | tf_op jit(solution)/shard_map/ppermute | solution.py:116
  (398 shorter events, 218.8 us)
Async XLA Ops:
  7.2 162.8 %all-gather.7.cloned.1.call-start = ((), (), s32[]{:S(2)}) async-start(), calls=%async_computation.5 | async-start | bytes 3981312 | tf_op jit(solution)/shard_map/all_gather | solution.py:646
  10.3 164.6 %all-gather.5.cloned.1.call-start = ((), (), s32[]{:S(2)}) async-start(), calls=%async_computation.2 | async-start | bytes 2985984 | tf_op jit(solution)/shard_map/all_gather | solution.py:649
  10.4 55.3 %collective-permute-start.1 = (bf16[1,512,1152]{2,1,0:T(8,128)(2,1)}, bf16[1,512,1152]{2,1,0:T(8,128)(2,1)S(1)}, u32[]{:S(2)}, u32[]{:S(2)}) collective-permute-start(bf16[1,512,1152]{2,1,0:T(8,128)(2,1)} %param.21), channel_id=1, source_target_pairs={{0,16},{8,24},{16,0},{24,8},{1,17},{9,25},{17,1},{25,9},{2,18},{10... | collective-permute-start | bytes 3538952 | tf_op jit(solution)/shard_map/ppermute | solution.py:44
  45.1 37.9 %collective-permute-start = (bf16[1,512,1152]{2,1,0:T(8,128)(2,1)}, bf16[1,512,1152]{2,1,0:T(8,128)(2,1)S(1)}, u32[]{:S(2)}, u32[]{:S(2)}) collective-permute-start(bf16[1,512,1152]{2,1,0:T(8,128)(2,1)} %param.21), channel_id=1, source_target_pairs={{0,8},{8,0},{16,24},{24,16},{1,9},{9,1},{17,25},{25,17},{2,10},{10... | collective-permute-start | bytes 3538952 | tf_op jit(solution)/shard_map/ppermute | solution.py:44
  50.1 19.6 %collective-permute-start.10 = (bf16[2240]{0:T(1024)(128)(2,1)S(1)}, bf16[2240]{0:T(1024)(128)(2,1)S(1)}, u32[]{:S(2)}, u32[]{:S(2)}) collective-permute-start(bf16[2240]{0:T(1024)(128)(2,1)S(1)} %concatenate.78), channel_id=1, source_target_pairs={{0,16},{8,24},{16,0},{24,8},{1,17},{9,25},{17,1},{25,9},{2,18},{10... | collective-permute-start | bytes 13448 | tf_op jit(solution)/shard_map/ppermute | solution.py:44
  50.6 418.0 %reduce-scatter.3.cloned.1.call-start = ((), (), s32[]{:S(2)}) async-start(), calls=%async_computation.3 | async-start | bytes 2985984 | tf_op jit(solution)/shard_map/reduce_scatter | solution.py:693
  50.9 20.1 %collective-permute-start.12 = (bf16[2240]{0:T(1024)(128)(2,1)S(1)}, bf16[2240]{0:T(1024)(128)(2,1)S(1)}, u32[]{:S(2)}, u32[]{:S(2)}) collective-permute-start(bf16[2240]{0:T(1024)(128)(2,1)S(1)} %concatenate.78), channel_id=1, source_target_pairs={{0,8},{8,0},{16,24},{24,16},{1,9},{9,1},{17,25},{25,17},{2,10},{10... | collective-permute-start | bytes 13448 | tf_op jit(solution)/shard_map/ppermute | solution.py:44
  84.9 28.0 %collective-permute-start.14 = (bf16[1,512,1152]{2,1,0:T(8,128)(2,1)S(1)}, bf16[1,512,1152]{2,1,0:T(8,128)(2,1)S(1)}, u32[]{:S(2)}, u32[]{:S(2)}) collective-permute-start(bf16[1,512,1152]{2,1,0:T(8,128)(2,1)S(1)} %copy-done.5), channel_id=1, source_target_pairs={{0,16},{8,24},{16,0},{24,8},{1,17},{9,25},{17,1},{25,9},{2,18},{10... | collective-permute-start | bytes 3538952 | tf_op jit(solution)/shard_map/ppermute | solution.py:44
  86.5 37.3 %collective-permute-start.13 = (bf16[1,512,1152]{2,1,0:T(8,128)(2,1)S(1)}, bf16[1,512,1152]{2,1,0:T(8,128)(2,1)S(1)}, u32[]{:S(2)}, u32[]{:S(2)}) collective-permute-start(bf16[1,512,1152]{2,1,0:T(8,128)(2,1)S(1)} %copy-done.5), channel_id=1, source_target_pairs={{0,8},{8,0},{16,24},{24,16},{1,9},{9,1},{17,25},{25,17},{2,10},{10... | collective-permute-start | bytes 3538952 | tf_op jit(solution)/shard_map/ppermute | solution.py:44
  168.2 29.1 %collective-permute-start.17 = (bf16[1,4,512,288]{2,3,1,0:T(8,128)(2,1)}, bf16[1,4,512,288]{2,3,1,0:T(8,128)(2,1)}, u32[]{:S(2)}, u32[]{:S(2)}) collective-permute-start(bf16[1,4,512,288]{2,3,1,0:T(8,128)(2,1)} %copy.90), channel_id=1, source_target_pairs={{0,16},{8,24},{16,0},{24,8},{1,17},{9,25},{17,1},{25,9},{2,18},{10... | collective-permute-start | bytes 3538952 | tf_op jit(solution)/shard_map/ppermute | solution.py:44
  169.8 29.1 %collective-permute-start.16 = (bf16[1,4,512,288]{2,3,1,0:T(8,128)(2,1)}, bf16[1,4,512,288]{2,3,1,0:T(8,128)(2,1)}, u32[]{:S(2)}, u32[]{:S(2)}) collective-permute-start(bf16[1,4,512,288]{2,3,1,0:T(8,128)(2,1)} %copy.90), channel_id=1, source_target_pairs={{0,8},{8,0},{16,24},{24,16},{1,9},{9,1},{17,25},{25,17},{2,10},{10... | collective-permute-start | bytes 3538952 | tf_op jit(solution)/shard_map/ppermute | solution.py:44
  173.2 38.4 %collective-permute-start.23 = (bf16[1152,288]{0,1:T(8,128)(2,1)}, bf16[1152,288]{0,1:T(8,128)(2,1)}, u32[]{:S(2)}, u32[]{:S(2)}) collective-permute-start(bf16[1152,288]{0,1:T(8,128)(2,1)} %copy.94), channel_id=1, source_target_pairs={{0,16},{8,24},{16,0},{24,8},{1,17},{9,25},{17,1},{25,9},{2,18},{10... | collective-permute-start | bytes 1990664 | tf_op jit(solution)/shard_map/ppermute | solution.py:44
  180.5 61.9 %collective-permute-start.22 = (bf16[1152,288]{0,1:T(8,128)(2,1)}, bf16[1152,288]{0,1:T(8,128)(2,1)}, u32[]{:S(2)}, u32[]{:S(2)}) collective-permute-start(bf16[1152,288]{0,1:T(8,128)(2,1)} %copy.94), channel_id=1, source_target_pairs={{0,8},{8,0},{16,24},{24,16},{1,9},{9,1},{17,25},{25,17},{2,10},{10... | collective-permute-start | bytes 1990664 | tf_op jit(solution)/shard_map/ppermute | solution.py:44
  185.5 33.7 %collective-permute-start.19 = (bf16[2,538,288]{1,2,0:T(8,128)(2,1)}, bf16[2,538,288]{1,2,0:T(8,128)(2,1)S(1)}, u32[]{:S(2)}, u32[]{:S(2)}) collective-permute-start(bf16[2,538,288]{1,2,0:T(8,128)(2,1)} %get-tuple-element.298), channel_id=1, source_target_pairs={{0,8},{8,0},{16,24},{24,16},{1,9},{9,1},{17,25},{25,17},{2,10},{10... | collective-permute-start | bytes 1859336 | tf_op jit(solution)/shard_map/ppermute | solution.py:44
  197.3 30.0 %collective-permute-start.20 = (bf16[2,538,288]{1,2,0:T(8,128)(2,1)}, bf16[2,538,288]{1,2,0:T(8,128)(2,1)}, u32[]{:S(2)}, u32[]{:S(2)}) collective-permute-start(bf16[2,538,288]{1,2,0:T(8,128)(2,1)} %get-tuple-element.297), channel_id=1, source_target_pairs={{0,16},{8,24},{16,0},{24,8},{1,17},{9,25},{17,1},{25,9},{2,18},{10... | collective-permute-start | bytes 1859336 | tf_op jit(solution)/shard_map/ppermute | solution.py:44
  198.9 43.5 %collective-permute-start.21 = (bf16[2,538,288]{1,2,0:T(8,128)(2,1)}, bf16[2,538,288]{1,2,0:T(8,128)(2,1)}, u32[]{:S(2)}, u32[]{:S(2)}) collective-permute-start(bf16[2,538,288]{1,2,0:T(8,128)(2,1)} %get-tuple-element.296), channel_id=1, source_target_pairs={{0,24},{8,16},{16,8},{24,0},{1,25},{9,17},{17,9},{25,1},{2,26},{10... | collective-permute-start | bytes 1859336 | tf_op jit(solution)/shard_map/ppermute | solution.py:44
  211.5 30.8 %collective-permute-start.24 = (bf16[1152,288]{0,1:T(8,128)(2,1)}, bf16[1152,288]{0,1:T(8,128)(2,1)}, u32[]{:S(2)}, u32[]{:S(2)}) collective-permute-start(bf16[1152,288]{0,1:T(8,128)(2,1)} %collective-permute-done.23), channel_id=1, source_target_pairs={{0,8},{8,0},{16,24},{24,16},{1,9},{9,1},{17,25},{25,17},{2,10},{10... | collective-permute-start | bytes 1990664 | tf_op jit(solution)/shard_map/ppermute | solution.py:44
  219.2 56.0 %collective-permute-start.18 = (bf16[1,4,512,288]{2,3,1,0:T(8,128)(2,1)}, bf16[1,4,512,288]{2,3,1,0:T(8,128)(2,1)}, u32[]{:S(2)}, u32[]{:S(2)}) collective-permute-start(bf16[1,4,512,288]{2,3,1,0:T(8,128)(2,1)} %collective-permute-done.17), channel_id=1, source_target_pairs={{0,8},{8,0},{16,24},{24,16},{1,9},{9,1},{17,25},{25,17},{2,10},{10... | collective-permute-start | bytes 3538952 | tf_op jit(solution)/shard_map/ppermute | solution.py:44
  333.3 33.8 %collective-permute-start.25 = (bf16[1,512,1152]{2,1,0:T(8,128)(2,1)}, bf16[1,512,1152]{2,1,0:T(8,128)(2,1)}, u32[]{:S(2)}, u32[]{:S(2)}) collective-permute-start(bf16[1,512,1152]{2,1,0:T(8,128)(2,1)} %get-tuple-element.159), channel_id=1, source_target_pairs={{0,8},{8,0},{16,24},{24,16},{1,9},{9,1},{17,25},{25,17},{2,10},{10... | collective-permute-start | bytes 3538952 | tf_op jit(solution)/shard_map/ppermute | solution.py:44
  338.9 28.1 %collective-permute-start.27 = (bf16[1,512,1152]{2,1,0:T(8,128)(2,1)S(1)}, bf16[1,512,1152]{2,1,0:T(8,128)(2,1)S(1)}, u32[]{:S(2)}, u32[]{:S(2)}) collective-permute-start(bf16[1,512,1152]{2,1,0:T(8,128)(2,1)S(1)} %add_convert_fusion.4), channel_id=1, source_target_pairs={{0,16},{8,24},{16,0},{24,8},{1,17},{9,25},{17,1},{25,9},{2,18},{10... | collective-permute-start | bytes 3538952 | tf_op jit(solution)/shard_map/ppermute | solution.py:44
  375.0 27.6 %collective-permute-start.29 = (bf16[1,512,1152]{2,1,0:T(8,128)(2,1)}, bf16[1,512,1152]{2,1,0:T(8,128)(2,1)}, u32[]{:S(2)}, u32[]{:S(2)}) collective-permute-start(bf16[1,512,1152]{2,1,0:T(8,128)(2,1)} %get-tuple-element.170), channel_id=1, source_target_pairs={{0,16},{8,24},{16,0},{24,8},{1,17},{9,25},{17,1},{25,9},{2,18},{10... | collective-permute-start | bytes 3538952 | tf_op jit(solution)/shard_map/ppermute | solution.py:44
  381.7 260.0 %reduce-scatter.5.cloned.1.call-start = ((), (), s32[]{:S(2)}) async-start(), calls=%async_computation.4 | async-start | bytes 3760128 | tf_op jit(solution)/shard_map/reduce_scatter | solution.py:868
  382.3 34.1 %collective-permute-start.28 = (bf16[1,512,1152]{2,1,0:T(8,128)(2,1)}, bf16[1,512,1152]{2,1,0:T(8,128)(2,1)S(1)}, u32[]{:S(2)}, u32[]{:S(2)}) collective-permute-start(bf16[1,512,1152]{2,1,0:T(8,128)(2,1)} %get-tuple-element.170), channel_id=1, source_target_pairs={{0,8},{8,0},{16,24},{24,16},{1,9},{9,1},{17,25},{25,17},{2,10},{10... | collective-permute-start | bytes 3538952 | tf_op jit(solution)/shard_map/ppermute | solution.py:44
  428.9 36.8 %collective-permute-start.32 = (bf16[1,512,1152]{2,1,0:T(8,128)(2,1)}, bf16[1,512,1152]{2,1,0:T(8,128)(2,1)}, u32[]{:S(2)}, u32[]{:S(2)}) collective-permute-start(bf16[1,512,1152]{2,1,0:T(8,128)(2,1)} %get-tuple-element.187), channel_id=1, source_target_pairs={{0,8},{8,0},{16,24},{24,16},{1,9},{9,1},{17,25},{25,17},{2,10},{10... | collective-permute-start | bytes 3538952 | tf_op jit(solution)/shard_map/ppermute | solution.py:44
  459.2 35.1 %collective-permute-start.33 = (bf16[2,288,538]{2,1,0:T(8,128)(2,1)}, bf16[2,288,538]{2,1,0:T(8,128)(2,1)}, u32[]{:S(2)}, u32[]{:S(2)}) collective-permute-start(bf16[2,288,538]{2,1,0:T(8,128)(2,1)} %copy.111), channel_id=1, source_target_pairs={{0,8},{8,0},{16,24},{24,16},{1,9},{9,1},{17,25},{25,17},{2,10},{10... | collective-permute-start | bytes 1859336 | tf_op jit(solution)/shard_map/ppermute | solution.py:44
  461.5 32.8 %collective-permute-start.34 = (bf16[2,288,538]{2,1,0:T(8,128)(2,1)}, bf16[2,288,538]{2,1,0:T(8,128)(2,1)}, u32[]{:S(2)}, u32[]{:S(2)}) collective-permute-start(bf16[2,288,538]{2,1,0:T(8,128)(2,1)} %copy.112), channel_id=1, source_target_pairs={{0,16},{8,24},{16,0},{24,8},{1,17},{9,25},{17,1},{25,9},{2,18},{10... | collective-permute-start | bytes 1859336 | tf_op jit(solution)/shard_map/ppermute | solution.py:44
  465.4 30.8 %collective-permute-start.35 = (bf16[2,288,538]{2,1,0:T(8,128)(2,1)}, bf16[2,288,538]{2,1,0:T(8,128)(2,1)}, u32[]{:S(2)}, u32[]{:S(2)}) collective-permute-start(bf16[2,288,538]{2,1,0:T(8,128)(2,1)} %copy.113), channel_id=1, source_target_pairs={{0,24},{8,16},{16,8},{24,0},{1,25},{9,17},{17,9},{25,1},{2,26},{10... | collective-permute-start | bytes 1859336 | tf_op jit(solution)/shard_map/ppermute | solution.py:44
  503.2 44.9 %collective-permute-start.36 = (bf16[1,512,1152]{2,1,0:T(8,128)(2,1)}, bf16[1,512,1152]{2,1,0:T(8,128)(2,1)}, u32[]{:S(2)}, u32[]{:S(2)}) collective-permute-start(bf16[1,512,1152]{2,1,0:T(8,128)(2,1)} %add_convert_fusion.3), channel_id=1, source_target_pairs={{0,16},{8,24},{16,0},{24,8},{1,17},{9,25},{17,1},{25,9},{2,18},{10... | collective-permute-start | bytes 3538952 | tf_op jit(solution)/shard_map/ppermute | solution.py:44
  578.9 28.4 %collective-permute-start.38 = (bf16[1,512,1152]{2,1,0:T(8,128)(2,1)}, bf16[1,512,1152]{2,1,0:T(8,128)(2,1)}, u32[]{:S(2)}, u32[]{:S(2)}) collective-permute-start(bf16[1,512,1152]{2,1,0:T(8,128)(2,1)} %get-tuple-element.215), channel_id=1, source_target_pairs={{0,8},{8,0},{16,24},{24,16},{1,9},{9,1},{17,25},{25,17},{2,10},{10... | collective-permute-start | bytes 3538952 | tf_op jit(solution)/shard_map/ppermute | solution.py:44
  596.6 23.9 %collective-permute-start.31 = (bf16[1,512,1152]{2,1,0:T(8,128)(2,1)}, bf16[1,512,1152]{2,1,0:T(8,128)(2,1)}, u32[]{:S(2)}, u32[]{:S(2)}) collective-permute-start(bf16[1,512,1152]{2,1,0:T(8,128)(2,1)} %get-tuple-element.181), channel_id=1, source_target_pairs={{0,8},{8,0},{16,24},{24,16},{1,9},{9,1},{17,25},{25,17},{2,10},{10... | collective-permute-start | bytes 3538952 | tf_op jit(solution)/shard_map/ppermute | solution.py:44
  597.1 26.7 %collective-permute-start.37 = (bf16[1,512,1152]{2,1,0:T(8,128)(2,1)}, bf16[1,512,1152]{2,1,0:T(8,128)(2,1)}, u32[]{:S(2)}, u32[]{:S(2)}) collective-permute-start(bf16[1,512,1152]{2,1,0:T(8,128)(2,1)} %get-tuple-element.213), channel_id=1, source_target_pairs={{0,8},{8,0},{16,24},{24,16},{1,9},{9,1},{17,25},{25,17},{2,10},{10... | collective-permute-start | bytes 3538952 | tf_op jit(solution)/shard_map/ppermute | solution.py:44
  611.3 26.8 %collective-permute-start.39 = (bf16[1,512,1152]{2,1,0:T(8,128)(2,1)S(1)}, bf16[1,512,1152]{2,1,0:T(8,128)(2,1)S(1)}, u32[]{:S(2)}, u32[]{:S(2)}) collective-permute-start(bf16[1,512,1152]{2,1,0:T(8,128)(2,1)S(1)} %add_convert_fusion.1), channel_id=1, source_target_pairs={{0,16},{8,24},{16,0},{24,8},{1,17},{9,25},{17,1},{25,9},{2,18},{10... | collective-permute-start | bytes 3538952 | tf_op jit(solution)/shard_map/ppermute | solution.py:44
  (106 other events, 1926.4 us)
Sparse Core Ops, SparseCore 0:
  10.8 76.4 all-gather.6
  89.4 56.4 all-gather.4
  381.8 75.7 reduce-scatter.2
  509.7 82.2 reduce-scatter.4

commit v5 on v4

--- a/solution.py
+++ b/solution.py
@@ -240,6 +240,93 @@
     return ((source // HEAD) * WIDE + source % HEAD == target).astype(dtype)
 
 
+def glue(kernel, me, inputs, shapes, name, scratch=()):
+    def spec(shape):
+        return pl.BlockSpec(shape, lambda i, me_ref: (0,) * len(shape))
+
+    return pl.pallas_call(
+        kernel,
+        grid_spec=pltpu.PrefetchScalarGridSpec(
+            num_scalar_prefetch=1,
+            grid=(1,),
+            in_specs=[spec(a.shape) for a in inputs],
+            out_specs=[spec(shape) for shape in shapes],
+            scratch_shapes=scratch,
+        ),
+        out_shape=[jax.ShapeDtypeStruct(shape, BF) for shape in shapes],
+        cost_estimate=cost(0, 4 * sum(a.size for a in inputs)),
+        compiler_params=pltpu.CompilerParams(vmem_limit_bytes=VMEM_BYTES),
+        name=name,
+    )(me.reshape(1), *inputs)
+
+
+def cut_lower(lower, me, count, split):
+    blocks, own, total = lower.shape
+    group = blocks // count
+
+    def kernel(me_ref, in_ref, *outs):
+        for j in range(count):
+            start = (me_ref[0] ^ j) * group
+            for h in range(group):
+                outs[j][h] = in_ref[start + h][:, :split]
+        outs[count][...] = jnp.concatenate([in_ref[f][:, split:] for f in range(blocks)], axis=-1)
+
+    shapes = [(group, own, split)] * count + [(own, blocks * (total - split))]
+    *down, output = glue(kernel, me, [lower], shapes, "cut_lower")
+    return down, output
+
+
+def build_weights(down, output, me):
+    count = len(down)
+    group, own, split = down[0].shape
+    width = count * own
+    hidden_count = group * split
+
+    def kernel(me_ref, *refs):
+        down_refs, output_refs = refs[:count], refs[count : 2 * count]
+        down_ref, turned_ref, output_ref, held_down, held_output = refs[2 * count :]
+        for j in range(count):
+            at = me_ref[0] ^ j
+            parts = [down_refs[j][h] for h in range(group)]
+            held_down[at] = jnp.concatenate(parts, axis=-1)
+            held_output[at] = output_refs[j][...]
+        turned = held_down[...].reshape(width, hidden_count)
+        turned_ref[...] = turned
+        down_ref[...] = turned.T
+        output_ref[...] = held_output[...].reshape(width, width).T.reshape(count, own, width)
+
+    shapes = [(hidden_count, width), (width, hidden_count), (count, own, width)]
+    scratch = [pltpu.VMEM((count, own, hidden_count), BF), pltpu.VMEM((count, own, width), BF)]
+    return glue(kernel, me, [*down, *output], shapes, "build_weights", scratch)
+
+
+def cut_down(grad, me, count, group):
+    width, hidden_count = grad.shape
+    own, split = width // count, hidden_count // group
+
+    def kernel(me_ref, in_ref, *outs):
+        for j in range(count):
+            start = pl.multiple_of((me_ref[0] ^ j) * own, own)
+            rows = in_ref[pl.ds(start, own), :]
+            for h in range(group):
+                outs[j][h] = rows[:, h * split : (h + 1) * split]
+
+    return glue(kernel, me, [grad], [(group, own, split)] * count, "cut_down")
+
+
+def merge_blocks(parts, me):
+    count = len(parts)
+    group, own, split = parts[0].shape
+
+    def kernel(me_ref, *refs):
+        out = refs[count]
+        for j in range(count):
+            for h in range(group):
+                out[(me_ref[0] ^ j) * group + h] = refs[j][h]
+
+    return glue(kernel, me, parts, [(count * group, own, split)], "merge_blocks")[0]
+
+
 def attend(qkv, wide_heads, chunk, kept):
     images, count, length, _ = qkv.shape
     heads = wide_heads // WIDE
@@ -274,15 +361,15 @@
             target = lax.broadcasted_iota(jnp.int32, (WIDE, heads * HEAD), 1)
             pick = ((source < HEAD) & (source + e * HEAD == target)).astype(F32).astype(BF)
             total = total + mm(mixed.astype(BF), pick)
-        mixed_ref[0, 0] = total.astype(BF)
+        mixed_ref[0, 0] = total.T.astype(BF)
 
     part = pl.BlockSpec((1, 1, rows, wide_heads), lambda i, b: (i, b, chunk, 0))
     shapes = [
-        jax.ShapeDtypeStruct((images, count, rows, heads * HEAD), BF),
+        jax.ShapeDtypeStruct((images, count, heads * HEAD, rows), BF),
         jax.ShapeDtypeStruct((images, count, length, wide_heads), BF),
         jax.ShapeDtypeStruct((images, count, length, wide_heads), F32),
     ]
-    outs = [pl.BlockSpec((1, 1, rows, heads * HEAD), lambda i, b: (i, b, 0, 0)), part, part]
+    outs = [pl.BlockSpec((1, 1, heads * HEAD, rows), lambda i, b: (i, b, 0, 0)), part, part]
     extra = list(kept)
     scores = images * count * rows * keys * heads
     return pl.pallas_call(
@@ -304,7 +391,7 @@
     images, count, length, width = tokens.shape
     me, w_output, w_up, up_turned, w_down, down_turned, b_output, gain, shift, b_up = weights
     rows = length // CHUNKS
-    own = mixed[0].shape[-1]
+    own = mixed[0].shape[-2]
     hidden_count = w_up.shape[1]
 
     def kernel(me_ref, *refs):
@@ -329,7 +416,7 @@
         x_one = tok_ref[0, 0].astype(F32) + bo_ref[...]
         pieces = []
         for i in range(count):
-            piece = mixed_refs[i][0, 0]
+            piece = mixed_refs[i][0, 0].T
             pieces.append(piece)
             x_one = x_one + mm(piece, wo_ref[me_ref[0] ^ i])
         cat_ref[0, 0] = jnp.concatenate(pieces, axis=-1)
@@ -373,7 +460,7 @@
             gb_ref[...] += summed
 
     def piece_spec(i):
-        return pl.BlockSpec((1, 1, rows, own), lambda im, b, me_ref: (im, b ^ i, 0, 0))
+        return pl.BlockSpec((1, 1, own, rows), lambda im, b, me_ref: (im, b ^ i, 0, 0))
 
     def whole_spec(array):
         return pl.BlockSpec(array.shape, lambda im, b, me_ref: (0,) * array.ndim)
@@ -635,17 +722,26 @@
     )
     small = spread(small)
     qkv_blocks, qkv_index = ring_gather(qkv_shard, 0)
-    tok_blocks = None
-    if images == 1 and count == 4:
+    tok_blocks, cot_blocks = None, None
+    fast = images == 1 and count == 4
+    if fast:
         near, across = swap(tokens, 1), swap(tokens, 2)
-        across, qkv_blocks = together(across, qkv_blocks)
+        across, cot_sent = together(across, cotangent)
+        cot_across = swap(cot_sent, 2)
+        across, cot_sent, qkv_blocks = together(across, cot_sent, qkv_blocks)
         tok_blocks = [tokens, near, across, swap(across, 1)]
     w_wide = place_wide(qkv_blocks, qkv_index, widen(3 * own, 3 * wide_heads))
-    cut = w_output.shape[0]
-    lower = jnp.concatenate([w_output, w_down], axis=0)
+    split = w_down.shape[0]
+    lower = jnp.concatenate([w_down.T, w_output.T], axis=1)
     lower = lax.all_gather(lower, "fsdp", axis=0)
-    output_cols = lower[:, :cut].reshape(width, own)
-    down_rows = lower[:, cut:]
+    if fast:
+        down_sent, output_cols = cut_lower(lower, me, count, split)
+    else:
+        output_cols = lower[:, :, split:].transpose(1, 0, 2).reshape(own, width)
+        down_sent = [
+            lax.dynamic_slice_in_dim(lower[:, :, :split], (me ^ j) * group, group, 0)
+            for j in range(count)
+        ]
     up_mat = lax.all_gather(w_up, "fsdp", axis=0, tiled=True)
 
     patches = images * length
@@ -654,15 +750,6 @@
     vectors = reorder([block[patches:].reshape(6, own) for block in small], me)
     vectors = jnp.concatenate(vectors, axis=1).astype(F32)
     g_one, s_one, b_out, g_two, s_two, b_dn = [vectors[i : i + 1] for i in range(6)]
-
-    output_parts = spread(output_cols)
-
-    def down_part(j):
-        start = (me ^ j) * group
-        return lax.dynamic_slice_in_dim(down_rows, start, group, 0)
-
-    down_sent = [down_part(j) for j in range(count)]
-    down_parts = [down_sent[0]] + [swap(down_sent[j], j) for j in range(1, count)]
 
     expand = widen(own, wide_heads)
     lane = np.arange(3 * wide_heads) % WIDE
@@ -686,6 +773,8 @@
     bias_wide = bias_wide * factor + ones.astype(np.float32)
 
     single = images == 1
+    down_exchanged = [down_sent[0]] + [swap(down_sent[j], j) for j in range(1, count)]
+    cot_begun = (cot_sent, None, cot_across) if fast else None
     w_turned = w_wide.T
 
     def scatter_up(up_grad):
@@ -693,6 +782,9 @@
         return lax.psum_scatter(blocks, "fsdp", scatter_dimension=0)
 
     def send_down(down_grad):
+        if fast:
+            sent = cut_down(down_grad, me, count, group)
+            return [sent[0]] + [swap(sent[j], j) for j in range(1, count)]
         shaped = down_grad.astype(BF).reshape(width, group, -1).transpose(1, 0, 2)
 
         def cols(j):
@@ -701,6 +793,8 @@
         return [cols(0)] + [swap(cols(j), j) for j in range(1, count)]
 
     def merge_down(got):
+        if fast:
+            return merge_blocks(got, me)
         return jnp.concatenate(reorder(got, me), axis=0)
 
     def run(tokens, bias_mask, cotangent, tok_blocks=None):
@@ -708,13 +802,20 @@
         if tok_blocks is None:
             tok_blocks = spread(tokens)
         tok_all = jnp.stack(tok_blocks, axis=1)
-        tok_all, cot_first = together(tok_all, cotangent)
-        cot_blocks = spread(cot_first)
         normed, _ = norm_parts(tok_all.astype(F32))
         h_one = (normed * g_one + s_one).astype(BF)
         product = jnp.einsum("ijld,de->ijle", h_one, w_wide, preferred_element_type=F32)
         qkv = (product * factor + bias_wide + bias_mask[..., None] * at_mask).astype(BF)
-        qkv, cot_blocks = together(qkv, cot_blocks)
+        if fast:
+            qkv, cot_across, down_parts, turned = together(
+                qkv, cot_begun[2], down_exchanged, w_turned
+            )
+            cot_blocks = [cotangent, swap(cot_begun[0], 1), cot_across, swap(cot_across, 1)]
+        else:
+            cot_blocks = spread(cotangent)
+            down_parts, turned = down_exchanged, w_turned
+        output_parts = spread(output_cols)
+        up_turned = up_mat.T
         cot_all = jnp.stack(cot_blocks, axis=1)
 
         kept_attend, kept_middle = (), ()
@@ -724,18 +825,23 @@
             mixed_chunks.append(spread(mixed))
         query_wide, mixed_exact = kept_attend
         mixed_exact, down_in, output_in = together(mixed_exact, down_parts, output_parts)
-        down_mat = jnp.concatenate(reorder(down_in, me), axis=2).reshape(-1, width)
-        output_mat = jnp.concatenate(reorder(output_in, me), axis=1)
-        output_mat = output_mat.reshape(count, own, width)
+        if fast:
+            down_mat, down_turned, output_mat = build_weights(down_in, output_in, me)
+        else:
+            down_turned = jnp.stack(reorder(down_in, me)).transpose(0, 2, 1, 3)
+            down_turned = down_turned.reshape(width, -1)
+            down_mat = down_turned.T
+            output_mat = jnp.concatenate(reorder(output_in, me), axis=0).T
+            output_mat = output_mat.reshape(count, own, width)
         own_rows = lax.dynamic_index_in_dim(output_mat, me, 0, keepdims=False)
         output_wide = mm(own_rows.T, expand).astype(BF)
         weights = (
             me,
             output_mat,
             up_mat,
-            up_mat.T,
+            up_turned,
             down_mat,
-            down_mat.T,
+            down_turned,
             b_out,
             g_two,
             s_two,
@@ -795,7 +901,13 @@
             preferred_element_type=F32,
         ).astype(BF if single else F32)
         grad_residual.append(residual)
-        attn_blocks, down_grad = together(spread(grad_attn), down_grad)
+        if fast:
+            across = swap(grad_attn, 2)
+            near = swap(grad_attn, 1)
+            across, down_grad = together(across, down_grad)
+            attn_blocks = [grad_attn, near, across, swap(across, 1)]
+        else:
+            attn_blocks = spread(grad_attn)
         grad_attn_all = jnp.stack(attn_blocks, axis=1)
         grad_mixed = mixed_back(grad_attn_all, output_wide, mixed_exact, 0, ())
 
@@ -834,7 +946,7 @@
         output_grad = jnp.einsum(
             "ijle,ijld->ed", mixed_all, grad_attn_cols, preferred_element_type=F32
         )
-        result = project_back(grads, tok_all, w_turned, g_one, s_one, expand.T)
+        result = project_back(grads, tok_all, turned, g_one, s_one, expand.T)
         qkv_grad, late, bias_grads = result[count:]
         grad_norm_one = collect(list(result[:count])).astype(F32)
 

time: 685 us -> 618 us (0.902)
  local copies, waits for them, and re-layouts: 125 us -> 54.9 us
  Pallas kernels: 194 us -> 213 us
  other arithmetic: 72.7 us -> 62 us
  starting transfers between devices: 47.7 us -> 38.5 us
    reduce_scatter x1, waiting for transfers between devices: 0.01 us -> 20.4 us  [scatter_up(): return lax.psum_scatter(blocks, 'fsdp', scatter_dimension=0)]
    ppermute x36, waiting for transfers between devices: 124 us -> 104 us  [swap(): return lax.ppermute(value, 'seq', [(i, i ^ bit) for i in range(count)])]
    pallas_call x0 -> x4, Pallas kernels: none -> 18.2 us  [glue(): pl.pallas_call(kernel, grid_spec=pltpu.PrefetchScalarGridSpec(num_scalar_...]
    dynamic_slice x5 -> x0, local copies, waits for them, and re-layouts: 14.6 us -> none  [the longest x4 13.1 us: cols(): return lax.dynamic_slice_in_dim(shaped, (me ^ j) * own, own, 1)]
    reshape x4 -> x0, local copies, waits for them, and re-layouts: 13.6 us -> none  [the longest x2 8.79 us: run(): down_mat = jnp.concatenate(reorder(down_in, me), axis=2).reshape(-1, width)]
    optimization_barrier x7 -> x1, local copies, waits for them, and re-layouts: 18.3 us -> 5.2 us  [together(): return lax.optimization_barrier(values)]
    concatenate x2 -> x0, local copies, waits for them, and re-layouts: 10.6 us -> none  [the longest x1 5.97 us: run(): output_mat = jnp.concatenate(reorder(output_in, me), axis=1)]
    select_n x7 -> x4, other arithmetic: 9.74 us -> 1.83 us  [reorder(): jnp.where(odd, blocks[j ^ bit], blocks[j])]
  transfers between devices with their start and end apart: 57 -> 57, of which waited for: 20 -> 18; matrix products, arithmetic and copies ran while one was open for 31% -> 23% of each run, Pallas kernels for 21% -> 26%
where the time goes in v5:
time: 618 us; the launch traced here: 608 us
  Pallas kernels  213 us (34%)
  waiting for transfers between devices  183 us (30%)
  other arithmetic  62 us (10%)
  local copies, waits for them, and re-layouts  54.9 us (9%)
  matrix products  41.7 us (7%)
  starting transfers between devices  38.5 us (6%)
  between operations  15 us (2%)
    ppermute x36, waiting for transfers between devices, swap(): return lax.ppermute(value, 'seq', [(i, i ^ bit) for i in range(count)])  104 us
    ppermute x14, waiting for transfers between devices, ring_shift(): lax.ppermute(value, 'fsdp', [(order[i], order[(i + step) % count]) for i...  55.9 us
    pallas_call x1, Pallas kernels, middle(): pl.pallas_call(kernel, grid_spec=pltpu.PrefetchScalarGridSpec(num_scalar_...  55.3 us
    pallas_call x2, Pallas kernels, attend_back(): pl.pallas_call(kernel, grid=(images, heads, steps), in_specs=[row_in, row...  51.5 us
    pallas_call x1, Pallas kernels, attend(): pl.pallas_call(kernel, grid=(images, count), in_specs=[part, pl.BlockSpec...  40 us
    pallas_call x1, Pallas kernels, project_back(): pl.pallas_call(kernel, grid=(images, count), in_specs=[piece_spec] * len(...  30 us
    reduce_scatter x1, waiting for transfers between devices, scatter_up(): return lax.psum_scatter(blocks, 'fsdp', scatter_dimension=0)  20.4 us
    ppermute x36, starting transfers between devices, swap(): return lax.ppermute(value, 'seq', [(i, i ^ bit) for i in range(count)])  19.5 us
  transfers between devices with their start and end apart: 57, of which 18 were waited for; matrix products, arithmetic and copies ran while one was open for 23% of the time, Pallas kernels for 26%

profile of v5, /device:TPU:0, one launch (start us, length us, event | category | flops | bytes accessed | tf_op | source)
XLA Modules:
  0.0 607.5 jit_solution(10911219441162277859)
XLA Ops:
  16.5 5.7 collective-permute-done.2.refs_1_
  25.5 10.8 %collective-permute-done.4.refs_3_ = bf16[144,864]{1,0:T(8,128)(2,1)S(1)} collective-permute-done((bf16[144,864]{1,0:T(8,128)(2,1)S(1)}, bf16[144,864]{1,0:T(8,128)(2,1)S(1)}, u32[]{:S(2)}, u32[]{:S(2)}) %collective-permute-start.4) | collective-permute-done | bytes 248864 | tf_op jit(solution)/shard_map/ppermute | solution.py:116
  36.3 6.7 %collective-permute-done.5.refs_4_ = bf16[144,864]{1,0:T(8,128)(2,1)S(1)} collective-permute-done((bf16[144,864]{1,0:T(8,128)(2,1)S(1)}, bf16[144,864]{1,0:T(8,128)(2,1)S(1)}, u32[]{:S(2)}, u32[]{:S(2)}) %collective-permute-start.5) | collective-permute-done | bytes 248864 | tf_op jit(solution)/shard_map/ppermute | solution.py:116
  45.7 4.2 concatenate.83
  52.0 13.3 %collective-permute-done.8.refs_7_ = bf16[144,864]{1,0:T(8,128)(2,1)S(1)} collective-permute-done((bf16[144,864]{1,0:T(8,128)(2,1)S(1)}, bf16[144,864]{1,0:T(8,128)(2,1)S(1)}, u32[]{:S(2)}, u32[]{:S(2)}) %collective-permute-start.8) | collective-permute-done | bytes 248864 | tf_op jit(solution)/shard_map/ppermute | solution.py:116
  74.1 8.9 %place_wide.1 = bf16[1152,1536]{1,0:T(8,128)(2,1)} custom-call(s32[8]{0:T(128)} %stack.101.index_ref, bf16[144,864]{1,0:T(8,128)(2,1)} %copy-done.21, bf16[144,864]{1,0:T(8,128)(2,1)} %copy-done.36, bf16[144,864]{1,0:T(8,128)(2,1)} %copy-done.37, bf16[144,864]{1,0:T(8,128)(2,1)} %copy-done.38, bf16[144,864]{1,0:T(8,128)(2,1)} %copy-done.39, ...), custom_call_target="tpu_custom_call" | custom-call | flops 23887872 | bytes 62208 | tf_op jit(solution)/shard_map/place_wide/pallas_call | solution.py:160
  83.0 5.9 copy.83
  94.0 4.3 cut_lower.1
  100.2 12.0 %fusion.22.q_ref = bf16[1,4,512,1536]{3,2,1,0:T(8,128)(2,1)} fusion(f32[1536]{0:T(1024)} %constant.277.clone, f32[4,512]{1,0:T(4,128)} %compare_select_fusion, f32[1536]{0:T(1024)} %fusion.56, f32[1536]{0:T(1024)} %constant.275.clone, bf16[1,512,1152]{2,1,0:T(8,128)(2,1)} %collective-permute-done.9, bf16[1,512,1152]{2,1,0:T(8,128)(2,1)} %collective-permute-done.1, ...), kind=kOutput, calls=%fused_computation.32 | convolution fusion | flops 7284719616 | bytes 14601216 | tf_op jit(solution)/shard_map/ijld,de->ijle/dot_general | solution.py:807
  112.2 5.7 collective-permute-done.15.refs_2_
  118.0 15.0 %collective-permute-done.16.refs_3_ = bf16[2,288,538]{2,1,0:T(8,128)(2,1)} collective-permute-done((bf16[2,288,538]{2,1,0:T(8,128)(2,1)}, bf16[2,288,538]{2,1,0:T(8,128)(2,1)}, u32[]{:S(2)}, u32[]{:S(2)}) %collective-permute-start.16) | collective-permute-done | bytes 619808 | tf_op jit(solution)/shard_map/ppermute | solution.py:44
  133.0 40.0 %attend.1 = (bf16[1,4,288,512]{3,2,1,0:T(8,128)(2,1)}, bf16[1,4,512,512]{3,2,1,0:T(8,128)(2,1)}, f32[1,4,512,512]{3,2,1,0:T(8,128)}) custom-call(bf16[1,4,512,1536]{3,2,1,0:T(8,128)(2,1)} %fusion.22.q_ref, bf16[1,2048,1536]{2,1,0:T(8,128)(2,1)} %bitcast.132), custom_call_target="tpu_custom_call" | custom-call | flops 134217728 | bytes 147456 | tf_op jit(solution)/shard_map/attend/pallas_call | solution.py:375
  175.6 40.4 %collective-permute-done.23.refs_6_ = bf16[288,1152]{1,0:T(8,128)(2,1)} collective-permute-done((bf16[288,1152]{1,0:T(8,128)(2,1)S(1)}, bf16[288,1152]{1,0:T(8,128)(2,1)}, u32[]{:S(2)}, u32[]{:S(2)}) %collective-permute-start.23) | collective-permute-done | bytes 663584 | tf_op jit(solution)/shard_map/ppermute | solution.py:44
  218.6 5.2 copy.84
  223.8 6.4 %build_weights.1 = (bf16[1076,1152]{1,0:T(8,128)(2,1)}, bf16[1152,1076]{1,0:T(8,128)(2,1)}, bf16[4,288,1152]{2,1,0:T(8,128)(2,1)}) custom-call(s32[1]{0:T(128)} %bitcast.me_ref, bf16[2,288,538]{2,1,0:T(8,128)(2,1)} %get-tuple-element.168.refs_0_, bf16[2,288,538]{2,1,0:T(8,128)(2,1)} %copy-done.22, bf16[2,288,538]{2,1,0:T(8,128)(2,1)} %collective-permute-done.15.refs_2_, ...), custom_call_target="tpu_custom_call" | custom-call | bytes 160416 | tf_op jit(solution)/shard_map/build_weights/pallas_call | solution.py:247
  234.4 55.3 %middle.1 = (bf16[1,4,512,1152]{3,2,1,0:T(8,128)(2,1)}, bf16[1,4,512,1076]{3,2,1,0:T(8,128)(2,1)}, bf16[1,4,512,1076]{3,2,1,0:T(8,128)(2,1)}, bf16[1,4,512,1152]...) custom-call(s32[1]{0:T(128)} %bitcast.me_ref, ...), custom_call_target="tpu_custom_call" | custom-call | flops 402259968 | bytes 846496 | tf_op jit(solution)/shard_map/middle/pallas_call | solution.py:475
  296.1 9.9 %fusion.2 = bf16[1152,1076]{0,1:T(8,128)(2,1)} fusion(bf16[1,4,512,1076]{3,2,1,0:T(8,128)(2,1)} %get-tuple-element.187, bf16[1,4,512,1152]{3,2,1,0:T(8,128)(2,1)S(1)} %copy-done.77), kind=kOutput, calls=%fused_computation.8 | convolution fusion | flops 5078444544 | bytes 11604992 | tf_op jit(solution)/shard_map/ijld,ijlf->df/dot_general | solution.py:885
  306.1 17.9 %collective-permute-done.27 = bf16[1,512,1152]{2,1,0:T(8,128)(2,1)S(1)} collective-permute-done((bf16[1,512,1152]{2,1,0:T(8,128)(2,1)S(1)}, bf16[1,512,1152]{2,1,0:T(8,128)(2,1)S(1)}, u32[]{:S(2)}, u32[]{:S(2)}) %collective-permute-start.27) | collective-permute-done | bytes 1179680 | tf_op jit(solution)/shard_map/ppermute | solution.py:44
  327.3 4.6 convert_reduce_fusion.3
  332.4 5.2 copy.88
  337.9 11.7 %fusion.3.in_ref = bf16[1152,1076]{1,0:T(8,128)(2,1)} fusion(bf16[1,4,512,1076]{3,2,1,0:T(8,128)(2,1)} %get-tuple-element.191, bf16[1,1,512,1152]{3,2,1,0:T(8,128)(2,1)} %bitcast.25, bf16[1,1,512,1152]{3,2,1,0:T(8,128)(2,1)} %bitcast.151, bf16[1,1,512,1152]{3,2,1,0:T(8,128)(2,1)} %bitcast.23, bf16[1,1,512,1152]{3,2,1,0:T(8,128)(2,1)} %bitcast.145), kind=kOutput, calls=%fused_computation.9 | convolution fusion | flops 5085522432 | bytes 11604992 | tf_op jit(solution)/shard_map/ijld,ijlf->df/dot_general | solution.py:897
  349.5 10.2 %collective-permute-done.29 = bf16[1,512,1152]{2,1,0:T(8,128)(2,1)} collective-permute-done((bf16[1,512,1152]{2,1,0:T(8,128)(2,1)}, bf16[1,512,1152]{2,1,0:T(8,128)(2,1)}, u32[]{:S(2)}, u32[]{:S(2)}) %collective-permute-start.29) | collective-permute-done | bytes 1179680 | tf_op jit(solution)/shard_map/ppermute | solution.py:44
  363.5 4.6 pad_maximum_fusion.2.grad_ref
  368.1 8.5 %mixed_back.1 = bf16[1,4,512,512]{3,2,1,0:T(8,128)(2,1)} custom-call(bf16[1,4,512,1152]{3,2,1,0:T(8,128)(2,1)} %pad_maximum_fusion.2.grad_ref, bf16[1152,512]{1,0:T(8,128)(2,1)} %convolution_convert_fusion.w_ref, f32[1,4,512,512]{3,2,1,0:T(8,128)} %get-tuple-element.193.exact_ref), custom_call_target="tpu_custom_call" | custom-call | flops 18874368 | bytes 190464 | tf_op jit(solution)/shard_map/mixed_back/pallas_call | solution.py:531
  393.6 20.4 %reduce-scatter.3.cloned.1.call-done = bf16[1,144,1076]{2,1,0:T(8,128)(2,1)} async-done(((bf16[8,144,1076]{2,1,0:T(8,128)(2,1)}), bf16[1,144,1076]{2,1,0:T(8,128)(2,1)}) %reduce-scatter.3.cloned.1.call-update) | async-done | bytes 309904 | tf_op jit(solution)/shard_map/reduce_scatter | solution.py:782
  417.9 25.7 %attend_back.2 = (bf16[1,2048,256]{2,1,0:T(8,128)(2,1)}, bf16[1,2048,256]{2,1,0:T(8,128)(2,1)}, bf16[1,2048,256]{2,1,0:T(8,128)(2,1)}) custom-call(bf16[1,2048,512]{2,1,0:T(8,128)(2,1)} %bitcast.143, bf16[1,2048,512]{2,1,0:T(8,128)(2,1)} %bitcast.138, bf16[1,2048,1536]{2,1,0:T(8,128)(2,1)} %bitcast.133, bf16[1,2048,1536]{2,1,0:T(8,128)(2,1)} %bitcast.134), custom_call_target="tpu_custom_call" | custom-call | flops 167772160 | bytes 229376 | tf_op jit(solution)/shard_map/attend_back/pallas_call | solution.py:593
  447.2 5.0 fusion.31
  460.1 25.8 %attend_back.3 = (bf16[1,2048,256]{2,1,0:T(8,128)(2,1)}, bf16[1,2048,256]{2,1,0:T(8,128)(2,1)}, bf16[1,2048,256]{2,1,0:T(8,128)(2,1)}) custom-call(bf16[1,2048,512]{2,1,0:T(8,128)(2,1)} %bitcast.144, bf16[1,2048,512]{2,1,0:T(8,128)(2,1)} %bitcast.139, bf16[1,2048,1536]{2,1,0:T(8,128)(2,1)} %bitcast.135, bf16[1,2048,1536]{2,1,0:T(8,128)(2,1)} %bitcast.136), custom_call_target="tpu_custom_call" | custom-call | flops 167772160 | bytes 229376 | tf_op jit(solution)/shard_map/attend_back/pallas_call | solution.py:593
  485.9 30.0 %project_back.1 = (bf16[1,512,1152]{2,1,0:T(8,128)(2,1)}, bf16[1,512,1152]{2,1,0:T(8,128)(2,1)}, bf16[1,512,1152]{2,1,0:T(8,128)(2,1)}, bf16[1,512,1152]{2,1,0:T...) custom-call(bf16[1,4,512,256]{3,2,1,0:T(8,128)(2,1)} %bitcast.152, ...), custom_call_target="tpu_custom_call" | custom-call | flops 113246208 | bytes 301056 | tf_op jit(solution)/shard_map/project_back/pallas_call | solution.py:668
  546.4 5.6 collective-permute-done.41
  556.9 14.2 %collective-permute-done.39 = bf16[1,512,1152]{2,1,0:T(8,128)(2,1)S(1)} collective-permute-done((bf16[1,512,1152]{2,1,0:T(8,128)(2,1)S(1)}, bf16[1,512,1152]{2,1,0:T(8,128)(2,1)S(1)}, u32[]{:S(2)}, u32[]{:S(2)}) %collective-permute-start.39) | collective-permute-done | bytes 1179680 | tf_op jit(solution)/shard_map/ppermute | solution.py:44
  578.4 7.8 %collective-permute-done.48 = bf16[4,144,288]{2,1,0:T(8,128)(2,1)S(1)} collective-permute-done((bf16[4,144,288]{2,1,0:T(8,128)(2,1)S(1)}, bf16[4,144,288]{2,1,0:T(8,128)(2,1)S(1)}, u32[]{:S(2)}, u32[]{:S(2)}) %collective-permute-start.48) | collective-permute-done | bytes 331808 | tf_op jit(solution)/shard_map/ppermute | solution.py:116
  (367 shorter events, 145.8 us)
Async XLA Ops:
  7.2 86.8 %all-gather.6.cloned.1.call-start = ((), (), s32[]{:S(2)}) async-start(), calls=%async_computation.5 | async-start | bytes 3981312 | tf_op jit(solution)/shard_map/all_gather | solution.py:736
  10.2 208.4 %all-gather.4.cloned.1.call-start = ((), (), s32[]{:S(2)}) async-start(), calls=%async_computation.2 | async-start | bytes 2985984 | tf_op jit(solution)/shard_map/all_gather | solution.py:745
  10.3 41.7 %collective-permute-start.1 = (bf16[1,512,1152]{2,1,0:T(8,128)(2,1)}, bf16[1,512,1152]{2,1,0:T(8,128)(2,1)}, u32[]{:S(2)}, u32[]{:S(2)}) collective-permute-start(bf16[1,512,1152]{2,1,0:T(8,128)(2,1)} %param.21), channel_id=1, source_target_pairs={{0,16},{8,24},{16,0},{24,8},{1,17},{9,25},{17,1},{25,9},{2,18},{10... | collective-permute-start | bytes 3538952 | tf_op jit(solution)/shard_map/ppermute | solution.py:44
  25.1 17.9 %collective-permute-start.5 = (bf16[144,864]{1,0:T(8,128)(2,1)S(1)}, bf16[144,864]{1,0:T(8,128)(2,1)S(1)}, u32[]{:S(2)}, u32[]{:S(2)}) collective-permute-start(bf16[144,864]{1,0:T(8,128)(2,1)S(1)} %collective-permute-done.3.refs_2_), channel_id=1, source_target_pairs={{0,1},{2,0},{4,2},{6,4},{7,6},{5,7},{3,5},{1,3},{8,9},{10,8},{12,1... | collective-permute-start | bytes 746504 | tf_op jit(solution)/shard_map/ppermute | solution.py:116
  44.9 43.9 %collective-permute-start = (bf16[1,512,1152]{2,1,0:T(8,128)(2,1)}, bf16[1,512,1152]{2,1,0:T(8,128)(2,1)}, u32[]{:S(2)}, u32[]{:S(2)}) collective-permute-start(bf16[1,512,1152]{2,1,0:T(8,128)(2,1)} %param.21), channel_id=1, source_target_pairs={{0,8},{8,0},{16,24},{24,16},{1,9},{9,1},{17,25},{25,17},{2,10},{10... | collective-permute-start | bytes 3538952 | tf_op jit(solution)/shard_map/ppermute | solution.py:44
  49.9 19.5 %collective-permute-start.10 = (bf16[2240]{0:T(1024)(128)(2,1)S(1)}, bf16[2240]{0:T(1024)(128)(2,1)S(1)}, u32[]{:S(2)}, u32[]{:S(2)}) collective-permute-start(bf16[2240]{0:T(1024)(128)(2,1)S(1)} %concatenate.83), channel_id=1, source_target_pairs={{0,16},{8,24},{16,0},{24,8},{1,17},{9,25},{17,1},{25,9},{2,18},{10... | collective-permute-start | bytes 13448 | tf_op jit(solution)/shard_map/ppermute | solution.py:44
  50.5 363.4 %reduce-scatter.3.cloned.1.call-start = ((), (), s32[]{:S(2)}) async-start(), calls=%async_computation.3 | async-start | bytes 2985984 | tf_op jit(solution)/shard_map/reduce_scatter | solution.py:782
  50.8 20.0 %collective-permute-start.12 = (bf16[2240]{0:T(1024)(128)(2,1)S(1)}, bf16[2240]{0:T(1024)(128)(2,1)S(1)}, u32[]{:S(2)}, u32[]{:S(2)}) collective-permute-start(bf16[2240]{0:T(1024)(128)(2,1)S(1)} %concatenate.83), channel_id=1, source_target_pairs={{0,8},{8,0},{16,24},{24,16},{1,9},{9,1},{17,25},{25,17},{2,10},{10... | collective-permute-start | bytes 13448 | tf_op jit(solution)/shard_map/ppermute | solution.py:44
  66.1 22.8 %collective-permute-start.9 = (bf16[1,512,1152]{2,1,0:T(8,128)(2,1)}, bf16[1,512,1152]{2,1,0:T(8,128)(2,1)}, u32[]{:S(2)}, u32[]{:S(2)}) collective-permute-start(bf16[1,512,1152]{2,1,0:T(8,128)(2,1)} %collective-permute-done.1), channel_id=1, source_target_pairs={{0,8},{8,0},{16,24},{24,16},{1,9},{9,1},{17,25},{25,17},{2,10},{10... | collective-permute-start | bytes 3538952 | tf_op jit(solution)/shard_map/ppermute | solution.py:44
  72.6 39.6 %collective-permute-start.13 = (bf16[1,512,1152]{2,1,0:T(8,128)(2,1)S(1)}, bf16[1,512,1152]{2,1,0:T(8,128)(2,1)S(1)}, u32[]{:S(2)}, u32[]{:S(2)}) collective-permute-start(bf16[1,512,1152]{2,1,0:T(8,128)(2,1)S(1)} %copy-done.5), channel_id=1, source_target_pairs={{0,16},{8,24},{16,0},{24,8},{1,17},{9,25},{17,1},{25,9},{2,18},{10... | collective-permute-start | bytes 3538952 | tf_op jit(solution)/shard_map/ppermute | solution.py:44
  98.4 19.6 %collective-permute-start.15 = (bf16[2,288,538]{2,1,0:T(8,128)(2,1)}, bf16[2,288,538]{2,1,0:T(8,128)(2,1)}, u32[]{:S(2)}, u32[]{:S(2)}) collective-permute-start(bf16[2,288,538]{2,1,0:T(8,128)(2,1)} %get-tuple-element.156), channel_id=1, source_target_pairs={{0,16},{8,24},{16,0},{24,8},{1,17},{9,25},{17,1},{25,9},{2,18},{10... | collective-permute-start | bytes 1859336 | tf_op jit(solution)/shard_map/ppermute | solution.py:44
  98.9 34.1 %collective-permute-start.16 = (bf16[2,288,538]{2,1,0:T(8,128)(2,1)}, bf16[2,288,538]{2,1,0:T(8,128)(2,1)}, u32[]{:S(2)}, u32[]{:S(2)}) collective-permute-start(bf16[2,288,538]{2,1,0:T(8,128)(2,1)} %get-tuple-element.157), channel_id=1, source_target_pairs={{0,24},{8,16},{16,8},{24,0},{1,25},{9,17},{17,9},{25,1},{2,26},{10... | collective-permute-start | bytes 1859336 | tf_op jit(solution)/shard_map/ppermute | solution.py:44
  173.0 45.0 %collective-permute-start.18 = (bf16[1,4,288,512]{3,2,1,0:T(8,128)(2,1)}, bf16[1,4,288,512]{3,2,1,0:T(8,128)(2,1)}, u32[]{:S(2)}, u32[]{:S(2)}) collective-permute-start(bf16[1,4,288,512]{3,2,1,0:T(8,128)(2,1)} %get-tuple-element.159.refs_0_), channel_id=1, source_target_pairs={{0,16},{8,24},{16,0},{24,8},{1,17},{9,25},{17,1},{25,9},{2,18},{10... | collective-permute-start | bytes 3538952 | tf_op jit(solution)/shard_map/ppermute | solution.py:44
  173.7 42.4 %collective-permute-start.23 = (bf16[288,1152]{1,0:T(8,128)(2,1)S(1)}, bf16[288,1152]{1,0:T(8,128)(2,1)}, u32[]{:S(2)}, u32[]{:S(2)}) collective-permute-start(bf16[288,1152]{1,0:T(8,128)(2,1)S(1)} %copy-done.23), channel_id=1, source_target_pairs={{0,16},{8,24},{16,0},{24,8},{1,17},{9,25},{17,1},{25,9},{2,18},{10... | collective-permute-start | bytes 1990664 | tf_op jit(solution)/shard_map/ppermute | solution.py:44
  175.1 55.1 %collective-permute-start.20 = (bf16[1,512,1152]{2,1,0:T(8,128)(2,1)S(1)}, bf16[1,512,1152]{2,1,0:T(8,128)(2,1)}, u32[]{:S(2)}, u32[]{:S(2)}) collective-permute-start(bf16[1,512,1152]{2,1,0:T(8,128)(2,1)S(1)} %copy-done.5), channel_id=1, source_target_pairs={{0,8},{8,0},{16,24},{24,16},{1,9},{9,1},{17,25},{25,17},{2,10},{10... | collective-permute-start | bytes 3538952 | tf_op jit(solution)/shard_map/ppermute | solution.py:44
  175.1 55.1 %collective-permute-start.21 = (bf16[1,512,1152]{2,1,0:T(8,128)(2,1)S(1)}, bf16[1,512,1152]{2,1,0:T(8,128)(2,1)}, u32[]{:S(2)}, u32[]{:S(2)}) collective-permute-start(bf16[1,512,1152]{2,1,0:T(8,128)(2,1)S(1)} %collective-permute-done.13), channel_id=1, source_target_pairs={{0,8},{8,0},{16,24},{24,16},{1,9},{9,1},{17,25},{25,17},{2,10},{10... | collective-permute-start | bytes 3538952 | tf_op jit(solution)/shard_map/ppermute | solution.py:44
  175.6 41.0 %collective-permute-start.22 = (bf16[288,1152]{1,0:T(8,128)(2,1)S(1)}, bf16[288,1152]{1,0:T(8,128)(2,1)S(1)}, u32[]{:S(2)}, u32[]{:S(2)}) collective-permute-start(bf16[288,1152]{1,0:T(8,128)(2,1)S(1)} %copy-done.23), channel_id=1, source_target_pairs={{0,8},{8,0},{16,24},{24,16},{1,9},{9,1},{17,25},{25,17},{2,10},{10... | collective-permute-start | bytes 1990664 | tf_op jit(solution)/shard_map/ppermute | solution.py:44
  217.5 16.9 %collective-permute-start.17 = (bf16[1,4,288,512]{3,2,1,0:T(8,128)(2,1)}, bf16[1,4,288,512]{3,2,1,0:T(8,128)(2,1)}, u32[]{:S(2)}, u32[]{:S(2)}) collective-permute-start(bf16[1,4,288,512]{3,2,1,0:T(8,128)(2,1)} %get-tuple-element.159.refs_0_), channel_id=1, source_target_pairs={{0,8},{8,0},{16,24},{24,16},{1,9},{9,1},{17,25},{25,17},{2,10},{10... | collective-permute-start | bytes 3538952 | tf_op jit(solution)/shard_map/ppermute | solution.py:44
  218.0 16.4 %collective-permute-start.19 = (bf16[1,4,288,512]{3,2,1,0:T(8,128)(2,1)}, bf16[1,4,288,512]{3,2,1,0:T(8,128)(2,1)}, u32[]{:S(2)}, u32[]{:S(2)}) collective-permute-start(bf16[1,4,288,512]{3,2,1,0:T(8,128)(2,1)} %collective-permute-done.18.refs_2_), channel_id=1, source_target_pairs={{0,8},{8,0},{16,24},{24,16},{1,9},{9,1},{17,25},{25,17},{2,10},{10... | collective-permute-start | bytes 3538952 | tf_op jit(solution)/shard_map/ppermute | solution.py:44
  290.2 33.8 %collective-permute-start.25 = (bf16[1,512,1152]{2,1,0:T(8,128)(2,1)}, bf16[1,512,1152]{2,1,0:T(8,128)(2,1)}, u32[]{:S(2)}, u32[]{:S(2)}) collective-permute-start(bf16[1,512,1152]{2,1,0:T(8,128)(2,1)} %get-tuple-element.181), channel_id=1, source_target_pairs={{0,8},{8,0},{16,24},{24,16},{1,9},{9,1},{17,25},{25,17},{2,10},{10... | collective-permute-start | bytes 3538952 | tf_op jit(solution)/shard_map/ppermute | solution.py:44
  295.6 28.4 %collective-permute-start.27 = (bf16[1,512,1152]{2,1,0:T(8,128)(2,1)S(1)}, bf16[1,512,1152]{2,1,0:T(8,128)(2,1)S(1)}, u32[]{:S(2)}, u32[]{:S(2)}) collective-permute-start(bf16[1,512,1152]{2,1,0:T(8,128)(2,1)S(1)} %add_convert_fusion.8), channel_id=1, source_target_pairs={{0,16},{8,24},{16,0},{24,8},{1,17},{9,25},{17,1},{25,9},{2,18},{10... | collective-permute-start | bytes 3538952 | tf_op jit(solution)/shard_map/ppermute | solution.py:44
  331.8 27.8 %collective-permute-start.29 = (bf16[1,512,1152]{2,1,0:T(8,128)(2,1)}, bf16[1,512,1152]{2,1,0:T(8,128)(2,1)}, u32[]{:S(2)}, u32[]{:S(2)}) collective-permute-start(bf16[1,512,1152]{2,1,0:T(8,128)(2,1)} %get-tuple-element.190), channel_id=1, source_target_pairs={{0,16},{8,24},{16,0},{24,8},{1,17},{9,25},{17,1},{25,9},{2,18},{10... | collective-permute-start | bytes 3538952 | tf_op jit(solution)/shard_map/ppermute | solution.py:44
  332.4 31.1 %collective-permute-start.28 = (bf16[1,512,1152]{2,1,0:T(8,128)(2,1)}, bf16[1,512,1152]{2,1,0:T(8,128)(2,1)}, u32[]{:S(2)}, u32[]{:S(2)}) collective-permute-start(bf16[1,512,1152]{2,1,0:T(8,128)(2,1)} %get-tuple-element.190), channel_id=1, source_target_pairs={{0,8},{8,0},{16,24},{24,16},{1,9},{9,1},{17,25},{25,17},{2,10},{10... | collective-permute-start | bytes 3538952 | tf_op jit(solution)/shard_map/ppermute | solution.py:44
  337.6 237.2 %reduce-scatter.5.cloned.1.call-start = ((), (), s32[]{:S(2)}) async-start(), calls=%async_computation.4 | async-start | bytes 3317760 | tf_op jit(solution)/shard_map/reduce_scatter | solution.py:980
  389.1 54.4 %collective-permute-start.33 = (bf16[2,288,538]{2,1,0:T(8,128)(2,1)}, bf16[2,288,538]{2,1,0:T(8,128)(2,1)}, u32[]{:S(2)}, u32[]{:S(2)}) collective-permute-start(bf16[2,288,538]{2,1,0:T(8,128)(2,1)} %get-tuple-element.213), channel_id=1, source_target_pairs={{0,8},{8,0},{16,24},{24,16},{1,9},{9,1},{17,25},{25,17},{2,10},{10... | collective-permute-start | bytes 1859336 | tf_op jit(solution)/shard_map/ppermute | solution.py:44
  389.1 54.5 %collective-permute-start.34 = (bf16[2,288,538]{2,1,0:T(8,128)(2,1)}, bf16[2,288,538]{2,1,0:T(8,128)(2,1)}, u32[]{:S(2)}, u32[]{:S(2)}) collective-permute-start(bf16[2,288,538]{2,1,0:T(8,128)(2,1)} %get-tuple-element.214), channel_id=1, source_target_pairs={{0,16},{8,24},{16,0},{24,8},{1,17},{9,25},{17,1},{25,9},{2,18},{10... | collective-permute-start | bytes 1859336 | tf_op jit(solution)/shard_map/ppermute | solution.py:44
  389.6 54.0 %collective-permute-start.35 = (bf16[2,288,538]{2,1,0:T(8,128)(2,1)}, bf16[2,288,538]{2,1,0:T(8,128)(2,1)}, u32[]{:S(2)}, u32[]{:S(2)}) collective-permute-start(bf16[2,288,538]{2,1,0:T(8,128)(2,1)} %get-tuple-element.215), channel_id=1, source_target_pairs={{0,24},{8,16},{16,8},{24,0},{1,25},{9,17},{17,9},{25,1},{2,26},{10... | collective-permute-start | bytes 1859336 | tf_op jit(solution)/shard_map/ppermute | solution.py:44
  413.9 72.0 %collective-permute-start.36 = (bf16[1,512,1152]{2,1,0:T(8,128)(2,1)}, bf16[1,512,1152]{2,1,0:T(8,128)(2,1)}, u32[]{:S(2)}, u32[]{:S(2)}) collective-permute-start(bf16[1,512,1152]{2,1,0:T(8,128)(2,1)} %add_convert_fusion.7), channel_id=1, source_target_pairs={{0,16},{8,24},{16,0},{24,8},{1,17},{9,25},{17,1},{25,9},{2,18},{10... | collective-permute-start | bytes 3538952 | tf_op jit(solution)/shard_map/ppermute | solution.py:44
  516.7 24.0 %collective-permute-start.38 = (bf16[1,512,1152]{2,1,0:T(8,128)(2,1)}, bf16[1,512,1152]{2,1,0:T(8,128)(2,1)}, u32[]{:S(2)}, u32[]{:S(2)}) collective-permute-start(bf16[1,512,1152]{2,1,0:T(8,128)(2,1)} %get-tuple-element.239), channel_id=1, source_target_pairs={{0,8},{8,0},{16,24},{24,16},{1,9},{9,1},{17,25},{25,17},{2,10},{10... | collective-permute-start | bytes 3538952 | tf_op jit(solution)/shard_map/ppermute | solution.py:44
  530.2 23.3 %collective-permute-start.31 = (bf16[1,512,1152]{2,1,0:T(8,128)(2,1)}, bf16[1,512,1152]{2,1,0:T(8,128)(2,1)}, u32[]{:S(2)}, u32[]{:S(2)}) collective-permute-start(bf16[1,512,1152]{2,1,0:T(8,128)(2,1)} %get-tuple-element.200), channel_id=1, source_target_pairs={{0,8},{8,0},{16,24},{24,16},{1,9},{9,1},{17,25},{25,17},{2,10},{10... | collective-permute-start | bytes 3538952 | tf_op jit(solution)/shard_map/ppermute | solution.py:44
  531.5 25.4 %collective-permute-start.37 = (bf16[1,512,1152]{2,1,0:T(8,128)(2,1)}, bf16[1,512,1152]{2,1,0:T(8,128)(2,1)}, u32[]{:S(2)}, u32[]{:S(2)}) collective-permute-start(bf16[1,512,1152]{2,1,0:T(8,128)(2,1)} %get-tuple-element.237), channel_id=1, source_target_pairs={{0,8},{8,0},{16,24},{24,16},{1,9},{9,1},{17,25},{25,17},{2,10},{10... | collective-permute-start | bytes 3538952 | tf_op jit(solution)/shard_map/ppermute | solution.py:44
  544.4 26.8 %collective-permute-start.39 = (bf16[1,512,1152]{2,1,0:T(8,128)(2,1)S(1)}, bf16[1,512,1152]{2,1,0:T(8,128)(2,1)S(1)}, u32[]{:S(2)}, u32[]{:S(2)}) collective-permute-start(bf16[1,512,1152]{2,1,0:T(8,128)(2,1)S(1)} %add_convert_fusion.5), channel_id=1, source_target_pairs={{0,16},{8,24},{16,0},{24,8},{1,17},{9,25},{17,1},{25,9},{2,18},{10... | collective-permute-start | bytes 3538952 | tf_op jit(solution)/shard_map/ppermute | solution.py:44
  (103 other events, 2006.4 us)
Sparse Core Ops, SparseCore 0:
  10.8 76.3 all-gather.5
  89.4 56.3 all-gather.3
  337.7 76.1 reduce-scatter.2
  447.3 70.7 reduce-scatter.4

commit v6 on v5

--- a/solution.py
+++ b/solution.py
@@ -314,6 +314,16 @@
     return glue(kernel, me, [grad], [(group, own, split)] * count, "cut_down")
 
 
+def hold_rows(grad, me, blocks):
+    rows = grad.shape[0] // blocks
+
+    def kernel(me_ref, in_ref, out_ref):
+        for f in range(blocks):
+            out_ref[f] = in_ref[f * rows : (f + 1) * rows]
+
+    return glue(kernel, me, [grad], [(blocks, rows, grad.shape[1])], "hold_rows")[0]
+
+
 def merge_blocks(parts, me):
     count = len(parts)
     group, own, split = parts[0].shape
@@ -327,10 +337,10 @@
     return glue(kernel, me, parts, [(count * group, own, split)], "merge_blocks")[0]
 
 
-def attend(qkv, wide_heads, chunk, kept):
+def attend(qkv, wide_heads, first, heads, kept):
     images, count, length, _ = qkv.shape
-    heads = wide_heads // WIDE
-    rows = length // CHUNKS
+    rows = length
+    half = first // heads
     keys = count * length
     flat = qkv.reshape(images, keys, 3 * wide_heads)
 
@@ -340,14 +350,15 @@
         @pl.when(pl.program_id(1) == 0)
         def _():
             for e in range(heads):
-                at = wide_heads + e * WIDE
+                at = wide_heads + (first + e) * WIDE
                 turned[e] = kv_ref[0, :, at : at + WIDE].T
 
         total = jnp.zeros((rows, heads * HEAD), F32)
         for e in range(heads):
             here = slice(e * WIDE, (e + 1) * WIDE)
             query = q_ref[0, 0, :, here]
-            v = kv_ref[0, :, 2 * wide_heads + e * WIDE : 2 * wide_heads + (e + 1) * WIDE]
+            at = 2 * wide_heads + (first + e) * WIDE
+            v = kv_ref[0, :, at : at + WIDE]
             scores = mm(query, turned[e])
             top = jnp.max(scores, axis=-1, keepdims=True)
             weights = jnp.exp2(scores - top).astype(BF)
@@ -363,7 +374,7 @@
             total = total + mm(mixed.astype(BF), pick)
         mixed_ref[0, 0] = total.T.astype(BF)
 
-    part = pl.BlockSpec((1, 1, rows, wide_heads), lambda i, b: (i, b, chunk, 0))
+    part = pl.BlockSpec((1, 1, rows, heads * WIDE), lambda i, b: (i, b, 0, half))
     shapes = [
         jax.ShapeDtypeStruct((images, count, heads * HEAD, rows), BF),
         jax.ShapeDtypeStruct((images, count, length, wide_heads), BF),
@@ -391,11 +402,13 @@
     images, count, length, width = tokens.shape
     me, w_output, w_up, up_turned, w_down, down_turned, b_output, gain, shift, b_up = weights
     rows = length // CHUNKS
-    own = mixed[0].shape[-2]
+    halves = len(mixed[0])
+    part_own = mixed[0][0].shape[-2]
+    mixed = [piece for pieces in mixed for piece in pieces]
     hidden_count = w_up.shape[1]
 
     def kernel(me_ref, *refs):
-        mixed_refs = refs[:count]
+        mixed_refs = refs[: count * halves]
         (
             tok_ref,
             cot_ref,
@@ -408,7 +421,7 @@
             g_ref,
             s_ref,
             bu_ref,
-        ) = refs[count : count + 11]
+        ) = refs[count * halves : count * halves + 11]
         outs = refs[-(6 + 2 * count) :]
         h_ref, z_ref, du_ref, cat_ref, x_ref, gb_ref = outs[:6]
         dh_refs, y_refs = outs[6 : 6 + count], outs[6 + count :]
@@ -416,7 +429,8 @@
         x_one = tok_ref[0, 0].astype(F32) + bo_ref[...]
         pieces = []
         for i in range(count):
-            piece = mixed_refs[i][0, 0].T
+            parts = [ref[0, 0] for ref in mixed_refs[i * halves : (i + 1) * halves]]
+            piece = jnp.concatenate(parts, axis=0).T
             pieces.append(piece)
             x_one = x_one + mm(piece, wo_ref[me_ref[0] ^ i])
         cat_ref[0, 0] = jnp.concatenate(pieces, axis=-1)
@@ -460,7 +474,7 @@
             gb_ref[...] += summed
 
     def piece_spec(i):
-        return pl.BlockSpec((1, 1, own, rows), lambda im, b, me_ref: (im, b ^ i, 0, 0))
+        return pl.BlockSpec((1, 1, part_own, rows), lambda im, b, me_ref: (im, b ^ i, 0, 0))
 
     def whole_spec(array):
         return pl.BlockSpec(array.shape, lambda im, b, me_ref: (0,) * array.ndim)
@@ -477,7 +491,7 @@
         grid_spec=pltpu.PrefetchScalarGridSpec(
             num_scalar_prefetch=1,
             grid=(images, count),
-            in_specs=[piece_spec(i) for i in range(count)]
+            in_specs=[piece_spec(i) for i in range(count) for _ in range(halves)]
             + [full, full]
             + [whole_spec(array) for array in constants]
             + [pl.BlockSpec(memory_space=pl.ANY)] * len(extra),
@@ -500,7 +514,7 @@
             jax.ShapeDtypeStruct((1, hidden_count), F32),
         ]
         + [jax.ShapeDtypeStruct((images, rows, width), BF)] * (2 * count),
-        input_output_aliases={1 + count + 11 + i: i for i in range(len(extra))},
+        input_output_aliases={1 + count * halves + 11 + i: i for i in range(len(extra))},
         cost_estimate=cost(
             all_rows * width * (width + 4 * hidden_count) * 2,
             all_rows * (width * 16 + hidden_count * 4) + (w_output.size + 2 * w_up.size) * 2,
@@ -777,8 +791,12 @@
     cot_begun = (cot_sent, None, cot_across) if fast else None
     w_turned = w_wide.T
 
+    def token_grads(tokens, residual, grad_norm):
+        normed, inverse = norm_parts(tokens.astype(F32))
+        return (residual + norm_back(grad_norm, normed, inverse, g_one)).astype(BF)
+
     def scatter_up(up_grad):
-        blocks = up_grad.astype(BF).reshape(fcount, width // fcount, -1)
+        blocks = up_grad if fast else up_grad.astype(BF).reshape(fcount, width // fcount, -1)
         return lax.psum_scatter(blocks, "fsdp", scatter_dimension=0)
 
     def send_down(down_grad):
@@ -807,9 +825,10 @@
         product = jnp.einsum("ijld,de->ijle", h_one, w_wide, preferred_element_type=F32)
         qkv = (product * factor + bias_wide + bias_mask[..., None] * at_mask).astype(BF)
         if fast:
-            qkv, cot_across, down_parts, turned = together(
-                qkv, cot_begun[2], down_exchanged, w_turned
+            qkv, cot_across, down_own, turned = together(
+                qkv, cot_begun[2], down_sent[0], w_turned
             )
+            down_parts = [down_own] + down_exchanged[1:]
             cot_blocks = [cotangent, swap(cot_begun[0], 1), cot_across, swap(cot_across, 1)]
         else:
             cot_blocks = spread(cotangent)
@@ -818,13 +837,20 @@
         up_turned = up_mat.T
         cot_all = jnp.stack(cot_blocks, axis=1)
 
-        kept_attend, kept_middle = (), ()
-        mixed_chunks = []
-        for c in range(CHUNKS):
-            mixed, *kept_attend = attend(qkv, wide_heads, c, kept_attend)
-            mixed_chunks.append(spread(mixed))
+        kept_middle = ()
+        halves = 2 if heads % 2 == 0 else 1
+        step = heads // halves
+        mixed, *kept_attend = attend(qkv, wide_heads, 0, step, ())
+        mixed_blocks = [[block] for block in spread(mixed)]
+        if halves == 2:
+            kept_attend, down_parts, output_parts = together(
+                kept_attend, down_parts, output_parts
+            )
+            mixed, *kept_attend = attend(qkv, wide_heads, step, step, kept_attend)
+            for pieces, block in zip(mixed_blocks, spread(mixed)):
+                pieces.append(block)
         query_wide, mixed_exact = kept_attend
-        mixed_exact, down_in, output_in = together(mixed_exact, down_parts, output_parts)
+        down_in, output_in = down_parts, output_parts
         if fast:
             down_mat, down_turned, output_mat = build_weights(down_in, output_in, me)
         else:
@@ -868,7 +894,7 @@
         hidden_parts = []
         early, up_bias_grad = 0.0, 0.0
         for c in range(CHUNKS):
-            result = middle(mixed_chunks[c], tok_all, cot_all, weights, c, kept_middle)
+            result = middle(mixed_blocks, tok_all, cot_all, weights, c, kept_middle)
             kept_middle, x_own, gb = result[:4], result[4], result[5]
             hidden_parts.append(list(result[6 : 6 + count]))
             out_parts.append(result[6 + count :])
@@ -888,6 +914,8 @@
             grad_hidden,
             preferred_element_type=F32,
         ).astype(BF if single else F32)
+        if fast:
+            up_grad = hold_rows(up_grad, me, fcount)
         incoming, up_grad = together(incoming, up_grad)
         if single:
             up_grad = scatter_up(up_grad)
@@ -915,8 +943,6 @@
         query_in = query_wide.reshape(wide_shape)
         grad_in = grad_mixed.reshape(wide_shape)
         flat_qkv = qkv.reshape(images, count * length, 3 * wide_heads)
-        halves = 2 if heads % 2 == 0 else 1
-        step = heads // halves
         grad_in, out_blocks, down_grad = together(grad_in, list(out_parts[0]), down_grad)
         if single:
             down_grad = send_down(down_grad)
@@ -948,20 +974,20 @@
         )
         result = project_back(grads, tok_all, turned, g_one, s_one, expand.T)
         qkv_grad, late, bias_grads = result[count:]
-        grad_norm_one = collect(list(result[:count])).astype(F32)
+        if fast:
+            norm_near, norm_across = collect_pair(list(result[:count]))
+            ends = (grad_residual[0], norm_near, swap(norm_across, 2))
+        else:
+            grad_norm = collect(list(result[:count])).astype(F32)
+            ends = token_grads(tokens, grad_residual[0], grad_norm)
 
         layer_out = (jnp.concatenate(x_parts, axis=1) + out_sum.astype(F32) + b_dn).astype(BF)
-        normed_one, inverse_one = norm_parts(tokens.astype(F32))
-        grad_tokens = (
-            jnp.concatenate(grad_residual, axis=1)
-            + norm_back(grad_norm_one, normed_one, inverse_one, g_one)
-        ).astype(BF)
         qkv_grad = qkv_grad if single else qkv_grad.astype(F32)
         sums = (down_grad, up_grad, output_grad, qkv_grad, early, up_bias_grad, late, bias_grads)
-        return sums, (layer_out, grad_tokens)
+        return sums, (layer_out, ends)
 
     if images == 1:
-        sums, (layer_out, grad_tokens) = run(tokens, bias_mask, cotangent, tok_blocks)
+        sums, (layer_out, ends) = run(tokens, bias_mask, cotangent, tok_blocks)
     else:
         items = (tokens[:, None], bias_mask[:, None], cotangent[:, None])
         shapes = jax.eval_shape(lambda item: run(*item)[0], jax.tree.map(lambda a: a[0], items))
@@ -971,8 +997,9 @@
             sums, results = run(*item)
             return jax.tree.map(jnp.add, totals, sums), results
 
-        sums, (layer_out, grad_tokens) = lax.scan(step, empty, items)
-        layer_out, grad_tokens = layer_out[:, 0], grad_tokens[:, 0]
+        sums, (layer_out, ends) = lax.scan(step, empty, items)
+        layer_out = layer_out[:, 0]
+        grad_tokens = ends[:, 0]
     down_grad, up_grad, output_grad, qkv_grad, early, up_bias_grad, late, bias_grads = sums
 
     down_pieces = down_grad if single else merge_down(send_down(down_grad))
@@ -1009,6 +1036,10 @@
         [to_owner] + sum_steps(),
     )
     final_down = final_down.astype(F32).T
+    if fast:
+        ends, four = together(ends, four)
+        residual, norm_near, norm_incoming = ends
+        grad_tokens = token_grads(tokens, residual, norm_near + norm_incoming.astype(F32))
     (
         gain_two_grad,
         shift_two_grad,

time: 618 us -> 586 us (0.948)
  waiting for transfers between devices: 183 us -> 134 us
  other arithmetic: 62 us -> 73.2 us
    ppermute x36 -> x39, waiting for transfers between devices: 104 us -> 48.7 us  [swap(): return lax.ppermute(value, 'seq', [(i, i ^ bit) for i in range(count)])]
    pallas_call x4 -> x5, Pallas kernels: 18.2 us -> 21.5 us  [glue(): pl.pallas_call(kernel, grid_spec=pltpu.PrefetchScalarGridSpec(num_scalar_...]
    ppermute x36 -> x39, starting transfers between devices: 19.5 us -> 22 us  [swap(): return lax.ppermute(value, 'seq', [(i, i ^ bit) for i in range(count)])]
    pallas_call x1 -> x2, Pallas kernels: 40 us -> 39.7 us  [attend(): pl.pallas_call(kernel, grid=(images, count), in_specs=[part, pl.BlockSpec...]
  transfers between devices with their start and end apart: 57 -> 60, of which waited for: 18 -> 17; matrix products, arithmetic and copies ran while one was open for 23% -> 26% of each run, Pallas kernels for 26% -> 27%
where the time goes in v6:
time: 586 us; the launch traced here: 576 us
  Pallas kernels  216 us (37%)
  waiting for transfers between devices  134 us (23%)
  other arithmetic  73.2 us (12%)
  local copies, waits for them, and re-layouts  53.6 us (9%)
  matrix products  41.9 us (7%)
  starting transfers between devices  41.5 us (7%)
  between operations  15.1 us (3%)
    pallas_call x1, Pallas kernels, middle(): pl.pallas_call(kernel, grid_spec=pltpu.PrefetchScalarGridSpec(num_scalar_...  55.8 us
    ppermute x14, waiting for transfers between devices, ring_shift(): lax.ppermute(value, 'fsdp', [(order[i], order[(i + step) % count]) for i...  52.1 us
    pallas_call x2, Pallas kernels, attend_back(): pl.pallas_call(kernel, grid=(images, heads, steps), in_specs=[row_in, row...  51.4 us
    ppermute x39, waiting for transfers between devices, swap(): return lax.ppermute(value, 'seq', [(i, i ^ bit) for i in range(count)])  48.7 us
    pallas_call x2, Pallas kernels, attend(): pl.pallas_call(kernel, grid=(images, count), in_specs=[part, pl.BlockSpec...  39.7 us
    pallas_call x1, Pallas kernels, project_back(): pl.pallas_call(kernel, grid=(images, count), in_specs=[piece_spec] * len(...  29.9 us
    reduce_scatter x1, waiting for transfers between devices, scatter_up(): return lax.psum_scatter(blocks, 'fsdp', scatter_dimension=0)  25.3 us
    ppermute x39, starting transfers between devices, swap(): return lax.ppermute(value, 'seq', [(i, i ^ bit) for i in range(count)])  22 us
  transfers between devices with their start and end apart: 60, of which 17 were waited for; matrix products, arithmetic and copies ran while one was open for 26% of the time, Pallas kernels for 27%

profile of v6, /device:TPU:0, one launch (start us, length us, event | category | flops | bytes accessed | tf_op | source)
XLA Modules:
  0.0 575.5 jit_solution(7140749399437578816)
XLA Ops:
  16.5 5.7 collective-permute-done.2.refs_1_
  25.5 10.8 %collective-permute-done.4.refs_3_ = bf16[144,864]{1,0:T(8,128)(2,1)S(1)} collective-permute-done((bf16[144,864]{1,0:T(8,128)(2,1)S(1)}, bf16[144,864]{1,0:T(8,128)(2,1)S(1)}, u32[]{:S(2)}, u32[]{:S(2)}) %collective-permute-start.4) | collective-permute-done | bytes 248864 | tf_op jit(solution)/shard_map/ppermute | solution.py:116
  36.3 6.7 %collective-permute-done.5.refs_4_ = bf16[144,864]{1,0:T(8,128)(2,1)S(1)} collective-permute-done((bf16[144,864]{1,0:T(8,128)(2,1)S(1)}, bf16[144,864]{1,0:T(8,128)(2,1)S(1)}, u32[]{:S(2)}, u32[]{:S(2)}) %collective-permute-start.5) | collective-permute-done | bytes 248864 | tf_op jit(solution)/shard_map/ppermute | solution.py:116
  52.0 13.3 %collective-permute-done.8.refs_7_ = bf16[144,864]{1,0:T(8,128)(2,1)S(1)} collective-permute-done((bf16[144,864]{1,0:T(8,128)(2,1)S(1)}, bf16[144,864]{1,0:T(8,128)(2,1)S(1)}, u32[]{:S(2)}, u32[]{:S(2)}) %collective-permute-start.8) | collective-permute-done | bytes 248864 | tf_op jit(solution)/shard_map/ppermute | solution.py:116
  74.1 8.9 %place_wide.1 = bf16[1152,1536]{1,0:T(8,128)(2,1)} custom-call(s32[8]{0:T(128)} %stack.101.index_ref, bf16[144,864]{1,0:T(8,128)(2,1)} %copy-done.15, bf16[144,864]{1,0:T(8,128)(2,1)} %copy-done.32, bf16[144,864]{1,0:T(8,128)(2,1)} %copy-done.33, bf16[144,864]{1,0:T(8,128)(2,1)} %copy-done.34, bf16[144,864]{1,0:T(8,128)(2,1)} %copy-done.35, ...), custom_call_target="tpu_custom_call" | custom-call | flops 23887872 | bytes 62208 | tf_op jit(solution)/shard_map/place_wide/pallas_call | solution.py:160
  83.0 5.9 %copy.103 = bf16[1152,1536]{0,1:T(8,128)(2,1)} copy(bf16[1152,1536]{1,0:T(8,128)(2,1)} %place_wide.1) | data formatting | bytes 7077888 | tf_op jit(solution)/shard_map/place_wide/pallas_call | solution.py:160
  88.9 5.3 convert_reduce_fusion
  105.6 11.4 %collective-permute-done.18.refs_6_ = bf16[288,1152]{1,0:T(8,128)(2,1)S(1)} collective-permute-done((bf16[288,1152]{1,0:T(8,128)(2,1)}, bf16[288,1152]{1,0:T(8,128)(2,1)S(1)}, u32[]{:S(2)}, u32[]{:S(2)}) %collective-permute-start.18) | collective-permute-done | bytes 663584 | tf_op jit(solution)/shard_map/ppermute | solution.py:44
  117.0 12.2 %fusion.22.q_ref = bf16[1,4,512,1536]{3,2,1,0:T(8,128)(2,1)} fusion(f32[1536]{0:T(1024)S(1)} %copy-done.80, f32[4,512]{1,0:T(4,128)S(1)} %copy-done.60, f32[1536]{0:T(1024)S(1)} %copy-done.64, f32[1536]{0:T(1024)S(1)} %copy-done.63, bf16[1,512,1152]{2,1,0:T(8,128)(2,1)} %collective-permute-done.9, bf16[1,512,1152]{2,1,0:T(8,128)(2,1)} %collective-permute-done.1, ...), kind=kOutput, calls=%fused_computation.32 | convolution fusion | flops 7284719616 | bytes 14601216 | tf_op jit(solution)/shard_map/ijld,de->ijle/dot_general | solution.py:825
  133.6 19.7 %attend.2 = (bf16[1,4,144,512]{3,2,1,0:T(8,128)(2,1)}, bf16[1,4,512,512]{3,2,1,0:T(8,128)(2,1)}, f32[1,4,512,512]{3,2,1,0:T(8,128)}) custom-call(bf16[1,4,512,1536]{3,2,1,0:T(8,128)(2,1)} %fusion.22.q_ref, bf16[1,2048,1536]{2,1,0:T(8,128)(2,1)} %bitcast.131), custom_call_target="tpu_custom_call" | custom-call | flops 67108864 | bytes 147456 | tf_op jit(solution)/shard_map/attend/pallas_call | solution.py:386
  154.0 20.0 %attend.3 = (bf16[1,4,144,512]{3,2,1,0:T(8,128)(2,1)}, bf16[1,4,512,512]{3,2,1,0:T(8,128)(2,1)}, f32[1,4,512,512]{3,2,1,0:T(8,128)}) custom-call(bf16[1,4,512,1536]{3,2,1,0:T(8,128)(2,1)} %fusion.22.q_ref, bf16[1,2048,1536]{2,1,0:T(8,128)(2,1)} %bitcast.132, ...), custom_call_target="tpu_custom_call", output_to_operand_aliasing={{1}: (2, {}), {2}: (3, {})} | custom-call | flops 67108864 | bytes 147456 | tf_op jit(solution)/shard_map/attend/pallas_call | solution.py:386
  176.7 5.2 copy.104
  182.5 7.3 %collective-permute-done.23.refs_5_ = bf16[1,4,144,512]{3,2,1,0:T(8,128)(2,1)} collective-permute-done((bf16[1,4,144,512]{3,2,1,0:T(8,128)(2,1)}, bf16[1,4,144,512]{3,2,1,0:T(8,128)(2,1)}, u32[]{:S(2)}, u32[]{:S(2)}) %collective-permute-start.23) | collective-permute-done | bytes 589856 | tf_op jit(solution)/shard_map/ppermute | solution.py:44
  193.6 6.5 %build_weights.1 = (bf16[1076,1152]{1,0:T(8,128)(2,1)}, bf16[1152,1076]{1,0:T(8,128)(2,1)}, bf16[4,288,1152]{2,1,0:T(8,128)(2,1)}) custom-call(s32[1]{0:T(128)} %bitcast.me_ref, bf16[2,288,538]{2,1,0:T(8,128)(2,1)} %get-tuple-element.174.refs_0_, bf16[2,288,538]{2,1,0:T(8,128)(2,1)} %copy-done.16, bf16[2,288,538]{2,1,0:T(8,128)(2,1)} %copy-done.17, ...), custom_call_target="tpu_custom_call" | custom-call | bytes 160416 | tf_op jit(solution)/shard_map/build_weights/pallas_call | solution.py:247
  201.6 55.8 %middle.1 = (bf16[1,4,512,1152]{3,2,1,0:T(8,128)(2,1)}, bf16[1,4,512,1076]{3,2,1,0:T(8,128)(2,1)}, bf16[1,4,512,1076]{3,2,1,0:T(8,128)(2,1)}, bf16[1,4,512,1152]...) custom-call(s32[1]{0:T(128)} %bitcast.me_ref, ...), custom_call_target="tpu_custom_call" | custom-call | flops 402259968 | bytes 846496 | tf_op jit(solution)/shard_map/middle/pallas_call | solution.py:489
  265.9 9.9 %fusion.2 = bf16[1152,1076]{0,1:T(8,128)(2,1)} fusion(bf16[1,4,512,1076]{3,2,1,0:T(8,128)(2,1)} %get-tuple-element.193, bf16[1,4,512,1152]{3,2,1,0:T(8,128)(2,1)S(1)} %copy-done.78), kind=kOutput, calls=%fused_computation.8 | convolution fusion | flops 5078444544 | bytes 11604992 | tf_op jit(solution)/shard_map/ijld,ijlf->df/dot_general | solution.py:911
  275.8 5.2 copy.106.in_ref
  284.4 8.5 %collective-permute-done.30 = bf16[1,512,1152]{2,1,0:T(8,128)(2,1)} collective-permute-done((bf16[1,512,1152]{2,1,0:T(8,128)(2,1)}, bf16[1,512,1152]{2,1,0:T(8,128)(2,1)}, u32[]{:S(2)}, u32[]{:S(2)}) %collective-permute-start.30) | collective-permute-done | bytes 1179680 | tf_op jit(solution)/shard_map/ppermute | solution.py:44
  297.1 4.7 convert_reduce_fusion.3
  303.7 11.6 %fusion.3.in_ref = bf16[1152,1076]{1,0:T(8,128)(2,1)} fusion(bf16[1,4,512,1076]{3,2,1,0:T(8,128)(2,1)} %get-tuple-element.197, bf16[1,1,512,1152]{3,2,1,0:T(8,128)(2,1)} %bitcast.25, bf16[1,1,512,1152]{3,2,1,0:T(8,128)(2,1)} %bitcast.150, bf16[1,1,512,1152]{3,2,1,0:T(8,128)(2,1)} %bitcast.23, bf16[1,1,512,1152]{3,2,1,0:T(8,128)(2,1)} %bitcast.144), kind=kOutput, calls=%fused_computation.9 | convolution fusion | flops 5085522432 | bytes 11604992 | tf_op jit(solution)/shard_map/ijld,ijlf->df/dot_general | solution.py:925
  315.3 14.3 %collective-permute-done.32 = bf16[1,512,1152]{2,1,0:T(8,128)(2,1)} collective-permute-done((bf16[1,512,1152]{2,1,0:T(8,128)(2,1)}, bf16[1,512,1152]{2,1,0:T(8,128)(2,1)}, u32[]{:S(2)}, u32[]{:S(2)}) %collective-permute-start.32) | collective-permute-done | bytes 1179680 | tf_op jit(solution)/shard_map/ppermute | solution.py:44
  333.5 4.6 pad_maximum_fusion.2.grad_ref
  338.1 8.7 %mixed_back.1 = bf16[1,4,512,512]{3,2,1,0:T(8,128)(2,1)} custom-call(bf16[1,4,512,1152]{3,2,1,0:T(8,128)(2,1)} %pad_maximum_fusion.2.grad_ref, bf16[1152,512]{1,0:T(8,128)(2,1)} %convolution_convert_fusion.w_ref, f32[1,4,512,512]{3,2,1,0:T(8,128)} %get-tuple-element.199.exact_ref), custom_call_target="tpu_custom_call" | custom-call | flops 18874368 | bytes 190464 | tf_op jit(solution)/shard_map/mixed_back/pallas_call | solution.py:545
  354.3 25.3 %reduce-scatter.3.cloned.1.call-done = bf16[1,144,1076]{2,1,0:T(8,128)(2,1)} async-done(((bf16[8,144,1076]{2,1,0:T(8,128)(2,1)}), bf16[1,144,1076]{2,1,0:T(8,128)(2,1)}) %reduce-scatter.3.cloned.1.call-update) | async-done | bytes 309904 | tf_op jit(solution)/shard_map/reduce_scatter | solution.py:800
  379.6 25.6 %attend_back.2 = (bf16[1,2048,256]{2,1,0:T(8,128)(2,1)}, bf16[1,2048,256]{2,1,0:T(8,128)(2,1)}, bf16[1,2048,256]{2,1,0:T(8,128)(2,1)}) custom-call(bf16[1,2048,512]{2,1,0:T(8,128)(2,1)} %bitcast.138, bf16[1,2048,512]{2,1,0:T(8,128)(2,1)} %bitcast.140, bf16[1,2048,1536]{2,1,0:T(8,128)(2,1)} %bitcast.133, bf16[1,2048,1536]{2,1,0:T(8,128)(2,1)} %bitcast.134), custom_call_target="tpu_custom_call" | custom-call | flops 167772160 | bytes 229376 | tf_op jit(solution)/shard_map/attend_back/pallas_call | solution.py:607
  420.9 5.0 fusion.31
  433.8 25.9 %attend_back.3 = (bf16[1,2048,256]{2,1,0:T(8,128)(2,1)}, bf16[1,2048,256]{2,1,0:T(8,128)(2,1)}, bf16[1,2048,256]{2,1,0:T(8,128)(2,1)}) custom-call(bf16[1,2048,512]{2,1,0:T(8,128)(2,1)} %bitcast.139, bf16[1,2048,512]{2,1,0:T(8,128)(2,1)} %bitcast.141, bf16[1,2048,1536]{2,1,0:T(8,128)(2,1)} %bitcast.135, bf16[1,2048,1536]{2,1,0:T(8,128)(2,1)} %bitcast.136), custom_call_target="tpu_custom_call" | custom-call | flops 167772160 | bytes 229376 | tf_op jit(solution)/shard_map/attend_back/pallas_call | solution.py:607
  459.7 29.9 %project_back.1 = (bf16[1,512,1152]{2,1,0:T(8,128)(2,1)}, bf16[1,512,1152]{2,1,0:T(8,128)(2,1)}, bf16[1,512,1152]{2,1,0:T(8,128)(2,1)}, bf16[1,512,1152]{2,1,0:T...) custom-call(bf16[1,4,512,256]{3,2,1,0:T(8,128)(2,1)} %bitcast.151, ...), custom_call_target="tpu_custom_call" | custom-call | flops 113246208 | bytes 301056 | tf_op jit(solution)/shard_map/project_back/pallas_call | solution.py:682
  504.8 7.3 %collective-permute-done.43 = bf16[4,144,288]{2,1,0:T(8,128)(2,1)} collective-permute-done((bf16[4,144,288]{2,1,0:T(8,128)(2,1)}, bf16[4,144,288]{2,1,0:T(8,128)(2,1)}, u32[]{:S(2)}, u32[]{:S(2)}) %collective-permute-start.43) | collective-permute-done | bytes 331808 | tf_op jit(solution)/shard_map/ppermute | solution.py:116
  538.9 5.7 collective-permute-done.51
  553.9 5.1 collective-permute-done.55
  560.5 4.5 collective-permute-done.42
  (382 shorter events, 164.3 us)
Async XLA Ops:
  7.2 87.6 %all-gather.6.cloned.1.call-start = ((), (), s32[]{:S(2)}) async-start(), calls=%async_computation.5 | async-start | bytes 3981312 | tf_op jit(solution)/shard_map/all_gather | solution.py:750
  10.2 166.5 %all-gather.4.cloned.1.call-start = ((), (), s32[]{:S(2)}) async-start(), calls=%async_computation.2 | async-start | bytes 2985984 | tf_op jit(solution)/shard_map/all_gather | solution.py:759
  10.3 41.7 %collective-permute-start.1 = (bf16[1,512,1152]{2,1,0:T(8,128)(2,1)}, bf16[1,512,1152]{2,1,0:T(8,128)(2,1)}, u32[]{:S(2)}, u32[]{:S(2)}) collective-permute-start(bf16[1,512,1152]{2,1,0:T(8,128)(2,1)} %param.21), channel_id=1, source_target_pairs={{0,16},{8,24},{16,0},{24,8},{1,17},{9,25},{17,1},{25,9},{2,18},{10... | collective-permute-start | bytes 3538952 | tf_op jit(solution)/shard_map/ppermute | solution.py:44
  44.9 44.0 %collective-permute-start = (bf16[1,512,1152]{2,1,0:T(8,128)(2,1)}, bf16[1,512,1152]{2,1,0:T(8,128)(2,1)}, u32[]{:S(2)}, u32[]{:S(2)}) collective-permute-start(bf16[1,512,1152]{2,1,0:T(8,128)(2,1)} %param.21), channel_id=1, source_target_pairs={{0,8},{8,0},{16,24},{24,16},{1,9},{9,1},{17,25},{25,17},{2,10},{10... | collective-permute-start | bytes 3538952 | tf_op jit(solution)/shard_map/ppermute | solution.py:44
  49.9 19.5 %collective-permute-start.10 = (bf16[2240]{0:T(1024)(128)(2,1)S(1)}, bf16[2240]{0:T(1024)(128)(2,1)S(1)}, u32[]{:S(2)}, u32[]{:S(2)}) collective-permute-start(bf16[2240]{0:T(1024)(128)(2,1)S(1)} %concatenate.83), channel_id=1, source_target_pairs={{0,16},{8,24},{16,0},{24,8},{1,17},{9,25},{17,1},{25,9},{2,18},{10... | collective-permute-start | bytes 13448 | tf_op jit(solution)/shard_map/ppermute | solution.py:44
  50.5 329.0 %reduce-scatter.3.cloned.1.call-start = ((), (), s32[]{:S(2)}) async-start(), calls=%async_computation.3 | async-start | bytes 2985984 | tf_op jit(solution)/shard_map/reduce_scatter | solution.py:800
  50.8 20.0 %collective-permute-start.12 = (bf16[2240]{0:T(1024)(128)(2,1)S(1)}, bf16[2240]{0:T(1024)(128)(2,1)S(1)}, u32[]{:S(2)}, u32[]{:S(2)}) collective-permute-start(bf16[2240]{0:T(1024)(128)(2,1)S(1)} %concatenate.83), channel_id=1, source_target_pairs={{0,8},{8,0},{16,24},{24,16},{1,9},{9,1},{17,25},{25,17},{2,10},{10... | collective-permute-start | bytes 13448 | tf_op jit(solution)/shard_map/ppermute | solution.py:44
  66.1 22.8 %collective-permute-start.9 = (bf16[1,512,1152]{2,1,0:T(8,128)(2,1)}, bf16[1,512,1152]{2,1,0:T(8,128)(2,1)}, u32[]{:S(2)}, u32[]{:S(2)}) collective-permute-start(bf16[1,512,1152]{2,1,0:T(8,128)(2,1)} %collective-permute-done.1), channel_id=1, source_target_pairs={{0,8},{8,0},{16,24},{24,16},{1,9},{9,1},{17,25},{25,17},{2,10},{10... | collective-permute-start | bytes 3538952 | tf_op jit(solution)/shard_map/ppermute | solution.py:44
  72.6 33.0 %collective-permute-start.13 = (bf16[1,512,1152]{2,1,0:T(8,128)(2,1)S(1)}, bf16[1,512,1152]{2,1,0:T(8,128)(2,1)S(1)}, u32[]{:S(2)}, u32[]{:S(2)}) collective-permute-start(bf16[1,512,1152]{2,1,0:T(8,128)(2,1)S(1)} %copy-done.4), channel_id=1, source_target_pairs={{0,16},{8,24},{16,0},{24,8},{1,17},{9,25},{17,1},{25,9},{2,18},{10... | collective-permute-start | bytes 3538952 | tf_op jit(solution)/shard_map/ppermute | solution.py:44
  103.5 50.4 %collective-permute-start.17 = (bf16[288,1152]{1,0:T(8,128)(2,1)S(1)}, bf16[288,1152]{1,0:T(8,128)(2,1)S(1)}, u32[]{:S(2)}, u32[]{:S(2)}) collective-permute-start(bf16[288,1152]{1,0:T(8,128)(2,1)S(1)} %copy-done.19), channel_id=1, source_target_pairs={{0,8},{8,0},{16,24},{24,16},{1,9},{9,1},{17,25},{25,17},{2,10},{10... | collective-permute-start | bytes 1990664 | tf_op jit(solution)/shard_map/ppermute | solution.py:44
  103.6 25.6 %collective-permute-start.14 = (bf16[2,288,538]{2,1,0:T(8,128)(2,1)}, bf16[2,288,538]{2,1,0:T(8,128)(2,1)S(1)}, u32[]{:S(2)}, u32[]{:S(2)}) collective-permute-start(bf16[2,288,538]{2,1,0:T(8,128)(2,1)} %get-tuple-element.165), channel_id=1, source_target_pairs={{0,8},{8,0},{16,24},{24,16},{1,9},{9,1},{17,25},{25,17},{2,10},{10... | collective-permute-start | bytes 1859336 | tf_op jit(solution)/shard_map/ppermute | solution.py:44
  104.1 28.7 %collective-permute-start.15 = (bf16[2,288,538]{2,1,0:T(8,128)(2,1)}, bf16[2,288,538]{2,1,0:T(8,128)(2,1)S(1)}, u32[]{:S(2)}, u32[]{:S(2)}) collective-permute-start(bf16[2,288,538]{2,1,0:T(8,128)(2,1)} %get-tuple-element.166), channel_id=1, source_target_pairs={{0,16},{8,24},{16,0},{24,8},{1,17},{9,25},{17,1},{25,9},{2,18},{10... | collective-permute-start | bytes 1859336 | tf_op jit(solution)/shard_map/ppermute | solution.py:44
  105.6 47.8 %collective-permute-start.16 = (bf16[2,288,538]{2,1,0:T(8,128)(2,1)}, bf16[2,288,538]{2,1,0:T(8,128)(2,1)S(1)}, u32[]{:S(2)}, u32[]{:S(2)}) collective-permute-start(bf16[2,288,538]{2,1,0:T(8,128)(2,1)} %get-tuple-element.167), channel_id=1, source_target_pairs={{0,24},{8,16},{16,8},{24,0},{1,25},{9,17},{17,9},{25,1},{2,26},{10... | collective-permute-start | bytes 1859336 | tf_op jit(solution)/shard_map/ppermute | solution.py:44
  116.9 37.0 %collective-permute-start.19 = (bf16[288,1152]{1,0:T(8,128)(2,1)S(1)}, bf16[288,1152]{1,0:T(8,128)(2,1)S(1)}, u32[]{:S(2)}, u32[]{:S(2)}) collective-permute-start(bf16[288,1152]{1,0:T(8,128)(2,1)S(1)} %collective-permute-done.18.refs_6_), channel_id=1, source_target_pairs={{0,8},{8,0},{16,24},{24,16},{1,9},{9,1},{17,25},{25,17},{2,10},{10... | collective-permute-start | bytes 1990664 | tf_op jit(solution)/shard_map/ppermute | solution.py:44
  129.2 53.2 %collective-permute-start.26 = (bf16[1,512,1152]{2,1,0:T(8,128)(2,1)S(1)}, bf16[1,512,1152]{2,1,0:T(8,128)(2,1)}, u32[]{:S(2)}, u32[]{:S(2)}) collective-permute-start(bf16[1,512,1152]{2,1,0:T(8,128)(2,1)S(1)} %copy-done.4), channel_id=1, source_target_pairs={{0,8},{8,0},{16,24},{24,16},{1,9},{9,1},{17,25},{25,17},{2,10},{10... | collective-permute-start | bytes 3538952 | tf_op jit(solution)/shard_map/ppermute | solution.py:44
  133.6 56.2 %collective-permute-start.27 = (bf16[1,512,1152]{2,1,0:T(8,128)(2,1)S(1)}, bf16[1,512,1152]{2,1,0:T(8,128)(2,1)}, u32[]{:S(2)}, u32[]{:S(2)}) collective-permute-start(bf16[1,512,1152]{2,1,0:T(8,128)(2,1)S(1)} %collective-permute-done.13), channel_id=1, source_target_pairs={{0,8},{8,0},{16,24},{24,16},{1,9},{9,1},{17,25},{25,17},{2,10},{10... | collective-permute-start | bytes 3538952 | tf_op jit(solution)/shard_map/ppermute | solution.py:44
  153.3 28.6 %collective-permute-start.22 = (bf16[1,4,144,512]{3,2,1,0:T(8,128)(2,1)}, bf16[1,4,144,512]{3,2,1,0:T(8,128)(2,1)}, u32[]{:S(2)}, u32[]{:S(2)}) collective-permute-start(bf16[1,4,144,512]{3,2,1,0:T(8,128)(2,1)} %get-tuple-element.161.refs_0_), channel_id=1, source_target_pairs={{0,16},{8,24},{16,0},{24,8},{1,17},{9,25},{17,1},{25,9},{2,18},{10... | collective-permute-start | bytes 1769480 | tf_op jit(solution)/shard_map/ppermute | solution.py:44
  257.9 35.0 %collective-permute-start.28 = (bf16[1,512,1152]{2,1,0:T(8,128)(2,1)}, bf16[1,512,1152]{2,1,0:T(8,128)(2,1)}, u32[]{:S(2)}, u32[]{:S(2)}) collective-permute-start(bf16[1,512,1152]{2,1,0:T(8,128)(2,1)} %get-tuple-element.187), channel_id=1, source_target_pairs={{0,8},{8,0},{16,24},{24,16},{1,9},{9,1},{17,25},{25,17},{2,10},{10... | collective-permute-start | bytes 3538952 | tf_op jit(solution)/shard_map/ppermute | solution.py:44
  264.3 28.6 %collective-permute-start.30 = (bf16[1,512,1152]{2,1,0:T(8,128)(2,1)}, bf16[1,512,1152]{2,1,0:T(8,128)(2,1)}, u32[]{:S(2)}, u32[]{:S(2)}) collective-permute-start(bf16[1,512,1152]{2,1,0:T(8,128)(2,1)} %add_convert_fusion.8), channel_id=1, source_target_pairs={{0,16},{8,24},{16,0},{24,8},{1,17},{9,25},{17,1},{25,9},{2,18},{10... | collective-permute-start | bytes 3538952 | tf_op jit(solution)/shard_map/ppermute | solution.py:44
  301.8 27.8 %collective-permute-start.32 = (bf16[1,512,1152]{2,1,0:T(8,128)(2,1)}, bf16[1,512,1152]{2,1,0:T(8,128)(2,1)}, u32[]{:S(2)}, u32[]{:S(2)}) collective-permute-start(bf16[1,512,1152]{2,1,0:T(8,128)(2,1)} %get-tuple-element.196), channel_id=1, source_target_pairs={{0,16},{8,24},{16,0},{24,8},{1,17},{9,25},{17,1},{25,9},{2,18},{10... | collective-permute-start | bytes 3538952 | tf_op jit(solution)/shard_map/ppermute | solution.py:44
  303.4 30.0 %collective-permute-start.31 = (bf16[1,512,1152]{2,1,0:T(8,128)(2,1)}, bf16[1,512,1152]{2,1,0:T(8,128)(2,1)}, u32[]{:S(2)}, u32[]{:S(2)}) collective-permute-start(bf16[1,512,1152]{2,1,0:T(8,128)(2,1)} %get-tuple-element.196), channel_id=1, source_target_pairs={{0,8},{8,0},{16,24},{24,16},{1,9},{9,1},{17,25},{25,17},{2,10},{10... | collective-permute-start | bytes 3538952 | tf_op jit(solution)/shard_map/ppermute | solution.py:44
  303.4 228.0 %reduce-scatter.5.cloned.1.call-start = ((), (), s32[]{:S(2)}) async-start(), calls=%async_computation.4 | async-start | bytes 3317760 | tf_op jit(solution)/shard_map/reduce_scatter | solution.py:1007
  351.1 54.0 %collective-permute-start.36 = (bf16[2,288,538]{2,1,0:T(8,128)(2,1)}, bf16[2,288,538]{2,1,0:T(8,128)(2,1)}, u32[]{:S(2)}, u32[]{:S(2)}) collective-permute-start(bf16[2,288,538]{2,1,0:T(8,128)(2,1)} %get-tuple-element.219), channel_id=1, source_target_pairs={{0,8},{8,0},{16,24},{24,16},{1,9},{9,1},{17,25},{25,17},{2,10},{10... | collective-permute-start | bytes 1859336 | tf_op jit(solution)/shard_map/ppermute | solution.py:44
  351.3 53.8 %collective-permute-start.37 = (bf16[2,288,538]{2,1,0:T(8,128)(2,1)}, bf16[2,288,538]{2,1,0:T(8,128)(2,1)}, u32[]{:S(2)}, u32[]{:S(2)}) collective-permute-start(bf16[2,288,538]{2,1,0:T(8,128)(2,1)} %get-tuple-element.220), channel_id=1, source_target_pairs={{0,16},{8,24},{16,0},{24,8},{1,17},{9,25},{17,1},{25,9},{2,18},{10... | collective-permute-start | bytes 1859336 | tf_op jit(solution)/shard_map/ppermute | solution.py:44
  352.9 52.3 %collective-permute-start.38 = (bf16[2,288,538]{2,1,0:T(8,128)(2,1)}, bf16[2,288,538]{2,1,0:T(8,128)(2,1)}, u32[]{:S(2)}, u32[]{:S(2)}) collective-permute-start(bf16[2,288,538]{2,1,0:T(8,128)(2,1)} %get-tuple-element.221), channel_id=1, source_target_pairs={{0,24},{8,16},{16,8},{24,0},{1,25},{9,17},{17,9},{25,1},{2,26},{10... | collective-permute-start | bytes 1859336 | tf_op jit(solution)/shard_map/ppermute | solution.py:44
  418.4 41.3 %collective-permute-start.39 = (bf16[1,512,1152]{2,1,0:T(8,128)(2,1)}, bf16[1,512,1152]{2,1,0:T(8,128)(2,1)}, u32[]{:S(2)}, u32[]{:S(2)}) collective-permute-start(bf16[1,512,1152]{2,1,0:T(8,128)(2,1)} %add_convert_fusion.7), channel_id=1, source_target_pairs={{0,16},{8,24},{16,0},{24,8},{1,17},{9,25},{17,1},{25,9},{2,18},{10... | collective-permute-start | bytes 3538952 | tf_op jit(solution)/shard_map/ppermute | solution.py:44
  431.7 96.2 %collective-permute-start.34 = (bf16[1,512,1152]{2,1,0:T(8,128)(2,1)}, bf16[1,512,1152]{2,1,0:T(8,128)(2,1)}, u32[]{:S(2)}, u32[]{:S(2)}) collective-permute-start(bf16[1,512,1152]{2,1,0:T(8,128)(2,1)} %get-tuple-element.206), channel_id=1, source_target_pairs={{0,8},{8,0},{16,24},{24,16},{1,9},{9,1},{17,25},{25,17},{2,10},{10... | collective-permute-start | bytes 3538952 | tf_op jit(solution)/shard_map/ppermute | solution.py:44
  493.2 21.9 %collective-permute-start.48 = (f32[6,288]{1,0:T(8,128)}, f32[6,288]{1,0:T(8,128)}, u32[]{:S(2)}, u32[]{:S(2)}) collective-permute-start(f32[6,288]{1,0:T(8,128)} %bitcast.128), channel_id=1, source_target_pairs={{0,24},{8,16},{16,8},{24,0},{1,25},{9,17},{17,9},{25,1},{2,26},{10... | collective-permute-start | bytes 20744 | tf_op jit(solution)/shard_map/ppermute | solution.py:44
  494.3 22.1 %collective-permute-start.46 = (f32[6,288]{1,0:T(8,128)}, f32[6,288]{1,0:T(8,128)}, u32[]{:S(2)}, u32[]{:S(2)}) collective-permute-start(f32[6,288]{1,0:T(8,128)} %get-tuple-element.279), channel_id=1, source_target_pairs={{0,8},{8,0},{16,24},{24,16},{1,9},{9,1},{17,25},{25,17},{2,10},{10... | collective-permute-start | bytes 20744 | tf_op jit(solution)/shard_map/ppermute | solution.py:44
  494.3 22.0 %collective-permute-start.47 = (f32[6,288]{1,0:T(8,128)}, f32[6,288]{1,0:T(8,128)}, u32[]{:S(2)}, u32[]{:S(2)}) collective-permute-start(f32[6,288]{1,0:T(8,128)} %get-tuple-element.320), channel_id=1, source_target_pairs={{0,16},{8,24},{16,0},{24,8},{1,17},{9,25},{17,1},{25,9},{2,18},{10... | collective-permute-start | bytes 20744 | tf_op jit(solution)/shard_map/ppermute | solution.py:44
  526.8 21.6 %collective-permute-start.40 = (bf16[1,512,1152]{2,1,0:T(8,128)(2,1)}, bf16[1,512,1152]{2,1,0:T(8,128)(2,1)}, u32[]{:S(2)}, u32[]{:S(2)}) collective-permute-start(bf16[1,512,1152]{2,1,0:T(8,128)(2,1)} %get-tuple-element.243), channel_id=1, source_target_pairs={{0,8},{8,0},{16,24},{24,16},{1,9},{9,1},{17,25},{25,17},{2,10},{10... | collective-permute-start | bytes 3538952 | tf_op jit(solution)/shard_map/ppermute | solution.py:44
  538.0 27.0 %collective-permute-start.42 = (bf16[1,512,1152]{2,1,0:T(8,128)(2,1)S(1)}, bf16[1,512,1152]{2,1,0:T(8,128)(2,1)S(1)}, u32[]{:S(2)}, u32[]{:S(2)}) collective-permute-start(bf16[1,512,1152]{2,1,0:T(8,128)(2,1)S(1)} %add_convert_fusion.5), channel_id=1, source_target_pairs={{0,16},{8,24},{16,0},{24,8},{1,17},{9,25},{17,1},{25,9},{2,18},{10... | collective-permute-start | bytes 3538952 | tf_op jit(solution)/shard_map/ppermute | solution.py:44
  (109 other events, 1869.2 us)
Sparse Core Ops, SparseCore 0:
  10.8 76.3 all-gather.5
  89.4 56.3 all-gather.3
  303.6 75.9 reduce-scatter.2
  408.9 71.2 reduce-scatter.4

commit v7 on v6

--- a/solution.py
+++ b/solution.py
@@ -790,6 +790,10 @@
     down_exchanged = [down_sent[0]] + [swap(down_sent[j], j) for j in range(1, count)]
     cot_begun = (cot_sent, None, cot_across) if fast else None
     w_turned = w_wide.T
+
+    def absolute_rows(grad):
+        parts = reorder(jnp.split(grad.astype(BF), count, axis=0), me)
+        return jnp.concatenate(parts, axis=0)
 
     def token_grads(tokens, residual, grad_norm):
         normed, inverse = norm_parts(tokens.astype(F32))
@@ -943,10 +947,18 @@
         query_in = query_wide.reshape(wide_shape)
         grad_in = grad_mixed.reshape(wide_shape)
         flat_qkv = qkv.reshape(images, count * length, 3 * wide_heads)
+        grad_attn_cols = lax.dynamic_slice_in_dim(grad_attn_all, me * own, own, 3)
+        output_grad = jnp.einsum(
+            "ijle,ijld->ed", mixed_all, grad_attn_cols, preferred_element_type=F32
+        )
         grad_in, out_blocks, down_grad = together(grad_in, list(out_parts[0]), down_grad)
         if single:
             down_grad = send_down(down_grad)
-            grad_in, up_grad = together(grad_in, up_grad)
+            if fast:
+                output_grad = absolute_rows(output_grad)
+            grad_in, up_grad, output_grad, early = together(
+                grad_in, up_grad, output_grad, early
+            )
         if count == 4:
             out_sum, out_across = collect_pair(out_blocks)
             grad_in, out_across = together(grad_in, out_across)
@@ -968,10 +980,6 @@
         grads = [
             [piece[k].reshape(images, count, length, -1) for piece in pieces] for k in range(3)
         ]
-        grad_attn_cols = lax.dynamic_slice_in_dim(grad_attn_all, me * own, own, 3)
-        output_grad = jnp.einsum(
-            "ijle,ijld->ed", mixed_all, grad_attn_cols, preferred_element_type=F32
-        )
         result = project_back(grads, tok_all, turned, g_one, s_one, expand.T)
         qkv_grad, late, bias_grads = result[count:]
         if fast:
@@ -1005,8 +1013,8 @@
     down_pieces = down_grad if single else merge_down(send_down(down_grad))
     final_up = (up_grad if single else scatter_up(up_grad)).astype(F32)
     final_down = lax.psum_scatter(down_pieces, "fsdp", scatter_dimension=0)
-    output_grad = reorder(jnp.split(output_grad.astype(BF), count, axis=0), me)
-    output_grad = jnp.concatenate(output_grad, axis=0)
+    if not fast:
+        output_grad = absolute_rows(output_grad)
     qkv_grad = qkv_grad.astype(BF).reshape(3, fcount, width // fcount, own)
     output_grad = output_grad.reshape(fcount, width // fcount, own)
 

time: 586 us -> 572 us (0.976)
  waiting for transfers between devices: 134 us -> 122 us
    reduce_scatter x1, waiting for transfers between devices: 25.3 us -> 12.8 us  [scatter_up(): return lax.psum_scatter(blocks, 'fsdp', scatter_dimension=0)]
    concatenate x8 -> x1, local copies, waits for them, and re-layouts: 8.87 us -> 2.23 us  [absolute_rows(): return jnp.concatenate(parts, axis=0)]
  transfers between devices with their start and end apart: 60 -> 60, of which waited for: 17 -> 17; matrix products, arithmetic and copies ran while one was open for 26% -> 26% of each run, Pallas kernels for 27% -> 28%
where the time goes in v7:
time: 572 us; the launch traced here: 561 us
  Pallas kernels  216 us (38%)
  waiting for transfers between devices  122 us (21%)
  other arithmetic  75.4 us (13%)
  local copies, waits for them, and re-layouts  48.9 us (9%)
  matrix products  41.9 us (7%)
  starting transfers between devices  41.5 us (7%)
  between operations  15.1 us (3%)
    pallas_call x1, Pallas kernels, middle(): pl.pallas_call(kernel, grid_spec=pltpu.PrefetchScalarGridSpec(num_scalar_...  55.8 us
    ppermute x14, waiting for transfers between devices, ring_shift(): lax.ppermute(value, 'fsdp', [(order[i], order[(i + step) % count]) for i...  52.5 us
    pallas_call x2, Pallas kernels, attend_back(): pl.pallas_call(kernel, grid=(images, heads, steps), in_specs=[row_in, row...  51.4 us
    ppermute x39, waiting for transfers between devices, swap(): return lax.ppermute(value, 'seq', [(i, i ^ bit) for i in range(count)])  48.8 us
    pallas_call x2, Pallas kernels, attend(): pl.pallas_call(kernel, grid=(images, count), in_specs=[part, pl.BlockSpec...  39.7 us
    pallas_call x1, Pallas kernels, project_back(): pl.pallas_call(kernel, grid=(images, count), in_specs=[piece_spec] * len(...  29.9 us
    ppermute x39, starting transfers between devices, swap(): return lax.ppermute(value, 'seq', [(i, i ^ bit) for i in range(count)])  21.9 us
    pallas_call x5, Pallas kernels, glue(): pl.pallas_call(kernel, grid_spec=pltpu.PrefetchScalarGridSpec(num_scalar_...  21.5 us
  transfers between devices with their start and end apart: 60, of which 17 were waited for; matrix products, arithmetic and copies ran while one was open for 26% of the time, Pallas kernels for 28%

profile of v7, /device:TPU:0, one launch (start us, length us, event | category | flops | bytes accessed | tf_op | source)
XLA Modules:
  0.0 561.2 jit_solution(16026373802838613990)
XLA Ops:
  16.5 5.7 %collective-permute-done.2.refs_1_ = bf16[144,864]{1,0:T(8,128)(2,1)S(1)} collective-permute-done((bf16[144,864]{1,0:T(8,128)(2,1)S(1)}, bf16[144,864]{1,0:T(8,128)(2,1)S(1)}, u32[]{:S(2)}, u32[]{:S(2)}) %collective-permute-start.2) | collective-permute-done | bytes 248864 | tf_op jit(solution)/shard_map/ppermute | solution.py:116
  25.5 10.8 %collective-permute-done.4.refs_3_ = bf16[144,864]{1,0:T(8,128)(2,1)S(1)} collective-permute-done((bf16[144,864]{1,0:T(8,128)(2,1)S(1)}, bf16[144,864]{1,0:T(8,128)(2,1)S(1)}, u32[]{:S(2)}, u32[]{:S(2)}) %collective-permute-start.4) | collective-permute-done | bytes 248864 | tf_op jit(solution)/shard_map/ppermute | solution.py:116
  36.3 6.7 %collective-permute-done.5.refs_4_ = bf16[144,864]{1,0:T(8,128)(2,1)S(1)} collective-permute-done((bf16[144,864]{1,0:T(8,128)(2,1)S(1)}, bf16[144,864]{1,0:T(8,128)(2,1)S(1)}, u32[]{:S(2)}, u32[]{:S(2)}) %collective-permute-start.5) | collective-permute-done | bytes 248864 | tf_op jit(solution)/shard_map/ppermute | solution.py:116
  52.0 13.3 %collective-permute-done.8.refs_7_ = bf16[144,864]{1,0:T(8,128)(2,1)S(1)} collective-permute-done((bf16[144,864]{1,0:T(8,128)(2,1)S(1)}, bf16[144,864]{1,0:T(8,128)(2,1)S(1)}, u32[]{:S(2)}, u32[]{:S(2)}) %collective-permute-start.8) | collective-permute-done | bytes 248864 | tf_op jit(solution)/shard_map/ppermute | solution.py:116
  74.1 8.9 %place_wide.1 = bf16[1152,1536]{1,0:T(8,128)(2,1)} custom-call(s32[8]{0:T(128)} %stack.112.index_ref, bf16[144,864]{1,0:T(8,128)(2,1)} %copy-done.15, bf16[144,864]{1,0:T(8,128)(2,1)} %copy-done.32, bf16[144,864]{1,0:T(8,128)(2,1)} %copy-done.33, bf16[144,864]{1,0:T(8,128)(2,1)} %copy-done.34, bf16[144,864]{1,0:T(8,128)(2,1)} %copy-done.35, ...), custom_call_target="tpu_custom_call" | custom-call | flops 23887872 | bytes 62208 | tf_op jit(solution)/shard_map/place_wide/pallas_call | solution.py:160
  83.0 5.9 %copy.103 = bf16[1152,1536]{0,1:T(8,128)(2,1)} copy(bf16[1152,1536]{1,0:T(8,128)(2,1)} %place_wide.1) | data formatting | bytes 7077888 | tf_op jit(solution)/shard_map/place_wide/pallas_call | solution.py:160
  88.9 5.2 convert_reduce_fusion
  105.5 11.4 %collective-permute-done.18.refs_6_ = bf16[288,1152]{1,0:T(8,128)(2,1)S(1)} collective-permute-done((bf16[288,1152]{1,0:T(8,128)(2,1)}, bf16[288,1152]{1,0:T(8,128)(2,1)S(1)}, u32[]{:S(2)}, u32[]{:S(2)}) %collective-permute-start.18) | collective-permute-done | bytes 663584 | tf_op jit(solution)/shard_map/ppermute | solution.py:44
  117.0 12.2 %fusion.22.q_ref = bf16[1,4,512,1536]{3,2,1,0:T(8,128)(2,1)} fusion(f32[1536]{0:T(1024)S(1)} %copy-done.83, f32[4,512]{1,0:T(4,128)S(1)} %copy-done.64, f32[1536]{0:T(1024)S(1)} %copy-done.68, f32[1536]{0:T(1024)S(1)} %copy-done.67, bf16[1,512,1152]{2,1,0:T(8,128)(2,1)} %collective-permute-done.9, bf16[1,512,1152]{2,1,0:T(8,128)(2,1)} %collective-permute-done.1, ...), kind=kOutput, calls=%fused_computation.32 | convolution fusion | flops 7284719616 | bytes 14601216 | tf_op jit(solution)/shard_map/ijld,de->ijle/dot_general | solution.py:829
  133.5 19.7 %attend.2 = (bf16[1,4,144,512]{3,2,1,0:T(8,128)(2,1)}, bf16[1,4,512,512]{3,2,1,0:T(8,128)(2,1)}, f32[1,4,512,512]{3,2,1,0:T(8,128)}) custom-call(bf16[1,4,512,1536]{3,2,1,0:T(8,128)(2,1)} %fusion.22.q_ref, bf16[1,2048,1536]{2,1,0:T(8,128)(2,1)} %bitcast.131), custom_call_target="tpu_custom_call" | custom-call | flops 67108864 | bytes 147456 | tf_op jit(solution)/shard_map/attend/pallas_call | solution.py:386
  153.9 20.0 %attend.3 = (bf16[1,4,144,512]{3,2,1,0:T(8,128)(2,1)}, bf16[1,4,512,512]{3,2,1,0:T(8,128)(2,1)}, f32[1,4,512,512]{3,2,1,0:T(8,128)}) custom-call(bf16[1,4,512,1536]{3,2,1,0:T(8,128)(2,1)} %fusion.22.q_ref, bf16[1,2048,1536]{2,1,0:T(8,128)(2,1)} %bitcast.132, ...), custom_call_target="tpu_custom_call", output_to_operand_aliasing={{1}: (2, {}), {2}: (3, {})} | custom-call | flops 67108864 | bytes 147456 | tf_op jit(solution)/shard_map/attend/pallas_call | solution.py:386
  176.7 5.2 copy.104
  182.5 7.3 %collective-permute-done.23.refs_5_ = bf16[1,4,144,512]{3,2,1,0:T(8,128)(2,1)} collective-permute-done((bf16[1,4,144,512]{3,2,1,0:T(8,128)(2,1)}, bf16[1,4,144,512]{3,2,1,0:T(8,128)(2,1)}, u32[]{:S(2)}, u32[]{:S(2)}) %collective-permute-start.23) | collective-permute-done | bytes 589856 | tf_op jit(solution)/shard_map/ppermute | solution.py:44
  193.7 6.5 %build_weights.1 = (bf16[1076,1152]{1,0:T(8,128)(2,1)}, bf16[1152,1076]{1,0:T(8,128)(2,1)}, bf16[4,288,1152]{2,1,0:T(8,128)(2,1)}) custom-call(s32[1]{0:T(128)} %bitcast.me_ref, bf16[2,288,538]{2,1,0:T(8,128)(2,1)} %get-tuple-element.176.refs_0_, bf16[2,288,538]{2,1,0:T(8,128)(2,1)} %copy-done.16, bf16[2,288,538]{2,1,0:T(8,128)(2,1)} %copy-done.17, ...), custom_call_target="tpu_custom_call" | custom-call | bytes 160416 | tf_op jit(solution)/shard_map/build_weights/pallas_call | solution.py:247
  201.6 55.8 %middle.1 = (bf16[1,4,512,1152]{3,2,1,0:T(8,128)(2,1)}, bf16[1,4,512,1076]{3,2,1,0:T(8,128)(2,1)}, bf16[1,4,512,1076]{3,2,1,0:T(8,128)(2,1)}, bf16[1,4,512,1152]...) custom-call(s32[1]{0:T(128)} %bitcast.me_ref, ...), custom_call_target="tpu_custom_call" | custom-call | flops 402259968 | bytes 846496 | tf_op jit(solution)/shard_map/middle/pallas_call | solution.py:489
  266.0 9.9 %fusion.2 = bf16[1152,1076]{0,1:T(8,128)(2,1)} fusion(bf16[1,4,512,1076]{3,2,1,0:T(8,128)(2,1)} %get-tuple-element.195, bf16[1,4,512,1152]{3,2,1,0:T(8,128)(2,1)S(1)} %copy-done.82), kind=kOutput, calls=%fused_computation.8 | convolution fusion | flops 5078444544 | bytes 11604992 | tf_op jit(solution)/shard_map/ijld,ijlf->df/dot_general | solution.py:915
  275.8 5.2 copy.106.in_ref
  284.5 8.5 %collective-permute-done.30 = bf16[1,512,1152]{2,1,0:T(8,128)(2,1)} collective-permute-done((bf16[1,512,1152]{2,1,0:T(8,128)(2,1)}, bf16[1,512,1152]{2,1,0:T(8,128)(2,1)}, u32[]{:S(2)}, u32[]{:S(2)}) %collective-permute-start.30) | collective-permute-done | bytes 1179680 | tf_op jit(solution)/shard_map/ppermute | solution.py:44
  297.1 4.7 convert_reduce_fusion.3
  303.7 11.7 %fusion.3.in_ref = bf16[1152,1076]{1,0:T(8,128)(2,1)} fusion(bf16[1,4,512,1076]{3,2,1,0:T(8,128)(2,1)} %get-tuple-element.199, bf16[1,1,512,1152]{3,2,1,0:T(8,128)(2,1)} %bitcast.25, bf16[1,1,512,1152]{3,2,1,0:T(8,128)(2,1)} %bitcast.150, bf16[1,1,512,1152]{3,2,1,0:T(8,128)(2,1)} %bitcast.23, bf16[1,1,512,1152]{3,2,1,0:T(8,128)(2,1)} %bitcast.144), kind=kOutput, calls=%fused_computation.9 | convolution fusion | flops 5085522432 | bytes 11604992 | tf_op jit(solution)/shard_map/ijld,ijlf->df/dot_general | solution.py:929
  315.4 14.3 %collective-permute-done.32 = bf16[1,512,1152]{2,1,0:T(8,128)(2,1)} collective-permute-done((bf16[1,512,1152]{2,1,0:T(8,128)(2,1)}, bf16[1,512,1152]{2,1,0:T(8,128)(2,1)}, u32[]{:S(2)}, u32[]{:S(2)}) %collective-permute-start.32) | collective-permute-done | bytes 1179680 | tf_op jit(solution)/shard_map/ppermute | solution.py:44
  333.6 4.6 pad_maximum_fusion.2.grad_ref
  338.1 8.6 %mixed_back.1 = bf16[1,4,512,512]{3,2,1,0:T(8,128)(2,1)} custom-call(bf16[1,4,512,1152]{3,2,1,0:T(8,128)(2,1)} %pad_maximum_fusion.2.grad_ref, bf16[1152,512]{1,0:T(8,128)(2,1)} %convolution_convert_fusion.w_ref, f32[1,4,512,512]{3,2,1,0:T(8,128)} %get-tuple-element.201.exact_ref), custom_call_target="tpu_custom_call" | custom-call | flops 18874368 | bytes 190464 | tf_op jit(solution)/shard_map/mixed_back/pallas_call | solution.py:545
  355.0 5.0 fusion.31
  366.3 12.8 %reduce-scatter.3.cloned.1.call-done = bf16[1,144,1076]{2,1,0:T(8,128)(2,1)} async-done(((bf16[8,144,1076]{2,1,0:T(8,128)(2,1)}), bf16[1,144,1076]{2,1,0:T(8,128)(2,1)}) %reduce-scatter.3.cloned.1.call-update) | async-done | bytes 309904 | tf_op jit(solution)/shard_map/reduce_scatter | solution.py:804
  379.2 25.6 %attend_back.2 = (bf16[1,2048,256]{2,1,0:T(8,128)(2,1)}, bf16[1,2048,256]{2,1,0:T(8,128)(2,1)}, bf16[1,2048,256]{2,1,0:T(8,128)(2,1)}) custom-call(bf16[1,2048,512]{2,1,0:T(8,128)(2,1)} %bitcast.138, bf16[1,2048,512]{2,1,0:T(8,128)(2,1)} %bitcast.140, bf16[1,2048,1536]{2,1,0:T(8,128)(2,1)} %bitcast.133, bf16[1,2048,1536]{2,1,0:T(8,128)(2,1)} %bitcast.134), custom_call_target="tpu_custom_call" | custom-call | flops 167772160 | bytes 229376 | tf_op jit(solution)/shard_map/attend_back/pallas_call | solution.py:607
  417.0 25.9 %attend_back.3 = (bf16[1,2048,256]{2,1,0:T(8,128)(2,1)}, bf16[1,2048,256]{2,1,0:T(8,128)(2,1)}, bf16[1,2048,256]{2,1,0:T(8,128)(2,1)}) custom-call(bf16[1,2048,512]{2,1,0:T(8,128)(2,1)} %bitcast.139, bf16[1,2048,512]{2,1,0:T(8,128)(2,1)} %bitcast.141, bf16[1,2048,1536]{2,1,0:T(8,128)(2,1)} %bitcast.135, bf16[1,2048,1536]{2,1,0:T(8,128)(2,1)} %bitcast.136), custom_call_target="tpu_custom_call" | custom-call | flops 167772160 | bytes 229376 | tf_op jit(solution)/shard_map/attend_back/pallas_call | solution.py:607
  443.8 29.9 %project_back.1 = (bf16[1,512,1152]{2,1,0:T(8,128)(2,1)}, bf16[1,512,1152]{2,1,0:T(8,128)(2,1)}, bf16[1,512,1152]{2,1,0:T(8,128)(2,1)}, bf16[1,512,1152]{2,1,0:T...) custom-call(bf16[1,4,512,256]{3,2,1,0:T(8,128)(2,1)} %bitcast.151, ...), custom_call_target="tpu_custom_call" | custom-call | flops 113246208 | bytes 301056 | tf_op jit(solution)/shard_map/project_back/pallas_call | solution.py:682
  490.6 7.2 %collective-permute-done.43 = bf16[4,144,288]{2,1,0:T(8,128)(2,1)} collective-permute-done((bf16[4,144,288]{2,1,0:T(8,128)(2,1)}, bf16[4,144,288]{2,1,0:T(8,128)(2,1)}, u32[]{:S(2)}, u32[]{:S(2)}) %collective-permute-start.43) | collective-permute-done | bytes 331808 | tf_op jit(solution)/shard_map/ppermute | solution.py:116
  524.0 6.2 %collective-permute-done.51 = bf16[4,144,288]{2,1,0:T(8,128)(2,1)S(1)} collective-permute-done((bf16[4,144,288]{2,1,0:T(8,128)(2,1)S(1)}, bf16[4,144,288]{2,1,0:T(8,128)(2,1)S(1)}, u32[]{:S(2)}, u32[]{:S(2)}) %collective-permute-start.51) | collective-permute-done | bytes 331808 | tf_op jit(solution)/shard_map/ppermute | solution.py:116
  539.5 5.1 collective-permute-done.55
  546.1 4.5 collective-permute-done.42
  (385 shorter events, 161.9 us)
Async XLA Ops:
  7.2 87.5 %all-gather.6.cloned.1.call-start = ((), (), s32[]{:S(2)}) async-start(), calls=%async_computation.5 | async-start | bytes 3981312 | tf_op jit(solution)/shard_map/all_gather | solution.py:750
  10.2 166.5 %all-gather.4.cloned.1.call-start = ((), (), s32[]{:S(2)}) async-start(), calls=%async_computation.2 | async-start | bytes 2985984 | tf_op jit(solution)/shard_map/all_gather | solution.py:759
  10.3 41.7 %collective-permute-start.1 = (bf16[1,512,1152]{2,1,0:T(8,128)(2,1)}, bf16[1,512,1152]{2,1,0:T(8,128)(2,1)}, u32[]{:S(2)}, u32[]{:S(2)}) collective-permute-start(bf16[1,512,1152]{2,1,0:T(8,128)(2,1)} %param.21), channel_id=1, source_target_pairs={{0,16},{8,24},{16,0},{24,8},{1,17},{9,25},{17,1},{25,9},{2,18},{10... | collective-permute-start | bytes 3538952 | tf_op jit(solution)/shard_map/ppermute | solution.py:44
  44.9 43.9 %collective-permute-start = (bf16[1,512,1152]{2,1,0:T(8,128)(2,1)}, bf16[1,512,1152]{2,1,0:T(8,128)(2,1)}, u32[]{:S(2)}, u32[]{:S(2)}) collective-permute-start(bf16[1,512,1152]{2,1,0:T(8,128)(2,1)} %param.21), channel_id=1, source_target_pairs={{0,8},{8,0},{16,24},{24,16},{1,9},{9,1},{17,25},{25,17},{2,10},{10... | collective-permute-start | bytes 3538952 | tf_op jit(solution)/shard_map/ppermute | solution.py:44
  49.9 19.5 %collective-permute-start.10 = (bf16[2240]{0:T(1024)(128)(2,1)S(1)}, bf16[2240]{0:T(1024)(128)(2,1)S(1)}, u32[]{:S(2)}, u32[]{:S(2)}) collective-permute-start(bf16[2240]{0:T(1024)(128)(2,1)S(1)} %concatenate.72), channel_id=1, source_target_pairs={{0,16},{8,24},{16,0},{24,8},{1,17},{9,25},{17,1},{25,9},{2,18},{10... | collective-permute-start | bytes 13448 | tf_op jit(solution)/shard_map/ppermute | solution.py:44
  50.5 328.6 %reduce-scatter.3.cloned.1.call-start = ((), (), s32[]{:S(2)}) async-start(), calls=%async_computation.3 | async-start | bytes 2985984 | tf_op jit(solution)/shard_map/reduce_scatter | solution.py:804
  50.8 20.0 %collective-permute-start.12 = (bf16[2240]{0:T(1024)(128)(2,1)S(1)}, bf16[2240]{0:T(1024)(128)(2,1)S(1)}, u32[]{:S(2)}, u32[]{:S(2)}) collective-permute-start(bf16[2240]{0:T(1024)(128)(2,1)S(1)} %concatenate.72), channel_id=1, source_target_pairs={{0,8},{8,0},{16,24},{24,16},{1,9},{9,1},{17,25},{25,17},{2,10},{10... | collective-permute-start | bytes 13448 | tf_op jit(solution)/shard_map/ppermute | solution.py:44
  66.1 22.8 %collective-permute-start.9 = (bf16[1,512,1152]{2,1,0:T(8,128)(2,1)}, bf16[1,512,1152]{2,1,0:T(8,128)(2,1)}, u32[]{:S(2)}, u32[]{:S(2)}) collective-permute-start(bf16[1,512,1152]{2,1,0:T(8,128)(2,1)} %collective-permute-done.1), channel_id=1, source_target_pairs={{0,8},{8,0},{16,24},{24,16},{1,9},{9,1},{17,25},{25,17},{2,10},{10... | collective-permute-start | bytes 3538952 | tf_op jit(solution)/shard_map/ppermute | solution.py:44
  72.6 32.9 %collective-permute-start.13 = (bf16[1,512,1152]{2,1,0:T(8,128)(2,1)S(1)}, bf16[1,512,1152]{2,1,0:T(8,128)(2,1)S(1)}, u32[]{:S(2)}, u32[]{:S(2)}) collective-permute-start(bf16[1,512,1152]{2,1,0:T(8,128)(2,1)S(1)} %copy-done.4), channel_id=1, source_target_pairs={{0,16},{8,24},{16,0},{24,8},{1,17},{9,25},{17,1},{25,9},{2,18},{10... | collective-permute-start | bytes 3538952 | tf_op jit(solution)/shard_map/ppermute | solution.py:44
  103.4 50.4 %collective-permute-start.17 = (bf16[288,1152]{1,0:T(8,128)(2,1)S(1)}, bf16[288,1152]{1,0:T(8,128)(2,1)S(1)}, u32[]{:S(2)}, u32[]{:S(2)}) collective-permute-start(bf16[288,1152]{1,0:T(8,128)(2,1)S(1)} %copy-done.19), channel_id=1, source_target_pairs={{0,8},{8,0},{16,24},{24,16},{1,9},{9,1},{17,25},{25,17},{2,10},{10... | collective-permute-start | bytes 1990664 | tf_op jit(solution)/shard_map/ppermute | solution.py:44
  103.5 25.6 %collective-permute-start.14 = (bf16[2,288,538]{2,1,0:T(8,128)(2,1)}, bf16[2,288,538]{2,1,0:T(8,128)(2,1)S(1)}, u32[]{:S(2)}, u32[]{:S(2)}) collective-permute-start(bf16[2,288,538]{2,1,0:T(8,128)(2,1)} %get-tuple-element.167), channel_id=1, source_target_pairs={{0,8},{8,0},{16,24},{24,16},{1,9},{9,1},{17,25},{25,17},{2,10},{10... | collective-permute-start | bytes 1859336 | tf_op jit(solution)/shard_map/ppermute | solution.py:44
  104.0 28.7 %collective-permute-start.15 = (bf16[2,288,538]{2,1,0:T(8,128)(2,1)}, bf16[2,288,538]{2,1,0:T(8,128)(2,1)S(1)}, u32[]{:S(2)}, u32[]{:S(2)}) collective-permute-start(bf16[2,288,538]{2,1,0:T(8,128)(2,1)} %get-tuple-element.168), channel_id=1, source_target_pairs={{0,16},{8,24},{16,0},{24,8},{1,17},{9,25},{17,1},{25,9},{2,18},{10... | collective-permute-start | bytes 1859336 | tf_op jit(solution)/shard_map/ppermute | solution.py:44
  105.5 47.7 %collective-permute-start.16 = (bf16[2,288,538]{2,1,0:T(8,128)(2,1)}, bf16[2,288,538]{2,1,0:T(8,128)(2,1)S(1)}, u32[]{:S(2)}, u32[]{:S(2)}) collective-permute-start(bf16[2,288,538]{2,1,0:T(8,128)(2,1)} %get-tuple-element.169), channel_id=1, source_target_pairs={{0,24},{8,16},{16,8},{24,0},{1,25},{9,17},{17,9},{25,1},{2,26},{10... | collective-permute-start | bytes 1859336 | tf_op jit(solution)/shard_map/ppermute | solution.py:44
  116.9 37.0 %collective-permute-start.19 = (bf16[288,1152]{1,0:T(8,128)(2,1)S(1)}, bf16[288,1152]{1,0:T(8,128)(2,1)S(1)}, u32[]{:S(2)}, u32[]{:S(2)}) collective-permute-start(bf16[288,1152]{1,0:T(8,128)(2,1)S(1)} %collective-permute-done.18.refs_6_), channel_id=1, source_target_pairs={{0,8},{8,0},{16,24},{24,16},{1,9},{9,1},{17,25},{25,17},{2,10},{10... | collective-permute-start | bytes 1990664 | tf_op jit(solution)/shard_map/ppermute | solution.py:44
  129.2 53.2 %collective-permute-start.26 = (bf16[1,512,1152]{2,1,0:T(8,128)(2,1)S(1)}, bf16[1,512,1152]{2,1,0:T(8,128)(2,1)}, u32[]{:S(2)}, u32[]{:S(2)}) collective-permute-start(bf16[1,512,1152]{2,1,0:T(8,128)(2,1)S(1)} %copy-done.4), channel_id=1, source_target_pairs={{0,8},{8,0},{16,24},{24,16},{1,9},{9,1},{17,25},{25,17},{2,10},{10... | collective-permute-start | bytes 3538952 | tf_op jit(solution)/shard_map/ppermute | solution.py:44
  133.5 56.3 %collective-permute-start.27 = (bf16[1,512,1152]{2,1,0:T(8,128)(2,1)S(1)}, bf16[1,512,1152]{2,1,0:T(8,128)(2,1)}, u32[]{:S(2)}, u32[]{:S(2)}) collective-permute-start(bf16[1,512,1152]{2,1,0:T(8,128)(2,1)S(1)} %collective-permute-done.13), channel_id=1, source_target_pairs={{0,8},{8,0},{16,24},{24,16},{1,9},{9,1},{17,25},{25,17},{2,10},{10... | collective-permute-start | bytes 3538952 | tf_op jit(solution)/shard_map/ppermute | solution.py:44
  153.3 28.7 %collective-permute-start.22 = (bf16[1,4,144,512]{3,2,1,0:T(8,128)(2,1)}, bf16[1,4,144,512]{3,2,1,0:T(8,128)(2,1)}, u32[]{:S(2)}, u32[]{:S(2)}) collective-permute-start(bf16[1,4,144,512]{3,2,1,0:T(8,128)(2,1)} %get-tuple-element.163.refs_0_), channel_id=1, source_target_pairs={{0,16},{8,24},{16,0},{24,8},{1,17},{9,25},{17,1},{25,9},{2,18},{10... | collective-permute-start | bytes 1769480 | tf_op jit(solution)/shard_map/ppermute | solution.py:44
  257.9 35.1 %collective-permute-start.28 = (bf16[1,512,1152]{2,1,0:T(8,128)(2,1)}, bf16[1,512,1152]{2,1,0:T(8,128)(2,1)}, u32[]{:S(2)}, u32[]{:S(2)}) collective-permute-start(bf16[1,512,1152]{2,1,0:T(8,128)(2,1)} %get-tuple-element.189), channel_id=1, source_target_pairs={{0,8},{8,0},{16,24},{24,16},{1,9},{9,1},{17,25},{25,17},{2,10},{10... | collective-permute-start | bytes 3538952 | tf_op jit(solution)/shard_map/ppermute | solution.py:44
  264.4 28.6 %collective-permute-start.30 = (bf16[1,512,1152]{2,1,0:T(8,128)(2,1)}, bf16[1,512,1152]{2,1,0:T(8,128)(2,1)}, u32[]{:S(2)}, u32[]{:S(2)}) collective-permute-start(bf16[1,512,1152]{2,1,0:T(8,128)(2,1)} %add_convert_fusion.8), channel_id=1, source_target_pairs={{0,16},{8,24},{16,0},{24,8},{1,17},{9,25},{17,1},{25,9},{2,18},{10... | collective-permute-start | bytes 3538952 | tf_op jit(solution)/shard_map/ppermute | solution.py:44
  301.9 27.8 %collective-permute-start.32 = (bf16[1,512,1152]{2,1,0:T(8,128)(2,1)}, bf16[1,512,1152]{2,1,0:T(8,128)(2,1)}, u32[]{:S(2)}, u32[]{:S(2)}) collective-permute-start(bf16[1,512,1152]{2,1,0:T(8,128)(2,1)} %get-tuple-element.198), channel_id=1, source_target_pairs={{0,16},{8,24},{16,0},{24,8},{1,17},{9,25},{17,1},{25,9},{2,18},{10... | collective-permute-start | bytes 3538952 | tf_op jit(solution)/shard_map/ppermute | solution.py:44
  303.5 30.1 %collective-permute-start.31 = (bf16[1,512,1152]{2,1,0:T(8,128)(2,1)}, bf16[1,512,1152]{2,1,0:T(8,128)(2,1)}, u32[]{:S(2)}, u32[]{:S(2)}) collective-permute-start(bf16[1,512,1152]{2,1,0:T(8,128)(2,1)} %get-tuple-element.198), channel_id=1, source_target_pairs={{0,8},{8,0},{16,24},{24,16},{1,9},{9,1},{17,25},{25,17},{2,10},{10... | collective-permute-start | bytes 3538952 | tf_op jit(solution)/shard_map/ppermute | solution.py:44
  303.5 213.5 %reduce-scatter.5.cloned.1.call-start = ((), (), s32[]{:S(2)}) async-start(), calls=%async_computation.4 | async-start | bytes 3317760 | tf_op jit(solution)/shard_map/reduce_scatter | solution.py:1015
  353.1 51.6 %collective-permute-start.36 = (bf16[2,288,538]{2,1,0:T(8,128)(2,1)}, bf16[2,288,538]{2,1,0:T(8,128)(2,1)}, u32[]{:S(2)}, u32[]{:S(2)}) collective-permute-start(bf16[2,288,538]{2,1,0:T(8,128)(2,1)} %get-tuple-element.222), channel_id=1, source_target_pairs={{0,8},{8,0},{16,24},{24,16},{1,9},{9,1},{17,25},{25,17},{2,10},{10... | collective-permute-start | bytes 1859336 | tf_op jit(solution)/shard_map/ppermute | solution.py:44
  353.1 51.6 %collective-permute-start.37 = (bf16[2,288,538]{2,1,0:T(8,128)(2,1)}, bf16[2,288,538]{2,1,0:T(8,128)(2,1)}, u32[]{:S(2)}, u32[]{:S(2)}) collective-permute-start(bf16[2,288,538]{2,1,0:T(8,128)(2,1)} %get-tuple-element.223), channel_id=1, source_target_pairs={{0,16},{8,24},{16,0},{24,8},{1,17},{9,25},{17,1},{25,9},{2,18},{10... | collective-permute-start | bytes 1859336 | tf_op jit(solution)/shard_map/ppermute | solution.py:44
  354.7 50.1 %collective-permute-start.38 = (bf16[2,288,538]{2,1,0:T(8,128)(2,1)}, bf16[2,288,538]{2,1,0:T(8,128)(2,1)}, u32[]{:S(2)}, u32[]{:S(2)}) collective-permute-start(bf16[2,288,538]{2,1,0:T(8,128)(2,1)} %get-tuple-element.224), channel_id=1, source_target_pairs={{0,24},{8,16},{16,8},{24,0},{1,25},{9,17},{17,9},{25,1},{2,26},{10... | collective-permute-start | bytes 1859336 | tf_op jit(solution)/shard_map/ppermute | solution.py:44
  408.4 35.4 %collective-permute-start.39 = (bf16[1,512,1152]{2,1,0:T(8,128)(2,1)}, bf16[1,512,1152]{2,1,0:T(8,128)(2,1)}, u32[]{:S(2)}, u32[]{:S(2)}) collective-permute-start(bf16[1,512,1152]{2,1,0:T(8,128)(2,1)} %add_convert_fusion.7), channel_id=1, source_target_pairs={{0,16},{8,24},{16,0},{24,8},{1,17},{9,25},{17,1},{25,9},{2,18},{10... | collective-permute-start | bytes 3538952 | tf_op jit(solution)/shard_map/ppermute | solution.py:44
  414.6 98.7 %collective-permute-start.34 = (bf16[1,512,1152]{2,1,0:T(8,128)(2,1)}, bf16[1,512,1152]{2,1,0:T(8,128)(2,1)}, u32[]{:S(2)}, u32[]{:S(2)}) collective-permute-start(bf16[1,512,1152]{2,1,0:T(8,128)(2,1)} %get-tuple-element.208), channel_id=1, source_target_pairs={{0,8},{8,0},{16,24},{24,16},{1,9},{9,1},{17,25},{25,17},{2,10},{10... | collective-permute-start | bytes 3538952 | tf_op jit(solution)/shard_map/ppermute | solution.py:44
  478.8 21.9 %collective-permute-start.48 = (f32[6,288]{1,0:T(8,128)}, f32[6,288]{1,0:T(8,128)}, u32[]{:S(2)}, u32[]{:S(2)}) collective-permute-start(f32[6,288]{1,0:T(8,128)} %bitcast.128), channel_id=1, source_target_pairs={{0,24},{8,16},{16,8},{24,0},{1,25},{9,17},{17,9},{25,1},{2,26},{10... | collective-permute-start | bytes 20744 | tf_op jit(solution)/shard_map/ppermute | solution.py:44
  479.4 22.4 %collective-permute-start.46 = (f32[6,288]{1,0:T(8,128)}, f32[6,288]{1,0:T(8,128)}, u32[]{:S(2)}, u32[]{:S(2)}) collective-permute-start(f32[6,288]{1,0:T(8,128)} %get-tuple-element.283), channel_id=1, source_target_pairs={{0,8},{8,0},{16,24},{24,16},{1,9},{9,1},{17,25},{25,17},{2,10},{10... | collective-permute-start | bytes 20744 | tf_op jit(solution)/shard_map/ppermute | solution.py:44
  479.5 22.4 %collective-permute-start.47 = (f32[6,288]{1,0:T(8,128)}, f32[6,288]{1,0:T(8,128)}, u32[]{:S(2)}, u32[]{:S(2)}) collective-permute-start(f32[6,288]{1,0:T(8,128)} %get-tuple-element.324), channel_id=1, source_target_pairs={{0,16},{8,24},{16,0},{24,8},{1,17},{9,25},{17,1},{25,9},{2,18},{10... | collective-permute-start | bytes 20744 | tf_op jit(solution)/shard_map/ppermute | solution.py:44
  512.5 21.6 %collective-permute-start.40 = (bf16[1,512,1152]{2,1,0:T(8,128)(2,1)}, bf16[1,512,1152]{2,1,0:T(8,128)(2,1)}, u32[]{:S(2)}, u32[]{:S(2)}) collective-permute-start(bf16[1,512,1152]{2,1,0:T(8,128)(2,1)} %get-tuple-element.246), channel_id=1, source_target_pairs={{0,8},{8,0},{16,24},{24,16},{1,9},{9,1},{17,25},{25,17},{2,10},{10... | collective-permute-start | bytes 3538952 | tf_op jit(solution)/shard_map/ppermute | solution.py:44
  523.5 27.1 %collective-permute-start.42 = (bf16[1,512,1152]{2,1,0:T(8,128)(2,1)S(1)}, bf16[1,512,1152]{2,1,0:T(8,128)(2,1)S(1)}, u32[]{:S(2)}, u32[]{:S(2)}) collective-permute-start(bf16[1,512,1152]{2,1,0:T(8,128)(2,1)S(1)} %add_convert_fusion.5), channel_id=1, source_target_pairs={{0,16},{8,24},{16,0},{24,8},{1,17},{9,25},{17,1},{25,9},{2,18},{10... | collective-permute-start | bytes 3538952 | tf_op jit(solution)/shard_map/ppermute | solution.py:44
  (112 other events, 1939.3 us)
Sparse Core Ops, SparseCore 0:
  10.8 76.3 all-gather.5
  89.4 56.3 all-gather.3
  303.6 75.5 reduce-scatter.2
  408.5 71.5 reduce-scatter.4
